TPU v7x, 32 devices: a whole 2x2x4 slice. The times are simulated.
32 devices in a mesh: dp: 8 (over y, x, core), tensor: 4 (over z).
Axes of the slice: x: 2, y: 2, z: 4, core: 2. Of those that a mesh axis runs over, the one named last changes fastest.
Arguments:
- tokens: bfloat16 [2048, 1152], P('dp'), may hold values from -6 to 6
- conditioning: bfloat16 [3, 1152], replicated, may hold values from -6 to 6
- latent_len: int32 [3], replicated, may hold values from 1 to 1024, 2048 in all
- w_ada: bfloat16 [1152, 6, 1152], P('dp', None, 'tensor'), may hold values from -0.1875 to 0.1875
- b_ada: bfloat16 [6, 1152], P(None, 'tensor'), may hold values from -1.75 to 1.75
- w_qkv: bfloat16 [1152, 3, 1152], P('dp', None, 'tensor'), may hold values from -0.1875 to 0.1875
- b_qv: bfloat16 [2, 1152], P(None, 'tensor'), may hold values from -1.75 to 1.75
- w_proj: bfloat16 [1152, 1152], P('tensor', 'dp'), may hold values from -1.5 to 1.5
- b_proj: bfloat16 [1152], replicated, may hold values from -1.75 to 1.75
- w_fc1: bfloat16 [1152, 4608], P('dp', 'tensor'), may hold values from -0.1875 to 0.1875
- b_fc1: bfloat16 [4608], P('tensor'), may hold values from -1.75 to 1.75
- w_fc2: bfloat16 [4608, 1152], P('tensor', 'dp'), may hold values from -0.09375 to 0.09375
- b_fc2: bfloat16 [1152], replicated, may hold values from -1.75 to 1.75
- cotangent: bfloat16 [2048, 1152], P('dp'), may hold values from -6 to 6
Outputs:
- block_out: bfloat16 [2048, 1152], P('dp')
- grad_tokens: float32 [2048, 1152], P('dp')
- grad_cond: float32 [3, 1152], replicated
- grad_w_ada: float32 [1152, 6, 1152], P('dp', None, 'tensor')
- grad_b_ada: float32 [6, 1152], P(None, 'tensor')
- grad_w_qkv: float32 [1152, 3, 1152], P('dp', None, 'tensor')
- grad_b_qv: float32 [2, 1152], P(None, 'tensor')
- grad_w_proj: float32 [1152, 1152], P('tensor', 'dp')
- grad_b_proj: float32 [1152], replicated
- grad_w_fc1: float32 [1152, 4608], P('dp', 'tensor')
- grad_b_fc1: float32 [4608], P('tensor')
- grad_w_fc2: float32 [4608, 1152], P('tensor', 'dp')
- grad_b_fc2: float32 [1152], replicated
Inputs may be any that keep to these rules, and one draw needn't show every extreme that they name: `latent_len`: the 3 latents lie end to end and fill all 2048 tokens; the longest has exactly 1024 tokens.
All inputs are finite; a program needn't handle non-finite values.
Results may differ from a plain program's by a relative error of at most 0.012.
The roundings to bfloat16 on the way count: a program that leaves them out, or rounds other values in their place, can miss the bound.
Values may be sent and summed in bfloat16 or wider, within the bound.
No kernel may reach another device: no remote copies, remote signals or barrier semaphores. Data moves between devices by JAX's collectives and lax.ppermute only.
A program may use at most 192 MiB of HBM per device.

v0:
```python
from functools import partial
import math

import jax
import jax.numpy as jnp
from jax import lax
from jax.sharding import PartitionSpec as P

DH = 72
SEQ = 1024


NORM_EPS = 1e-06
HIGHEST_PRECISION = lax.Precision.HIGHEST


def from_behind(block, axis, distance):
    devices = range(lax.axis_size(axis))
    route = [(i - distance, i) for i in devices if i - distance in devices]
    return lax.ppermute(block, axis, route)


def layer_norm(values):
    average = jnp.mean(values, axis=-1, keepdims=True)
    centred = values - average
    spread = jnp.mean(centred * centred, axis=-1, keepdims=True)
    return centred * lax.rsqrt(spread + NORM_EPS)


def modulated(values, shift_part, scales):
    return layer_norm(values) * (1.0 + scales) + shift_part


def latent_index(latent_len, first_row, row_count, token_total):
    positions = first_row + jnp.arange(row_count, dtype=jnp.int32)
    latent_ends = jnp.cumsum(latent_len, dtype=jnp.int32)
    found_ids = jnp.sum(
        (positions[:, None] >= latent_ends[None, :]).astype(jnp.int32), axis=1, dtype=jnp.int32
    )
    inside = (positions >= 0) & (positions < token_total)
    return jnp.where(inside, found_ids, -1)


def local(
    tokens,
    conditioning,
    latent_len,
    w_ada,
    b_ada,
    w_qkv,
    b_qv,
    w_proj,
    b_proj,
    w_fc1,
    b_fc1,
    w_fc2,
    b_fc2,
    cotangent,
):
    row_count = tokens.shape[0]
    model_width = tokens.shape[1]
    local_width = w_qkv.shape[2]
    head_count = local_width // DH
    latent_count = conditioning.shape[0]
    token_total = row_count * lax.axis_size("dp")
    reach_blocks = (SEQ - 2) // row_count + 1
    score_scale = 1.0 / math.sqrt(DH)
    full_ada, full_qkv, full_proj, full_fc1, full_fc2 = (
        lax.all_gather(w_ada, "dp", axis=0, tiled=True),
        lax.all_gather(w_qkv, "dp", axis=0, tiled=True),
        lax.all_gather(w_proj, "dp", axis=1, tiled=True),
        lax.all_gather(w_fc1, "dp", axis=0, tiled=True),
        lax.all_gather(w_fc2, "dp", axis=1, tiled=True),
    )
    cond_float = conditioning.astype(jnp.float32)
    activated = jax.nn.silu(cond_float).astype(jnp.bfloat16)
    mod_part = (
        jnp.einsum("ld,dkf->lkf", activated, full_ada, preferred_element_type=jnp.float32)
        + b_ada.astype(jnp.float32)[None]
    )
    modulation = lax.all_gather(mod_part, "tensor", axis=2, tiled=True)
    first_row = lax.axis_index("dp") * row_count
    own_ids = latent_index(latent_len, first_row, row_count, token_total)
    one_hot = (own_ids[:, None] == jnp.arange(latent_count, dtype=jnp.int32)[None, :]).astype(
        jnp.float32
    )
    per_token = jnp.dot(
        one_hot, modulation.reshape(latent_count, 6 * model_width), precision=HIGHEST_PRECISION
    )
    per_token = per_token.reshape(row_count, 6, model_width)
    inputs = tokens.astype(jnp.float32)
    hidden_one = modulated(inputs, per_token[:, 0], per_token[:, 1]).astype(jnp.bfloat16)
    bias_three = jnp.stack([b_qv[0], jnp.zeros_like(b_qv[0]), b_qv[1]]).astype(jnp.float32)
    projected = (
        jnp.einsum("td,dkf->tkf", hidden_one, full_qkv, preferred_element_type=jnp.float32)
        + bias_three[None]
    )
    projected = projected.astype(jnp.bfloat16)
    queries = projected[:, 0]
    key_value = projected[:, 1:]
    pieces = []
    window_ids = []
    for offset in range(-reach_blocks, reach_blocks + 1):
        if offset == 0:
            pieces.append(key_value)
        else:
            pieces.append(from_behind(key_value, "dp", -offset))
        window_ids.append(
            latent_index(latent_len, first_row + offset * row_count, row_count, token_total)
        )
    window_kv = jnp.concatenate(pieces, axis=0)
    key_ids = jnp.concatenate(window_ids, axis=0)
    window_rows = window_kv.shape[0]
    allowed = own_ids[:, None] == key_ids[None, :]
    query_heads = jnp.transpose(queries.reshape(row_count, head_count, DH), (1, 0, 2))
    key_heads = jnp.transpose(window_kv[:, 0].reshape(window_rows, head_count, DH), (1, 0, 2))
    value_heads = jnp.transpose(window_kv[:, 1].reshape(window_rows, head_count, DH), (1, 0, 2))

    def head_scores(query_head, key_head):
        raw_scores = (
            jnp.einsum("qe,ke->qk", query_head, key_head, preferred_element_type=jnp.float32)
            * score_scale
        )
        return jnp.where(allowed, raw_scores, -1e30)

    def forward_head(operands):
        query_head, key_head, value_head = operands
        scores = head_scores(query_head, key_head)
        largest = jnp.max(scores, axis=1, keepdims=True)
        weights_raw = jnp.exp(scores - largest)
        totals = jnp.sum(weights_raw, axis=1, keepdims=True)
        probabilities = (weights_raw / totals).astype(jnp.bfloat16)
        mixed_head = jnp.einsum(
            "qk,ke->qe", probabilities, value_head, preferred_element_type=jnp.float32
        )
        return (mixed_head.astype(jnp.bfloat16), (largest + jnp.log(totals))[:, 0])

    head_out, log_totals = lax.map(forward_head, (query_heads, key_heads, value_heads))
    attended = jnp.transpose(head_out, (1, 0, 2)).reshape(row_count, local_width)

    def over_heads(partial_sum):
        shares = lax.psum_scatter(partial_sum, "tensor", scatter_dimension=0, tiled=True)
        return lax.all_gather(shares, "tensor", axis=0, tiled=True)

    attn_out = over_heads(
        jnp.dot(attended, full_proj, preferred_element_type=jnp.float32)
    ) + b_proj.astype(jnp.float32)
    residual_mid = inputs + per_token[:, 2] * attn_out
    hidden_two = modulated(residual_mid, per_token[:, 3], per_token[:, 4]).astype(jnp.bfloat16)
    pre_act = jnp.dot(hidden_two, full_fc1, preferred_element_type=jnp.float32) + b_fc1.astype(
        jnp.float32
    )
    gelu_out = jax.nn.gelu(pre_act, approximate=True).astype(jnp.bfloat16)
    mlp_out = over_heads(
        jnp.dot(gelu_out, full_fc2, preferred_element_type=jnp.float32)
    ) + b_fc2.astype(jnp.float32)
    result = (residual_mid + per_token[:, 5] * mlp_out).astype(jnp.bfloat16)
    back_ada, back_qkv, back_proj, back_fc1, back_fc2 = (
        full_ada,
        full_qkv,
        full_proj,
        full_fc1,
        full_fc2,
    )

    def input_side(partial_sum):
        shares = lax.psum_scatter(partial_sum, "tensor", scatter_dimension=0, tiled=True)
        return lax.all_gather(shares, "tensor", axis=0, tiled=True)

    upstream = cotangent.astype(jnp.float32)
    d_mlp = (upstream * per_token[:, 5]).astype(jnp.bfloat16)
    d_gate_two = upstream * mlp_out
    grad_b_fc2 = jnp.sum(d_mlp.astype(jnp.float32), axis=0)
    grad_w_fc2 = jnp.einsum("tf,td->fd", gelu_out, d_mlp, preferred_element_type=jnp.float32)
    d_gelu = jnp.einsum("td,fd->tf", d_mlp, back_fc2, preferred_element_type=jnp.float32)
    gelu_value, gelu_pull = jax.vjp(partial(jax.nn.gelu, approximate=True), pre_act)
    d_pre = gelu_pull(d_gelu)[0].astype(jnp.bfloat16)
    grad_b_fc1 = jnp.sum(d_pre.astype(jnp.float32), axis=0)
    grad_w_fc1 = jnp.einsum("td,tf->df", hidden_two, d_pre, preferred_element_type=jnp.float32)
    d_hidden_two = input_side(
        jnp.einsum("tf,df->td", d_pre, back_fc1, preferred_element_type=jnp.float32)
    )
    norm_two, second_pull = jax.vjp(modulated, residual_mid, per_token[:, 3], per_token[:, 4])
    d_mid_norm, d_shift_two, d_scale_two = second_pull(d_hidden_two)
    d_mid = upstream + d_mid_norm
    d_attn = (d_mid * per_token[:, 2]).astype(jnp.bfloat16)
    d_gate_one = d_mid * attn_out
    grad_b_proj = jnp.sum(d_attn.astype(jnp.float32), axis=0)
    grad_w_proj = jnp.einsum("tf,td->fd", attended, d_attn, preferred_element_type=jnp.float32)
    d_attended = jnp.einsum(
        "td,fd->tf", d_attn, back_proj, preferred_element_type=jnp.float32
    ).astype(jnp.bfloat16)
    d_heads = jnp.transpose(d_attended.reshape(row_count, head_count, DH), (1, 0, 2))

    def backward_head(operands):
        query_head, key_head, value_head, d_head, log_total = operands
        scores = head_scores(query_head, key_head)
        probabilities = jnp.exp(scores - log_total[:, None])
        d_value = jnp.einsum(
            "qk,qe->ke",
            probabilities.astype(jnp.bfloat16),
            d_head,
            preferred_element_type=jnp.float32,
        )
        d_probs = jnp.einsum("qe,ke->qk", d_head, value_head, preferred_element_type=jnp.float32)
        inner_sum = jnp.sum(probabilities * d_probs, axis=1, keepdims=True)
        d_scores = (probabilities * (d_probs - inner_sum)).astype(jnp.bfloat16)
        d_query = (
            jnp.einsum("qk,ke->qe", d_scores, key_head, preferred_element_type=jnp.float32)
            * score_scale
        )
        d_key = (
            jnp.einsum("qk,qe->ke", d_scores, query_head, preferred_element_type=jnp.float32)
            * score_scale
        )
        return (d_query, d_key, d_value)

    d_query_heads, d_key_heads, d_value_heads = lax.map(
        backward_head, (query_heads, key_heads, value_heads, d_heads, log_totals)
    )
    d_queries = jnp.transpose(d_query_heads, (1, 0, 2)).reshape(row_count, local_width)
    d_keys = jnp.transpose(d_key_heads, (1, 0, 2)).reshape(window_rows, local_width)
    d_values = jnp.transpose(d_value_heads, (1, 0, 2)).reshape(window_rows, local_width)
    d_window = jnp.stack([d_keys, d_values], axis=1)
    d_key_value = d_window[reach_blocks * row_count : (reach_blocks + 1) * row_count]
    for offset in range(-reach_blocks, reach_blocks + 1):
        if offset != 0:
            sent_block = d_window[
                (offset + reach_blocks) * row_count : (offset + reach_blocks + 1) * row_count
            ]
            d_key_value = d_key_value + from_behind(sent_block, "dp", offset)
    d_projected = jnp.concatenate([d_queries[:, None], d_key_value], axis=1).astype(jnp.bfloat16)
    d_proj_float = d_projected.astype(jnp.float32)
    grad_b_qv = jnp.stack(
        [jnp.sum(d_proj_float[:, 0], axis=0), jnp.sum(d_proj_float[:, 2], axis=0)]
    )
    grad_w_qkv = jnp.einsum(
        "td,tkf->dkf", hidden_one, d_projected, preferred_element_type=jnp.float32
    )
    d_hidden_one = input_side(
        jnp.einsum("tkf,dkf->td", d_projected, back_qkv, preferred_element_type=jnp.float32)
    )
    norm_one, first_pull = jax.vjp(modulated, inputs, per_token[:, 0], per_token[:, 1])
    d_input_norm, d_shift_one, d_scale_one = first_pull(d_hidden_one)
    grad_tokens = d_mid + d_input_norm
    d_per_token = jnp.stack(
        [d_shift_one, d_scale_one, d_gate_one, d_shift_two, d_scale_two, d_gate_two], axis=1
    ).astype(jnp.bfloat16)
    tensor_start = lax.axis_index("tensor") * local_width
    d_mine = lax.dynamic_slice_in_dim(d_per_token, tensor_start, local_width, 2).astype(jnp.float32)
    d_latent = jnp.einsum("tl,tkf->lkf", one_hot, d_mine, precision=HIGHEST_PRECISION)
    grad_w_ada = jnp.einsum(
        "ld,lkf->dkf", activated.astype(jnp.float32), d_latent, precision=HIGHEST_PRECISION
    )
    grad_b_ada = jnp.sum(d_latent, axis=0)
    d_activated = jnp.einsum(
        "lkf,dkf->ld", d_latent, back_ada.astype(jnp.float32), precision=HIGHEST_PRECISION
    )
    d_activated = lax.psum(d_activated, ("dp", "tensor"))
    silu_value, silu_pull = jax.vjp(jax.nn.silu, cond_float)
    grad_cond = silu_pull(d_activated)[0]
    sent_ada, sent_qkv, sent_proj, sent_fc1, sent_fc2 = (
        lax.psum_scatter(grad_w_ada, "dp", scatter_dimension=0, tiled=True),
        lax.psum_scatter(grad_w_qkv, "dp", scatter_dimension=0, tiled=True),
        lax.psum_scatter(grad_w_proj, "dp", scatter_dimension=1, tiled=True),
        lax.psum_scatter(grad_w_fc1, "dp", scatter_dimension=0, tiled=True),
        lax.psum_scatter(grad_w_fc2, "dp", scatter_dimension=1, tiled=True),
    )
    bias_total = lax.psum((grad_b_ada, grad_b_qv, grad_b_proj, grad_b_fc1, grad_b_fc2), "dp")
    return (
        result,
        grad_tokens,
        grad_cond,
        sent_ada,
        bias_total[0],
        sent_qkv,
        bias_total[1],
        sent_proj,
        bias_total[2],
        sent_fc1,
        bias_total[3],
        sent_fc2,
        bias_total[4],
    )


def solution(mesh):
    in_specs = (
        P("dp", None),
        P(),
        P(),
        P("dp", None, "tensor"),
        P(None, "tensor"),
        P("dp", None, "tensor"),
        P(None, "tensor"),
        P("tensor", "dp"),
        P(),
        P("dp", "tensor"),
        P("tensor"),
        P("tensor", "dp"),
        P(),
        P("dp", None),
    )
    out_specs = (
        P("dp", None),
        P("dp", None),
        P(),
        P("dp", None, "tensor"),
        P(None, "tensor"),
        P("dp", None, "tensor"),
        P(None, "tensor"),
        P("tensor", "dp"),
        P(),
        P("dp", "tensor"),
        P("tensor"),
        P("tensor", "dp"),
        P(),
    )
    return jax.shard_map(local, mesh=mesh, in_specs=in_specs, out_specs=out_specs, check_vma=False)
```

profile of v0, /device:TPU:0, one launch (start us, length us, event | category | flops | bytes accessed | tf_op | source)
XLA Modules:
  0.0 933.1 jit_solution(14773621297947582617)
XLA Ops:
  11.7 42.4 %all-gather.9.cloned.1.call-done = bf16[1152,6,288]{2,0,1:T(8,128)(2,1)} async-done(((bf16[144,6,288]{2,0,1:T(8,128)(2,1)}), bf16[1152,6,288]{2,0,1:T(8,128)(2,1)}) %all-gather.9.cloned.1.call-update) | async-done | bytes 3981328 | tf_op jit(solution)/shard_map/all_gather | solution.py:69
  57.7 42.4 %all_gather.31 = f32[3,6,1152]{1,0,2:T(4,128)S(1)} all-gather(f32[3,6,288]{1,0,2:T(4,128)S(1)} %copy.48), channel_id=1, replica_groups=mesh['dp'=8,'tensor'=4] {'tensor'}, dimensions={2}, use_global_device_ids=true | all-gather | bytes 103680 | tf_op jit(solution)/shard_map/all_gather | solution.py:81
  118.7 21.6 %all_gather.33 = bf16[288,1152]{0,1:T(8,128)(2,1)} all-gather(bf16[288,144]{0,1:T(8,128)(2,1)S(1)} %copy-done.37), channel_id=1, replica_groups=mesh['dp'=8,'tensor'=4] {'dp'}, dimensions={1}, use_global_device_ids=true | all-gather | bytes 746496 | tf_op jit(solution)/shard_map/all_gather | solution.py:71
  149.0 9.0 collective-permute-done.5
  168.6 20.7 %while.28 = (s32[]{:T(128)}, bf16[4,256,72]{1,2,0:T(8,128)(2,1)S(1)}, f32[4,256]{1,0:T(4,128)}, bf16[4,256,72]{2,1,0:T(8,128)(2,1)S(1)}, bf16[4,2304,72]{2,1,0:T...) while((s32[]{:T(128)}, ...), condition=%wide.region_15.16_spmd.clone, body=%wide.region_12.15_spmd.clone.sunk | while | flops 175195904 | bytes 8385641 | solution.py:138
  192.3 37.3 %reduce-scatter.10.cloned.1.call-done = f32[64,1152]{1,0:T(8,128)} async-done(((f32[256,1152]{1,0:T(8,128)}), f32[64,1152]{1,0:T(8,128)}) %reduce-scatter.10.cloned.1.call-update) | async-done | bytes 294928 | tf_op jit(solution)/shard_map/reduce_scatter | solution.py:142
  231.7 28.6 %all-gather.13.cloned.1.call-done = f32[256,1152]{1,0:T(8,128)} async-done(((f32[64,1152]{1,0:T(8,128)}), f32[256,1152]{1,0:T(8,128)}) %all-gather.13.cloned.1.call-update) | async-done | bytes 1179664 | tf_op jit(solution)/shard_map/all_gather | solution.py:143
  266.7 24.7 %all-gather.17.cloned.1.call-done = bf16[1152,1152]{0,1:T(8,128)(2,1)} async-done(((bf16[1152,144]{0,1:T(8,128)(2,1)}), bf16[1152,1152]{0,1:T(8,128)(2,1)}) %all-gather.17.cloned.1.call-update) | async-done | bytes 2654224 | tf_op jit(solution)/shard_map/all_gather | solution.py:73
  295.2 28.3 %all-gather.15.cloned.1.call-done = bf16[1152,1152]{1,0:T(8,128)(2,1)} async-done(((bf16[144,1152]{1,0:T(8,128)(2,1)}), bf16[1152,1152]{1,0:T(8,128)(2,1)}) %all-gather.15.cloned.1.call-update) | async-done | bytes 2654224 | tf_op jit(solution)/shard_map/all_gather | solution.py:72
  323.4 5.4 convert_reduce_fusion.2
  333.0 3.9 fusion.128
  337.0 24.1 %reduce-scatter.14.cloned.1.call-done = f32[64,1152]{1,0:T(8,128)} async-done(((f32[256,1152]{1,0:T(8,128)}), f32[64,1152]{1,0:T(8,128)}) %reduce-scatter.14.cloned.1.call-update) | async-done | bytes 294928 | tf_op jit(solution)/shard_map/reduce_scatter | solution.py:167
  361.2 30.2 %reduce-scatter.12.cloned.1.call-done = f32[64,1152]{1,0:T(8,128)} async-done(((f32[256,1152]{1,0:T(8,128)}), f32[64,1152]{1,0:T(8,128)}) %reduce-scatter.12.cloned.1.call-update) | async-done | bytes 294928 | tf_op jit(solution)/shard_map/reduce_scatter | solution.py:142
  392.1 30.0 %all-gather.21.cloned.1.call-done = f32[256,1152]{1,0:T(8,128)} async-done(((f32[64,1152]{1,0:T(8,128)}), f32[256,1152]{1,0:T(8,128)}) %all-gather.21.cloned.1.call-update) | async-done | bytes 1179664 | tf_op jit(solution)/shard_map/all_gather | solution.py:168
  424.7 28.4 %all-gather.19.cloned.1.call-done = f32[256,1152]{1,0:T(8,128)} async-done(((f32[64,1152]{1,0:T(8,128)}), f32[256,1152]{1,0:T(8,128)}) %all-gather.19.cloned.1.call-update) | async-done | bytes 1179664 | tf_op jit(solution)/shard_map/all_gather | solution.py:143
  461.5 29.3 %while.29 = (s32[]{:T(128)}, bf16[4,256,72]{1,2,0:T(8,128)(2,1)}, f32[4,2304,72]{1,2,0:T(8,128)}, f32[4,2304,72]{1,2,0:T(8,128)}, bf16[4,256,72]{2,1,0:T(8,128)(...) while((s32[]{:T(128)}, bf16[4,256,72]{1,2,0:T(8,128)(2,1)}, ...), condition=%wide.region_25.26_spmd.clone, body=%wide.region_23.25_spmd.clone.sunk | while | flops 430755584 | bytes 27638988 | solution.py:218
  499.5 4.6 collective-permute-start.13
  507.9 4.1 collective-permute-done.10
  517.8 9.6 %collective-permute-done.14 = f32[256,2,288]{0,2,1:T(8,128)S(1)} collective-permute-done((f32[256,2,288]{0,2,1:T(8,128)S(1)}, f32[256,2,288]{0,2,1:T(8,128)S(1)}, u32[]{:S(2)}, u32[]{:S(2)}) %collective-permute-start.14) | collective-permute-done | bytes 589856 | tf_op jit(solution)/shard_map/ppermute | solution.py:20
  527.4 22.0 %collective-permute-done.15 = f32[256,2,288]{0,2,1:T(8,128)S(1)} collective-permute-done((f32[256,2,288]{0,2,1:T(8,128)S(1)}, f32[256,2,288]{0,2,1:T(8,128)S(1)}, u32[]{:S(2)}, u32[]{:S(2)}) %collective-permute-start.15) | collective-permute-done | bytes 589856 | tf_op jit(solution)/shard_map/ppermute | solution.py:20
  552.1 31.0 %reduce-scatter.16.cloned.1.call-done = f32[64,1152]{1,0:T(8,128)} async-done(((f32[256,1152]{1,0:T(8,128)}), f32[64,1152]{1,0:T(8,128)}) %reduce-scatter.16.cloned.1.call-update) | async-done | bytes 294928 | tf_op jit(solution)/shard_map/reduce_scatter | solution.py:167
  585.9 4.4 fusion.144
  591.3 4.7 fusion.127
  600.5 13.1 %all-gather.23.cloned.1.call-done = f32[256,1152]{1,0:T(8,128)} async-done(((f32[64,1152]{1,0:T(8,128)}), f32[256,1152]{1,0:T(8,128)}) %all-gather.23.cloned.1.call-update) | async-done | bytes 1179664 | tf_op jit(solution)/shard_map/all_gather | solution.py:168
  622.1 7.0 fusion.112
  631.3 25.7 %all-reduce = (f32[6,288]{1,0:T(8,128)}, f32[2,288]{1,0:T(2,128)}, f32[1152]{0:T(1024)}, f32[1152]{0:T(1024)}, f32[1152]{0:T(1024)}) all-reduce(f32[6,288]{1,0:T(8,128)} %get-tuple-element.243, f32[2,288]{1,0:T(2,128)S(1)} %pad_maximum_fusion.4, f32[1152]{0:T(1024)} %get-tuple-element.214, ...), channel_id=1, replica_groups=mesh['dp'=8,'tensor'=4] {'dp'}, use_global_device_ids=true, to_apply=%region_32.33 | all-reduce | flops 5760 | bytes 46080 | tf_op jit(solution)/shard_map/psum | solution.py:269
  657.0 6.7 convolution_bitcast_fusion.2
  663.7 39.3 %psum.42 = f32[3,1152]{1,0:T(4,128)S(1)} all-reduce(f32[3,1152]{1,0:T(4,128)S(1)} %convolution_bitcast_fusion.2), channel_id=1, replica_groups=mesh['dp'=8,'tensor'=4] {'dp','tensor'}, use_global_device_ids=true, to_apply=%region_29.30 | all-reduce | flops 3456 | bytes 27648 | tf_op jit(solution)/shard_map/psum | solution.py:259
  708.5 9.1 reduce-scatter.24.cloned.1.call-done
  717.7 61.2 %reduce-scatter.26.cloned.1.call-done = f32[1152,144]{0,1:T(8,128)} async-done(((f32[1152,1152]{0,1:T(8,128)}), f32[1152,144]{0,1:T(8,128)}) %reduce-scatter.26.cloned.1.call-update) | async-done | bytes 663568 | tf_op jit(solution)/shard_map/reduce_scatter | solution.py:267
  778.8 60.8 %reduce-scatter.20.cloned.1.call-done = f32[144,3,288]{2,0,1:T(8,128)} async-done(((f32[1152,3,288]{2,0,1:T(8,128)}), f32[144,3,288]{2,0,1:T(8,128)}) %reduce-scatter.20.cloned.1.call-update) | async-done | bytes 497680 | tf_op jit(solution)/shard_map/reduce_scatter | solution.py:264
  839.6 86.5 %reduce-scatter.18.cloned.1.call-done = f32[144,6,288]{2,0,1:T(8,128)} async-done(((f32[1152,6,288]{2,0,1:T(8,128)}), f32[144,6,288]{2,0,1:T(8,128)}) %reduce-scatter.18.cloned.1.call-update) | async-done | bytes 995344 | tf_op jit(solution)/shard_map/reduce_scatter | solution.py:263
  (361 shorter events, 171.4 us)
Async XLA Ops:
  7.2 46.9 %all-gather.9.cloned.1.call-start = ((), (), s32[]{:S(2)}) async-start(), calls=%async_computation.9 | async-start | bytes 5971968 | tf_op jit(solution)/shard_map/all_gather | solution.py:69
  8.0 99.7 %all-gather.11.cloned.1.call-start = ((), (), s32[]{:S(2)}) async-start(), calls=%async_computation.10 | async-start | bytes 2985984 | tf_op jit(solution)/shard_map/all_gather | solution.py:70
  8.7 220.9 %reduce-scatter.10.cloned.1.call-start = ((), (), s32[]{:S(2)}) async-start(), calls=%async_computation.11 | async-start | bytes 1474560 | tf_op jit(solution)/shard_map/reduce_scatter | solution.py:142
  110.8 33.1 %collective-permute-start = (bf16[256,2,288]{0,2,1:T(8,128)(2,1)S(1)}, bf16[256,2,288]{0,2,1:T(8,128)(2,1)}, u32[]{:S(2)}, u32[]{:S(2)}) collective-permute-start(bf16[256,2,288]{0,2,1:T(8,128)(2,1)S(1)} %slice.100), channel_id=1, source_target_pairs={{0,16},{4,20},{8,24},{12,28},{1,17},{5,21},{9,25},{13,29},{2,18},{... | collective-permute-start | bytes 884744 | tf_op jit(solution)/shard_map/ppermute | solution.py:20
  114.7 31.5 %collective-permute-start.1 = (bf16[256,2,288]{0,2,1:T(8,128)(2,1)S(1)}, bf16[256,2,288]{0,2,1:T(8,128)(2,1)S(1)}, u32[]{:S(2)}, u32[]{:S(2)}) collective-permute-start(bf16[256,2,288]{0,2,1:T(8,128)(2,1)S(1)} %slice.100), channel_id=1, source_target_pairs={{0,12},{4,16},{8,20},{12,24},{16,28},{1,13},{5,17},{9,21},{13,25},... | collective-permute-start | bytes 884744 | tf_op jit(solution)/shard_map/ppermute | solution.py:20
  116.1 31.5 %collective-permute-start.2 = (bf16[256,2,288]{0,2,1:T(8,128)(2,1)S(1)}, bf16[256,2,288]{0,2,1:T(8,128)(2,1)S(1)}, u32[]{:S(2)}, u32[]{:S(2)}) collective-permute-start(bf16[256,2,288]{0,2,1:T(8,128)(2,1)S(1)} %slice.100), channel_id=1, source_target_pairs={{0,8},{4,12},{8,16},{12,20},{16,24},{20,28},{1,9},{5,13},{9,17},{1... | collective-permute-start | bytes 884744 | tf_op jit(solution)/shard_map/ppermute | solution.py:20
  140.4 8.5 collective-permute-start.3
  143.9 14.1 %collective-permute-start.5 = (bf16[256,2,288]{0,2,1:T(8,128)(2,1)S(1)}, bf16[256,2,288]{0,2,1:T(8,128)(2,1)S(1)}, u32[]{:S(2)}, u32[]{:S(2)}) collective-permute-start(bf16[256,2,288]{0,2,1:T(8,128)(2,1)S(1)} %slice.100), channel_id=1, source_target_pairs={{8,0},{12,4},{16,8},{20,12},{24,16},{28,20},{9,1},{13,5},{17,9},{2... | collective-permute-start | bytes 884744 | tf_op jit(solution)/shard_map/ppermute | solution.py:20
  146.2 13.9 %collective-permute-start.6 = (bf16[256,2,288]{0,2,1:T(8,128)(2,1)S(1)}, bf16[256,2,288]{0,2,1:T(8,128)(2,1)S(1)}, u32[]{:S(2)}, u32[]{:S(2)}) collective-permute-start(bf16[256,2,288]{0,2,1:T(8,128)(2,1)S(1)} %slice.100), channel_id=1, source_target_pairs={{12,0},{16,4},{20,8},{24,12},{28,16},{13,1},{17,5},{21,9},{25,13},... | collective-permute-start | bytes 884744 | tf_op jit(solution)/shard_map/ppermute | solution.py:20
  147.6 15.9 %collective-permute-start.7 = (bf16[256,2,288]{0,2,1:T(8,128)(2,1)S(1)}, bf16[256,2,288]{0,2,1:T(8,128)(2,1)S(1)}, u32[]{:S(2)}, u32[]{:S(2)}) collective-permute-start(bf16[256,2,288]{0,2,1:T(8,128)(2,1)S(1)} %slice.100), channel_id=1, source_target_pairs={{16,0},{20,4},{24,8},{28,12},{17,1},{21,5},{25,9},{29,13},{18,2},{... | collective-permute-start | bytes 884744 | tf_op jit(solution)/shard_map/ppermute | solution.py:20
  192.3 68.0 %all-gather.13.cloned.1.call-start = ((), (), s32[]{:S(2)}) async-start(), calls=%async_computation.12 | async-start | bytes 1474560 | tf_op jit(solution)/shard_map/all_gather | solution.py:143
  229.7 61.7 %all-gather.17.cloned.1.call-start = ((), (), s32[]{:S(2)}) async-start(), calls=%async_computation.14 | async-start | bytes 2985984 | tf_op jit(solution)/shard_map/all_gather | solution.py:73
  230.3 93.2 %all-gather.15.cloned.1.call-start = ((), (), s32[]{:S(2)}) async-start(), calls=%async_computation.13 | async-start | bytes 2985984 | tf_op jit(solution)/shard_map/all_gather | solution.py:72
  230.8 130.3 %reduce-scatter.14.cloned.1.call-start = ((), (), s32[]{:S(2)}) async-start(), calls=%async_computation.17 | async-start | bytes 1474560 | tf_op jit(solution)/shard_map/reduce_scatter | solution.py:167
  331.8 59.6 %reduce-scatter.12.cloned.1.call-start = ((), (), s32[]{:S(2)}) async-start(), calls=%async_computation.15 | async-start | bytes 1474560 | tf_op jit(solution)/shard_map/reduce_scatter | solution.py:142
  337.0 85.1 %all-gather.21.cloned.1.call-start = ((), (), s32[]{:S(2)}) async-start(), calls=%async_computation.18 | async-start | bytes 1474560 | tf_op jit(solution)/shard_map/all_gather | solution.py:168
  361.1 92.0 %all-gather.19.cloned.1.call-start = ((), (), s32[]{:S(2)}) async-start(), calls=%async_computation.16 | async-start | bytes 1474560 | tf_op jit(solution)/shard_map/all_gather | solution.py:143
  391.4 191.6 %reduce-scatter.16.cloned.1.call-start = ((), (), s32[]{:S(2)}) async-start(), calls=%async_computation.19 | async-start | bytes 1474560 | tf_op jit(solution)/shard_map/reduce_scatter | solution.py:167
  493.7 18.3 %collective-permute-start.10 = (f32[256,2,288]{0,2,1:T(8,128)S(1)}, f32[256,2,288]{0,2,1:T(8,128)S(1)}, u32[]{:S(2)}, u32[]{:S(2)}) collective-permute-start(f32[256,2,288]{0,2,1:T(8,128)S(1)} %get-tuple-element.232), channel_id=1, source_target_pairs={{8,0},{12,4},{16,8},{20,12},{24,16},{28,20},{9,1},{13,5},{17,9},{2... | collective-permute-start | bytes 1769480 | tf_op jit(solution)/shard_map/ppermute | solution.py:20
  495.1 19.3 %collective-permute-start.11 = (f32[256,2,288]{0,2,1:T(8,128)S(1)}, f32[256,2,288]{0,2,1:T(8,128)S(1)}, u32[]{:S(2)}, u32[]{:S(2)}) collective-permute-start(f32[256,2,288]{0,2,1:T(8,128)S(1)} %get-tuple-element.233), channel_id=1, source_target_pairs={{4,0},{8,4},{12,8},{16,12},{20,16},{24,20},{28,24},{5,1},{9,5},{13... | collective-permute-start | bytes 1769480 | tf_op jit(solution)/shard_map/ppermute | solution.py:20
  496.4 19.3 %collective-permute-start.12 = (f32[256,2,288]{0,2,1:T(8,128)S(1)}, f32[256,2,288]{0,2,1:T(8,128)S(1)}, u32[]{:S(2)}, u32[]{:S(2)}) collective-permute-start(f32[256,2,288]{0,2,1:T(8,128)S(1)} %get-tuple-element.234), channel_id=1, source_target_pairs={{0,4},{4,8},{8,12},{12,16},{16,20},{20,24},{24,28},{1,5},{5,9},{9,... | collective-permute-start | bytes 1769480 | tf_op jit(solution)/shard_map/ppermute | solution.py:20
  499.5 18.3 %collective-permute-start.13 = (f32[256,2,288]{0,2,1:T(8,128)S(1)}, f32[256,2,288]{0,2,1:T(8,128)S(1)}, u32[]{:S(2)}, u32[]{:S(2)}) collective-permute-start(f32[256,2,288]{0,2,1:T(8,128)S(1)} %get-tuple-element.235), channel_id=1, source_target_pairs={{0,8},{4,12},{8,16},{12,20},{16,24},{20,28},{1,9},{5,13},{9,17},{1... | collective-permute-start | bytes 1769480 | tf_op jit(solution)/shard_map/ppermute | solution.py:20
  504.0 23.3 %collective-permute-start.14 = (f32[256,2,288]{0,2,1:T(8,128)S(1)}, f32[256,2,288]{0,2,1:T(8,128)S(1)}, u32[]{:S(2)}, u32[]{:S(2)}) collective-permute-start(f32[256,2,288]{0,2,1:T(8,128)S(1)} %get-tuple-element.237), channel_id=1, source_target_pairs={{0,12},{4,16},{8,20},{12,24},{16,28},{1,13},{5,17},{9,21},{13,25},... | collective-permute-start | bytes 1769480 | tf_op jit(solution)/shard_map/ppermute | solution.py:20
  512.0 37.4 %collective-permute-start.15 = (f32[256,2,288]{0,2,1:T(8,128)S(1)}, f32[256,2,288]{0,2,1:T(8,128)S(1)}, u32[]{:S(2)}, u32[]{:S(2)}) collective-permute-start(f32[256,2,288]{0,2,1:T(8,128)S(1)} %get-tuple-element.236), channel_id=1, source_target_pairs={{0,16},{4,20},{8,24},{12,28},{1,17},{5,21},{9,25},{13,29},{2,18},{... | collective-permute-start | bytes 1769480 | tf_op jit(solution)/shard_map/ppermute | solution.py:20
  514.4 35.0 %collective-permute-start.8 = (f32[256,2,288]{0,2,1:T(8,128)S(1)}, f32[256,2,288]{0,2,1:T(8,128)S(1)}, u32[]{:S(2)}, u32[]{:S(2)}) collective-permute-start(f32[256,2,288]{0,2,1:T(8,128)S(1)} %get-tuple-element.230), channel_id=1, source_target_pairs={{16,0},{20,4},{24,8},{28,12},{17,1},{21,5},{25,9},{29,13},{18,2},{... | collective-permute-start | bytes 1769480 | tf_op jit(solution)/shard_map/ppermute | solution.py:20
  515.7 33.7 %collective-permute-start.9 = (f32[256,2,288]{0,2,1:T(8,128)S(1)}, f32[256,2,288]{0,2,1:T(8,128)S(1)}, u32[]{:S(2)}, u32[]{:S(2)}) collective-permute-start(f32[256,2,288]{0,2,1:T(8,128)S(1)} %get-tuple-element.231), channel_id=1, source_target_pairs={{12,0},{16,4},{20,8},{24,12},{28,16},{13,1},{17,5},{21,9},{25,13},... | collective-permute-start | bytes 1769480 | tf_op jit(solution)/shard_map/ppermute | solution.py:20
  552.0 61.6 %all-gather.23.cloned.1.call-start = ((), (), s32[]{:S(2)}) async-start(), calls=%async_computation.20 | async-start | bytes 1474560 | tf_op jit(solution)/shard_map/all_gather | solution.py:168
  583.0 125.5 %reduce-scatter.22.cloned.1.call-start = ((), (), s32[]{:S(2)}) async-start(), calls=%async_computation.23 | async-start | bytes 1990656 | tf_op jit(solution)/shard_map/reduce_scatter | solution.py:265
  584.9 132.8 %reduce-scatter.24.cloned.1.call-start = ((), (), s32[]{:S(2)}) async-start(), calls=%async_computation.24 | async-start | bytes 5971968 | tf_op jit(solution)/shard_map/reduce_scatter | solution.py:266
  590.3 188.5 %reduce-scatter.26.cloned.1.call-start = ((), (), s32[]{:S(2)}) async-start(), calls=%async_computation.25 | async-start | bytes 5971968 | tf_op jit(solution)/shard_map/reduce_scatter | solution.py:267
  596.1 243.5 %reduce-scatter.20.cloned.1.call-start = ((), (), s32[]{:S(2)}) async-start(), calls=%async_computation.22 | async-start | bytes 5971968 | tf_op jit(solution)/shard_map/reduce_scatter | solution.py:264
  600.5 325.7 %reduce-scatter.18.cloned.1.call-start = ((), (), s32[]{:S(2)}) async-start(), calls=%async_computation.21 | async-start | bytes 11943936 | tf_op jit(solution)/shard_map/reduce_scatter | solution.py:263
  (80 other events, 832.5 us)
Sparse Core Ops, SparseCore 0:
  10.0 44.0 all-gather.8
  56.0 30.3 all-gather.10
  192.4 37.2 reduce-scatter.9
  231.1 29.1 all-gather.12
  262.0 29.3 all-gather.16
  293.1 30.2 all-gather.14
  331.9 29.1 reduce-scatter.13
  363.4 27.8 reduce-scatter.11
  392.9 29.1 all-gather.20
  423.5 29.5 all-gather.18
  552.1 30.8 reduce-scatter.15
  584.4 29.1 all-gather.22
  617.6 38.8 reduce-scatter.21
  660.3 57.3 reduce-scatter.23
  721.9 56.9 reduce-scatter.25
  782.7 56.8 reduce-scatter.19
  843.9 82.1 reduce-scatter.17
where the time goes:
time: 943 us; the launch traced here: 933 us
  waiting for transfers between devices  589 us (62%)
  blocking collectives  129 us (14%)
  matrix products  95.6 us (10%)
  starting transfers between devices  35.6 us (4%)
  local copies, waits for them, and re-layouts  34.5 us (4%)
  other arithmetic  34 us (4%)
  between operations  15.4 us (2%)
    reduce_scatter x1, waiting for transfers between devices, local(): lax.psum_scatter(grad_w_ada, 'dp', scatter_dimension=0, tiled=True)  86.5 us
    reduce_scatter x2, waiting for transfers between devices, over_heads(): lax.psum_scatter(partial_sum, 'tensor', scatter_dimension=0, tiled=True)  67.5 us
    reduce_scatter x1, waiting for transfers between devices, local(): lax.psum_scatter(grad_w_fc2, 'dp', scatter_dimension=1, tiled=True)  61.2 us
    reduce_scatter x1, waiting for transfers between devices, local(): lax.psum_scatter(grad_w_qkv, 'dp', scatter_dimension=0, tiled=True)  60.8 us
    all_gather x2, waiting for transfers between devices, over_heads(): return lax.all_gather(shares, 'tensor', axis=0, tiled=True)  56.9 us
    reduce_scatter x2, waiting for transfers between devices, input_side(): lax.psum_scatter(partial_sum, 'tensor', scatter_dimension=0, tiled=True)  55.1 us
    ppermute x16, waiting for transfers between devices, from_behind(): return lax.ppermute(block, axis, route)  50.4 us
    all_gather x2, waiting for transfers between devices, input_side(): return lax.all_gather(shares, 'tensor', axis=0, tiled=True)  43.1 us
  transfers between devices with their start and end apart: 33, of which 22 were waited for; matrix products, arithmetic and copies ran while one was open for 7% of the time, Pallas kernels for 0%

commit v1 on v0

v1 whole, which is shorter than its diff:
```python
import math

import jax
import jax.numpy as jnp
from jax import lax
from jax.experimental import pallas as pl
from jax.experimental.pallas import tpu as pltpu
from jax.sharding import PartitionSpec as P

DH = 72
SEQ = 1024
NORM_EPS = 1e-06
NEGATIVE = -1e30
SCALE = 1.0 / math.sqrt(DH)
VMEM_BYTES = 40 * 1024 * 1024
BF16 = jnp.bfloat16
F32 = jnp.float32


def swap(block, axis, bits):
    route = [(i, i ^ bits) for i in range(lax.axis_size(axis))]
    return lax.ppermute(block, axis, route)


def exchange(blocks, axis):
    return lax.all_to_all(blocks, axis, 0, 0, tiled=True)


def gather(block, axis, count):
    return exchange(jnp.broadcast_to(block[None], (count,) + block.shape), axis)


def gather_rows(block):
    count = lax.axis_size("dp")
    if count > 8:
        return lax.all_gather(block, "dp", axis=0, tiled=True)
    me = lax.axis_index("dp")
    held = [block] + [swap(block, "dp", bits) for bits in range(2, count, 2)]
    other = swap(jnp.stack(held), "dp", 1)
    full = jnp.zeros((count,) + block.shape, block.dtype)
    for step in range(count // 2):
        full = lax.dynamic_update_index_in_dim(full, held[step], me ^ (2 * step), 0)
        full = lax.dynamic_update_index_in_dim(full, other[step], me ^ (2 * step + 1), 0)
    return full.reshape((count * block.shape[0],) + block.shape[1:])


def scatter_rows(partial):
    count = lax.axis_size("dp")
    share = partial.shape[0] // count
    if count > 8:
        return lax.psum_scatter(partial.astype(F32), "dp", scatter_dimension=0, tiled=True)
    me = lax.axis_index("dp")
    core = me % 2
    blocks = partial.reshape(count // 2, 2, share, partial.shape[1])
    theirs = lax.dynamic_index_in_dim(blocks, 1 - core, 1, keepdims=False)
    ours = lax.dynamic_index_in_dim(blocks, core, 1, keepdims=False)
    both = (ours.astype(F32) + swap(theirs, "dp", 1).astype(F32)).astype(BF16)
    chip = me // 2
    total = lax.dynamic_index_in_dim(both, chip, 0, keepdims=False).astype(F32)
    for step in range(1, count // 2):
        sent = lax.dynamic_index_in_dim(both, chip ^ step, 0, keepdims=False)
        total = total + swap(sent, "dp", 2 * step).astype(F32)
    return total


def sum_shares(partial, axis):
    count = lax.axis_size(axis)
    blocks = partial.astype(BF16).reshape((count, partial.shape[0] // count) + partial.shape[1:])
    return jnp.sum(exchange(blocks, axis).astype(F32), axis=0)


def gather_shares(share, axis):
    count = lax.axis_size(axis)
    parts = gather(share, axis, count)
    return parts.reshape((count * share.shape[0],) + share.shape[1:])


def tile_range(meta_ref, latents, tile, core):
    lane = lax.broadcasted_iota(jnp.int32, (1, 256), 1)
    first = tile * 512 + core * 128
    last = first + 383
    place = first + lane + jnp.where(lane >= 128, 128, 0)
    begin = jnp.zeros((1, 256), jnp.int32)
    finish = jnp.zeros((1, 256), jnp.int32)
    low = jnp.int32(0)
    high = jnp.int32(0)
    start = jnp.int32(0)
    for number in range(latents):
        end = start + meta_ref[1 + number]
        inside = (place >= start) & (place < end)
        begin = jnp.where(inside, start, begin)
        finish = jnp.where(inside, end, finish)
        low = jnp.where((first >= start) & (first < end), start, low)
        high = jnp.where((last >= start) & (last < end), end, high)
        start = end
    return begin, finish, low // 256, (high + 255) // 256


def pair(ref, tile, start):
    left = ref[2 * tile, :, start : start + 128]
    right = ref[2 * tile + 1, :, start : start + 128]
    return jnp.concatenate([left, right], axis=1)


def key_mask(block, begin, finish):
    place = block * 256 + lax.broadcasted_iota(jnp.int32, (256, 256), 0)
    return (place >= begin) & (place < finish)


def forward_kernel(latents, meta_ref, packed_ref, out_ref, exact_ref, log_ref, keys, scores):
    blocks = packed_ref.shape[0]
    core = meta_ref[0]
    for block in range(blocks):
        keys[block] = packed_ref[block, :, :256].astype(F32).T.astype(BF16)
    for tile in range(blocks // 2):
        begin, finish, low, high = tile_range(meta_ref, latents, tile, core)
        query = pair(packed_ref, tile, 512)

        def score(block, largest):
            raw = jnp.dot(keys[block], query, preferred_element_type=F32) * SCALE
            raw = jnp.where(key_mask(block, begin, finish), raw, NEGATIVE)
            scores[block] = raw
            return jnp.maximum(largest, jnp.max(raw, axis=0, keepdims=True))

        largest = lax.fori_loop(low, high, score, jnp.full((1, 256), NEGATIVE, F32))

        def mix(block, carry):
            total, mixed = carry
            weights = jnp.exp(scores[block] - largest)
            total = total + jnp.sum(weights, axis=0, keepdims=True)
            values = packed_ref[block, :, 256:512]
            mixed = mixed + jnp.dot(values, weights.astype(BF16), preferred_element_type=F32)
            return total, mixed

        total, mixed = lax.fori_loop(
            low, high, mix, (jnp.zeros((1, 256), F32), jnp.zeros((DH, 256), F32))
        )
        mixed = mixed / total
        log_total = largest + jnp.log(total)
        for half in range(2):
            part = mixed[:, half * 128 : half * 128 + 128]
            exact_ref[2 * tile + half] = part
            out_ref[2 * tile + half] = part.astype(BF16)
            log_ref[2 * tile + half] = log_total[:, half * 128 : half * 128 + 128]


def backward_kernel(
    latents, meta_ref, packed_ref, grad_ref, exact_ref, log_ref, out_ref, keys, values, d_keys, d_values
):
    blocks = packed_ref.shape[0]
    core = meta_ref[0]
    for block in range(blocks):
        keys[block] = packed_ref[block, :, :256].astype(F32).T.astype(BF16)
        values[block] = packed_ref[block, :, 256:512].astype(F32).T.astype(BF16)
    d_keys[...] = jnp.zeros_like(d_keys)
    d_values[...] = jnp.zeros_like(d_values)
    by_query = (((1,), (1,)), ((), ()))
    for tile in range(blocks // 2):
        begin, finish, low, high = tile_range(meta_ref, latents, tile, core)
        query = pair(packed_ref, tile, 512)
        grad = pair(grad_ref, tile, 0)
        inner = jnp.sum(grad.astype(F32) * pair(exact_ref, tile, 0), axis=0, keepdims=True)
        log_total = pair(log_ref, tile, 0)

        def step(block, d_query):
            raw = jnp.dot(keys[block], query, preferred_element_type=F32) * SCALE
            probs = jnp.where(key_mask(block, begin, finish), jnp.exp(raw - log_total), 0.0)
            d_probs = jnp.dot(values[block], grad, preferred_element_type=F32)
            d_scores = (probs * (d_probs - inner)).astype(BF16)
            d_values[block] += lax.dot_general(
                grad, probs.astype(BF16), by_query, preferred_element_type=F32
            )
            d_keys[block] += lax.dot_general(query, d_scores, by_query, preferred_element_type=F32)
            key_rows = packed_ref[block, :, :256]
            return d_query + jnp.dot(key_rows, d_scores, preferred_element_type=F32)

        d_query = lax.fori_loop(low, high, step, jnp.zeros((DH, 256), F32)) * SCALE
        for half in range(2):
            part = d_query[:, half * 128 : half * 128 + 128]
            out_ref[2 * tile + half, :, 512:640] = part.astype(BF16)
    for block in range(blocks):
        out_ref[block, :, :256] = (d_keys[block] * SCALE).astype(BF16)
        out_ref[block, :, 256:512] = d_values[block].astype(BF16)


def attend_forward(meta, packed):
    blocks = packed.shape[0]
    shape = jax.ShapeDtypeStruct
    return pl.pallas_call(
        lambda *refs: forward_kernel(meta.shape[0] - 1, *refs),
        out_shape=(
            shape((blocks, DH, 128), BF16),
            shape((blocks, DH, 128), F32),
            shape((blocks, 1, 128), F32),
        ),
        in_specs=[
            pl.BlockSpec(memory_space=pltpu.SMEM),
            pl.BlockSpec(memory_space=pltpu.VMEM),
        ],
        out_specs=tuple([pl.BlockSpec(memory_space=pltpu.VMEM)] * 3),
        scratch_shapes=[
            pltpu.VMEM((blocks, 256, DH), BF16),
            pltpu.VMEM((blocks, 256, 256), F32),
        ],
        compiler_params=pltpu.CompilerParams(vmem_limit_bytes=VMEM_BYTES),
        cost_estimate=pl.CostEstimate(flops=10**9, bytes_accessed=4 * 10**6, transcendentals=10**6),
        name="attend_forward",
    )(meta, packed)


def attend_backward(meta, packed, grad, exact, log_total):
    blocks = packed.shape[0]
    return pl.pallas_call(
        lambda *refs: backward_kernel(meta.shape[0] - 1, *refs),
        out_shape=jax.ShapeDtypeStruct(packed.shape, BF16),
        in_specs=[pl.BlockSpec(memory_space=pltpu.SMEM)]
        + [pl.BlockSpec(memory_space=pltpu.VMEM)] * 4,
        out_specs=pl.BlockSpec(memory_space=pltpu.VMEM),
        scratch_shapes=[
            pltpu.VMEM((blocks, 256, DH), BF16),
            pltpu.VMEM((blocks, 256, DH), BF16),
            pltpu.VMEM((blocks, DH, 256), F32),
            pltpu.VMEM((blocks, DH, 256), F32),
        ],
        compiler_params=pltpu.CompilerParams(vmem_limit_bytes=VMEM_BYTES),
        cost_estimate=pl.CostEstimate(flops=3 * 10**9, bytes_accessed=4 * 10**6, transcendentals=10**6),
        name="attend_backward",
    )(meta, packed, grad, exact, log_total)


class HeadSplit:
    def __init__(self, latent_len, rows):
        self.rows = rows
        self.meta = jnp.concatenate([lax.axis_index("dp").astype(jnp.int32)[None] % 2, latent_len])

    def forward(self, projected):
        heads, rows = projected.shape[1], self.rows
        query = projected[0].reshape(heads, DH, 2, rows // 2).transpose(0, 2, 1, 3)
        key = jnp.broadcast_to(projected[1][:, None], (heads, 2, DH, rows))
        value = jnp.broadcast_to(projected[2][:, None], (heads, 2, DH, rows))
        packed = jnp.concatenate([key, value, query], axis=3)
        self.packed = exchange(packed.reshape(heads * 2, DH, rows * 5 // 2), "dp")
        out, self.exact, self.log_total = attend_forward(self.meta, self.packed)
        return self.unsplit(exchange(out, "dp")).reshape(heads * DH, rows)

    def unsplit(self, parts):
        heads = parts.shape[0] // 2
        parts = parts.reshape(heads, 2, DH, self.rows // 2).transpose(0, 2, 1, 3)
        return parts.reshape(heads, DH, self.rows)

    def backward(self, d_attended):
        rows = self.rows
        heads = d_attended.shape[0] // DH
        grad = d_attended.reshape(heads, DH, 2, rows // 2).transpose(0, 2, 1, 3)
        grad = exchange(grad.reshape(heads * 2, DH, rows // 2), "dp")
        out = attend_backward(self.meta, self.packed, grad, self.exact, self.log_total)
        parts = exchange(out, "dp")
        d_query = self.unsplit(parts[:, :, 2 * rows :])
        halves = parts.reshape(heads, 2, DH, rows * 5 // 2)[..., : 2 * rows].astype(F32)
        d_key_value = (halves[:, 0] + halves[:, 1]).astype(BF16)
        return jnp.stack([d_query, d_key_value[..., :rows], d_key_value[..., rows:]])


class Window:
    def __init__(self, latent_len, rows):
        self.rows = rows
        self.reach = (SEQ - 2) // rows + 1
        total = rows * lax.axis_size("dp")
        first = lax.axis_index("dp") * rows
        own = latent_index(latent_len, first, rows, total)
        ids = [
            latent_index(latent_len, first + offset * rows, rows, total)
            for offset in range(-self.reach, self.reach + 1)
        ]
        self.allowed = own[:, None] == jnp.concatenate(ids)[None, :]

    def from_behind(self, block, distance):
        devices = range(lax.axis_size("dp"))
        return lax.ppermute(
            block, "dp", [(i - distance, i) for i in devices if i - distance in devices]
        )

    def head_scores(self, query, key):
        raw = jnp.einsum("eq,ek->qk", query, key, preferred_element_type=F32) * SCALE
        return jnp.where(self.allowed, raw, NEGATIVE)

    def forward(self, projected):
        key_value = projected[1:]
        pieces = [
            key_value if offset == 0 else self.from_behind(key_value, -offset)
            for offset in range(-self.reach, self.reach + 1)
        ]
        window = jnp.concatenate(pieces, axis=3)
        self.operands = (projected[0], window[0], window[1])

        def one(operands):
            query, key, value = operands
            scores = self.head_scores(query, key)
            largest = jnp.max(scores, axis=1, keepdims=True)
            weights = jnp.exp(scores - largest)
            totals = jnp.sum(weights, axis=1, keepdims=True)
            probs = (weights / totals).astype(BF16)
            mixed = jnp.einsum("qk,ek->eq", probs, value, preferred_element_type=F32)
            return mixed.astype(BF16), (largest + jnp.log(totals))[:, 0]

        out, self.log_total = lax.map(one, self.operands)
        return out.reshape(-1, self.rows)

    def backward(self, d_attended):
        rows, reach = self.rows, self.reach
        grads = d_attended.reshape(-1, DH, rows)

        def one(operands):
            query, key, value, grad, log_total = operands
            probs = jnp.exp(self.head_scores(query, key) - log_total[:, None])
            d_value = jnp.einsum("qk,eq->ek", probs.astype(BF16), grad, preferred_element_type=F32)
            d_probs = jnp.einsum("eq,ek->qk", grad, value, preferred_element_type=F32)
            inner = jnp.sum(probs * d_probs, axis=1, keepdims=True)
            d_scores = (probs * (d_probs - inner)).astype(BF16)
            d_query = jnp.einsum("qk,ek->eq", d_scores, key, preferred_element_type=F32) * SCALE
            d_key = jnp.einsum("qk,eq->ek", d_scores, query, preferred_element_type=F32) * SCALE
            return d_query, d_key, d_value

        d_query, d_key, d_value = lax.map(one, self.operands + (grads, self.log_total))
        d_window = jnp.stack([d_key, d_value])
        d_key_value = d_window[..., reach * rows : (reach + 1) * rows]
        for offset in range(-reach, reach + 1):
            if offset != 0:
                block = d_window[..., (offset + reach) * rows : (offset + reach + 1) * rows]
                d_key_value = d_key_value + self.from_behind(block, offset)
        return jnp.concatenate([d_query[None], d_key_value]).astype(BF16)


def latent_index(latent_len, first_row, row_count, token_total):
    positions = first_row + jnp.arange(row_count, dtype=jnp.int32)
    ends = jnp.cumsum(latent_len, dtype=jnp.int32)
    found = jnp.sum((positions[:, None] >= ends[None, :]).astype(jnp.int32), axis=1, dtype=jnp.int32)
    return jnp.where((positions >= 0) & (positions < token_total), found, -1)


def normed(values):
    average = jnp.mean(values, axis=-1, keepdims=True)
    centred = values - average
    spread = jnp.mean(centred * centred, axis=-1, keepdims=True)
    inverse = lax.rsqrt(spread + NORM_EPS)
    return centred * inverse, inverse


def norm_back(unit, inverse, grad):
    along = jnp.mean(grad * unit, axis=-1, keepdims=True)
    return inverse * (grad - jnp.mean(grad, axis=-1, keepdims=True) - unit * along)


def pick(rows_by_latent, ids):
    out = jnp.zeros((ids.shape[0], rows_by_latent.shape[1]), F32)
    for number in range(rows_by_latent.shape[0]):
        out = jnp.where(ids[:, None] == number, rows_by_latent[number][None], out)
    return out


def gelu_pair(value):
    root = math.sqrt(2.0 / math.pi)
    bend = jnp.tanh(root * (value + 0.044715 * value * value * value))
    slope = root * (1.0 + 3.0 * 0.044715 * value * value)
    gelu = 0.5 * value * (1.0 + bend)
    return gelu, 0.5 * (1.0 + bend) + 0.5 * value * (1.0 - bend * bend) * slope


def local(
    tokens,
    conditioning,
    latent_len,
    w_ada,
    b_ada,
    w_qkv,
    b_qv,
    w_proj,
    b_proj,
    w_fc1,
    b_fc1,
    w_fc2,
    b_fc2,
    cotangent,
):
    rows, width = tokens.shape
    share_width = w_qkv.shape[0]
    features = w_qkv.shape[2]
    units = w_fc1.shape[1]
    heads = features // DH
    latents = conditioning.shape[0]
    n_dp, n_tensor = lax.axis_size("dp"), lax.axis_size("tensor")
    my_dp, my_tensor = lax.axis_index("dp"), lax.axis_index("tensor")
    total = rows * n_dp
    share = rows // n_tensor

    full_qkv = gather_rows(w_qkv.reshape(share_width, 3 * features))
    full_late = gather_rows(jnp.concatenate([w_fc1, w_fc2.T, w_proj.T], axis=1))
    full_fc1 = full_late[:, :units]
    full_fc2 = full_late[:, units : 2 * units]
    full_proj = full_late[:, 2 * units :]

    cond = conditioning.astype(F32)
    gate = 1.0 / (1.0 + jnp.exp(-cond))
    activated = (cond * gate).astype(BF16)
    own_activated = lax.dynamic_slice_in_dim(activated, my_dp * share_width, share_width, 1)
    flat_ada = w_ada.reshape(share_width, 6 * features)
    mod_part = jnp.dot(own_activated, flat_ada, preferred_element_type=F32)
    mod_mine = jnp.sum(gather(mod_part, "dp", n_dp), axis=0) + b_ada.astype(F32).reshape(1, -1)
    modulation = gather(mod_mine, "tensor", n_tensor)
    modulation = modulation.reshape(n_tensor, latents, 6, features).transpose(2, 1, 0, 3)
    modulation = modulation.reshape(6, latents, width)

    ids = latent_index(latent_len, my_dp * rows, rows, total)
    own_ids = lax.dynamic_slice_in_dim(ids, my_tensor * share, share, 0)

    def own(values):
        return lax.dynamic_slice_in_dim(values, my_tensor * share, share, 0)

    unit_one, inverse_one = normed(tokens.astype(F32))
    hidden_one = (unit_one * (1.0 + pick(modulation[1], ids)) + pick(modulation[0], ids)).astype(BF16)
    bias = jnp.concatenate([b_qv[0], jnp.zeros_like(b_qv[0]), b_qv[1]]).astype(F32)
    projected = lax.dot_general(
        full_qkv, hidden_one, (((0,), (1,)), ((), ())), preferred_element_type=F32
    )
    projected = (projected + bias[:, None]).astype(BF16).reshape(3, heads, DH, rows)
    split = HeadSplit if 2 * heads == n_dp else Window
    attention = split(latent_len, rows)
    attended = attention.forward(projected)
    attn_part = lax.dot_general(
        attended, full_proj, (((0,), (1,)), ((), ())), preferred_element_type=F32
    )
    attn_out = sum_shares(attn_part, "tensor") + b_proj.astype(F32)
    own_tokens = own(tokens).astype(F32)
    gate_one = pick(modulation[2], own_ids)
    residual_mid = own_tokens + gate_one * attn_out
    unit_two, inverse_two = normed(residual_mid)
    scale_two = 1.0 + pick(modulation[4], own_ids)
    hidden_two_own = (unit_two * scale_two + pick(modulation[3], own_ids)).astype(BF16)
    hidden_two = gather_shares(hidden_two_own, "tensor")

    d_mlp = (cotangent.astype(F32) * pick(modulation[5], ids)).astype(BF16)
    d_gelu = jnp.dot(d_mlp, full_fc2, preferred_element_type=F32)
    pre_act = jnp.dot(hidden_two, full_fc1, preferred_element_type=F32) + b_fc1.astype(F32)
    gelu_out, gelu_slope = gelu_pair(pre_act)
    gelu_out = gelu_out.astype(BF16)
    d_pre_wide = d_gelu * gelu_slope
    d_pre = d_pre_wide.astype(BF16)
    by_last = (((1,), (1,)), ((), ()))
    by_token = (((0,), (0,)), ((), ()))
    d_two_part = lax.dot_general(d_pre, full_fc1, by_last, preferred_element_type=F32)
    d_hidden_two = sum_shares(d_two_part, "tensor")
    own_cotangent = own(cotangent).astype(F32)
    d_mid = own_cotangent + norm_back(unit_two, inverse_two, d_hidden_two * scale_two)
    d_attn_own = (d_mid * gate_one).astype(BF16)
    d_attn = gather_shares(d_attn_own, "tensor")

    mlp_part = lax.dot_general(gelu_out, full_fc2, by_last, preferred_element_type=F32)
    mlp_out = sum_shares(mlp_part, "tensor") + b_fc2.astype(F32)
    gate_two = pick(modulation[5], own_ids)
    result = gather_shares((residual_mid + gate_two * mlp_out).astype(BF16), "tensor")

    d_attended = lax.dot_general(
        full_proj, d_attn, (((0,), (1,)), ((), ())), preferred_element_type=F32
    ).astype(BF16)
    d_projected = attention.backward(d_attended).reshape(3 * features, rows)
    d_one_part = lax.dot_general(
        d_projected, full_qkv, (((0,), (1,)), ((), ())), preferred_element_type=F32
    )
    d_hidden_one = sum_shares(d_one_part, "tensor")
    own_unit, own_inverse = own(unit_one), own(inverse_one)
    scale_one = 1.0 + pick(modulation[1], own_ids)
    grad_own = d_mid + norm_back(own_unit, own_inverse, d_hidden_one * scale_one)
    grad_tokens = gather_shares(grad_own.astype(BF16), "tensor").astype(F32)

    grad_fc1 = lax.dot_general(hidden_two, d_pre, by_token, preferred_element_type=F32)
    grad_fc2 = lax.dot_general(d_mlp, gelu_out, by_token, preferred_element_type=F32)
    grad_proj = lax.dot_general(
        d_attn, attended, (((0,), (1,)), ((), ())), preferred_element_type=F32
    )
    grad_late = jnp.concatenate(
        [grad_fc1.astype(BF16), grad_fc2.astype(BF16), grad_proj.astype(BF16)], axis=1
    )
    grad_late = scatter_rows(grad_late)
    grad_qkv = lax.dot_general(
        hidden_one, d_projected, (((0,), (1,)), ((), ())), preferred_element_type=F32
    )
    grad_qkv = scatter_rows(grad_qkv.astype(BF16)).reshape(share_width, 3, features)

    d_float = d_projected.astype(F32).reshape(3, features, rows)
    bias_part = jnp.concatenate(
        [
            jnp.sum(d_mlp.astype(F32), axis=0),
            jnp.sum(d_attn.astype(F32), axis=0),
            jnp.sum(d_pre.astype(F32), axis=0),
            jnp.sum(d_float[0], axis=1),
            jnp.sum(d_float[2], axis=1),
        ]
    )
    bias_total = jnp.sum(gather(bias_part, "dp", n_dp), axis=0)

    d_token = jnp.stack(
        [
            d_hidden_one,
            d_hidden_one * own_unit,
            d_mid * attn_out,
            d_hidden_two,
            d_hidden_two * unit_two,
            own_cotangent * mlp_out,
        ],
        axis=1,
    ).astype(BF16)
    one_hot = (jnp.arange(latents, dtype=jnp.int32)[:, None] == own_ids[None, :]).astype(BF16)
    d_mod_part = jnp.dot(one_hot, d_token.reshape(share, 6 * width), preferred_element_type=F32)
    d_mod_part = d_mod_part.reshape(latents * 6, n_tensor, features).transpose(1, 0, 2)
    d_mod_mine = jnp.sum(exchange(d_mod_part, "tensor"), axis=0)
    d_mod = jnp.sum(gather(d_mod_mine, "dp", n_dp), axis=0).reshape(latents, 6 * features)
    grad_b_ada = jnp.sum(d_mod, axis=0).reshape(6, features)
    grad_w_ada = lax.dot_general(
        own_activated.astype(F32), d_mod, by_token, precision=lax.Precision.HIGHEST
    ).reshape(share_width, 6, features)
    high = d_mod.astype(BF16)
    low = (d_mod - high.astype(F32)).astype(BF16)
    d_active = lax.dot_general(
        jnp.concatenate([high, low]), flat_ada, by_last, preferred_element_type=F32
    )
    d_active = d_active[:latents] + d_active[latents:]
    d_active = jnp.sum(gather(d_active, "tensor", n_tensor), axis=0)
    d_active = gather(d_active, "dp", n_dp).transpose(1, 0, 2).reshape(latents, width)
    grad_cond = d_active * (gate * (1.0 + cond * (1.0 - gate)))

    return (
        result,
        grad_tokens,
        grad_cond,
        grad_w_ada,
        grad_b_ada,
        grad_qkv,
        bias_total[2 * width + units :].reshape(2, features),
        grad_late[:, 2 * units :].T,
        bias_total[width : 2 * width],
        grad_late[:, :units],
        bias_total[2 * width : 2 * width + units],
        grad_late[:, units : 2 * units].T,
        bias_total[:width],
    )


def solution(mesh):
    in_specs = (
        P("dp", None),
        P(),
        P(),
        P("dp", None, "tensor"),
        P(None, "tensor"),
        P("dp", None, "tensor"),
        P(None, "tensor"),
        P("tensor", "dp"),
        P(),
        P("dp", "tensor"),
        P("tensor"),
        P("tensor", "dp"),
        P(),
        P("dp", None),
    )
    out_specs = (
        P("dp", None),
        P("dp", None),
        P(),
        P("dp", None, "tensor"),
        P(None, "tensor"),
        P("dp", None, "tensor"),
        P(None, "tensor"),
        P("tensor", "dp"),
        P(),
        P("dp", "tensor"),
        P("tensor"),
        P("tensor", "dp"),
        P(),
    )
    return jax.shard_map(local, mesh=mesh, in_specs=in_specs, out_specs=out_specs, check_vma=False)
```

time: 943 us -> 454 us (0.48)
  waiting for transfers between devices: 589 us -> 177 us
  blocking collectives: 129 us -> 0 us
  matrix products: 95.6 us -> 38.7 us
  starting transfers between devices: 35.6 us -> 89 us
  local copies, waits for them, and re-layouts: 34.5 us -> 79 us
  Pallas kernels: 0 us -> 15.7 us
  other arithmetic: 34 us -> 48.7 us
  between operations: 15.4 us -> 2.59 us
    reduce_scatter x9 -> x0, waiting for transfers between devices: 340 us -> none  [the longest x1 86.5 us: local(): lax.psum_scatter(grad_w_ada, 'dp', scatter_dimension=0, tiled=True)]
    all_gather x8 -> x0, waiting for transfers between devices: 196 us -> none  [the longest x2 56.9 us: over_heads(): return lax.all_gather(shares, 'tensor', axis=0, tiled=True)]
    all_to_all x0 -> x19, waiting for transfers between devices: none -> 150 us  [exchange(): return lax.all_to_all(blocks, axis, 0, 0, tiled=True)]
    all_to_all x0 -> x19, starting transfers between devices: none -> 71.9 us  [exchange(): return lax.all_to_all(blocks, axis, 0, 0, tiled=True)]
    psum x2 -> x0, blocking collectives: 65 us -> none  [the longest x1 39.3 us: local(): d_activated = lax.psum(d_activated, ('dp', 'tensor'))]
    all_gather x2 -> x0, blocking collectives: 64 us -> none  [the longest x1 42.4 us: local(): modulation = lax.all_gather(mod_part, 'tensor', axis=2, tiled=True)]
    dot_general x45 -> x16, matrix products: 95.6 us -> 38.7 us  [the longest x1 4.24 us: local(): d_gelu = jnp.dot(d_mlp, full_fc2, preferred_element_type=F32)]
    ppermute x16, waiting for transfers between devices: 50.4 us -> 26.6 us  [swap(): return lax.ppermute(block, axis, route)]
  transfers between devices with their start and end apart: 33 -> 35, of which waited for: 22 -> 20; matrix products, arithmetic and copies ran while one was open for 7% -> 27% of each run, Pallas kernels for 0% -> 2%
where the time goes in v1:
time: 454 us; the launch traced here: 451 us
  waiting for transfers between devices  177 us (39%)
  starting transfers between devices  89 us (20%)
  local copies, waits for them, and re-layouts  79 us (17%)
  other arithmetic  48.7 us (11%)
  matrix products  38.7 us (9%)
  Pallas kernels  15.7 us (3%)
    all_to_all x19, waiting for transfers between devices, exchange(): return lax.all_to_all(blocks, axis, 0, 0, tiled=True)  150 us
    all_to_all x19, starting transfers between devices, exchange(): return lax.all_to_all(blocks, axis, 0, 0, tiled=True)  71.9 us
    ppermute x16, waiting for transfers between devices, swap(): return lax.ppermute(block, axis, route)  26.6 us
    ppermute x16, starting transfers between devices, swap(): return lax.ppermute(block, axis, route)  17.1 us
    dynamic_update_slice x8, local copies, waits for them, and re-layouts, gather_rows(): lax.dynamic_update_index_in_dim(full, other[step], me ^ 2 * step + 1, 0)  15 us
    dynamic_update_slice x7, local copies, waits for them, and re-layouts, gather_rows(): full = lax.dynamic_update_index_in_dim(full, held[step], me ^ 2 * step, 0)  9.95 us
    concatenate x1, local copies, waits for them, and re-layouts, local(): jnp.concatenate([grad_fc1.astype(BF16), grad_fc2.astype(BF16), grad_proj....  9.19 us
  transfers between devices with their start and end apart: 35, of which 20 were waited for; matrix products, arithmetic and copies ran while one was open for 27% of the time, Pallas kernels for 2%

profile of v1, /device:TPU:0, one launch (start us, length us, event | category | flops | bytes accessed | tf_op | source)
XLA Modules:
  0.0 450.6 jit_solution(2153452266954882592)
XLA Ops:
  2.8 3.9 collective-permute-start.6
  19.6 34.7 %all-to-all-done = f32[8,3,1728]{2,1,0:T(4,128)S(1)} async-done(((f32[8,3,1728]{2,1,0:T(4,128)}), f32[8,3,1728]{2,1,0:T(4,128)S(1)}, u32[]{:S(2)}, u32[]{:S(2)}) %all-to-all-start) | async-done | bytes 165920 | tf_op jit(solution)/shard_map/all_to_all | solution.py:26
  59.0 4.9 %all-to-all-start.1 = ((f32[4,3,1728]{2,1,0:T(4,128)}), f32[4,3,1728]{2,1,0:T(4,128)S(1)}, u32[]{:S(2)}, u32[]{:S(2)}) async-start(f32[4,3,1728]{2,1,0:T(4,128)} %broadcast_in_dim.407), calls=%async_computation.1 | async-start | bytes 229376 | tf_op jit(solution)/shard_map/all_to_all | solution.py:26
  66.2 3.9 all-to-all-done.1
  95.4 11.9 %all-to-all-done.2.refs_1_ = bf16[8,72,640]{2,1,0:T(8,128)(2,1)S(1)} async-done(((bf16[8,72,640]{2,1,0:T(8,128)(2,1)}), bf16[8,72,640]{2,1,0:T(8,128)(2,1)S(1)}, u32[]{:S(2)}, u32[]{:S(2)}) %all-to-all-start.2) | async-done | bytes 737312 | tf_op jit(solution)/shard_map/all_to_all | solution.py:26
  107.3 7.3 %attend_forward.1 = (bf16[8,72,128]{2,1,0:T(8,128)(2,1)}, f32[8,72,128]{2,1,0:T(8,128)S(1)}, f32[8,1,128]{2,1,0:T(1,128)S(1)}) custom-call(s32[4]{0:T(128)S(1)} %pad_add_fusion.refs_0_, bf16[8,72,640]{2,1,0:T(8,128)(2,1)S(1)} %all-to-all-done.2.refs_1_), custom_call_target="tpu_custom_call" | custom-call | flops 1000000000 | bytes 4000000 | tf_op jit(solution)/shard_map/attend_forward/pallas_call | solution.py:189
  139.7 5.1 %all-to-all-start.4 = ((bf16[4,64,1152]{2,1,0:T(8,128)(2,1)}), bf16[4,64,1152]{2,1,0:T(8,128)(2,1)S(1)}, u32[]{:S(2)}, u32[]{:S(2)}) async-start(bf16[4,64,1152]{2,1,0:T(8,128)(2,1)} %bitcast.21), calls=%async_computation.4 | async-start | bytes 1179648 | tf_op jit(solution)/shard_map/all_to_all | solution.py:26
  145.7 14.8 %all-to-all-done.4 = bf16[4,64,1152]{2,1,0:T(8,128)(2,1)S(1)} async-done(((bf16[4,64,1152]{2,1,0:T(8,128)(2,1)}), bf16[4,64,1152]{2,1,0:T(8,128)(2,1)S(1)}, u32[]{:S(2)}, u32[]{:S(2)}) %all-to-all-start.4) | async-done | bytes 589856 | tf_op jit(solution)/shard_map/all_to_all | solution.py:26
  162.3 3.7 all-to-all-start.5
  166.2 14.9 %all-to-all-done.5 = bf16[4,64,1152]{2,1,0:T(8,128)(2,1)S(1)} async-done(((bf16[4,64,1152]{2,1,0:T(8,128)(2,1)}), bf16[4,64,1152]{2,1,0:T(8,128)(2,1)S(1)}, u32[]{:S(2)}, u32[]{:S(2)}) %all-to-all-start.5) | async-done | bytes 589856 | tf_op jit(solution)/shard_map/all_to_all | solution.py:26
  184.0 4.2 convert_reduce_fusion.1
  188.3 3.8 convolution_convert_fusion.5
  195.6 4.1 convolution_convert_fusion.6
  199.6 11.3 %all-to-all-done.8 = bf16[4,64,1152]{2,1,0:T(8,128)(2,1)S(1)} async-done(((bf16[4,64,1152]{2,1,0:T(8,128)(2,1)}), bf16[4,64,1152]{2,1,0:T(8,128)(2,1)S(1)}, u32[]{:S(2)}, u32[]{:S(2)}) %all-to-all-start.8) | async-done | bytes 589856 | tf_op jit(solution)/shard_map/all_to_all | solution.py:26
  210.9 4.2 all-to-all-start.6
  215.4 15.1 %all-to-all-done.6 = bf16[4,64,1152]{2,1,0:T(8,128)(2,1)} async-done(((bf16[4,64,1152]{2,1,0:T(8,128)(2,1)}), bf16[4,64,1152]{2,1,0:T(8,128)(2,1)}, u32[]{:S(2)}, u32[]{:S(2)}) %all-to-all-start.6) | async-done | bytes 589856 | tf_op jit(solution)/shard_map/all_to_all | solution.py:26
  249.3 5.3 %all-to-all-done.9 = bf16[4,64,1152]{2,1,0:T(8,128)(2,1)S(1)} async-done(((bf16[4,64,1152]{2,1,0:T(8,128)(2,1)}), bf16[4,64,1152]{2,1,0:T(8,128)(2,1)S(1)}, u32[]{:S(2)}, u32[]{:S(2)}) %all-to-all-start.9) | async-done | bytes 589856 | tf_op jit(solution)/shard_map/all_to_all | solution.py:26
  261.6 4.4 all-to-all-done.10.refs_2_
  266.0 8.5 %attend_backward.1 = bf16[8,72,640]{2,1,0:T(8,128)(2,1)} custom-call(s32[4]{0:T(128)S(1)} %pad_add_fusion.refs_0_, bf16[8,72,640]{2,1,0:T(8,128)(2,1)S(1)} %all-to-all-done.2.refs_1_, bf16[8,72,128]{2,1,0:T(8,128)(2,1)S(1)} %all-to-all-done.10.refs_2_, f32[8,72,128]{2,1,0:T(8,128)S(1)} %get-tuple-element.17.refs_3_, f32[8,1,128]{2,1,0:T(1,128)S(1)} %get-tuple-element.18.refs_4_), custom_call_target="tpu_custom_call" | custom-call | flops 3000000000 | bytes 4000000 | tf_op jit(solution)/shard_map/attend_backward/pallas_call | solution.py:213
  278.0 6.4 %pad_maximum_fusion = bf16[1152,2592]{0,1:T(8,128)(2,1)} fusion(bf16[1152,288]{0,1:T(8,128)(2,1)} %convolution_convert_fusion.3, bf16[1152,1152]{0,1:T(8,128)(2,1)} %convolution_convert_fusion, bf16[1152,1152]{0,1:T(8,128)(2,1)} %convolution_convert_fusion.1), kind=kLoop, calls=%fused_computation.4 | loop fusion | flops 17915904 | bytes 11943936 | tf_op jit(solution)/shard_map/concatenate | solution.py:480
  284.5 9.2 %copy.91 = bf16[1152,2592]{1,0:T(8,128)(2,1)} copy(bf16[1152,2592]{0,1:T(8,128)(2,1)} %pad_maximum_fusion) | data formatting | bytes 11943936 | tf_op jit(solution)/shard_map/concatenate | solution.py:480
  294.6 3.7 all-to-all-start.7
  299.7 15.4 %all-to-all-done.7 = bf16[4,64,1152]{2,1,0:T(8,128)(2,1)S(1)} async-done(((bf16[4,64,1152]{2,1,0:T(8,128)(2,1)}), bf16[4,64,1152]{2,1,0:T(8,128)(2,1)S(1)}, u32[]{:S(2)}, u32[]{:S(2)}) %all-to-all-start.7) | async-done | bytes 589856 | tf_op jit(solution)/shard_map/all_to_all | solution.py:26
  315.9 3.8 all-to-all-start.18
  328.8 3.8 dynamic-slice_bitcast_fusion
  341.0 3.7 all-to-all-done.12
  353.4 4.0 all-to-all-start.14
  365.2 4.1 all-to-all-start.15
  371.7 4.8 %all-to-all-done.15 = f32[8,18,288]{2,1,0:T(8,128)} async-done(((f32[8,18,288]{2,1,0:T(8,128)}), f32[8,18,288]{2,1,0:T(8,128)}, u32[]{:S(2)}, u32[]{:S(2)}) %all-to-all-start.15) | async-done | bytes 165920 | tf_op jit(solution)/shard_map/all_to_all | solution.py:26
  398.4 4.2 all-to-all-start.13
  421.4 9.1 %collective-permute-done.15 = bf16[144,2592]{1,0:T(8,128)(2,1)} collective-permute-done((bf16[144,2592]{1,0:T(8,128)(2,1)}, bf16[144,2592]{1,0:T(8,128)(2,1)}, u32[]{:S(2)}, u32[]{:S(2)}) %collective-permute-start.15) | collective-permute-done | bytes 746528 | tf_op jit(solution)/shard_map/ppermute | solution.py:22
  430.5 15.3 %collective-permute-done.14 = bf16[144,2592]{1,0:T(8,128)(2,1)} collective-permute-done((bf16[144,2592]{1,0:T(8,128)(2,1)}, bf16[144,2592]{1,0:T(8,128)(2,1)}, u32[]{:S(2)}, u32[]{:S(2)}) %collective-permute-start.14) | collective-permute-done | bytes 746528 | tf_op jit(solution)/shard_map/ppermute | solution.py:22
  (462 shorter events, 194.6 us)
Async XLA Ops:
  2.8 68.8 %collective-permute-start.6 = (bf16[144,2592]{1,0:T(8,128)(2,1)}, bf16[144,2592]{1,0:T(8,128)(2,1)}, u32[]{:S(2)}, u32[]{:S(2)}) collective-permute-start(bf16[144,2592]{1,0:T(8,128)(2,1)} %get-tuple-element.116), channel_id=1, source_target_pairs={{0,24},{4,28},{8,16},{12,20},{16,8},{20,12},{24,0},{28,4},{1,25},{... | collective-permute-start | bytes 2239496 | tf_op jit(solution)/shard_map/ppermute | solution.py:22
  6.7 65.0 %collective-permute-start.5 = (bf16[144,2592]{1,0:T(8,128)(2,1)}, bf16[144,2592]{1,0:T(8,128)(2,1)}, u32[]{:S(2)}, u32[]{:S(2)}) collective-permute-start(bf16[144,2592]{1,0:T(8,128)(2,1)} %get-tuple-element.116), channel_id=1, source_target_pairs={{0,16},{4,20},{8,24},{12,28},{16,0},{20,4},{24,8},{28,12},{1,17},{... | collective-permute-start | bytes 2239496 | tf_op jit(solution)/shard_map/ppermute | solution.py:22
  8.4 46.0 %collective-permute-start.2 = (bf16[144,864]{1,0:T(8,128)(2,1)}, bf16[144,864]{1,0:T(8,128)(2,1)S(1)}, u32[]{:S(2)}, u32[]{:S(2)}) collective-permute-start(bf16[144,864]{1,0:T(8,128)(2,1)} %reshape.376), channel_id=1, source_target_pairs={{0,24},{4,28},{8,16},{12,20},{16,8},{20,12},{24,0},{28,4},{1,25},{... | collective-permute-start | bytes 746504 | tf_op jit(solution)/shard_map/ppermute | solution.py:22
  9.8 46.3 %collective-permute-start.1 = (bf16[144,864]{1,0:T(8,128)(2,1)}, bf16[144,864]{1,0:T(8,128)(2,1)}, u32[]{:S(2)}, u32[]{:S(2)}) collective-permute-start(bf16[144,864]{1,0:T(8,128)(2,1)} %reshape.376), channel_id=1, source_target_pairs={{0,16},{4,20},{8,24},{12,28},{16,0},{20,4},{24,8},{28,12},{1,17},{... | collective-permute-start | bytes 746504 | tf_op jit(solution)/shard_map/ppermute | solution.py:22
  9.9 46.2 %collective-permute-start = (bf16[144,864]{1,0:T(8,128)(2,1)}, bf16[144,864]{1,0:T(8,128)(2,1)}, u32[]{:S(2)}, u32[]{:S(2)}) collective-permute-start(bf16[144,864]{1,0:T(8,128)(2,1)} %reshape.376), channel_id=1, source_target_pairs={{0,8},{4,12},{8,0},{12,4},{16,24},{20,28},{24,16},{28,20},{1,9},{5... | collective-permute-start | bytes 746504 | tf_op jit(solution)/shard_map/ppermute | solution.py:22
  14.8 39.5 %all-to-all-start = ((f32[8,3,1728]{2,1,0:T(4,128)}), f32[8,3,1728]{2,1,0:T(4,128)S(1)}, u32[]{:S(2)}, u32[]{:S(2)}) async-start(f32[8,3,1728]{2,1,0:T(4,128)} %broadcast_in_dim.406), calls=%async_computation | async-start | bytes 458752 | tf_op jit(solution)/shard_map/all_to_all | solution.py:26
  54.4 19.5 %collective-permute-start.4 = (bf16[144,2592]{1,0:T(8,128)(2,1)}, bf16[144,2592]{1,0:T(8,128)(2,1)S(1)}, u32[]{:S(2)}, u32[]{:S(2)}) collective-permute-start(bf16[144,2592]{1,0:T(8,128)(2,1)} %get-tuple-element.116), channel_id=1, source_target_pairs={{0,8},{4,12},{8,0},{12,4},{16,24},{20,28},{24,16},{28,20},{1,9},{5... | collective-permute-start | bytes 2239496 | tf_op jit(solution)/shard_map/ppermute | solution.py:22
  58.3 18.5 %collective-permute-start.3 = (bf16[4,144,864]{2,1,0:T(8,128)(2,1)}, bf16[4,144,864]{2,1,0:T(8,128)(2,1)}, u32[]{:S(2)}, u32[]{:S(2)}) collective-permute-start(bf16[4,144,864]{2,1,0:T(8,128)(2,1)} %pad_maximum_fusion.2), channel_id=1, source_target_pairs={{0,4},{4,0},{8,12},{12,8},{16,20},{20,16},{24,28},{28,24},{1,5},{5... | collective-permute-start | bytes 2985992 | tf_op jit(solution)/shard_map/ppermute | solution.py:22
  59.0 11.1 %all-to-all-start.1 = ((f32[4,3,1728]{2,1,0:T(4,128)}), f32[4,3,1728]{2,1,0:T(4,128)S(1)}, u32[]{:S(2)}, u32[]{:S(2)}) async-start(f32[4,3,1728]{2,1,0:T(4,128)} %broadcast_in_dim.407), calls=%async_computation.1 | async-start | bytes 229376 | tf_op jit(solution)/shard_map/all_to_all | solution.py:26
  76.9 46.8 %collective-permute-start.7 = (bf16[4,144,2592]{2,1,0:T(8,128)(2,1)}, bf16[4,144,2592]{2,1,0:T(8,128)(2,1)}, u32[]{:S(2)}, u32[]{:S(2)}) collective-permute-start(bf16[4,144,2592]{2,1,0:T(8,128)(2,1)} %pad_maximum_fusion.1), channel_id=1, source_target_pairs={{0,4},{4,0},{8,12},{12,8},{16,20},{20,16},{24,28},{28,24},{1,5},{5... | collective-permute-start | bytes 8957960 | tf_op jit(solution)/shard_map/ppermute | solution.py:22
  91.7 15.6 %all-to-all-start.2 = ((bf16[8,72,640]{2,1,0:T(8,128)(2,1)}), bf16[8,72,640]{2,1,0:T(8,128)(2,1)S(1)}, u32[]{:S(2)}, u32[]{:S(2)}) async-start(bf16[8,72,640]{2,1,0:T(8,128)(2,1)} %bitcast.11), calls=%async_computation.2 | async-start | bytes 1474560 | tf_op jit(solution)/shard_map/all_to_all | solution.py:26
  114.5 9.0 %all-to-all-start.3 = ((bf16[8,72,128]{2,1,0:T(8,128)(2,1)}), bf16[8,72,128]{2,1,0:T(8,128)(2,1)S(1)}, u32[]{:S(2)}, u32[]{:S(2)}) async-start(bf16[8,72,128]{2,1,0:T(8,128)(2,1)} %get-tuple-element.16), calls=%async_computation.3 | async-start | bytes 294912 | tf_op jit(solution)/shard_map/all_to_all | solution.py:26
  139.7 20.8 %all-to-all-start.4 = ((bf16[4,64,1152]{2,1,0:T(8,128)(2,1)}), bf16[4,64,1152]{2,1,0:T(8,128)(2,1)S(1)}, u32[]{:S(2)}, u32[]{:S(2)}) async-start(bf16[4,64,1152]{2,1,0:T(8,128)(2,1)} %bitcast.21), calls=%async_computation.4 | async-start | bytes 1179648 | tf_op jit(solution)/shard_map/all_to_all | solution.py:26
  162.3 18.8 %all-to-all-start.5 = ((bf16[4,64,1152]{2,1,0:T(8,128)(2,1)}), bf16[4,64,1152]{2,1,0:T(8,128)(2,1)S(1)}, u32[]{:S(2)}, u32[]{:S(2)}) async-start(bf16[4,64,1152]{2,1,0:T(8,128)(2,1)} %broadcast_in_dim.459), calls=%async_computation.5 | async-start | bytes 1179648 | tf_op jit(solution)/shard_map/all_to_all | solution.py:26
  192.1 18.8 %all-to-all-start.8 = ((bf16[4,64,1152]{2,1,0:T(8,128)(2,1)}), bf16[4,64,1152]{2,1,0:T(8,128)(2,1)S(1)}, u32[]{:S(2)}, u32[]{:S(2)}) async-start(bf16[4,64,1152]{2,1,0:T(8,128)(2,1)} %bitcast.168), calls=%async_computation.8 | async-start | bytes 1179648 | tf_op jit(solution)/shard_map/all_to_all | solution.py:26
  210.9 19.6 %all-to-all-start.6 = ((bf16[4,64,1152]{2,1,0:T(8,128)(2,1)}), bf16[4,64,1152]{2,1,0:T(8,128)(2,1)}, u32[]{:S(2)}, u32[]{:S(2)}) async-start(bf16[4,64,1152]{2,1,0:T(8,128)(2,1)} %bitcast.167), calls=%async_computation.6 | async-start | bytes 1179648 | tf_op jit(solution)/shard_map/all_to_all | solution.py:26
  235.8 18.8 %all-to-all-start.9 = ((bf16[4,64,1152]{2,1,0:T(8,128)(2,1)}), bf16[4,64,1152]{2,1,0:T(8,128)(2,1)S(1)}, u32[]{:S(2)}, u32[]{:S(2)}) async-start(bf16[4,64,1152]{2,1,0:T(8,128)(2,1)} %broadcast_in_dim.464), calls=%async_computation.9 | async-start | bytes 1179648 | tf_op jit(solution)/shard_map/all_to_all | solution.py:26
  274.5 19.3 %all-to-all-start.11 = ((bf16[8,72,640]{2,1,0:T(8,128)(2,1)}), bf16[8,72,640]{2,1,0:T(8,128)(2,1)S(1)}, u32[]{:S(2)}, u32[]{:S(2)}) async-start(bf16[8,72,640]{2,1,0:T(8,128)(2,1)} %attend_backward.1), calls=%async_computation.11 | async-start | bytes 1474560 | tf_op jit(solution)/shard_map/all_to_all | solution.py:26
  294.6 20.4 %all-to-all-start.7 = ((bf16[4,64,1152]{2,1,0:T(8,128)(2,1)}), bf16[4,64,1152]{2,1,0:T(8,128)(2,1)S(1)}, u32[]{:S(2)}, u32[]{:S(2)}) async-start(bf16[4,64,1152]{2,1,0:T(8,128)(2,1)} %broadcast_in_dim.460), calls=%async_computation.7 | async-start | bytes 1179648 | tf_op jit(solution)/shard_map/all_to_all | solution.py:26
  315.9 9.4 %all-to-all-start.18 = ((f32[8,1,4032]{2,1,0:T(1,128)}), f32[8,1,4032]{2,1,0:T(1,128)S(1)}, u32[]{:S(2)}, u32[]{:S(2)}) async-start(f32[8,1,4032]{2,1,0:T(1,128)} %broadcast_in_dim.472), calls=%async_computation.18 | async-start | bytes 262144 | tf_op jit(solution)/shard_map/all_to_all | solution.py:26
  325.2 19.4 %all-to-all-start.12 = ((bf16[4,64,1152]{2,1,0:T(8,128)(2,1)}), bf16[4,64,1152]{2,1,0:T(8,128)(2,1)S(1)}, u32[]{:S(2)}, u32[]{:S(2)}) async-start(bf16[4,64,1152]{2,1,0:T(8,128)(2,1)} %bitcast.166), calls=%async_computation.12 | async-start | bytes 1179648 | tf_op jit(solution)/shard_map/all_to_all | solution.py:26
  332.6 71.4 %collective-permute-start.12 = (bf16[4,144,2592]{2,1,0:T(8,128)(2,1)}, bf16[4,144,2592]{2,1,0:T(8,128)(2,1)}, u32[]{:S(2)}, u32[]{:S(2)}) collective-permute-start(bf16[4,144,2592]{2,1,0:T(8,128)(2,1)} %dynamic-slice_bitcast_fusion), channel_id=1, source_target_pairs={{0,4},{4,0},{8,12},{12,8},{16,20},{20,16},{24,28},{28,24},{1,5},{5... | collective-permute-start | bytes 8957960 | tf_op jit(solution)/shard_map/ppermute | solution.py:22
  339.1 30.1 %collective-permute-start.8 = (bf16[4,144,864]{2,1,0:T(8,128)(2,1)}, bf16[4,144,864]{2,1,0:T(8,128)(2,1)}, u32[]{:S(2)}, u32[]{:S(2)}) collective-permute-start(bf16[4,144,864]{2,1,0:T(8,128)(2,1)} %dynamic-slice_bitcast_fusion.1), channel_id=1, source_target_pairs={{0,4},{4,0},{8,12},{12,8},{16,20},{20,16},{24,28},{28,24},{1,5},{5... | collective-permute-start | bytes 2985992 | tf_op jit(solution)/shard_map/ppermute | solution.py:22
  353.4 10.1 %all-to-all-start.14 = ((f32[4,18,288]{2,1,0:T(8,128)}), f32[4,18,288]{2,1,0:T(8,128)}, u32[]{:S(2)}, u32[]{:S(2)}) async-start(f32[4,18,288]{2,1,0:T(8,128)} %bitcast.169), calls=%async_computation.14 | async-start | bytes 294912 | tf_op jit(solution)/shard_map/all_to_all | solution.py:26
  365.2 11.4 %all-to-all-start.15 = ((f32[8,18,288]{2,1,0:T(8,128)}), f32[8,18,288]{2,1,0:T(8,128)}, u32[]{:S(2)}, u32[]{:S(2)}) async-start(f32[8,18,288]{2,1,0:T(8,128)} %broadcast_in_dim.469), calls=%async_computation.15 | async-start | bytes 589824 | tf_op jit(solution)/shard_map/all_to_all | solution.py:26
  382.8 29.1 %collective-permute-start.11 = (bf16[144,864]{1,0:T(8,128)(2,1)}, bf16[144,864]{1,0:T(8,128)(2,1)}, u32[]{:S(2)}, u32[]{:S(2)}) collective-permute-start(bf16[144,864]{1,0:T(8,128)(2,1)} %get-tuple-element.113), channel_id=1, source_target_pairs={{0,24},{4,28},{8,16},{12,20},{16,8},{20,12},{24,0},{28,4},{1,25},{... | collective-permute-start | bytes 746504 | tf_op jit(solution)/shard_map/ppermute | solution.py:22
  383.3 29.2 %collective-permute-start.10 = (bf16[144,864]{1,0:T(8,128)(2,1)}, bf16[144,864]{1,0:T(8,128)(2,1)}, u32[]{:S(2)}, u32[]{:S(2)}) collective-permute-start(bf16[144,864]{1,0:T(8,128)(2,1)} %get-tuple-element.114), channel_id=1, source_target_pairs={{0,16},{4,20},{8,24},{12,28},{16,0},{20,4},{24,8},{28,12},{1,17},{... | collective-permute-start | bytes 746504 | tf_op jit(solution)/shard_map/ppermute | solution.py:22
  384.8 27.8 %collective-permute-start.9 = (bf16[144,864]{1,0:T(8,128)(2,1)S(1)}, bf16[144,864]{1,0:T(8,128)(2,1)}, u32[]{:S(2)}, u32[]{:S(2)}) collective-permute-start(bf16[144,864]{1,0:T(8,128)(2,1)S(1)} %get-tuple-element.112), channel_id=1, source_target_pairs={{0,8},{4,12},{8,0},{12,4},{16,24},{20,28},{24,16},{28,20},{1,9},{5... | collective-permute-start | bytes 746504 | tf_op jit(solution)/shard_map/ppermute | solution.py:22
  398.4 20.9 %all-to-all-start.13 = ((bf16[4,64,1152]{2,1,0:T(8,128)(2,1)}), bf16[4,64,1152]{2,1,0:T(8,128)(2,1)}, u32[]{:S(2)}, u32[]{:S(2)}) async-start(bf16[4,64,1152]{2,1,0:T(8,128)(2,1)} %broadcast_in_dim.468), calls=%async_computation.13 | async-start | bytes 1179648 | tf_op jit(solution)/shard_map/all_to_all | solution.py:26
  409.1 21.4 %collective-permute-start.15 = (bf16[144,2592]{1,0:T(8,128)(2,1)}, bf16[144,2592]{1,0:T(8,128)(2,1)}, u32[]{:S(2)}, u32[]{:S(2)}) collective-permute-start(bf16[144,2592]{1,0:T(8,128)(2,1)} %get-tuple-element.108), channel_id=1, source_target_pairs={{0,24},{4,28},{8,16},{12,20},{16,8},{20,12},{24,0},{28,4},{1,25},{... | collective-permute-start | bytes 2239496 | tf_op jit(solution)/shard_map/ppermute | solution.py:22
  410.4 35.4 %collective-permute-start.14 = (bf16[144,2592]{1,0:T(8,128)(2,1)}, bf16[144,2592]{1,0:T(8,128)(2,1)}, u32[]{:S(2)}, u32[]{:S(2)}) collective-permute-start(bf16[144,2592]{1,0:T(8,128)(2,1)} %get-tuple-element.109), channel_id=1, source_target_pairs={{0,16},{4,20},{8,24},{12,28},{16,0},{20,4},{24,8},{28,12},{1,17},{... | collective-permute-start | bytes 2239496 | tf_op jit(solution)/shard_map/ppermute | solution.py:22
  411.9 34.0 %collective-permute-start.13 = (bf16[144,2592]{1,0:T(8,128)(2,1)}, bf16[144,2592]{1,0:T(8,128)(2,1)}, u32[]{:S(2)}, u32[]{:S(2)}) collective-permute-start(bf16[144,2592]{1,0:T(8,128)(2,1)} %get-tuple-element.107), channel_id=1, source_target_pairs={{0,8},{4,12},{8,0},{12,4},{16,24},{20,28},{24,16},{28,20},{1,9},{5... | collective-permute-start | bytes 2239496 | tf_op jit(solution)/shard_map/ppermute | solution.py:22
  (122 other events, 1486.4 us)

commit v2 on v1

--- a/solution.py
+++ b/solution.py
@@ -30,37 +30,65 @@
     return exchange(jnp.broadcast_to(block[None], (count,) + block.shape), axis)
 
 
-def gather_rows(block):
+def after(value, *others):
+    return lax.optimization_barrier((value,) + others)[0]
+
+
+def choose(core, first, second):
+    return jnp.where(core == 0, first, second), jnp.where(core == 0, second, first)
+
+
+def gather_pair_now(first, second):
     count = lax.axis_size("dp")
-    if count > 8:
-        return lax.all_gather(block, "dp", axis=0, tiled=True)
-    me = lax.axis_index("dp")
-    held = [block] + [swap(block, "dp", bits) for bits in range(2, count, 2)]
-    other = swap(jnp.stack(held), "dp", 1)
-    full = jnp.zeros((count,) + block.shape, block.dtype)
+    both = jnp.stack([first, second])
+    blocks = jnp.broadcast_to(both[None], (count // 2,) + both.shape)
+    mine = exchange(blocks.reshape((count,) + first.shape), "dp").reshape(-1, first.shape[1])
+    return mine, swap(mine, "dp", 1)
+
+
+def gather_pair_beside(first, second):
+    count = lax.axis_size("dp")
+    core, chip = lax.axis_index("dp") % 2, lax.axis_index("dp") // 2
+    keep, send = choose(core, first, second)
+    theirs = swap(send, "dp", 1)
+    rows = jnp.concatenate(choose(core, keep, theirs))
+    full = jnp.zeros((count // 2,) + rows.shape, rows.dtype)
     for step in range(count // 2):
-        full = lax.dynamic_update_index_in_dim(full, held[step], me ^ (2 * step), 0)
-        full = lax.dynamic_update_index_in_dim(full, other[step], me ^ (2 * step + 1), 0)
-    return full.reshape((count * block.shape[0],) + block.shape[1:])
-
-
-def scatter_rows(partial):
+        part = swap(rows, "dp", 2 * step) if step else rows
+        full = lax.dynamic_update_index_in_dim(full, part, chip ^ step, 0)
+    mine = full.reshape(-1, rows.shape[1])
+    return mine, swap(mine, "dp", 1)
+
+
+def scatter_pair(mine, other):
     count = lax.axis_size("dp")
-    share = partial.shape[0] // count
-    if count > 8:
-        return lax.psum_scatter(partial.astype(F32), "dp", scatter_dimension=0, tiled=True)
-    me = lax.axis_index("dp")
-    core = me % 2
-    blocks = partial.reshape(count // 2, 2, share, partial.shape[1])
-    theirs = lax.dynamic_index_in_dim(blocks, 1 - core, 1, keepdims=False)
-    ours = lax.dynamic_index_in_dim(blocks, core, 1, keepdims=False)
-    both = (ours.astype(F32) + swap(theirs, "dp", 1).astype(F32)).astype(BF16)
-    chip = me // 2
-    total = lax.dynamic_index_in_dim(both, chip, 0, keepdims=False).astype(F32)
+    core, chip = lax.axis_index("dp") % 2, lax.axis_index("dp") // 2
+    total = (mine + swap(other.astype(BF16), "dp", 1).astype(F32)).astype(BF16)
+    blocks = total.reshape(count // 2, total.shape[0] // (count // 2), total.shape[1])
+    rows = lax.dynamic_index_in_dim(blocks, chip, 0, keepdims=False).astype(F32)
     for step in range(1, count // 2):
-        sent = lax.dynamic_index_in_dim(both, chip ^ step, 0, keepdims=False)
-        total = total + swap(sent, "dp", 2 * step).astype(F32)
+        sent = lax.dynamic_index_in_dim(blocks, chip ^ step, 0, keepdims=False)
+        rows = rows + swap(sent, "dp", 2 * step).astype(F32)
+    half = rows.shape[0] // 2
+    keep, send = choose(core, rows[:half], rows[half:])
+    return choose(core, keep, swap(send, "dp", 1))
+
+
+def sum_beside(partial, axis):
+    count, me = lax.axis_size(axis), lax.axis_index(axis)
+    blocks = partial.astype(BF16).reshape((count, partial.shape[0] // count) + partial.shape[1:])
+    total = lax.dynamic_index_in_dim(blocks, me, 0, keepdims=False).astype(F32)
+    for bits in range(1, count):
+        sent = lax.dynamic_index_in_dim(blocks, me ^ bits, 0, keepdims=False)
+        total = total + swap(sent, axis, bits).astype(F32)
     return total
+
+
+def gather_beside(share, axis):
+    count, me = lax.axis_size(axis), lax.axis_index(axis)
+    parts = jnp.stack([share] + [swap(share, axis, bits) for bits in range(1, count)])
+    ordered = [lax.dynamic_index_in_dim(parts, me ^ place, 0, keepdims=False) for place in range(count)]
+    return jnp.concatenate(ordered)
 
 
 def sum_shares(partial, axis):
@@ -393,11 +421,11 @@
     total = rows * n_dp
     share = rows // n_tensor
 
-    full_qkv = gather_rows(w_qkv.reshape(share_width, 3 * features))
-    full_late = gather_rows(jnp.concatenate([w_fc1, w_fc2.T, w_proj.T], axis=1))
-    full_fc1 = full_late[:, :units]
-    full_fc2 = full_late[:, units : 2 * units]
-    full_proj = full_late[:, 2 * units :]
+    core = my_dp % 2
+    qk = w_qkv[:, :2].reshape(share_width, 2 * features)
+    vp = jnp.concatenate([w_qkv[:, 2], w_proj.T], axis=1)
+    early_mine, early_other = gather_pair_now(qk, vp)
+    full_vp = choose(core, early_other, early_mine)[0]
 
     cond = conditioning.astype(F32)
     gate = 1.0 / (1.0 + jnp.exp(-cond))
@@ -418,17 +446,22 @@
 
     unit_one, inverse_one = normed(tokens.astype(F32))
     hidden_one = (unit_one * (1.0 + pick(modulation[1], ids)) + pick(modulation[0], ids)).astype(BF16)
+    by_hidden = (((0,), (1,)), ((), ()))
+    by_last = (((1,), (1,)), ((), ()))
+    by_token = (((0,), (0,)), ((), ()))
+    blank = jnp.zeros((features, rows), BF16)
     bias = jnp.concatenate([b_qv[0], jnp.zeros_like(b_qv[0]), b_qv[1]]).astype(F32)
-    projected = lax.dot_general(
-        full_qkv, hidden_one, (((0,), (1,)), ((), ())), preferred_element_type=F32
-    )
+    from_mine = lax.dot_general(early_mine, hidden_one, by_hidden, preferred_element_type=F32)
+    from_other = lax.dot_general(early_other, hidden_one, by_hidden, preferred_element_type=F32)
+    projected = jnp.concatenate(choose(core, from_mine, from_other))[: 3 * features]
     projected = (projected + bias[:, None]).astype(BF16).reshape(3, heads, DH, rows)
     split = HeadSplit if 2 * heads == n_dp else Window
     attention = split(latent_len, rows)
     attended = attention.forward(projected)
-    attn_part = lax.dot_general(
-        attended, full_proj, (((0,), (1,)), ((), ())), preferred_element_type=F32
-    )
+    attended_low = jnp.concatenate([blank, attended])
+    attn_part = lax.dot_general(attended_low, full_vp, (((0,), (1,)), ((), ())), preferred_element_type=F32)
+    late_mine, late_other = gather_pair_beside(after(w_fc1, attended), after(w_fc2.T, attended))
+    full_fc1, full_fc2 = choose(core, late_mine, late_other)
     attn_out = sum_shares(attn_part, "tensor") + b_proj.astype(F32)
     own_tokens = own(tokens).astype(F32)
     gate_one = pick(modulation[2], own_ids)
@@ -445,8 +478,6 @@
     gelu_out = gelu_out.astype(BF16)
     d_pre_wide = d_gelu * gelu_slope
     d_pre = d_pre_wide.astype(BF16)
-    by_last = (((1,), (1,)), ((), ()))
-    by_token = (((0,), (0,)), ((), ()))
     d_two_part = lax.dot_general(d_pre, full_fc1, by_last, preferred_element_type=F32)
     d_hidden_two = sum_shares(d_two_part, "tensor")
     own_cotangent = own(cotangent).astype(F32)
@@ -454,37 +485,48 @@
     d_attn_own = (d_mid * gate_one).astype(BF16)
     d_attn = gather_shares(d_attn_own, "tensor")
 
-    mlp_part = lax.dot_general(gelu_out, full_fc2, by_last, preferred_element_type=F32)
-    mlp_out = sum_shares(mlp_part, "tensor") + b_fc2.astype(F32)
+    left_mine, left_other = choose(core, hidden_two, d_mlp)
+    right_mine, right_other = choose(core, d_pre, gelu_out)
+    grad_fc1, grad_fc2 = scatter_pair(
+        lax.dot_general(left_mine, right_mine, by_token, preferred_element_type=F32),
+        lax.dot_general(left_other, right_other, by_token, preferred_element_type=F32),
+    )
+
+    mlp_part = lax.dot_general(
+        after(gelu_out, d_attn), full_fc2, by_last, preferred_element_type=F32
+    )
+    mlp_out = sum_beside(mlp_part, "tensor") + b_fc2.astype(F32)
     gate_two = pick(modulation[5], own_ids)
-    result = gather_shares((residual_mid + gate_two * mlp_out).astype(BF16), "tensor")
-
-    d_attended = lax.dot_general(
-        full_proj, d_attn, (((0,), (1,)), ((), ())), preferred_element_type=F32
-    ).astype(BF16)
+    result = gather_beside((residual_mid + gate_two * mlp_out).astype(BF16), "tensor")
+
+    d_attended = lax.dot_general(full_vp, d_attn, by_hidden, preferred_element_type=F32)
+    d_attended = d_attended[features:].astype(BF16)
     d_projected = attention.backward(d_attended).reshape(3 * features, rows)
+    d_qk = d_projected[: 2 * features]
+    d_value = d_projected[2 * features :]
+    d_mine, d_other = choose(core, d_qk, jnp.concatenate([d_value, blank]))
     d_one_part = lax.dot_general(
-        d_projected, full_qkv, (((0,), (1,)), ((), ())), preferred_element_type=F32
-    )
+        d_mine, early_mine, (((0,), (1,)), ((), ())), preferred_element_type=F32
+    ) + lax.dot_general(d_other, early_other, (((0,), (1,)), ((), ())), preferred_element_type=F32)
     d_hidden_one = sum_shares(d_one_part, "tensor")
     own_unit, own_inverse = own(unit_one), own(inverse_one)
     scale_one = 1.0 + pick(modulation[1], own_ids)
     grad_own = d_mid + norm_back(own_unit, own_inverse, d_hidden_one * scale_one)
-    grad_tokens = gather_shares(grad_own.astype(BF16), "tensor").astype(F32)
-
-    grad_fc1 = lax.dot_general(hidden_two, d_pre, by_token, preferred_element_type=F32)
-    grad_fc2 = lax.dot_general(d_mlp, gelu_out, by_token, preferred_element_type=F32)
-    grad_proj = lax.dot_general(
-        d_attn, attended, (((0,), (1,)), ((), ())), preferred_element_type=F32
-    )
-    grad_late = jnp.concatenate(
-        [grad_fc1.astype(BF16), grad_fc2.astype(BF16), grad_proj.astype(BF16)], axis=1
-    )
-    grad_late = scatter_rows(grad_late)
-    grad_qkv = lax.dot_general(
-        hidden_one, d_projected, (((0,), (1,)), ((), ())), preferred_element_type=F32
-    )
-    grad_qkv = scatter_rows(grad_qkv.astype(BF16)).reshape(share_width, 3, features)
+    grad_tokens = gather_beside(grad_own.astype(BF16), "tensor").astype(F32)
+
+    left = jnp.concatenate([hidden_one, d_attn])
+    right_qk = jnp.concatenate([d_qk, jnp.zeros_like(d_qk)], axis=1)
+    right_vp = jnp.concatenate(
+        [jnp.concatenate([d_value, blank]), attended_low], axis=1
+    )
+    right_mine, right_other = choose(core, right_qk, right_vp)
+    by_rows = (((0,), (1,)), ((), ()))
+    grad_qk, grad_vp = scatter_pair(
+        lax.dot_general(left, right_mine, by_rows, preferred_element_type=F32),
+        lax.dot_general(left, right_other, by_rows, preferred_element_type=F32),
+    )
+    grad_qkv = jnp.concatenate([grad_qk, grad_vp[:, :features]], axis=1)
+    grad_qkv = grad_qkv.reshape(share_width, 3, features)
 
     d_float = d_projected.astype(F32).reshape(3, features, rows)
     bias_part = jnp.concatenate(
@@ -496,24 +538,25 @@
             jnp.sum(d_float[2], axis=1),
         ]
     )
-    bias_total = jnp.sum(gather(bias_part, "dp", n_dp), axis=0)
-
-    d_token = jnp.stack(
-        [
-            d_hidden_one,
-            d_hidden_one * own_unit,
-            d_mid * attn_out,
-            d_hidden_two,
-            d_hidden_two * unit_two,
-            own_cotangent * mlp_out,
-        ],
-        axis=1,
-    ).astype(BF16)
+    bias_rows = bias_part.reshape(-1, features)
+
     one_hot = (jnp.arange(latents, dtype=jnp.int32)[:, None] == own_ids[None, :]).astype(BF16)
-    d_mod_part = jnp.dot(one_hot, d_token.reshape(share, 6 * width), preferred_element_type=F32)
-    d_mod_part = d_mod_part.reshape(latents * 6, n_tensor, features).transpose(1, 0, 2)
+
+    def by_latent(parts):
+        joined = jnp.concatenate([part.astype(BF16) for part in parts], axis=1)
+        sums = jnp.dot(one_hot, joined, preferred_element_type=F32)
+        return sums.reshape(latents, len(parts), n_tensor, features)
+
+    d_mod_last = by_latent(
+        [d_mid * attn_out, d_hidden_two, d_hidden_two * unit_two, own_cotangent * mlp_out]
+    )
+    d_mod_first = by_latent([d_hidden_one, d_hidden_one * own_unit])
+    d_mod_part = jnp.concatenate([d_mod_first, d_mod_last], axis=1).transpose(2, 0, 1, 3)
+    d_mod_part = d_mod_part.reshape(n_tensor, latents * 6, features)
     d_mod_mine = jnp.sum(exchange(d_mod_part, "tensor"), axis=0)
-    d_mod = jnp.sum(gather(d_mod_mine, "dp", n_dp), axis=0).reshape(latents, 6 * features)
+    sums = jnp.sum(gather(jnp.concatenate([d_mod_mine, bias_rows]), "dp", n_dp), axis=0)
+    d_mod = sums[: 6 * latents].reshape(latents, 6 * features)
+    bias_total = sums[6 * latents :].reshape(-1)
     grad_b_ada = jnp.sum(d_mod, axis=0).reshape(6, features)
     grad_w_ada = lax.dot_general(
         own_activated.astype(F32), d_mod, by_token, precision=lax.Precision.HIGHEST
@@ -524,8 +567,9 @@
         jnp.concatenate([high, low]), flat_ada, by_last, preferred_element_type=F32
     )
     d_active = d_active[:latents] + d_active[latents:]
-    d_active = jnp.sum(gather(d_active, "tensor", n_tensor), axis=0)
-    d_active = gather(d_active, "dp", n_dp).transpose(1, 0, 2).reshape(latents, width)
+    d_active = gather(d_active, ("dp", "tensor"), n_dp * n_tensor)
+    d_active = jnp.sum(d_active.reshape(n_dp, n_tensor, latents, share_width), axis=1)
+    d_active = d_active.transpose(1, 0, 2).reshape(latents, width)
     grad_cond = d_active * (gate * (1.0 + cond * (1.0 - gate)))
 
     return (
@@ -536,11 +580,11 @@
         grad_b_ada,
         grad_qkv,
         bias_total[2 * width + units :].reshape(2, features),
-        grad_late[:, 2 * units :].T,
+        grad_vp[:, features:].T,
         bias_total[width : 2 * width],
-        grad_late[:, :units],
+        grad_fc1,
         bias_total[2 * width : 2 * width + units],
-        grad_late[:, units : 2 * units].T,
+        grad_fc2.T,
         bias_total[:width],
     )
 

time: 454 us -> 394 us (0.87)
  waiting for transfers between devices: 177 us -> 145 us
  local copies, waits for them, and re-layouts: 79 us -> 49.2 us
  blocking collectives: 0 us -> 26.5 us
  starting transfers between devices: 89 us -> 75.4 us
  other arithmetic: 48.7 us -> 36.5 us
    all_to_all x19 -> x13, waiting for transfers between devices: 150 us -> 84.1 us  [exchange(): return lax.all_to_all(blocks, axis, 0, 0, tiled=True)]
    ppermute x16 -> x25, waiting for transfers between devices: 26.6 us -> 60.7 us  [swap(): return lax.ppermute(block, axis, route)]
    all_to_all x0 -> x2, blocking collectives: none -> 26.5 us  [exchange(): return lax.all_to_all(blocks, axis, 0, 0, tiled=True)]
    dynamic_update_slice x15 -> x3, local copies, waits for them, and re-layouts: 25 us -> 3.76 us  [gather_pair_beside(): full = lax.dynamic_update_index_in_dim(full, part, chip ^ step, 0)]
    all_to_all x19 -> x13, starting transfers between devices: 71.9 us -> 51.3 us  [exchange(): return lax.all_to_all(blocks, axis, 0, 0, tiled=True)]
    concatenate x1 -> x2, local copies, waits for them, and re-layouts: 9.19 us -> 1.47 us  [the longest x1 0.75 us: local(): attended_low = jnp.concatenate([blank, attended])]
    ppermute x16 -> x25, starting transfers between devices: 17.1 us -> 24 us  [swap(): return lax.ppermute(block, axis, route)]
    dot_general x10 -> x13, matrix products: 25.6 us -> 29 us  [the longest x1 4.13 us: local(): lax.dot_general(left_other, right_other, by_token, preferred_element_type...]
  transfers between devices with their start and end apart: 35 -> 38, of which waited for: 20 -> 20; matrix products, arithmetic and copies ran while one was open for 27% -> 23% of each run, Pallas kernels for 2% -> 2%
where the time goes in v2:
time: 394 us; the launch traced here: 391 us
  waiting for transfers between devices  145 us (37%)
  starting transfers between devices  75.4 us (19%)
  local copies, waits for them, and re-layouts  49.2 us (12%)
  matrix products  42.5 us (11%)
  other arithmetic  36.5 us (9%)
  blocking collectives  26.5 us (7%)
  Pallas kernels  14.3 us (4%)
    all_to_all x13, waiting for transfers between devices, exchange(): return lax.all_to_all(blocks, axis, 0, 0, tiled=True)  84.1 us
    ppermute x25, waiting for transfers between devices, swap(): return lax.ppermute(block, axis, route)  60.7 us
    all_to_all x13, starting transfers between devices, exchange(): return lax.all_to_all(blocks, axis, 0, 0, tiled=True)  51.3 us
    all_to_all x2, blocking collectives, exchange(): return lax.all_to_all(blocks, axis, 0, 0, tiled=True)  26.5 us
    ppermute x25, starting transfers between devices, swap(): return lax.ppermute(block, axis, route)  24 us
    unnamed x190, local copies, waits for them, and re-layouts  9.43 us
    pallas_call x1, Pallas kernels, attend_backward(): pl.pallas_call(lambda *refs: backward_kernel(meta.shape[0] - 1, *refs), o...  8.06 us
  transfers between devices with their start and end apart: 38, of which 20 were waited for; matrix products, arithmetic and copies ran while one was open for 23% of the time, Pallas kernels for 2%

profile of v2, /device:TPU:0, one launch (start us, length us, event | category | flops | bytes accessed | tf_op | source)
XLA Modules:
  0.0 391.3 jit_solution(1655734556218898914)
XLA Ops:
  5.0 5.2 %all-to-all-start = ((f32[8,3,1728]{2,1,0:T(4,128)}), f32[8,3,1728]{2,1,0:T(4,128)S(1)}, u32[]{:S(2)}, u32[]{:S(2)}) async-start(f32[8,3,1728]{2,1,0:T(4,128)} %broadcast_in_dim.378), calls=%async_computation | async-start | bytes 458752 | tf_op jit(solution)/shard_map/all_to_all | solution.py:26
  11.4 5.3 %all-to-all-done = f32[8,3,1728]{2,1,0:T(4,128)S(1)} async-done(((f32[8,3,1728]{2,1,0:T(4,128)}), f32[8,3,1728]{2,1,0:T(4,128)S(1)}, u32[]{:S(2)}, u32[]{:S(2)}) %all-to-all-start) | async-done | bytes 165920 | tf_op jit(solution)/shard_map/all_to_all | solution.py:26
  18.0 3.6 all-to-all-start.2
  22.1 19.4 %all-to-all-done.2 = bf16[8,144,576]{2,1,0:T(8,128)(2,1)S(1)} async-done(((bf16[8,144,576]{2,1,0:T(8,128)(2,1)}), bf16[8,144,576]{2,1,0:T(8,128)(2,1)S(1)}, u32[]{:S(2)}, u32[]{:S(2)}) %all-to-all-start.2) | async-done | bytes 1327136 | tf_op jit(solution)/shard_map/all_to_all | solution.py:26
  43.9 4.9 %all-to-all-start.1 = ((f32[4,3,1728]{2,1,0:T(4,128)}), f32[4,3,1728]{2,1,0:T(4,128)S(1)}, u32[]{:S(2)}, u32[]{:S(2)}) async-start(f32[4,3,1728]{2,1,0:T(4,128)} %broadcast_in_dim.379), calls=%async_computation.1 | async-start | bytes 229376 | tf_op jit(solution)/shard_map/all_to_all | solution.py:26
  48.9 6.1 %all-to-all-done.1 = f32[4,3,1728]{2,1,0:T(4,128)S(1)} async-done(((f32[4,3,1728]{2,1,0:T(4,128)}), f32[4,3,1728]{2,1,0:T(4,128)S(1)}, u32[]{:S(2)}, u32[]{:S(2)}) %all-to-all-start.1) | async-done | bytes 82976 | tf_op jit(solution)/shard_map/all_to_all | solution.py:26
  56.9 3.6 fusion.2
  64.4 3.5 all-to-all-start.3
  68.1 11.9 %all-to-all-done.3.refs_1_ = bf16[8,72,640]{2,1,0:T(8,128)(2,1)S(1)} async-done(((bf16[8,72,640]{2,1,0:T(8,128)(2,1)}), bf16[8,72,640]{2,1,0:T(8,128)(2,1)S(1)}, u32[]{:S(2)}, u32[]{:S(2)}) %all-to-all-start.3) | async-done | bytes 737312 | tf_op jit(solution)/shard_map/all_to_all | solution.py:26
  80.0 6.2 %attend_forward.1 = (bf16[8,72,128]{2,1,0:T(8,128)(2,1)S(1)}, f32[8,72,128]{2,1,0:T(8,128)S(1)}, f32[8,1,128]{2,1,0:T(1,128)S(1)}) custom-call(s32[4]{0:T(128)S(1)} %pad_add_fusion.refs_0_, bf16[8,72,640]{2,1,0:T(8,128)(2,1)S(1)} %all-to-all-done.3.refs_1_), custom_call_target="tpu_custom_call" | custom-call | flops 1000000000 | bytes 4000000 | tf_op jit(solution)/shard_map/attend_forward/pallas_call | solution.py:217
  86.3 8.2 %all_to_all.75 = bf16[8,72,128]{2,1,0:T(8,128)(2,1)S(1)} all-to-all(bf16[8,72,128]{2,1,0:T(8,128)(2,1)S(1)} %get-tuple-element.19), channel_id=1, replica_groups=mesh['dp'=8,'tensor'=4] {'dp'}, dimensions={0} | all-to-all | bytes 294912 | tf_op jit(solution)/shard_map/all_to_all | solution.py:26
  104.9 4.3 %all-to-all-start.5 = ((bf16[4,64,1152]{2,1,0:T(8,128)(2,1)}), bf16[4,64,1152]{2,1,0:T(8,128)(2,1)}, u32[]{:S(2)}, u32[]{:S(2)}) async-start(bf16[4,64,1152]{2,1,0:T(8,128)(2,1)} %bitcast.178), calls=%async_computation.5 | async-start | bytes 1179648 | tf_op jit(solution)/shard_map/all_to_all | solution.py:26
  118.8 21.1 %collective-permute-done.3 = bf16[288,1152]{1,0:T(8,128)(2,1)S(1)} collective-permute-done((bf16[288,1152]{1,0:T(8,128)(2,1)}, bf16[288,1152]{1,0:T(8,128)(2,1)S(1)}, u32[]{:S(2)}, u32[]{:S(2)}) %collective-permute-start.3) | collective-permute-done | bytes 663584 | tf_op jit(solution)/shard_map/ppermute | solution.py:22
  145.8 4.5 %all-to-all-start.6 = ((bf16[4,64,1152]{2,1,0:T(8,128)(2,1)}), bf16[4,64,1152]{2,1,0:T(8,128)(2,1)S(1)}, u32[]{:S(2)}, u32[]{:S(2)}) async-start(bf16[4,64,1152]{2,1,0:T(8,128)(2,1)} %broadcast_in_dim.428), calls=%async_computation.6 | async-start | bytes 1179648 | tf_op jit(solution)/shard_map/all_to_all | solution.py:26
  150.3 16.5 %all-to-all-done.6 = bf16[4,64,1152]{2,1,0:T(8,128)(2,1)S(1)} async-done(((bf16[4,64,1152]{2,1,0:T(8,128)(2,1)}), bf16[4,64,1152]{2,1,0:T(8,128)(2,1)S(1)}, u32[]{:S(2)}, u32[]{:S(2)}) %all-to-all-start.6) | async-done | bytes 589856 | tf_op jit(solution)/shard_map/all_to_all | solution.py:26
  166.9 4.1 %multiply_convert_fusion.1 = (bf16[256,1152]{1,0:T(8,128)(2,1)}, f32[256,1152]{1,0:T(8,128)S(1)}) fusion(f32[1152]{0:T(1024)S(1)} %convert_element_type.217, bf16[256,1152]{1,0:T(8,128)(2,1)S(1)} %bitcast.175, bf16[1152,1152]{1,0:T(8,128)(2,1)} %bitcast.22, bf16[1152,1152]{1,0:T(8,128)(2,1)} %collective-permute-done.5, pred[]{:T(512)S(6)} %eq.48), kind=kOutput, calls=%fused_computation.38 | convolution fusion | flops 683753472 | bytes 7672321 | tf_op jit(solution)/shard_map/dot_general | solution.py:476
  171.1 4.0 %convert_reduce_fusion.1 = (f32[1152]{0:T(1024)}, bf16[256,1152]{1,0:T(8,128)(2,1)S(1)}) fusion(f32[256,1152]{1,0:T(8,128)S(1)} %get-tuple-element.193, bf16[1152,1152]{1,0:T(8,128)(2,1)} %collective-permute-done.5, bf16[1152,1152]{1,0:T(8,128)(2,1)} %bitcast.22, pred[]{:T(512)S(6)} %eq.48, bf16[256,1152]{1,0:T(8,128)(2,1)S(1)} %copy-done.15, ...), kind=kOutput, calls=%fused_computation.32 | convolution fusion | flops 688765824 | bytes 7686913 | tf_op jit(solution)/shard_map/dot_general | solution.py:475
  178.3 18.3 %all_to_all.76 = bf16[4,64,1152]{2,1,0:T(8,128)(2,1)S(1)} all-to-all(bf16[4,64,1152]{2,1,0:T(8,128)(2,1)S(1)} %bitcast.179), channel_id=1, replica_groups=mesh['dp'=8,'tensor'=4] {'tensor'}, dimensions={0} | all-to-all | bytes 1179648 | tf_op jit(solution)/shard_map/all_to_all | solution.py:26
  200.5 3.5 all-to-all-start.8
  207.4 4.1 %convolution_convert_fusion = bf16[1152,1152]{1,0:T(8,128)(2,1)} fusion(bf16[256,1152]{1,0:T(8,128)(2,1)} %get-tuple-element.22, bf16[256,1152]{1,0:T(8,128)(2,1)} %copy-done.90, bf16[256,1152]{1,0:T(8,128)(2,1)} %bitcast.176, pred[]{:T(512)S(6)} %eq.48, bf16[256,1152]{1,0:T(8,128)(2,1)} %param.27, f32[1152]{0:T(1024)} %copy-done.42, f32[1152]{0:T(1024)} %copy-done.45, ...), kind=kOutput, calls=%fused_computation | convolution fusion | flops 683163648 | bytes 5028097 | tf_op jit(solution)/shard_map/dot_general | solution.py:492
  211.5 7.6 %all-to-all-done.8 = bf16[4,64,1152]{2,1,0:T(8,128)(2,1)S(1)} async-done(((bf16[4,64,1152]{2,1,0:T(8,128)(2,1)}), bf16[4,64,1152]{2,1,0:T(8,128)(2,1)S(1)}, u32[]{:S(2)}, u32[]{:S(2)}) %all-to-all-start.8) | async-done | bytes 589856 | tf_op jit(solution)/shard_map/all_to_all | solution.py:26
  236.3 3.9 all-to-all-done.9.refs_2_
  240.1 8.1 %attend_backward.1 = bf16[8,72,640]{2,1,0:T(8,128)(2,1)} custom-call(s32[4]{0:T(128)S(1)} %pad_add_fusion.refs_0_, bf16[8,72,640]{2,1,0:T(8,128)(2,1)S(1)} %all-to-all-done.3.refs_1_, bf16[8,72,128]{2,1,0:T(8,128)(2,1)S(1)} %all-to-all-done.9.refs_2_, f32[8,72,128]{2,1,0:T(8,128)S(1)} %get-tuple-element.23.refs_3_, f32[8,1,128]{2,1,0:T(1,128)S(1)} %get-tuple-element.24.refs_4_), custom_call_target="tpu_custom_call" | custom-call | flops 3000000000 | bytes 4000000 | tf_op jit(solution)/shard_map/attend_backward/pallas_call | solution.py:241
  248.2 3.9 all-to-all-start.10
  262.3 6.2 %collective-permute-done.10 = bf16[64,1152]{1,0:T(8,128)(2,1)S(1)} collective-permute-done((bf16[64,1152]{1,0:T(8,128)(2,1)S(1)}, bf16[64,1152]{1,0:T(8,128)(2,1)S(1)}, u32[]{:S(2)}, u32[]{:S(2)}) %collective-permute-start.10) | collective-permute-done | bytes 147488 | tf_op jit(solution)/shard_map/ppermute | solution.py:22
  284.5 4.3 %all-to-all-start.11 = ((bf16[4,64,1152]{2,1,0:T(8,128)(2,1)}), bf16[4,64,1152]{2,1,0:T(8,128)(2,1)}, u32[]{:S(2)}, u32[]{:S(2)}) async-start(bf16[4,64,1152]{2,1,0:T(8,128)(2,1)} %bitcast.47), calls=%async_computation.11 | async-start | bytes 1179648 | tf_op jit(solution)/shard_map/all_to_all | solution.py:26
  297.2 12.7 %collective-permute-done.22 = bf16[288,1152]{1,0:T(8,128)(2,1)} collective-permute-done((bf16[288,1152]{1,0:T(8,128)(2,1)}, bf16[288,1152]{1,0:T(8,128)(2,1)}, u32[]{:S(2)}, u32[]{:S(2)}) %collective-permute-start.22) | collective-permute-done | bytes 663584 | tf_op jit(solution)/shard_map/ppermute | solution.py:22
  325.6 7.2 %all-to-all-done.12 = f32[4,18,288]{2,1,0:T(8,128)S(1)} async-done(((f32[4,18,288]{2,1,0:T(8,128)}), f32[4,18,288]{2,1,0:T(8,128)S(1)}, u32[]{:S(2)}, u32[]{:S(2)}) %all-to-all-start.12) | async-done | bytes 82976 | tf_op jit(solution)/shard_map/all_to_all | solution.py:26
  333.7 4.1 %all-to-all-start.13 = ((f32[8,32,288]{2,1,0:T(8,128)}), f32[8,32,288]{2,1,0:T(8,128)}, u32[]{:S(2)}, u32[]{:S(2)}) async-start(f32[8,32,288]{2,1,0:T(8,128)} %broadcast_in_dim.441), calls=%async_computation.13 | async-start | bytes 786432 | tf_op jit(solution)/shard_map/all_to_all | solution.py:26
  340.0 6.1 %all-to-all-done.13 = f32[8,32,288]{2,1,0:T(8,128)} async-done(((f32[8,32,288]{2,1,0:T(8,128)}), f32[8,32,288]{2,1,0:T(8,128)}, u32[]{:S(2)}, u32[]{:S(2)}) %all-to-all-start.13) | async-done | bytes 294944 | tf_op jit(solution)/shard_map/all_to_all | solution.py:26
  371.2 7.0 %collective-permute-done.18 = bf16[288,576]{1,0:T(8,128)(2,1)} collective-permute-done((bf16[288,576]{1,0:T(8,128)(2,1)}, bf16[288,576]{1,0:T(8,128)(2,1)}, u32[]{:S(2)}, u32[]{:S(2)}) %collective-permute-start.18) | collective-permute-done | bytes 331808 | tf_op jit(solution)/shard_map/ppermute | solution.py:22
  378.2 6.7 %collective-permute-done.17 = bf16[288,576]{1,0:T(8,128)(2,1)} collective-permute-done((bf16[288,576]{1,0:T(8,128)(2,1)}, bf16[288,576]{1,0:T(8,128)(2,1)}, u32[]{:S(2)}, u32[]{:S(2)}) %collective-permute-start.17) | collective-permute-done | bytes 331808 | tf_op jit(solution)/shard_map/ppermute | solution.py:22
  (414 shorter events, 152.8 us)
Async XLA Ops:
  5.0 11.8 %all-to-all-start = ((f32[8,3,1728]{2,1,0:T(4,128)}), f32[8,3,1728]{2,1,0:T(4,128)S(1)}, u32[]{:S(2)}, u32[]{:S(2)}) async-start(f32[8,3,1728]{2,1,0:T(4,128)} %broadcast_in_dim.378), calls=%async_computation | async-start | bytes 458752 | tf_op jit(solution)/shard_map/all_to_all | solution.py:26
  18.0 23.5 %all-to-all-start.2 = ((bf16[8,144,576]{2,1,0:T(8,128)(2,1)}), bf16[8,144,576]{2,1,0:T(8,128)(2,1)S(1)}, u32[]{:S(2)}, u32[]{:S(2)}) async-start(bf16[8,144,576]{2,1,0:T(8,128)(2,1)} %bitcast.7), calls=%async_computation.2 | async-start | bytes 2949120 | tf_op jit(solution)/shard_map/all_to_all | solution.py:26
  43.2 17.8 %collective-permute-start = (bf16[1152,576]{0,1:T(8,128)(2,1)}, bf16[1152,576]{0,1:T(8,128)(2,1)}, u32[]{:S(2)}, u32[]{:S(2)}) collective-permute-start(bf16[1152,576]{0,1:T(8,128)(2,1)} %copy.101), channel_id=1, source_target_pairs={{0,4},{4,0},{8,12},{12,8},{16,20},{20,16},{24,28},{28,24},{1,5},{5... | collective-permute-start | bytes 3981320 | tf_op jit(solution)/shard_map/ppermute | solution.py:22
  64.4 15.6 %all-to-all-start.3 = ((bf16[8,72,640]{2,1,0:T(8,128)(2,1)}), bf16[8,72,640]{2,1,0:T(8,128)(2,1)S(1)}, u32[]{:S(2)}, u32[]{:S(2)}) async-start(bf16[8,72,640]{2,1,0:T(8,128)(2,1)} %bitcast.12), calls=%async_computation.3 | async-start | bytes 1474560 | tf_op jit(solution)/shard_map/all_to_all | solution.py:26
  98.8 18.1 %collective-permute-start.2 = (bf16[288,1152]{1,0:T(8,128)(2,1)}, bf16[288,1152]{1,0:T(8,128)(2,1)}, u32[]{:S(2)}, u32[]{:S(2)}) collective-permute-start(bf16[288,1152]{1,0:T(8,128)(2,1)} %pad_maximum_fusion.7), channel_id=1, source_target_pairs={{0,8},{4,12},{8,0},{12,4},{16,24},{20,28},{24,16},{28,20},{1,9},{5... | collective-permute-start | bytes 1990664 | tf_op jit(solution)/shard_map/ppermute | solution.py:22
  104.9 37.7 %all-to-all-start.5 = ((bf16[4,64,1152]{2,1,0:T(8,128)(2,1)}), bf16[4,64,1152]{2,1,0:T(8,128)(2,1)}, u32[]{:S(2)}, u32[]{:S(2)}) async-start(bf16[4,64,1152]{2,1,0:T(8,128)(2,1)} %bitcast.178), calls=%async_computation.5 | async-start | bytes 1179648 | tf_op jit(solution)/shard_map/all_to_all | solution.py:26
  109.3 30.6 %collective-permute-start.3 = (bf16[288,1152]{1,0:T(8,128)(2,1)}, bf16[288,1152]{1,0:T(8,128)(2,1)S(1)}, u32[]{:S(2)}, u32[]{:S(2)}) collective-permute-start(bf16[288,1152]{1,0:T(8,128)(2,1)} %pad_maximum_fusion.7), channel_id=1, source_target_pairs={{0,16},{4,20},{8,24},{12,28},{16,0},{20,4},{24,8},{28,12},{1,17},{... | collective-permute-start | bytes 1990664 | tf_op jit(solution)/shard_map/ppermute | solution.py:22
  109.9 30.9 %collective-permute-start.4 = (bf16[288,1152]{1,0:T(8,128)(2,1)}, bf16[288,1152]{1,0:T(8,128)(2,1)S(1)}, u32[]{:S(2)}, u32[]{:S(2)}) collective-permute-start(bf16[288,1152]{1,0:T(8,128)(2,1)} %pad_maximum_fusion.7), channel_id=1, source_target_pairs={{0,24},{4,28},{8,16},{12,20},{16,8},{20,12},{24,0},{28,4},{1,25},{... | collective-permute-start | bytes 1990664 | tf_op jit(solution)/shard_map/ppermute | solution.py:22
  141.7 25.2 %collective-permute-start.5 = (bf16[1152,1152]{1,0:T(8,128)(2,1)}, bf16[1152,1152]{1,0:T(8,128)(2,1)}, u32[]{:S(2)}, u32[]{:S(2)}) collective-permute-start(bf16[1152,1152]{1,0:T(8,128)(2,1)} %bitcast.22), channel_id=1, source_target_pairs={{0,4},{4,0},{8,12},{12,8},{16,20},{20,16},{24,28},{28,24},{1,5},{5... | collective-permute-start | bytes 7962632 | tf_op jit(solution)/shard_map/ppermute | solution.py:22
  145.8 21.1 %all-to-all-start.6 = ((bf16[4,64,1152]{2,1,0:T(8,128)(2,1)}), bf16[4,64,1152]{2,1,0:T(8,128)(2,1)S(1)}, u32[]{:S(2)}, u32[]{:S(2)}) async-start(bf16[4,64,1152]{2,1,0:T(8,128)(2,1)} %broadcast_in_dim.428), calls=%async_computation.6 | async-start | bytes 1179648 | tf_op jit(solution)/shard_map/all_to_all | solution.py:26
  200.5 18.6 %all-to-all-start.8 = ((bf16[4,64,1152]{2,1,0:T(8,128)(2,1)}), bf16[4,64,1152]{2,1,0:T(8,128)(2,1)S(1)}, u32[]{:S(2)}, u32[]{:S(2)}) async-start(bf16[4,64,1152]{2,1,0:T(8,128)(2,1)} %broadcast_in_dim.437), calls=%async_computation.8 | async-start | bytes 1179648 | tf_op jit(solution)/shard_map/all_to_all | solution.py:26
  211.5 60.8 %collective-permute-start.20 = (bf16[1152,1152]{1,0:T(8,128)(2,1)}, bf16[1152,1152]{1,0:T(8,128)(2,1)}, u32[]{:S(2)}, u32[]{:S(2)}) collective-permute-start(bf16[1152,1152]{1,0:T(8,128)(2,1)} %convolution_convert_fusion), channel_id=1, source_target_pairs={{0,4},{4,0},{8,12},{12,8},{16,20},{20,16},{24,28},{28,24},{1,5},{5... | collective-permute-start | bytes 7962632 | tf_op jit(solution)/shard_map/ppermute | solution.py:22
  226.0 26.2 %collective-permute-start.8 = (bf16[64,1152]{1,0:T(8,128)(2,1)}, bf16[64,1152]{1,0:T(8,128)(2,1)}, u32[]{:S(2)}, u32[]{:S(2)}) collective-permute-start(bf16[64,1152]{1,0:T(8,128)(2,1)} %get-tuple-element.169), channel_id=1, source_target_pairs={{0,3},{1,2},{2,1},{3,0},{4,7},{5,6},{6,5},{7,4},{8,11},{9,10},{10,... | collective-permute-start | bytes 442376 | tf_op jit(solution)/shard_map/ppermute | solution.py:22
  227.4 24.7 %collective-permute-start.7 = (bf16[64,1152]{1,0:T(8,128)(2,1)}, bf16[64,1152]{1,0:T(8,128)(2,1)}, u32[]{:S(2)}, u32[]{:S(2)}) collective-permute-start(bf16[64,1152]{1,0:T(8,128)(2,1)} %get-tuple-element.170), channel_id=1, source_target_pairs={{0,2},{1,3},{2,0},{3,1},{4,6},{5,7},{6,4},{7,5},{8,10},{9,11},{10,... | collective-permute-start | bytes 442376 | tf_op jit(solution)/shard_map/ppermute | solution.py:22
  227.4 24.7 %collective-permute-start.6 = (bf16[64,1152]{1,0:T(8,128)(2,1)}, bf16[64,1152]{1,0:T(8,128)(2,1)}, u32[]{:S(2)}, u32[]{:S(2)}) collective-permute-start(bf16[64,1152]{1,0:T(8,128)(2,1)} %get-tuple-element.168), channel_id=1, source_target_pairs={{0,1},{1,0},{2,3},{3,2},{4,5},{5,4},{6,7},{7,6},{8,9},{9,8},{10,11... | collective-permute-start | bytes 442376 | tf_op jit(solution)/shard_map/ppermute | solution.py:22
  248.2 22.1 %all-to-all-start.10 = ((bf16[8,72,640]{2,1,0:T(8,128)(2,1)}), bf16[8,72,640]{2,1,0:T(8,128)(2,1)S(1)}, u32[]{:S(2)}, u32[]{:S(2)}) async-start(bf16[8,72,640]{2,1,0:T(8,128)(2,1)} %attend_backward.1), calls=%async_computation.10 | async-start | bytes 1474560 | tf_op jit(solution)/shard_map/all_to_all | solution.py:26
  255.1 13.4 %collective-permute-start.10 = (bf16[64,1152]{1,0:T(8,128)(2,1)S(1)}, bf16[64,1152]{1,0:T(8,128)(2,1)S(1)}, u32[]{:S(2)}, u32[]{:S(2)}) collective-permute-start(bf16[64,1152]{1,0:T(8,128)(2,1)S(1)} %get-tuple-element.154), channel_id=1, source_target_pairs={{0,2},{1,3},{2,0},{3,1},{4,6},{5,7},{6,4},{7,5},{8,10},{9,11},{10,... | collective-permute-start | bytes 442376 | tf_op jit(solution)/shard_map/ppermute | solution.py:22
  255.1 13.4 %collective-permute-start.9 = (bf16[64,1152]{1,0:T(8,128)(2,1)S(1)}, bf16[64,1152]{1,0:T(8,128)(2,1)}, u32[]{:S(2)}, u32[]{:S(2)}) collective-permute-start(bf16[64,1152]{1,0:T(8,128)(2,1)S(1)} %get-tuple-element.154), channel_id=1, source_target_pairs={{0,1},{1,0},{2,3},{3,2},{4,5},{5,4},{6,7},{7,6},{8,9},{9,8},{10,11... | collective-permute-start | bytes 442376 | tf_op jit(solution)/shard_map/ppermute | solution.py:22
  278.2 19.0 %collective-permute-start.23 = (bf16[288,1152]{1,0:T(8,128)(2,1)}, bf16[288,1152]{1,0:T(8,128)(2,1)S(1)}, u32[]{:S(2)}, u32[]{:S(2)}) collective-permute-start(bf16[288,1152]{1,0:T(8,128)(2,1)} %get-tuple-element.140), channel_id=1, source_target_pairs={{0,24},{4,28},{8,16},{12,20},{16,8},{20,12},{24,0},{28,4},{1,25},{... | collective-permute-start | bytes 1990664 | tf_op jit(solution)/shard_map/ppermute | solution.py:22
  280.7 29.1 %collective-permute-start.22 = (bf16[288,1152]{1,0:T(8,128)(2,1)}, bf16[288,1152]{1,0:T(8,128)(2,1)}, u32[]{:S(2)}, u32[]{:S(2)}) collective-permute-start(bf16[288,1152]{1,0:T(8,128)(2,1)} %get-tuple-element.141), channel_id=1, source_target_pairs={{0,16},{4,20},{8,24},{12,28},{16,0},{20,4},{24,8},{28,12},{1,17},{... | collective-permute-start | bytes 1990664 | tf_op jit(solution)/shard_map/ppermute | solution.py:22
  281.3 28.9 %collective-permute-start.21 = (bf16[288,1152]{1,0:T(8,128)(2,1)S(1)}, bf16[288,1152]{1,0:T(8,128)(2,1)}, u32[]{:S(2)}, u32[]{:S(2)}) collective-permute-start(bf16[288,1152]{1,0:T(8,128)(2,1)S(1)} %get-tuple-element.139), channel_id=1, source_target_pairs={{0,8},{4,12},{8,0},{12,4},{16,24},{20,28},{24,16},{28,20},{1,9},{5... | collective-permute-start | bytes 1990664 | tf_op jit(solution)/shard_map/ppermute | solution.py:22
  284.5 27.7 %all-to-all-start.11 = ((bf16[4,64,1152]{2,1,0:T(8,128)(2,1)}), bf16[4,64,1152]{2,1,0:T(8,128)(2,1)}, u32[]{:S(2)}, u32[]{:S(2)}) async-start(bf16[4,64,1152]{2,1,0:T(8,128)(2,1)} %bitcast.47), calls=%async_computation.11 | async-start | bytes 1179648 | tf_op jit(solution)/shard_map/all_to_all | solution.py:26
  295.9 63.1 %collective-permute-start.15 = (bf16[1152,576]{0,1:T(8,128)(2,1)}, bf16[1152,576]{0,1:T(8,128)(2,1)}, u32[]{:S(2)}, u32[]{:S(2)}) collective-permute-start(bf16[1152,576]{0,1:T(8,128)(2,1)} %convolution_convert_fusion.1), channel_id=1, source_target_pairs={{0,4},{4,0},{8,12},{12,8},{16,20},{20,16},{24,28},{28,24},{1,5},{5... | collective-permute-start | bytes 3981320 | tf_op jit(solution)/shard_map/ppermute | solution.py:22
  315.9 21.8 %collective-permute-start.14 = (bf16[64,1152]{1,0:T(8,128)(2,1)S(1)}, bf16[64,1152]{1,0:T(8,128)(2,1)S(1)}, u32[]{:S(2)}, u32[]{:S(2)}) collective-permute-start(bf16[64,1152]{1,0:T(8,128)(2,1)S(1)} %get-tuple-element.148), channel_id=1, source_target_pairs={{0,3},{1,2},{2,1},{3,0},{4,7},{5,6},{6,5},{7,4},{8,11},{9,10},{10,... | collective-permute-start | bytes 442376 | tf_op jit(solution)/shard_map/ppermute | solution.py:22
  317.5 20.3 %collective-permute-start.13 = (bf16[64,1152]{1,0:T(8,128)(2,1)S(1)}, bf16[64,1152]{1,0:T(8,128)(2,1)S(1)}, u32[]{:S(2)}, u32[]{:S(2)}) collective-permute-start(bf16[64,1152]{1,0:T(8,128)(2,1)S(1)} %get-tuple-element.148), channel_id=1, source_target_pairs={{0,2},{1,3},{2,0},{3,1},{4,6},{5,7},{6,4},{7,5},{8,10},{9,11},{10,... | collective-permute-start | bytes 442376 | tf_op jit(solution)/shard_map/ppermute | solution.py:22
  317.5 20.3 %collective-permute-start.12 = (bf16[64,1152]{1,0:T(8,128)(2,1)S(1)}, bf16[64,1152]{1,0:T(8,128)(2,1)}, u32[]{:S(2)}, u32[]{:S(2)}) collective-permute-start(bf16[64,1152]{1,0:T(8,128)(2,1)S(1)} %get-tuple-element.148), channel_id=1, source_target_pairs={{0,1},{1,0},{2,3},{3,2},{4,5},{5,4},{6,7},{7,6},{8,9},{9,8},{10,11... | collective-permute-start | bytes 442376 | tf_op jit(solution)/shard_map/ppermute | solution.py:22
  325.6 61.1 %collective-permute-start.24 = (f32[144,1152]{1,0:T(8,128)}, f32[144,1152]{1,0:T(8,128)}, u32[]{:S(2)}, u32[]{:S(2)}) collective-permute-start(f32[144,1152]{1,0:T(8,128)} %slice_select_fusion), channel_id=1, source_target_pairs={{0,4},{4,0},{8,12},{12,8},{16,20},{20,16},{24,28},{28,24},{1,5},{5... | collective-permute-start | bytes 1990664 | tf_op jit(solution)/shard_map/ppermute | solution.py:22
  333.7 12.5 %all-to-all-start.13 = ((f32[8,32,288]{2,1,0:T(8,128)}), f32[8,32,288]{2,1,0:T(8,128)}, u32[]{:S(2)}, u32[]{:S(2)}) async-start(f32[8,32,288]{2,1,0:T(8,128)} %broadcast_in_dim.441), calls=%async_computation.13 | async-start | bytes 786432 | tf_op jit(solution)/shard_map/all_to_all | solution.py:26
  350.0 19.0 %all-to-all-start.14 = ((f32[32,1,432]{2,1,0:T(1,128)}), f32[32,1,432]{2,1,0:T(1,128)S(1)}, u32[]{:S(2)}, u32[]{:S(2)}) async-start(f32[32,1,432]{2,1,0:T(1,128)} %reshape.425), calls=%async_computation.14 | async-start | bytes 131072 | tf_op jit(solution)/shard_map/all_to_all | solution.py:26
  365.5 12.7 %collective-permute-start.18 = (bf16[288,576]{1,0:T(8,128)(2,1)}, bf16[288,576]{1,0:T(8,128)(2,1)}, u32[]{:S(2)}, u32[]{:S(2)}) collective-permute-start(bf16[288,576]{1,0:T(8,128)(2,1)} %get-tuple-element.145), channel_id=1, source_target_pairs={{0,24},{4,28},{8,16},{12,20},{16,8},{20,12},{24,0},{28,4},{1,25},{... | collective-permute-start | bytes 995336 | tf_op jit(solution)/shard_map/ppermute | solution.py:22
  367.8 17.2 %collective-permute-start.17 = (bf16[288,576]{1,0:T(8,128)(2,1)}, bf16[288,576]{1,0:T(8,128)(2,1)}, u32[]{:S(2)}, u32[]{:S(2)}) collective-permute-start(bf16[288,576]{1,0:T(8,128)(2,1)} %get-tuple-element.146), channel_id=1, source_target_pairs={{0,16},{4,20},{8,24},{12,28},{16,0},{20,4},{24,8},{28,12},{1,17},{... | collective-permute-start | bytes 995336 | tf_op jit(solution)/shard_map/ppermute | solution.py:22
  368.3 16.9 %collective-permute-start.16 = (bf16[288,576]{1,0:T(8,128)(2,1)S(1)}, bf16[288,576]{1,0:T(8,128)(2,1)}, u32[]{:S(2)}, u32[]{:S(2)}) collective-permute-start(bf16[288,576]{1,0:T(8,128)(2,1)S(1)} %get-tuple-element.144), channel_id=1, source_target_pairs={{0,8},{4,12},{8,0},{12,4},{16,24},{20,28},{24,16},{28,20},{1,9},{5... | collective-permute-start | bytes 995336 | tf_op jit(solution)/shard_map/ppermute | solution.py:22
  (99 other events, 1275.3 us)

commit v3 on v2

--- a/solution.py
+++ b/solution.py
@@ -38,37 +38,41 @@
     return jnp.where(core == 0, first, second), jnp.where(core == 0, second, first)
 
 
-def gather_pair_now(first, second):
-    count = lax.axis_size("dp")
-    both = jnp.stack([first, second])
-    blocks = jnp.broadcast_to(both[None], (count // 2,) + both.shape)
-    mine = exchange(blocks.reshape((count,) + first.shape), "dp").reshape(-1, first.shape[1])
+def pair_rows(first, second):
+    core = lax.axis_index("dp") % 2
+    keep, send = choose(core, first, second)
+    return jnp.concatenate(choose(core, keep, swap(send, "dp", 1)))
+
+
+def chip_parts(rows):
+    count = lax.axis_size("dp") // 2
+    return [rows] + [swap(rows, "dp", 2 * step) for step in range(1, count)]
+
+
+def assemble(parts):
+    chip = lax.axis_index("dp") // 2
+    full = jnp.zeros((len(parts),) + parts[0].shape, parts[0].dtype)
+    for step, part in enumerate(parts):
+        full = lax.dynamic_update_index_in_dim(full, part, chip ^ step, 0)
+    mine = full.reshape(-1, parts[0].shape[1])
     return mine, swap(mine, "dp", 1)
 
 
-def gather_pair_beside(first, second):
-    count = lax.axis_size("dp")
-    core, chip = lax.axis_index("dp") % 2, lax.axis_index("dp") // 2
-    keep, send = choose(core, first, second)
-    theirs = swap(send, "dp", 1)
-    rows = jnp.concatenate(choose(core, keep, theirs))
-    full = jnp.zeros((count // 2,) + rows.shape, rows.dtype)
-    for step in range(count // 2):
-        part = swap(rows, "dp", 2 * step) if step else rows
-        full = lax.dynamic_update_index_in_dim(full, part, chip ^ step, 0)
-    mine = full.reshape(-1, rows.shape[1])
-    return mine, swap(mine, "dp", 1)
-
-
-def scatter_pair(mine, other):
-    count = lax.axis_size("dp")
-    core, chip = lax.axis_index("dp") % 2, lax.axis_index("dp") // 2
+def pair_total(mine, other):
+    count = lax.axis_size("dp") // 2
     total = (mine + swap(other.astype(BF16), "dp", 1).astype(F32)).astype(BF16)
-    blocks = total.reshape(count // 2, total.shape[0] // (count // 2), total.shape[1])
-    rows = lax.dynamic_index_in_dim(blocks, chip, 0, keepdims=False).astype(F32)
-    for step in range(1, count // 2):
-        sent = lax.dynamic_index_in_dim(blocks, chip ^ step, 0, keepdims=False)
-        rows = rows + swap(sent, "dp", 2 * step).astype(F32)
+    return total.reshape(count, total.shape[0] // count, total.shape[1])
+
+
+def chip_share(blocks, step):
+    chip = lax.axis_index("dp") // 2
+    sent = lax.dynamic_index_in_dim(blocks, chip ^ step, 0, keepdims=False)
+    return swap(sent, "dp", 2 * step) if step else sent
+
+
+def finish_pair(parts):
+    core = lax.axis_index("dp") % 2
+    rows = sum(part.astype(F32) for part in parts)
     half = rows.shape[0] // 2
     keep, send = choose(core, rows[:half], rows[half:])
     return choose(core, keep, swap(send, "dp", 1))
@@ -91,10 +95,14 @@
     return jnp.concatenate(ordered)
 
 
+def exchange_shares(partial, axis):
+    count = lax.axis_size(axis)
+    blocks = partial.reshape((count, partial.shape[0] // count) + partial.shape[1:])
+    return exchange(blocks, axis)
+
+
 def sum_shares(partial, axis):
-    count = lax.axis_size(axis)
-    blocks = partial.astype(BF16).reshape((count, partial.shape[0] // count) + partial.shape[1:])
-    return jnp.sum(exchange(blocks, axis).astype(F32), axis=0)
+    return jnp.sum(exchange_shares(partial, axis).astype(F32), axis=0)
 
 
 def gather_shares(share, axis):
@@ -261,13 +269,14 @@
         self.rows = rows
         self.meta = jnp.concatenate([lax.axis_index("dp").astype(jnp.int32)[None] % 2, latent_len])
 
-    def forward(self, projected):
+    def forward(self, projected, beside):
         heads, rows = projected.shape[1], self.rows
         query = projected[0].reshape(heads, DH, 2, rows // 2).transpose(0, 2, 1, 3)
         key = jnp.broadcast_to(projected[1][:, None], (heads, 2, DH, rows))
         value = jnp.broadcast_to(projected[2][:, None], (heads, 2, DH, rows))
         packed = jnp.concatenate([key, value, query], axis=3)
-        self.packed = exchange(packed.reshape(heads * 2, DH, rows * 5 // 2), "dp")
+        packed = exchange(packed.reshape(heads * 2, DH, rows * 5 // 2), "dp")
+        self.packed = after(packed, beside)
         out, self.exact, self.log_total = attend_forward(self.meta, self.packed)
         return self.unsplit(exchange(out, "dp")).reshape(heads * DH, rows)
 
@@ -276,13 +285,13 @@
         parts = parts.reshape(heads, 2, DH, self.rows // 2).transpose(0, 2, 1, 3)
         return parts.reshape(heads, DH, self.rows)
 
-    def backward(self, d_attended):
+    def backward(self, d_attended, beside):
         rows = self.rows
         heads = d_attended.shape[0] // DH
         grad = d_attended.reshape(heads, DH, 2, rows // 2).transpose(0, 2, 1, 3)
         grad = exchange(grad.reshape(heads * 2, DH, rows // 2), "dp")
         out = attend_backward(self.meta, self.packed, grad, self.exact, self.log_total)
-        parts = exchange(out, "dp")
+        parts = after(exchange(out, "dp"), beside)
         d_query = self.unsplit(parts[:, :, 2 * rows :])
         halves = parts.reshape(heads, 2, DH, rows * 5 // 2)[..., : 2 * rows].astype(F32)
         d_key_value = (halves[:, 0] + halves[:, 1]).astype(BF16)
@@ -312,7 +321,7 @@
         raw = jnp.einsum("eq,ek->qk", query, key, preferred_element_type=F32) * SCALE
         return jnp.where(self.allowed, raw, NEGATIVE)
 
-    def forward(self, projected):
+    def forward(self, projected, beside):
         key_value = projected[1:]
         pieces = [
             key_value if offset == 0 else self.from_behind(key_value, -offset)
@@ -334,7 +343,7 @@
         out, self.log_total = lax.map(one, self.operands)
         return out.reshape(-1, self.rows)
 
-    def backward(self, d_attended):
+    def backward(self, d_attended, beside):
         rows, reach = self.rows, self.reach
         grads = d_attended.reshape(-1, DH, rows)
 
@@ -424,8 +433,7 @@
     core = my_dp % 2
     qk = w_qkv[:, :2].reshape(share_width, 2 * features)
     vp = jnp.concatenate([w_qkv[:, 2], w_proj.T], axis=1)
-    early_mine, early_other = gather_pair_now(qk, vp)
-    full_vp = choose(core, early_other, early_mine)[0]
+    early_mine, early_other = assemble(chip_parts(pair_rows(qk, vp)))
 
     cond = conditioning.astype(F32)
     gate = 1.0 / (1.0 + jnp.exp(-cond))
@@ -446,22 +454,24 @@
 
     unit_one, inverse_one = normed(tokens.astype(F32))
     hidden_one = (unit_one * (1.0 + pick(modulation[1], ids)) + pick(modulation[0], ids)).astype(BF16)
-    by_hidden = (((0,), (1,)), ((), ()))
     by_last = (((1,), (1,)), ((), ()))
     by_token = (((0,), (0,)), ((), ()))
-    blank = jnp.zeros((features, rows), BF16)
+    by_rows = (((0,), (1,)), ((), ()))
     bias = jnp.concatenate([b_qv[0], jnp.zeros_like(b_qv[0]), b_qv[1]]).astype(F32)
-    from_mine = lax.dot_general(early_mine, hidden_one, by_hidden, preferred_element_type=F32)
-    from_other = lax.dot_general(early_other, hidden_one, by_hidden, preferred_element_type=F32)
-    projected = jnp.concatenate(choose(core, from_mine, from_other))[: 3 * features]
-    projected = (projected + bias[:, None]).astype(BF16).reshape(3, heads, DH, rows)
+    bias = jnp.concatenate([bias, jnp.zeros((features,), F32)]).reshape(2, 2 * features)
+    bias_mine, bias_other = choose(core, bias[0], bias[1])
+    from_mine = jnp.dot(hidden_one, early_mine, preferred_element_type=F32) + bias_mine
+    from_other = jnp.dot(hidden_one, early_other, preferred_element_type=F32) + bias_other
+    joined = choose(core, from_mine.astype(BF16).T, from_other.astype(BF16).T)
+    projected = jnp.concatenate(joined)[: 3 * features].reshape(3, heads, DH, rows)
+    full_proj = choose(core, early_other, early_mine)[0][:, features:]
+    full_proj = after(full_proj, projected)
+    late_rows = pair_rows(after(w_fc1, projected), after(w_fc2.T, projected))
     split = HeadSplit if 2 * heads == n_dp else Window
     attention = split(latent_len, rows)
-    attended = attention.forward(projected)
-    attended_low = jnp.concatenate([blank, attended])
-    attn_part = lax.dot_general(attended_low, full_vp, (((0,), (1,)), ((), ())), preferred_element_type=F32)
-    late_mine, late_other = gather_pair_beside(after(w_fc1, attended), after(w_fc2.T, attended))
-    full_fc1, full_fc2 = choose(core, late_mine, late_other)
+    attended = attention.forward(projected, (full_proj, late_rows))
+    attn_part = lax.dot_general(attended, full_proj, by_rows, preferred_element_type=F32).astype(BF16)
+    late_parts = chip_parts(after(late_rows, attn_part))
     attn_out = sum_shares(attn_part, "tensor") + b_proj.astype(F32)
     own_tokens = own(tokens).astype(F32)
     gate_one = pick(modulation[2], own_ids)
@@ -470,63 +480,69 @@
     scale_two = 1.0 + pick(modulation[4], own_ids)
     hidden_two_own = (unit_two * scale_two + pick(modulation[3], own_ids)).astype(BF16)
     hidden_two = gather_shares(hidden_two_own, "tensor")
+    late_mine, late_other = assemble(after(late_parts, hidden_two_own))
 
     d_mlp = (cotangent.astype(F32) * pick(modulation[5], ids)).astype(BF16)
-    d_gelu = jnp.dot(d_mlp, full_fc2, preferred_element_type=F32)
-    pre_act = jnp.dot(hidden_two, full_fc1, preferred_element_type=F32) + b_fc1.astype(F32)
-    gelu_out, gelu_slope = gelu_pair(pre_act)
+    left_mine, left_other = choose(core, hidden_two, d_mlp)
+    from_mine = jnp.dot(left_mine, late_mine, preferred_element_type=F32)
+    from_other = jnp.dot(left_other, late_other, preferred_element_type=F32)
+    pre_act, d_gelu = choose(core, from_mine, from_other)
+    gelu_out, gelu_slope = gelu_pair(pre_act + b_fc1.astype(F32))
     gelu_out = gelu_out.astype(BF16)
-    d_pre_wide = d_gelu * gelu_slope
-    d_pre = d_pre_wide.astype(BF16)
-    d_two_part = lax.dot_general(d_pre, full_fc1, by_last, preferred_element_type=F32)
-    d_hidden_two = sum_shares(d_two_part, "tensor")
+    d_pre = (d_gelu * gelu_slope).astype(BF16)
+    right_mine, right_other = choose(core, d_pre, gelu_out)
+    back_mine = lax.dot_general(right_mine, late_mine, by_last, preferred_element_type=F32)
+    back_other = lax.dot_general(right_other, late_other, by_last, preferred_element_type=F32)
+    d_two_part, mlp_part = choose(core, back_mine.astype(BF16), back_other.astype(BF16))
+    d_hidden_two = exchange_shares(d_two_part, "tensor")
+
+    right_mine, right_other = after((right_mine, right_other), d_two_part)
+    sent = lax.dot_general(left_other, right_other, by_token, preferred_element_type=F32)
+    kept = lax.dot_general(left_mine, right_mine, by_token, preferred_element_type=F32)
+    late_total = pair_total(kept, sent)
+    d_hidden_two, late_total = lax.optimization_barrier((d_hidden_two, late_total))
+    late_grads = [chip_share(late_total, step) for step in range(n_dp // 2 - 1)]
+
+    d_hidden_two = jnp.sum(d_hidden_two.astype(F32), axis=0)
     own_cotangent = own(cotangent).astype(F32)
     d_mid = own_cotangent + norm_back(unit_two, inverse_two, d_hidden_two * scale_two)
     d_attn_own = (d_mid * gate_one).astype(BF16)
-    d_attn = gather_shares(d_attn_own, "tensor")
-
-    left_mine, left_other = choose(core, hidden_two, d_mlp)
-    right_mine, right_other = choose(core, d_pre, gelu_out)
-    grad_fc1, grad_fc2 = scatter_pair(
-        lax.dot_general(left_mine, right_mine, by_token, preferred_element_type=F32),
-        lax.dot_general(left_other, right_other, by_token, preferred_element_type=F32),
-    )
-
-    mlp_part = lax.dot_general(
-        after(gelu_out, d_attn), full_fc2, by_last, preferred_element_type=F32
-    )
-    mlp_out = sum_beside(mlp_part, "tensor") + b_fc2.astype(F32)
+    d_attn = after(gather_shares(d_attn_own, "tensor"), late_grads)
+
+    d_attended = jnp.dot(d_attn, full_proj, preferred_element_type=F32).astype(BF16).T
+    mlp_out = sum_beside(after(mlp_part, d_attended), "tensor") + b_fc2.astype(F32)
     gate_two = pick(modulation[5], own_ids)
-    result = gather_beside((residual_mid + gate_two * mlp_out).astype(BF16), "tensor")
-
-    d_attended = lax.dot_general(full_vp, d_attn, by_hidden, preferred_element_type=F32)
-    d_attended = d_attended[features:].astype(BF16)
-    d_projected = attention.backward(d_attended).reshape(3 * features, rows)
+    result_own = (residual_mid + gate_two * mlp_out).astype(BF16)
+    d_projected = attention.backward(d_attended, result_own).reshape(3 * features, rows)
+    result = gather_beside(result_own, "tensor")
+    blank = jnp.zeros((features, rows), BF16)
     d_qk = d_projected[: 2 * features]
     d_value = d_projected[2 * features :]
     d_mine, d_other = choose(core, d_qk, jnp.concatenate([d_value, blank]))
     d_one_part = lax.dot_general(
-        d_mine, early_mine, (((0,), (1,)), ((), ())), preferred_element_type=F32
-    ) + lax.dot_general(d_other, early_other, (((0,), (1,)), ((), ())), preferred_element_type=F32)
-    d_hidden_one = sum_shares(d_one_part, "tensor")
+        d_mine, early_mine, by_rows, preferred_element_type=F32
+    ) + lax.dot_general(d_other, early_other, by_rows, preferred_element_type=F32)
+    d_one_part = d_one_part.astype(BF16)
+    d_hidden_one = exchange_shares(d_one_part, "tensor")
+
+    left = jnp.concatenate([hidden_one, d_attn])
+    right_qk = jnp.concatenate([d_qk, jnp.zeros_like(d_qk)], axis=1)
+    right_vp = jnp.concatenate(
+        [jnp.concatenate([d_value, blank]), jnp.concatenate([blank, attended])], axis=1
+    )
+    right_mine, right_other = choose(core, right_qk, right_vp)
+    right_mine, right_other = after((right_mine, right_other), d_one_part)
+    sent = lax.dot_general(left, right_other, by_rows, preferred_element_type=F32)
+    kept = lax.dot_general(left, right_mine, by_rows, preferred_element_type=F32)
+    early_total = pair_total(kept, sent)
+    late_last = chip_share(after(late_total, d_one_part), n_dp // 2 - 1)
+    d_hidden_one, early_total = lax.optimization_barrier((d_hidden_one, early_total))
+    early_grads = [chip_share(early_total, step) for step in range(n_dp // 2)]
+
+    d_hidden_one = jnp.sum(d_hidden_one.astype(F32), axis=0)
     own_unit, own_inverse = own(unit_one), own(inverse_one)
     scale_one = 1.0 + pick(modulation[1], own_ids)
     grad_own = d_mid + norm_back(own_unit, own_inverse, d_hidden_one * scale_one)
-    grad_tokens = gather_beside(grad_own.astype(BF16), "tensor").astype(F32)
-
-    left = jnp.concatenate([hidden_one, d_attn])
-    right_qk = jnp.concatenate([d_qk, jnp.zeros_like(d_qk)], axis=1)
-    right_vp = jnp.concatenate(
-        [jnp.concatenate([d_value, blank]), attended_low], axis=1
-    )
-    right_mine, right_other = choose(core, right_qk, right_vp)
-    by_rows = (((0,), (1,)), ((), ()))
-    grad_qk, grad_vp = scatter_pair(
-        lax.dot_general(left, right_mine, by_rows, preferred_element_type=F32),
-        lax.dot_general(left, right_other, by_rows, preferred_element_type=F32),
-    )
-    grad_qkv = jnp.concatenate([grad_qk, grad_vp[:, :features]], axis=1)
-    grad_qkv = grad_qkv.reshape(share_width, 3, features)
 
     d_float = d_projected.astype(F32).reshape(3, features, rows)
     bias_part = jnp.concatenate(
@@ -553,6 +569,7 @@
     d_mod_first = by_latent([d_hidden_one, d_hidden_one * own_unit])
     d_mod_part = jnp.concatenate([d_mod_first, d_mod_last], axis=1).transpose(2, 0, 1, 3)
     d_mod_part = d_mod_part.reshape(n_tensor, latents * 6, features)
+    grad_tokens = gather_beside(after(grad_own.astype(BF16), d_mod_part), "tensor").astype(F32)
     d_mod_mine = jnp.sum(exchange(d_mod_part, "tensor"), axis=0)
     sums = jnp.sum(gather(jnp.concatenate([d_mod_mine, bias_rows]), "dp", n_dp), axis=0)
     d_mod = sums[: 6 * latents].reshape(latents, 6 * features)
@@ -571,6 +588,11 @@
     d_active = jnp.sum(d_active.reshape(n_dp, n_tensor, latents, share_width), axis=1)
     d_active = d_active.transpose(1, 0, 2).reshape(latents, width)
     grad_cond = d_active * (gate * (1.0 + cond * (1.0 - gate)))
+
+    grad_fc1, grad_fc2 = finish_pair(late_grads + [late_last])
+    grad_qk, grad_vp = finish_pair(early_grads)
+    grad_qkv = jnp.concatenate([grad_qk, grad_vp[:, :features]], axis=1)
+    grad_qkv = grad_qkv.reshape(share_width, 3, features)
 
     return (
         result,

time: 394 us -> 390 us (0.990)
  blocking collectives: 26.5 us -> 8.1 us
  local copies, waits for them, and re-layouts: 49.2 us -> 67.5 us
  waiting for transfers between devices: 145 us -> 132 us
  other arithmetic: 36.5 us -> 45.7 us
  matrix products: 42.5 us -> 35.5 us
  starting transfers between devices: 75.4 us -> 80.8 us
    all_to_all x13, waiting for transfers between devices: 84.1 us -> 63.6 us  [exchange(): return lax.all_to_all(blocks, axis, 0, 0, tiled=True)]
    all_to_all x2 -> x1, blocking collectives: 26.5 us -> 8.1 us  [exchange(): return lax.all_to_all(blocks, axis, 0, 0, tiled=True)]
    ppermute x25 -> x29, waiting for transfers between devices: 60.7 us -> 68.2 us  [swap(): return lax.ppermute(block, axis, route)]
    broadcast_in_dim x18, local copies, waits for them, and re-layouts: 1.44 us -> 8.9 us  [pick(): out = jnp.where(ids[:, None] == number, rows_by_latent[number][None], out)]
    dot_general x10, matrix products: 25.6 us -> 20 us  [the longest x1 3.92 us: local(): from_mine = jnp.dot(left_mine, late_mine, preferred_element_type=F32)]
    ppermute x25 -> x29, starting transfers between devices: 24 us -> 29.5 us  [swap(): return lax.ppermute(block, axis, route)]
    select_n x2 -> x6, other arithmetic: 0.14 us -> 4.36 us  [choose(): jnp.where(core == 0, first, second)]
    unnamed x190 -> x187, local copies, waits for them, and re-layouts: 9.43 us -> 7.79 us
  transfers between devices with their start and end apart: 38 -> 42, of which waited for: 20 -> 19; matrix products, arithmetic and copies ran while one was open for 23% -> 25% of each run, Pallas kernels for 2% -> 2%
where the time goes in v3:
time: 390 us; the launch traced here: 385 us
  waiting for transfers between devices  132 us (34%)
  starting transfers between devices  80.8 us (21%)
  local copies, waits for them, and re-layouts  67.5 us (17%)
  other arithmetic  45.7 us (12%)
  matrix products  35.5 us (9%)
  Pallas kernels  13 us (3%)
  blocking collectives  8.1 us (2%)
    ppermute x29, waiting for transfers between devices, swap(): return lax.ppermute(block, axis, route)  68.2 us
    all_to_all x13, waiting for transfers between devices, exchange(): return lax.all_to_all(blocks, axis, 0, 0, tiled=True)  63.6 us
    all_to_all x13, starting transfers between devices, exchange(): return lax.all_to_all(blocks, axis, 0, 0, tiled=True)  51.2 us
    ppermute x29, starting transfers between devices, swap(): return lax.ppermute(block, axis, route)  29.5 us
    broadcast_in_dim x18, local copies, waits for them, and re-layouts, pick(): out = jnp.where(ids[:, None] == number, rows_by_latent[number][None], out)  8.9 us
    all_to_all x1, blocking collectives, exchange(): return lax.all_to_all(blocks, axis, 0, 0, tiled=True)  8.1 us
  transfers between devices with their start and end apart: 42, of which 19 were waited for; matrix products, arithmetic and copies ran while one was open for 25% of the time, Pallas kernels for 2%

profile of v3, /device:TPU:0, one launch (start us, length us, event | category | flops | bytes accessed | tf_op | source)
XLA Modules:
  0.0 384.6 jit_solution(12593372898714743758)
XLA Ops:
  5.5 4.8 %all-to-all-start = ((f32[8,3,1728]{2,1,0:T(4,128)}), f32[8,3,1728]{2,1,0:T(4,128)}, u32[]{:S(2)}, u32[]{:S(2)}) async-start(f32[8,3,1728]{2,1,0:T(4,128)} %broadcast_in_dim.390), calls=%async_computation | async-start | bytes 458752 | tf_op jit(solution)/shard_map/all_to_all | solution.py:26
  16.7 7.6 %collective-permute-done.1 = bf16[288,576]{1,0:T(8,128)(2,1)S(1)} collective-permute-done((bf16[288,576]{1,0:T(8,128)(2,1)S(1)}, bf16[288,576]{1,0:T(8,128)(2,1)S(1)}, u32[]{:S(2)}, u32[]{:S(2)}) %collective-permute-start.1) | collective-permute-done | bytes 331808 | tf_op jit(solution)/shard_map/ppermute | solution.py:22
  24.4 8.8 %collective-permute-done.2 = bf16[288,576]{1,0:T(8,128)(2,1)S(1)} collective-permute-done((bf16[288,576]{1,0:T(8,128)(2,1)S(1)}, bf16[288,576]{1,0:T(8,128)(2,1)S(1)}, u32[]{:S(2)}, u32[]{:S(2)}) %collective-permute-start.2) | collective-permute-done | bytes 331808 | tf_op jit(solution)/shard_map/ppermute | solution.py:22
  37.2 5.0 %all-to-all-start.1 = ((f32[4,3,1728]{2,1,0:T(4,128)}), f32[4,3,1728]{2,1,0:T(4,128)S(1)}, u32[]{:S(2)}, u32[]{:S(2)}) async-start(f32[4,3,1728]{2,1,0:T(4,128)} %broadcast_in_dim.391), calls=%async_computation.1 | async-start | bytes 229376 | tf_op jit(solution)/shard_map/all_to_all | solution.py:26
  42.9 5.5 %all-to-all-done.1 = f32[4,3,1728]{2,1,0:T(4,128)S(1)} async-done(((f32[4,3,1728]{2,1,0:T(4,128)}), f32[4,3,1728]{2,1,0:T(4,128)S(1)}, u32[]{:S(2)}, u32[]{:S(2)}) %all-to-all-start.1) | async-done | bytes 82976 | tf_op jit(solution)/shard_map/all_to_all | solution.py:26
  58.0 4.8 %fusion.1 = (f32[256,1152]{1,0:T(8,128)}, bf16[256,1152]{1,0:T(8,128)(2,1)S(1)}, f32[1152]{0:T(1024)}, bf16[256,1152]{1,0:T(8,128)(2,1)}) fusion(bf16[256,1152]{1,0:T(8,128)(2,1)S(1)} %copy-done.1, f32[256]{0:T(256)} %add_rsqrt_fusion, f32[256]{0:T(256)S(1)} %broadcast_multiply_fusion, f32[1152]{0:T(1024)S(1)} %broadcast_in_dim.419, ...), kind=kLoop, calls=%fused_computation.13 | loop fusion | flops 6192000 | bytes 3587840 | tf_op jit(solution)/shard_map/mul | solution.py:383
  70.3 3.5 all-to-all-start.2
  80.9 4.9 %all-to-all-done.2.refs_1_ = bf16[8,72,640]{2,1,0:T(8,128)(2,1)S(1)} async-done(((bf16[8,72,640]{2,1,0:T(8,128)(2,1)}), bf16[8,72,640]{2,1,0:T(8,128)(2,1)S(1)}, u32[]{:S(2)}, u32[]{:S(2)}) %all-to-all-start.2) | async-done | bytes 737312 | tf_op jit(solution)/shard_map/all_to_all | solution.py:26
  85.8 5.5 %attend_forward.1 = (bf16[8,72,128]{2,1,0:T(8,128)(2,1)S(1)}, f32[8,72,128]{2,1,0:T(8,128)S(1)}, f32[8,1,128]{2,1,0:T(1,128)S(1)}) custom-call(s32[4]{0:T(128)S(1)} %pad_add_fusion.refs_0_, bf16[8,72,640]{2,1,0:T(8,128)(2,1)S(1)} %all-to-all-done.2.refs_1_), custom_call_target="tpu_custom_call" | custom-call | flops 1000000000 | bytes 4000000 | tf_op jit(solution)/shard_map/attend_forward/pallas_call | solution.py:225
  91.4 8.1 %all_to_all.70 = bf16[8,72,128]{2,1,0:T(8,128)(2,1)S(1)} all-to-all(bf16[8,72,128]{2,1,0:T(8,128)(2,1)S(1)} %get-tuple-element.42), channel_id=1, replica_groups=mesh['dp'=8,'tensor'=4] {'dp'}, dimensions={0} | all-to-all | bytes 294912 | tf_op jit(solution)/shard_map/all_to_all | solution.py:26
  101.1 4.5 %all-to-all-start.4 = ((bf16[4,64,1152]{2,1,0:T(8,128)(2,1)}), bf16[4,64,1152]{2,1,0:T(8,128)(2,1)}, u32[]{:S(2)}, u32[]{:S(2)}) async-start(bf16[4,64,1152]{2,1,0:T(8,128)(2,1)} %bitcast.187), calls=%async_computation.4 | async-start | bytes 1179648 | tf_op jit(solution)/shard_map/all_to_all | solution.py:26
  111.7 9.7 %all-to-all-done.4 = bf16[4,64,1152]{2,1,0:T(8,128)(2,1)} async-done(((bf16[4,64,1152]{2,1,0:T(8,128)(2,1)}), bf16[4,64,1152]{2,1,0:T(8,128)(2,1)}, u32[]{:S(2)}, u32[]{:S(2)}) %all-to-all-start.4) | async-done | bytes 589856 | tf_op jit(solution)/shard_map/all_to_all | solution.py:26
  126.2 13.2 %collective-permute-done.7 = bf16[288,1152]{1,0:T(8,128)(2,1)} collective-permute-done((bf16[288,1152]{1,0:T(8,128)(2,1)S(1)}, bf16[288,1152]{1,0:T(8,128)(2,1)}, u32[]{:S(2)}, u32[]{:S(2)}) %collective-permute-start.7) | collective-permute-done | bytes 663584 | tf_op jit(solution)/shard_map/ppermute | solution.py:22
  148.9 4.6 %all-to-all-start.5 = ((bf16[4,64,1152]{2,1,0:T(8,128)(2,1)}), bf16[4,64,1152]{2,1,0:T(8,128)(2,1)S(1)}, u32[]{:S(2)}, u32[]{:S(2)}) async-start(bf16[4,64,1152]{2,1,0:T(8,128)(2,1)} %broadcast_in_dim.444), calls=%async_computation.5 | async-start | bytes 1179648 | tf_op jit(solution)/shard_map/all_to_all | solution.py:26
  153.4 16.6 %all-to-all-done.5 = bf16[4,64,1152]{2,1,0:T(8,128)(2,1)S(1)} async-done(((bf16[4,64,1152]{2,1,0:T(8,128)(2,1)}), bf16[4,64,1152]{2,1,0:T(8,128)(2,1)S(1)}, u32[]{:S(2)}, u32[]{:S(2)}) %all-to-all-start.5) | async-done | bytes 589856 | tf_op jit(solution)/shard_map/all_to_all | solution.py:26
  174.2 3.9 %convert_reduce_fusion.1 = (f32[1152]{0:T(1024)}, bf16[256,1152]{1,0:T(8,128)(2,1)S(1)}, f32[256,1152]{1,0:T(8,128)S(1)}) fusion(f32[1152]{0:T(1024)S(1)} %convert_element_type.220, f32[256,1152]{1,0:T(8,128)S(1)} %fusion.70, pred[]{:T(512)S(6)} %eq.49, bf16[256,1152]{1,0:T(8,128)(2,1)S(1)} %get-tuple-element.196, bf16[1152,1152]{1,0:T(8,128)(2,1)} %bitcast.25), kind=kOutput, calls=%fused_computation.31 | convolution fusion | flops 686553984 | bytes 6202369 | tf_op jit(solution)/shard_map/dot_general | solution.py:487
  181.6 3.9 %broadcast_select_fusion = (bf16[256,1152]{1,0:T(8,128)(2,1)}, bf16[256,1152]{1,0:T(8,128)(2,1)}) fusion(bf16[256,1152]{1,0:T(8,128)(2,1)S(1)} %convolution_convert_fusion.2, pred[]{:T(512)S(6)} %eq.49, bf16[256,1152]{1,0:T(8,128)(2,1)S(1)} %broadcast_select_fusion.3, bf16[1152,1152]{1,0:T(8,128)(2,1)} %collective-permute-done.9), kind=kOutput, calls=%fused_computation.81 | convolution fusion | flops 680361984 | bytes 5013505 | tf_op jit(solution)/shard_map/dot_general | solution.py:495
  187.9 4.2 %all-to-all-start.6 = ((bf16[4,64,1152]{2,1,0:T(8,128)(2,1)}), bf16[4,64,1152]{2,1,0:T(8,128)(2,1)}, u32[]{:S(2)}, u32[]{:S(2)}) async-start(bf16[4,64,1152]{2,1,0:T(8,128)(2,1)} %bitcast.199), calls=%async_computation.6 | async-start | bytes 1179648 | tf_op jit(solution)/shard_map/all_to_all | solution.py:26
  193.2 4.4 %add_convert_fusion = bf16[1152,1152]{1,0:T(8,128)(2,1)} fusion(bf16[1152,1152]{1,0:T(8,128)(2,1)} %collective-permute-done.10, bf16[256,1152]{1,0:T(8,128)(2,1)} %copy-done.12, bf16[256,1152]{1,0:T(8,128)(2,1)S(1)} %get-tuple-element.48), kind=kOutput, calls=%fused_computation.1 | convolution fusion | flops 683458560 | bytes 6488064 | tf_op jit(solution)/shard_map/dot_general | solution.py:501
  197.7 11.3 %all-to-all-done.6 = bf16[4,64,1152]{2,1,0:T(8,128)(2,1)} async-done(((bf16[4,64,1152]{2,1,0:T(8,128)(2,1)}), bf16[4,64,1152]{2,1,0:T(8,128)(2,1)}, u32[]{:S(2)}, u32[]{:S(2)}) %all-to-all-start.6) | async-done | bytes 589856 | tf_op jit(solution)/shard_map/all_to_all | solution.py:26
  214.2 3.5 all-to-all-start.7
  225.8 11.6 %collective-permute-done.11 = bf16[288,1152]{1,0:T(8,128)(2,1)} collective-permute-done((bf16[288,1152]{1,0:T(8,128)(2,1)}, bf16[288,1152]{1,0:T(8,128)(2,1)}, u32[]{:S(2)}, u32[]{:S(2)}) %collective-permute-start.11) | collective-permute-done | bytes 663584 | tf_op jit(solution)/shard_map/ppermute | solution.py:22
  242.5 3.4 all-to-all-start.8
  252.8 7.5 %attend_backward.1 = bf16[8,72,640]{2,1,0:T(8,128)(2,1)} custom-call(s32[4]{0:T(128)S(1)} %pad_add_fusion.refs_0_, bf16[8,72,640]{2,1,0:T(8,128)(2,1)S(1)} %all-to-all-done.2.refs_1_, bf16[8,72,128]{2,1,0:T(8,128)(2,1)S(1)} %all-to-all-done.8.refs_2_, f32[8,72,128]{2,1,0:T(8,128)S(1)} %get-tuple-element.54.refs_3_, f32[8,1,128]{2,1,0:T(1,128)S(1)} %get-tuple-element.55.refs_4_), custom_call_target="tpu_custom_call" | custom-call | flops 3000000000 | bytes 4000000 | tf_op jit(solution)/shard_map/attend_backward/pallas_call | solution.py:249
  260.3 4.2 %all-to-all-start.9 = ((bf16[8,72,640]{2,1,0:T(8,128)(2,1)}), bf16[8,72,640]{2,1,0:T(8,128)(2,1)S(1)}, u32[]{:S(2)}, u32[]{:S(2)}) async-start(bf16[8,72,640]{2,1,0:T(8,128)(2,1)} %attend_backward.1), calls=%async_computation.9 | async-start | bytes 1474560 | tf_op jit(solution)/shard_map/all_to_all | solution.py:26
  274.6 7.4 %collective-permute-done.17 = bf16[64,1152]{1,0:T(8,128)(2,1)S(1)} collective-permute-done((bf16[64,1152]{1,0:T(8,128)(2,1)S(1)}, bf16[64,1152]{1,0:T(8,128)(2,1)S(1)}, u32[]{:S(2)}, u32[]{:S(2)}) %collective-permute-start.17) | collective-permute-done | bytes 147488 | tf_op jit(solution)/shard_map/ppermute | solution.py:22
  299.3 4.2 %all-to-all-start.10 = ((bf16[4,64,1152]{2,1,0:T(8,128)(2,1)}), bf16[4,64,1152]{2,1,0:T(8,128)(2,1)}, u32[]{:S(2)}, u32[]{:S(2)}) async-start(bf16[4,64,1152]{2,1,0:T(8,128)(2,1)} %bitcast.54), calls=%async_computation.10 | async-start | bytes 1179648 | tf_op jit(solution)/shard_map/all_to_all | solution.py:26
  316.3 4.3 %all-to-all-done.10 = bf16[4,64,1152]{2,1,0:T(8,128)(2,1)} async-done(((bf16[4,64,1152]{2,1,0:T(8,128)(2,1)}), bf16[4,64,1152]{2,1,0:T(8,128)(2,1)}, u32[]{:S(2)}, u32[]{:S(2)}) %all-to-all-start.10) | async-done | bytes 589856 | tf_op jit(solution)/shard_map/all_to_all | solution.py:26
  337.5 7.0 %all-to-all-done.11 = f32[4,18,288]{2,1,0:T(8,128)S(1)} async-done(((f32[4,18,288]{2,1,0:T(8,128)}), f32[4,18,288]{2,1,0:T(8,128)S(1)}, u32[]{:S(2)}, u32[]{:S(2)}) %all-to-all-start.11) | async-done | bytes 82976 | tf_op jit(solution)/shard_map/all_to_all | solution.py:26
  345.3 3.5 all-to-all-start.12
  353.9 11.1 %collective-permute-done.25 = bf16[288,576]{1,0:T(8,128)(2,1)S(1)} collective-permute-done((bf16[288,576]{1,0:T(8,128)(2,1)}, bf16[288,576]{1,0:T(8,128)(2,1)S(1)}, u32[]{:S(2)}, u32[]{:S(2)}) %collective-permute-start.25) | collective-permute-done | bytes 331808 | tf_op jit(solution)/shard_map/ppermute | solution.py:22
  375.8 4.2 %all-to-all-done.13 = f32[32,1,432]{2,1,0:T(1,128)S(1)} async-done(((f32[32,1,432]{2,1,0:T(1,128)}), f32[32,1,432]{2,1,0:T(1,128)S(1)}, u32[]{:S(2)}, u32[]{:S(2)}) %all-to-all-start.13) | async-done | bytes 55328 | tf_op jit(solution)/shard_map/all_to_all | solution.py:26
  (427 shorter events, 175.6 us)
Async XLA Ops:
  5.5 30.0 %all-to-all-start = ((f32[8,3,1728]{2,1,0:T(4,128)}), f32[8,3,1728]{2,1,0:T(4,128)}, u32[]{:S(2)}, u32[]{:S(2)}) async-start(f32[8,3,1728]{2,1,0:T(4,128)} %broadcast_in_dim.390), calls=%async_computation | async-start | bytes 458752 | tf_op jit(solution)/shard_map/all_to_all | solution.py:26
  15.0 18.3 %collective-permute-start.2 = (bf16[288,576]{1,0:T(8,128)(2,1)S(1)}, bf16[288,576]{1,0:T(8,128)(2,1)S(1)}, u32[]{:S(2)}, u32[]{:S(2)}) collective-permute-start(bf16[288,576]{1,0:T(8,128)(2,1)S(1)} %pad_maximum_fusion.12), channel_id=1, source_target_pairs={{0,16},{4,20},{8,24},{12,28},{16,0},{20,4},{24,8},{28,12},{1,17},{... | collective-permute-start | bytes 995336 | tf_op jit(solution)/shard_map/ppermute | solution.py:22
  16.5 16.8 %collective-permute-start.3 = (bf16[288,576]{1,0:T(8,128)(2,1)S(1)}, bf16[288,576]{1,0:T(8,128)(2,1)S(1)}, u32[]{:S(2)}, u32[]{:S(2)}) collective-permute-start(bf16[288,576]{1,0:T(8,128)(2,1)S(1)} %pad_maximum_fusion.12), channel_id=1, source_target_pairs={{0,24},{4,28},{8,16},{12,20},{16,8},{20,12},{24,0},{28,4},{1,25},{... | collective-permute-start | bytes 995336 | tf_op jit(solution)/shard_map/ppermute | solution.py:22
  35.2 27.7 %collective-permute-start.4 = (bf16[1152,576]{0,1:T(8,128)(2,1)}, bf16[1152,576]{0,1:T(8,128)(2,1)S(1)}, u32[]{:S(2)}, u32[]{:S(2)}) collective-permute-start(bf16[1152,576]{0,1:T(8,128)(2,1)} %copy.102), channel_id=1, source_target_pairs={{0,4},{4,0},{8,12},{12,8},{16,20},{20,16},{24,28},{28,24},{1,5},{5... | collective-permute-start | bytes 3981320 | tf_op jit(solution)/shard_map/ppermute | solution.py:22
  70.3 15.6 %all-to-all-start.2 = ((bf16[8,72,640]{2,1,0:T(8,128)(2,1)}), bf16[8,72,640]{2,1,0:T(8,128)(2,1)S(1)}, u32[]{:S(2)}, u32[]{:S(2)}) async-start(bf16[8,72,640]{2,1,0:T(8,128)(2,1)} %bitcast.183), calls=%async_computation.2 | async-start | bytes 1474560 | tf_op jit(solution)/shard_map/all_to_all | solution.py:26
  101.1 20.3 %all-to-all-start.4 = ((bf16[4,64,1152]{2,1,0:T(8,128)(2,1)}), bf16[4,64,1152]{2,1,0:T(8,128)(2,1)}, u32[]{:S(2)}, u32[]{:S(2)}) async-start(bf16[4,64,1152]{2,1,0:T(8,128)(2,1)} %bitcast.187), calls=%async_computation.4 | async-start | bytes 1179648 | tf_op jit(solution)/shard_map/all_to_all | solution.py:26
  108.2 17.9 %collective-permute-start.6 = (bf16[288,1152]{1,0:T(8,128)(2,1)S(1)}, bf16[288,1152]{1,0:T(8,128)(2,1)}, u32[]{:S(2)}, u32[]{:S(2)}) collective-permute-start(bf16[288,1152]{1,0:T(8,128)(2,1)S(1)} %copy-done.6), channel_id=1, source_target_pairs={{0,8},{4,12},{8,0},{12,4},{16,24},{20,28},{24,16},{28,20},{1,9},{5... | collective-permute-start | bytes 1990664 | tf_op jit(solution)/shard_map/ppermute | solution.py:22
  108.8 30.6 %collective-permute-start.7 = (bf16[288,1152]{1,0:T(8,128)(2,1)S(1)}, bf16[288,1152]{1,0:T(8,128)(2,1)}, u32[]{:S(2)}, u32[]{:S(2)}) collective-permute-start(bf16[288,1152]{1,0:T(8,128)(2,1)S(1)} %copy-done.6), channel_id=1, source_target_pairs={{0,16},{4,20},{8,24},{12,28},{16,0},{20,4},{24,8},{28,12},{1,17},{... | collective-permute-start | bytes 1990664 | tf_op jit(solution)/shard_map/ppermute | solution.py:22
  109.4 30.0 %collective-permute-start.8 = (bf16[288,1152]{1,0:T(8,128)(2,1)S(1)}, bf16[288,1152]{1,0:T(8,128)(2,1)}, u32[]{:S(2)}, u32[]{:S(2)}) collective-permute-start(bf16[288,1152]{1,0:T(8,128)(2,1)S(1)} %copy-done.6), channel_id=1, source_target_pairs={{0,24},{4,28},{8,16},{12,20},{16,8},{20,12},{24,0},{28,4},{1,25},{... | collective-permute-start | bytes 1990664 | tf_op jit(solution)/shard_map/ppermute | solution.py:22
  148.0 23.2 %collective-permute-start.9 = (bf16[1152,1152]{1,0:T(8,128)(2,1)}, bf16[1152,1152]{1,0:T(8,128)(2,1)}, u32[]{:S(2)}, u32[]{:S(2)}) collective-permute-start(bf16[1152,1152]{1,0:T(8,128)(2,1)} %bitcast.25), channel_id=1, source_target_pairs={{0,4},{4,0},{8,12},{12,8},{16,20},{20,16},{24,28},{28,24},{1,5},{5... | collective-permute-start | bytes 7962632 | tf_op jit(solution)/shard_map/ppermute | solution.py:22
  148.9 21.1 %all-to-all-start.5 = ((bf16[4,64,1152]{2,1,0:T(8,128)(2,1)}), bf16[4,64,1152]{2,1,0:T(8,128)(2,1)S(1)}, u32[]{:S(2)}, u32[]{:S(2)}) async-start(bf16[4,64,1152]{2,1,0:T(8,128)(2,1)} %broadcast_in_dim.444), calls=%async_computation.5 | async-start | bytes 1179648 | tf_op jit(solution)/shard_map/all_to_all | solution.py:26
  187.9 21.1 %all-to-all-start.6 = ((bf16[4,64,1152]{2,1,0:T(8,128)(2,1)}), bf16[4,64,1152]{2,1,0:T(8,128)(2,1)}, u32[]{:S(2)}, u32[]{:S(2)}) async-start(bf16[4,64,1152]{2,1,0:T(8,128)(2,1)} %bitcast.199), calls=%async_computation.6 | async-start | bytes 1179648 | tf_op jit(solution)/shard_map/all_to_all | solution.py:26
  214.2 24.3 %all-to-all-start.7 = ((bf16[4,64,1152]{2,1,0:T(8,128)(2,1)}), bf16[4,64,1152]{2,1,0:T(8,128)(2,1)S(1)}, u32[]{:S(2)}, u32[]{:S(2)}) async-start(bf16[4,64,1152]{2,1,0:T(8,128)(2,1)} %broadcast_in_dim.453), calls=%async_computation.7 | async-start | bytes 1179648 | tf_op jit(solution)/shard_map/all_to_all | solution.py:26
  220.6 16.9 %collective-permute-start.11 = (bf16[288,1152]{1,0:T(8,128)(2,1)}, bf16[288,1152]{1,0:T(8,128)(2,1)}, u32[]{:S(2)}, u32[]{:S(2)}) collective-permute-start(bf16[288,1152]{1,0:T(8,128)(2,1)} %get-tuple-element.184), channel_id=1, source_target_pairs={{0,8},{4,12},{8,0},{12,4},{16,24},{20,28},{24,16},{28,20},{1,9},{5... | collective-permute-start | bytes 1990664 | tf_op jit(solution)/shard_map/ppermute | solution.py:22
  222.0 16.6 %collective-permute-start.12 = (bf16[288,1152]{1,0:T(8,128)(2,1)}, bf16[288,1152]{1,0:T(8,128)(2,1)}, u32[]{:S(2)}, u32[]{:S(2)}) collective-permute-start(bf16[288,1152]{1,0:T(8,128)(2,1)} %get-tuple-element.183), channel_id=1, source_target_pairs={{0,16},{4,20},{8,24},{12,28},{16,0},{20,4},{24,8},{28,12},{1,17},{... | collective-permute-start | bytes 1990664 | tf_op jit(solution)/shard_map/ppermute | solution.py:22
  247.7 16.9 %collective-permute-start.13 = (bf16[64,1152]{1,0:T(8,128)(2,1)}, bf16[64,1152]{1,0:T(8,128)(2,1)}, u32[]{:S(2)}, u32[]{:S(2)}) collective-permute-start(bf16[64,1152]{1,0:T(8,128)(2,1)} %get-tuple-element.216), channel_id=1, source_target_pairs={{0,1},{1,0},{2,3},{3,2},{4,5},{5,4},{6,7},{7,6},{8,9},{9,8},{10,11... | collective-permute-start | bytes 442376 | tf_op jit(solution)/shard_map/ppermute | solution.py:22
  249.4 15.1 %collective-permute-start.14 = (bf16[64,1152]{1,0:T(8,128)(2,1)}, bf16[64,1152]{1,0:T(8,128)(2,1)}, u32[]{:S(2)}, u32[]{:S(2)}) collective-permute-start(bf16[64,1152]{1,0:T(8,128)(2,1)} %get-tuple-element.218), channel_id=1, source_target_pairs={{0,2},{1,3},{2,0},{3,1},{4,6},{5,7},{6,4},{7,5},{8,10},{9,11},{10,... | collective-permute-start | bytes 442376 | tf_op jit(solution)/shard_map/ppermute | solution.py:22
  251.8 12.8 %collective-permute-start.15 = (bf16[64,1152]{1,0:T(8,128)(2,1)}, bf16[64,1152]{1,0:T(8,128)(2,1)}, u32[]{:S(2)}, u32[]{:S(2)}) collective-permute-start(bf16[64,1152]{1,0:T(8,128)(2,1)} %get-tuple-element.217), channel_id=1, source_target_pairs={{0,3},{1,2},{2,1},{3,0},{4,7},{5,6},{6,5},{7,4},{8,11},{9,10},{10,... | collective-permute-start | bytes 442376 | tf_op jit(solution)/shard_map/ppermute | solution.py:22
  260.3 24.4 %all-to-all-start.9 = ((bf16[8,72,640]{2,1,0:T(8,128)(2,1)}), bf16[8,72,640]{2,1,0:T(8,128)(2,1)S(1)}, u32[]{:S(2)}, u32[]{:S(2)}) async-start(bf16[8,72,640]{2,1,0:T(8,128)(2,1)} %attend_backward.1), calls=%async_computation.9 | async-start | bytes 1474560 | tf_op jit(solution)/shard_map/all_to_all | solution.py:26
  268.1 14.0 %collective-permute-start.17 = (bf16[64,1152]{1,0:T(8,128)(2,1)S(1)}, bf16[64,1152]{1,0:T(8,128)(2,1)S(1)}, u32[]{:S(2)}, u32[]{:S(2)}) collective-permute-start(bf16[64,1152]{1,0:T(8,128)(2,1)S(1)} %get-tuple-element.200), channel_id=1, source_target_pairs={{0,2},{1,3},{2,0},{3,1},{4,6},{5,7},{6,4},{7,5},{8,10},{9,11},{10,... | collective-permute-start | bytes 442376 | tf_op jit(solution)/shard_map/ppermute | solution.py:22
  292.6 14.9 %collective-permute-start.27 = (bf16[288,1152]{1,0:T(8,128)(2,1)S(1)}, bf16[288,1152]{1,0:T(8,128)(2,1)}, u32[]{:S(2)}, u32[]{:S(2)}) collective-permute-start(bf16[288,1152]{1,0:T(8,128)(2,1)S(1)} %dynamic-slice_bitcast_fusion), channel_id=1, source_target_pairs={{0,24},{4,28},{8,16},{12,20},{16,8},{20,12},{24,0},{28,4},{1,25},{... | collective-permute-start | bytes 1990664 | tf_op jit(solution)/shard_map/ppermute | solution.py:22
  299.3 21.3 %all-to-all-start.10 = ((bf16[4,64,1152]{2,1,0:T(8,128)(2,1)}), bf16[4,64,1152]{2,1,0:T(8,128)(2,1)}, u32[]{:S(2)}, u32[]{:S(2)}) async-start(bf16[4,64,1152]{2,1,0:T(8,128)(2,1)} %bitcast.54), calls=%async_computation.10 | async-start | bytes 1179648 | tf_op jit(solution)/shard_map/all_to_all | solution.py:26
  310.2 24.4 %collective-permute-start.28 = (f32[144,1152]{1,0:T(8,128)}, f32[144,1152]{1,0:T(8,128)}, u32[]{:S(2)}, u32[]{:S(2)}) collective-permute-start(f32[144,1152]{1,0:T(8,128)} %slice_select_fusion.1), channel_id=1, source_target_pairs={{0,4},{4,0},{8,12},{12,8},{16,20},{20,16},{24,28},{28,24},{1,5},{5... | collective-permute-start | bytes 1990664 | tf_op jit(solution)/shard_map/ppermute | solution.py:22
  325.3 23.5 %collective-permute-start.20 = (bf16[64,1152]{1,0:T(8,128)(2,1)S(1)}, bf16[64,1152]{1,0:T(8,128)(2,1)S(1)}, u32[]{:S(2)}, u32[]{:S(2)}) collective-permute-start(bf16[64,1152]{1,0:T(8,128)(2,1)S(1)} %get-tuple-element.60), channel_id=1, source_target_pairs={{0,1},{1,0},{2,3},{3,2},{4,5},{5,4},{6,7},{7,6},{8,9},{9,8},{10,11... | collective-permute-start | bytes 442376 | tf_op jit(solution)/shard_map/ppermute | solution.py:22
  325.3 26.3 %collective-permute-start.21 = (bf16[64,1152]{1,0:T(8,128)(2,1)S(1)}, bf16[64,1152]{1,0:T(8,128)(2,1)}, u32[]{:S(2)}, u32[]{:S(2)}) collective-permute-start(bf16[64,1152]{1,0:T(8,128)(2,1)S(1)} %get-tuple-element.60), channel_id=1, source_target_pairs={{0,2},{1,3},{2,0},{3,1},{4,6},{5,7},{6,4},{7,5},{8,10},{9,11},{10,... | collective-permute-start | bytes 442376 | tf_op jit(solution)/shard_map/ppermute | solution.py:22
  327.2 24.4 %collective-permute-start.22 = (bf16[64,1152]{1,0:T(8,128)(2,1)S(1)}, bf16[64,1152]{1,0:T(8,128)(2,1)}, u32[]{:S(2)}, u32[]{:S(2)}) collective-permute-start(bf16[64,1152]{1,0:T(8,128)(2,1)S(1)} %get-tuple-element.60), channel_id=1, source_target_pairs={{0,3},{1,2},{2,1},{3,0},{4,7},{5,6},{6,5},{7,4},{8,11},{9,10},{10,... | collective-permute-start | bytes 442376 | tf_op jit(solution)/shard_map/ppermute | solution.py:22
  330.7 23.1 %collective-permute-start.23 = (bf16[288,576]{1,0:T(8,128)(2,1)}, bf16[288,576]{1,0:T(8,128)(2,1)}, u32[]{:S(2)}, u32[]{:S(2)}) collective-permute-start(bf16[288,576]{1,0:T(8,128)(2,1)} %get-tuple-element.188), channel_id=1, source_target_pairs={{0,8},{4,12},{8,0},{12,4},{16,24},{20,28},{24,16},{28,20},{1,9},{5... | collective-permute-start | bytes 995336 | tf_op jit(solution)/shard_map/ppermute | solution.py:22
  331.3 13.2 %all-to-all-start.11 = ((f32[4,18,288]{2,1,0:T(8,128)}), f32[4,18,288]{2,1,0:T(8,128)S(1)}, u32[]{:S(2)}, u32[]{:S(2)}) async-start(f32[4,18,288]{2,1,0:T(8,128)} %copy.109), calls=%async_computation.11 | async-start | bytes 294912 | tf_op jit(solution)/shard_map/all_to_all | solution.py:26
  334.7 19.2 %collective-permute-start.24 = (bf16[288,576]{1,0:T(8,128)(2,1)}, bf16[288,576]{1,0:T(8,128)(2,1)}, u32[]{:S(2)}, u32[]{:S(2)}) collective-permute-start(bf16[288,576]{1,0:T(8,128)(2,1)} %get-tuple-element.190), channel_id=1, source_target_pairs={{0,16},{4,20},{8,24},{12,28},{16,0},{20,4},{24,8},{28,12},{1,17},{... | collective-permute-start | bytes 995336 | tf_op jit(solution)/shard_map/ppermute | solution.py:22
  345.3 21.1 %all-to-all-start.12 = ((f32[8,32,288]{2,1,0:T(8,128)}), f32[8,32,288]{2,1,0:T(8,128)S(1)}, u32[]{:S(2)}, u32[]{:S(2)}) async-start(f32[8,32,288]{2,1,0:T(8,128)} %broadcast_in_dim.457), calls=%async_computation.12 | async-start | bytes 786432 | tf_op jit(solution)/shard_map/all_to_all | solution.py:26
  348.8 16.2 %collective-permute-start.25 = (bf16[288,576]{1,0:T(8,128)(2,1)}, bf16[288,576]{1,0:T(8,128)(2,1)S(1)}, u32[]{:S(2)}, u32[]{:S(2)}) collective-permute-start(bf16[288,576]{1,0:T(8,128)(2,1)} %get-tuple-element.189), channel_id=1, source_target_pairs={{0,24},{4,28},{8,16},{12,20},{16,8},{20,12},{24,0},{28,4},{1,25},{... | collective-permute-start | bytes 995336 | tf_op jit(solution)/shard_map/ppermute | solution.py:22
  366.3 15.9 %collective-permute-start.26 = (f32[144,576]{1,0:T(8,128)S(1)}, f32[144,576]{1,0:T(8,128)S(1)}, u32[]{:S(2)}, u32[]{:S(2)}) collective-permute-start(f32[144,576]{1,0:T(8,128)S(1)} %slice_select_fusion.3), channel_id=1, source_target_pairs={{0,4},{4,0},{8,12},{12,8},{16,20},{20,16},{24,28},{28,24},{1,5},{5... | collective-permute-start | bytes 995336 | tf_op jit(solution)/shard_map/ppermute | solution.py:22
  (100 other events, 866.8 us)

commit v4 on v3

--- a/solution.py
+++ b/solution.py
@@ -78,14 +78,14 @@
     return choose(core, keep, swap(send, "dp", 1))
 
 
-def sum_beside(partial, axis):
+def parts_beside(partial, axis):
     count, me = lax.axis_size(axis), lax.axis_index(axis)
-    blocks = partial.astype(BF16).reshape((count, partial.shape[0] // count) + partial.shape[1:])
-    total = lax.dynamic_index_in_dim(blocks, me, 0, keepdims=False).astype(F32)
+    blocks = partial.reshape((count, partial.shape[0] // count) + partial.shape[1:])
+    parts = [lax.dynamic_index_in_dim(blocks, me, 0, keepdims=False)]
     for bits in range(1, count):
         sent = lax.dynamic_index_in_dim(blocks, me ^ bits, 0, keepdims=False)
-        total = total + swap(sent, axis, bits).astype(F32)
-    return total
+        parts.append(swap(sent, axis, bits))
+    return parts
 
 
 def gather_beside(share, axis):
@@ -99,16 +99,6 @@
     count = lax.axis_size(axis)
     blocks = partial.reshape((count, partial.shape[0] // count) + partial.shape[1:])
     return exchange(blocks, axis)
-
-
-def sum_shares(partial, axis):
-    return jnp.sum(exchange_shares(partial, axis).astype(F32), axis=0)
-
-
-def gather_shares(share, axis):
-    count = lax.axis_size(axis)
-    parts = gather(share, axis, count)
-    return parts.reshape((count * share.shape[0],) + share.shape[1:])
 
 
 def tile_range(meta_ref, latents, tile, core):
@@ -269,33 +259,20 @@
         self.rows = rows
         self.meta = jnp.concatenate([lax.axis_index("dp").astype(jnp.int32)[None] % 2, latent_len])
 
-    def forward(self, projected, beside):
-        heads, rows = projected.shape[1], self.rows
-        query = projected[0].reshape(heads, DH, 2, rows // 2).transpose(0, 2, 1, 3)
-        key = jnp.broadcast_to(projected[1][:, None], (heads, 2, DH, rows))
-        value = jnp.broadcast_to(projected[2][:, None], (heads, 2, DH, rows))
-        packed = jnp.concatenate([key, value, query], axis=3)
-        packed = exchange(packed.reshape(heads * 2, DH, rows * 5 // 2), "dp")
-        self.packed = after(packed, beside)
+    def forward(self, packed, beside):
+        self.packed = after(exchange(packed, "dp"), beside)
         out, self.exact, self.log_total = attend_forward(self.meta, self.packed)
-        return self.unsplit(exchange(out, "dp")).reshape(heads * DH, rows)
+        return self.unsplit(exchange(out, "dp")).reshape(-1, self.rows)
 
     def unsplit(self, parts):
         heads = parts.shape[0] // 2
         parts = parts.reshape(heads, 2, DH, self.rows // 2).transpose(0, 2, 1, 3)
         return parts.reshape(heads, DH, self.rows)
 
-    def backward(self, d_attended, beside):
-        rows = self.rows
-        heads = d_attended.shape[0] // DH
-        grad = d_attended.reshape(heads, DH, 2, rows // 2).transpose(0, 2, 1, 3)
-        grad = exchange(grad.reshape(heads * 2, DH, rows // 2), "dp")
+    def backward(self, grad, beside):
+        grad = exchange(grad, "dp")
         out = attend_backward(self.meta, self.packed, grad, self.exact, self.log_total)
-        parts = after(exchange(out, "dp"), beside)
-        d_query = self.unsplit(parts[:, :, 2 * rows :])
-        halves = parts.reshape(heads, 2, DH, rows * 5 // 2)[..., : 2 * rows].astype(F32)
-        d_key_value = (halves[:, 0] + halves[:, 1]).astype(BF16)
-        return jnp.stack([d_query, d_key_value[..., :rows], d_key_value[..., rows:]])
+        return after(exchange(out, "dp"), beside)
 
 
 class Window:
@@ -321,7 +298,11 @@
         raw = jnp.einsum("eq,ek->qk", query, key, preferred_element_type=F32) * SCALE
         return jnp.where(self.allowed, raw, NEGATIVE)
 
-    def forward(self, projected, beside):
+    def forward(self, packed, beside):
+        rows = self.rows
+        split = packed.reshape(-1, 2, DH, rows * 5 // 2)
+        query = jnp.concatenate([split[:, 0, :, 2 * rows :], split[:, 1, :, 2 * rows :]], axis=2)
+        projected = jnp.stack([query, split[:, 0, :, :rows], split[:, 0, :, rows : 2 * rows]])
         key_value = projected[1:]
         pieces = [
             key_value if offset == 0 else self.from_behind(key_value, -offset)
@@ -343,9 +324,10 @@
         out, self.log_total = lax.map(one, self.operands)
         return out.reshape(-1, self.rows)
 
-    def backward(self, d_attended, beside):
+    def backward(self, grad, beside):
         rows, reach = self.rows, self.reach
-        grads = d_attended.reshape(-1, DH, rows)
+        halves = grad.reshape(-1, 2, DH, rows // 2)
+        grads = jnp.concatenate([halves[:, 0], halves[:, 1]], axis=2)
 
         def one(operands):
             query, key, value, grad, log_total = operands
@@ -365,7 +347,275 @@
             if offset != 0:
                 block = d_window[..., (offset + reach) * rows : (offset + reach + 1) * rows]
                 d_key_value = d_key_value + self.from_behind(block, offset)
-        return jnp.concatenate([d_query[None], d_key_value]).astype(BF16)
+        wide = jnp.concatenate([d_key_value[0], d_key_value[1]], axis=2)
+        wide = jnp.stack([wide, jnp.zeros_like(wide)], axis=1)
+        halves = d_query.reshape(-1, DH, 2, rows // 2).transpose(0, 2, 1, 3)
+        packed = jnp.concatenate([wide, halves], axis=3).astype(BF16)
+        return packed.reshape(-1, DH, rows * 5 // 2)
+
+
+META = 4
+
+
+def vmem(count):
+    return [pl.BlockSpec(memory_space=pltpu.VMEM)] * count
+
+
+def call(body, name, meta, arrays, outs, scratch=(), anywhere=0):
+    return pl.pallas_call(
+        body,
+        out_shape=tuple(jax.ShapeDtypeStruct(shape, kind) for shape, kind in outs),
+        in_specs=[pl.BlockSpec(memory_space=pltpu.SMEM)]
+        + [pl.BlockSpec(memory_space=pl.ANY)] * anywhere
+        + vmem(len(arrays) - anywhere),
+        out_specs=tuple(vmem(len(outs))),
+        scratch_shapes=list(scratch),
+        compiler_params=pltpu.CompilerParams(vmem_limit_bytes=VMEM_BYTES),
+        cost_estimate=pl.CostEstimate(flops=1, bytes_accessed=1, transcendentals=0),
+        name=name,
+    )(meta, *arrays)
+
+
+def row_masks(meta_ref, latents, first, rows):
+    place = first + lax.broadcasted_iota(jnp.int32, (rows, 1), 0)
+    ids = jnp.zeros((rows, 1), jnp.int32)
+    end = jnp.int32(0)
+    for number in range(latents - 1):
+        end = end + meta_ref[META + number]
+        ids = ids + (place >= end).astype(jnp.int32)
+    return [(ids == number).astype(F32) for number in range(latents)]
+
+
+def rows_of(mod_ref, masks, feature):
+    out = masks[0] * mod_ref[feature : feature + 1, :]
+    for number in range(1, len(masks)):
+        row = number * 6 + feature
+        out = out + masks[number] * mod_ref[row : row + 1, :]
+    return out
+
+
+def latent_sums(out_ref, masks, values, feature, features):
+    rounded = values.astype(BF16).astype(F32)
+    for number, mask in enumerate(masks):
+        row = number * features + feature
+        out_ref[row : row + 1, :] = jnp.sum(mask * rounded, axis=0, keepdims=True)
+
+
+def own_rows(meta_ref, ref, share):
+    start = pl.multiple_of(meta_ref[2] * share, share)
+    return ref[pl.ds(start, share), :].astype(F32)
+
+
+def on_core(meta_ref, body, mine, other):
+    @pl.when(meta_ref[0] == 0)
+    def _():
+        body(mine, other)
+
+    @pl.when(meta_ref[0] != 0)
+    def _():
+        body(other, mine)
+
+
+def project_kernel(
+    latents, meta_ref, tokens_ref, cot_ref, mod_ref, bias_ref, mine_ref, other_ref,
+    hidden_ref, d_mlp_ref, packed_ref,
+):
+    rows, width = tokens_ref.shape
+    masks = row_masks(meta_ref, latents, meta_ref[1], rows)
+    unit, _ = normed(tokens_ref[...].astype(F32))
+    hidden = unit * (1.0 + rows_of(mod_ref, masks, 1)) + rows_of(mod_ref, masks, 0)
+    hidden_ref[...] = hidden.astype(BF16)
+    d_mlp_ref[...] = (cot_ref[...].astype(F32) * rows_of(mod_ref, masks, 5)).astype(BF16)
+    heads = packed_ref.shape[0] // 2
+    features = heads * DH
+
+    def body(qk_ref, vp_ref):
+        left = hidden_ref[...]
+        both = jnp.dot(left, qk_ref[...], preferred_element_type=F32) + bias_ref[0:1, :]
+        both = both.T
+        value = jnp.dot(left, vp_ref[...], preferred_element_type=F32) + bias_ref[1:2, :]
+        value = value.T
+        for head in range(heads):
+            start = head * DH
+            query = both[start : start + DH].astype(BF16)
+            key = both[features + start : features + start + DH].astype(BF16)
+            val = value[start : start + DH].astype(BF16)
+            for half in range(2):
+                packed_ref[2 * head + half, :, :rows] = key
+                packed_ref[2 * head + half, :, rows : 2 * rows] = val
+                packed_ref[2 * head + half, :, 2 * rows :] = query[
+                    :, half * (rows // 2) : (half + 1) * (rows // 2)
+                ]
+
+    on_core(meta_ref, body, mine_ref, other_ref)
+
+
+def middle_kernel(
+    latents, meta_ref, parts_ref, tokens_ref, mod_ref, bias_ref, sent_ref, attn_ref, mid_ref
+):
+    copies, share, width = parts_ref.shape
+    masks = row_masks(meta_ref, latents, meta_ref[1] + meta_ref[2] * share, share)
+    attn = bias_ref[...].astype(F32)
+    for part in range(copies):
+        attn = attn + parts_ref[part].astype(F32)
+    attn_ref[...] = attn
+    mid = own_rows(meta_ref, tokens_ref, share) + rows_of(mod_ref, masks, 2) * attn
+    mid_ref[...] = mid
+    unit, _ = normed(mid)
+    hidden = unit * (1.0 + rows_of(mod_ref, masks, 4)) + rows_of(mod_ref, masks, 3)
+    for part in range(copies):
+        sent_ref[part] = hidden.astype(BF16)
+
+
+def mlp_kernel(count, meta_ref, *refs):
+    mine_parts, other_parts = refs[:count], refs[count : 2 * count]
+    hidden_ref, d_mlp_ref, bias_ref = refs[2 * count : 2 * count + 3]
+    d_two_ref, mlp_ref, gelu_ref, d_pre_ref, d_bias_ref = refs[2 * count + 3 : 2 * count + 8]
+    mine_ref, other_ref, d_two_sum, mlp_sum, sems = refs[2 * count + 8 :]
+    block = mine_parts[0].shape[0]
+    copies = []
+    for place, (parts, whole) in enumerate(((mine_parts, mine_ref), (other_parts, other_ref))):
+        for step, part in enumerate(parts):
+            start = pl.multiple_of((meta_ref[3] ^ step) * block, 16)
+            copies.append(
+                pltpu.make_async_copy(
+                    part, whole.at[pl.ds(start, block), :], sems.at[place * count + step]
+                )
+            )
+    for copy in copies:
+        copy.start()
+    for copy in copies:
+        copy.wait()
+    d_two_sum[...] = jnp.zeros_like(d_two_sum)
+    mlp_sum[...] = jnp.zeros_like(mlp_sum)
+    tile = 384
+    by_last = (((1,), (1,)), ((), ()))
+
+    def body(fc1_ref, fc2_ref):
+        def step(number, carry):
+            units = pl.ds(pl.multiple_of(number * tile, tile), tile)
+            fc1, fc2 = fc1_ref[:, units], fc2_ref[:, units]
+            pre = jnp.dot(hidden_ref[...], fc1, preferred_element_type=F32)
+            gelu, slope = gelu_pair(pre + bias_ref[:, units].astype(F32))
+            grad = jnp.dot(d_mlp_ref[...], fc2, preferred_element_type=F32)
+            d_pre = (grad * slope).astype(BF16)
+            gelu = gelu.astype(BF16)
+            gelu_ref[:, units] = gelu
+            d_pre_ref[:, units] = d_pre
+            d_bias_ref[:, units] = jnp.sum(d_pre.astype(F32), axis=0, keepdims=True)
+            d_two_sum[...] += lax.dot_general(d_pre, fc1, by_last, preferred_element_type=F32)
+            mlp_sum[...] += lax.dot_general(gelu, fc2, by_last, preferred_element_type=F32)
+            return carry
+
+        lax.fori_loop(0, fc1_ref.shape[1] // tile, step, 0)
+
+    on_core(meta_ref, body, mine_ref, other_ref)
+    d_two_ref[...] = d_two_sum[...].astype(BF16)
+    mlp_ref[...] = mlp_sum[...].astype(BF16)
+
+
+def middle_back_kernel(
+    latents, meta_ref, parts_ref, mid_in_ref, attn_ref, cot_ref, mod_ref, sent_ref, d_mid_ref, sums_ref
+):
+    copies, share, width = parts_ref.shape
+    masks = row_masks(meta_ref, latents, meta_ref[1] + meta_ref[2] * share, share)
+    d_hidden = parts_ref[0].astype(F32)
+    for part in range(1, copies):
+        d_hidden = d_hidden + parts_ref[part].astype(F32)
+    unit, inverse = normed(mid_in_ref[...])
+    d_mid = own_rows(meta_ref, cot_ref, share) + norm_back(
+        unit, inverse, d_hidden * (1.0 + rows_of(mod_ref, masks, 4))
+    )
+    d_mid_ref[...] = d_mid
+    d_attn = (d_mid * rows_of(mod_ref, masks, 2)).astype(BF16)
+    for part in range(copies):
+        sent_ref[part] = d_attn
+    latent_sums(sums_ref, masks, d_mid * attn_ref[...], 0, 3)
+    latent_sums(sums_ref, masks, d_hidden, 1, 3)
+    latent_sums(sums_ref, masks, d_hidden * unit, 2, 3)
+
+
+def result_kernel(
+    latents, count, meta_ref, *refs
+):
+    parts = refs[:count]
+    mid_ref, cot_ref, mod_ref, bias_ref, result_ref, sums_ref = refs[count:]
+    share = result_ref.shape[0]
+    masks = row_masks(meta_ref, latents, meta_ref[1] + meta_ref[2] * share, share)
+    mlp = bias_ref[...].astype(F32)
+    for part in parts:
+        mlp = mlp + part[...].astype(F32)
+    result_ref[...] = (mid_ref[...] + rows_of(mod_ref, masks, 5) * mlp).astype(BF16)
+    latent_sums(sums_ref, masks, own_rows(meta_ref, cot_ref, share) * mlp, 0, 1)
+
+
+def spread_kernel(meta_ref, d_attn_ref, proj_ref, packed_ref, d_bias_ref):
+    grad = jnp.dot(d_attn_ref[...], proj_ref[...], preferred_element_type=F32).T
+    half = grad.shape[1] // 2
+    for place in range(packed_ref.shape[0]):
+        start = place // 2 * DH
+        side = place % 2 * half
+        packed_ref[place] = grad[start : start + DH, side : side + half].astype(BF16)
+    d_bias_ref[...] = jnp.sum(d_attn_ref[...].astype(F32), axis=0, keepdims=True)
+
+
+def unspread_kernel(meta_ref, parts_ref, mine_ref, other_ref, d_one_ref, d_qk_ref, d_vp_ref):
+    heads = parts_ref.shape[0] // 2
+    rows = d_one_ref.shape[0]
+    query, key, value = [], [], []
+    for head in range(heads):
+        left = parts_ref[2 * head].astype(F32)
+        right = parts_ref[2 * head + 1].astype(F32)
+        both = left[:, : 2 * rows] + right[:, : 2 * rows]
+        key.append(both[:, :rows])
+        value.append(both[:, rows:])
+        query.append(jnp.concatenate([left[:, 2 * rows :], right[:, 2 * rows :]], axis=1))
+    d_qk_ref[...] = jnp.concatenate(query + key, axis=0).T.astype(BF16)
+    blank = jnp.zeros((heads * DH, rows), F32)
+    d_vp_ref[...] = jnp.concatenate(value + [blank], axis=0).T.astype(BF16)
+    tile = 384
+    by_last = (((1,), (1,)), ((), ()))
+
+    def body(qk_ref, vp_ref):
+        def step(number, carry):
+            columns = pl.ds(pl.multiple_of(number * tile, tile), tile)
+            total = lax.dot_general(d_qk_ref[...], qk_ref[columns, :], by_last, preferred_element_type=F32)
+            total += lax.dot_general(d_vp_ref[...], vp_ref[columns, :], by_last, preferred_element_type=F32)
+            d_one_ref[:, columns] = total.astype(BF16)
+            return carry
+
+        lax.fori_loop(0, qk_ref.shape[0] // tile, step, 0)
+
+    on_core(meta_ref, body, mine_ref, other_ref)
+
+
+def first_back_kernel(
+    latents, meta_ref, parts_ref, tokens_ref, d_mid_ref, mod_ref, mid_sums_ref, last_sums_ref,
+    grad_ref, sent_ref, first_sums,
+):
+    copies, share, width = parts_ref.shape
+    masks = row_masks(meta_ref, latents, meta_ref[1] + meta_ref[2] * share, share)
+    d_hidden = parts_ref[0].astype(F32)
+    for part in range(1, copies):
+        d_hidden = d_hidden + parts_ref[part].astype(F32)
+    unit, inverse = normed(own_rows(meta_ref, tokens_ref, share))
+    grad = d_mid_ref[...] + norm_back(unit, inverse, d_hidden * (1.0 + rows_of(mod_ref, masks, 1)))
+    grad_ref[...] = grad.astype(BF16)
+    latent_sums(first_sums, masks, d_hidden, 0, 2)
+    latent_sums(first_sums, masks, d_hidden * unit, 1, 2)
+    columns = width // copies
+    for number in range(latents):
+        for feature in range(6):
+            if feature < 2:
+                row = first_sums[number * 2 + feature : number * 2 + feature + 1, :]
+            elif feature < 5:
+                place = number * 3 + feature - 2
+                row = mid_sums_ref[place : place + 1, :]
+            else:
+                row = last_sums_ref[number : number + 1, :]
+            place = number * 6 + feature
+            for part in range(copies):
+                sent_ref[part, place : place + 1, :] = row[:, part * columns : (part + 1) * columns]
 
 
 def latent_index(latent_len, first_row, row_count, token_total):
@@ -386,13 +636,6 @@
 def norm_back(unit, inverse, grad):
     along = jnp.mean(grad * unit, axis=-1, keepdims=True)
     return inverse * (grad - jnp.mean(grad, axis=-1, keepdims=True) - unit * along)
-
-
-def pick(rows_by_latent, ids):
-    out = jnp.zeros((ids.shape[0], rows_by_latent.shape[1]), F32)
-    for number in range(rows_by_latent.shape[0]):
-        out = jnp.where(ids[:, None] == number, rows_by_latent[number][None], out)
-    return out
 
 
 def gelu_pair(value):
@@ -427,13 +670,12 @@
     latents = conditioning.shape[0]
     n_dp, n_tensor = lax.axis_size("dp"), lax.axis_size("tensor")
     my_dp, my_tensor = lax.axis_index("dp"), lax.axis_index("tensor")
-    total = rows * n_dp
     share = rows // n_tensor
 
     core = my_dp % 2
     qk = w_qkv[:, :2].reshape(share_width, 2 * features)
     vp = jnp.concatenate([w_qkv[:, 2], w_proj.T], axis=1)
-    early_mine, early_other = assemble(chip_parts(pair_rows(qk, vp)))
+    early_parts = chip_parts(pair_rows(qk, vp))
 
     cond = conditioning.astype(F32)
     gate = 1.0 / (1.0 + jnp.exp(-cond))
@@ -441,136 +683,141 @@
     own_activated = lax.dynamic_slice_in_dim(activated, my_dp * share_width, share_width, 1)
     flat_ada = w_ada.reshape(share_width, 6 * features)
     mod_part = jnp.dot(own_activated, flat_ada, preferred_element_type=F32)
-    mod_mine = jnp.sum(gather(mod_part, "dp", n_dp), axis=0) + b_ada.astype(F32).reshape(1, -1)
-    modulation = gather(mod_mine, "tensor", n_tensor)
-    modulation = modulation.reshape(n_tensor, latents, 6, features).transpose(2, 1, 0, 3)
-    modulation = modulation.reshape(6, latents, width)
-
-    ids = latent_index(latent_len, my_dp * rows, rows, total)
-    own_ids = lax.dynamic_slice_in_dim(ids, my_tensor * share, share, 0)
-
-    def own(values):
-        return lax.dynamic_slice_in_dim(values, my_tensor * share, share, 0)
-
-    unit_one, inverse_one = normed(tokens.astype(F32))
-    hidden_one = (unit_one * (1.0 + pick(modulation[1], ids)) + pick(modulation[0], ids)).astype(BF16)
+    mod_part = mod_part.reshape(latents * 6, features)
+    mod_mine = jnp.sum(gather(mod_part, "dp", n_dp), axis=0)
+    mod_mine = mod_mine + jnp.tile(b_ada.astype(F32), (latents, 1))
+    modulation = gather(mod_mine, "tensor", n_tensor).transpose(1, 0, 2).reshape(6 * latents, width)
+
+    mod_rows, early_parts = lax.optimization_barrier((modulation, early_parts))
+    early_mine, early_other = assemble(early_parts)
+    meta = jnp.stack([core, my_dp * rows, my_tensor, my_dp // 2]).astype(jnp.int32)
+    meta = jnp.concatenate([meta, latent_len])
     by_last = (((1,), (1,)), ((), ()))
     by_token = (((0,), (0,)), ((), ()))
     by_rows = (((0,), (1,)), ((), ()))
-    bias = jnp.concatenate([b_qv[0], jnp.zeros_like(b_qv[0]), b_qv[1]]).astype(F32)
-    bias = jnp.concatenate([bias, jnp.zeros((features,), F32)]).reshape(2, 2 * features)
-    bias_mine, bias_other = choose(core, bias[0], bias[1])
-    from_mine = jnp.dot(hidden_one, early_mine, preferred_element_type=F32) + bias_mine
-    from_other = jnp.dot(hidden_one, early_other, preferred_element_type=F32) + bias_other
-    joined = choose(core, from_mine.astype(BF16).T, from_other.astype(BF16).T)
-    projected = jnp.concatenate(joined)[: 3 * features].reshape(3, heads, DH, rows)
-    full_proj = choose(core, early_other, early_mine)[0][:, features:]
-    full_proj = after(full_proj, projected)
-    late_rows = pair_rows(after(w_fc1, projected), after(w_fc2.T, projected))
+    bias = jnp.concatenate([b_qv[0], jnp.zeros_like(b_qv[0]), b_qv[1], jnp.zeros_like(b_qv[0])])
+    hidden_one, d_mlp, packed = call(
+        lambda *refs: project_kernel(latents, *refs),
+        "project",
+        meta,
+        (tokens, cotangent, mod_rows, bias.astype(F32).reshape(2, -1), early_mine, early_other),
+        (((rows, width), BF16), ((rows, width), BF16), ((2 * heads, DH, rows * 5 // 2), BF16)),
+    )
+    full_proj = choose(core, after(early_other, packed), early_mine)[0][:, features:]
+    late_rows = pair_rows(after(w_fc1, packed), after(w_fc2.T, packed))
     split = HeadSplit if 2 * heads == n_dp else Window
     attention = split(latent_len, rows)
-    attended = attention.forward(projected, (full_proj, late_rows))
+    attended = attention.forward(packed, (full_proj, late_rows))
     attn_part = lax.dot_general(attended, full_proj, by_rows, preferred_element_type=F32).astype(BF16)
-    late_parts = chip_parts(after(late_rows, attn_part))
-    attn_out = sum_shares(attn_part, "tensor") + b_proj.astype(F32)
-    own_tokens = own(tokens).astype(F32)
-    gate_one = pick(modulation[2], own_ids)
-    residual_mid = own_tokens + gate_one * attn_out
-    unit_two, inverse_two = normed(residual_mid)
-    scale_two = 1.0 + pick(modulation[4], own_ids)
-    hidden_two_own = (unit_two * scale_two + pick(modulation[3], own_ids)).astype(BF16)
-    hidden_two = gather_shares(hidden_two_own, "tensor")
-    late_mine, late_other = assemble(after(late_parts, hidden_two_own))
-
-    d_mlp = (cotangent.astype(F32) * pick(modulation[5], ids)).astype(BF16)
+    late_parts = chip_parts(after(late_rows, attended))
+    attn_parts = exchange_shares(attn_part, "tensor")
+    hidden_blocks, attn_out, residual_mid = call(
+        lambda *refs: middle_kernel(latents, *refs),
+        "middle",
+        meta,
+        (attn_parts, tokens, mod_rows, b_proj.reshape(1, -1)),
+        (((n_tensor, share, width), BF16), ((share, width), F32), ((share, width), F32)),
+    )
+    hidden_two = exchange(hidden_blocks, "tensor").reshape(rows, width)
+
+    late_parts = after(late_parts, hidden_two)
+    mlp_meta = meta
+    if len(late_parts) > 4:
+        late_mine, late_other = assemble(late_parts)
+        late_parts, swapped = [late_mine], [late_other]
+        mlp_meta = meta.at[3].set(0)
+    else:
+        swapped = [swap(part, "dp", 1) for part in late_parts]
+    count = len(late_parts)
+    d_two_part, mlp_part, gelu_out, d_pre, d_bias_fc1 = call(
+        lambda *refs: mlp_kernel(count, *refs),
+        "mlp",
+        mlp_meta,
+        (*late_parts, *swapped, hidden_two, d_mlp, b_fc1.reshape(1, -1)),
+        (((rows, width), BF16), ((rows, width), BF16), ((rows, units), BF16), ((rows, units), BF16))
+        + (((1, units), F32),),
+        [pltpu.VMEM((width, units), BF16)] * 2
+        + [pltpu.VMEM((rows, width), F32)] * 2
+        + [pltpu.SemaphoreType.DMA((2 * count,))],
+        2 * count,
+    )
+    d_two_parts = exchange_shares(d_two_part, "tensor")
+
     left_mine, left_other = choose(core, hidden_two, d_mlp)
-    from_mine = jnp.dot(left_mine, late_mine, preferred_element_type=F32)
-    from_other = jnp.dot(left_other, late_other, preferred_element_type=F32)
-    pre_act, d_gelu = choose(core, from_mine, from_other)
-    gelu_out, gelu_slope = gelu_pair(pre_act + b_fc1.astype(F32))
-    gelu_out = gelu_out.astype(BF16)
-    d_pre = (d_gelu * gelu_slope).astype(BF16)
     right_mine, right_other = choose(core, d_pre, gelu_out)
-    back_mine = lax.dot_general(right_mine, late_mine, by_last, preferred_element_type=F32)
-    back_other = lax.dot_general(right_other, late_other, by_last, preferred_element_type=F32)
-    d_two_part, mlp_part = choose(core, back_mine.astype(BF16), back_other.astype(BF16))
-    d_hidden_two = exchange_shares(d_two_part, "tensor")
-
-    right_mine, right_other = after((right_mine, right_other), d_two_part)
     sent = lax.dot_general(left_other, right_other, by_token, preferred_element_type=F32)
     kept = lax.dot_general(left_mine, right_mine, by_token, preferred_element_type=F32)
     late_total = pair_total(kept, sent)
-    d_hidden_two, late_total = lax.optimization_barrier((d_hidden_two, late_total))
+    d_two_parts, late_total = lax.optimization_barrier((d_two_parts, late_total))
     late_grads = [chip_share(late_total, step) for step in range(n_dp // 2 - 1)]
 
-    d_hidden_two = jnp.sum(d_hidden_two.astype(F32), axis=0)
-    own_cotangent = own(cotangent).astype(F32)
-    d_mid = own_cotangent + norm_back(unit_two, inverse_two, d_hidden_two * scale_two)
-    d_attn_own = (d_mid * gate_one).astype(BF16)
-    d_attn = after(gather_shares(d_attn_own, "tensor"), late_grads)
-
-    d_attended = jnp.dot(d_attn, full_proj, preferred_element_type=F32).astype(BF16).T
-    mlp_out = sum_beside(after(mlp_part, d_attended), "tensor") + b_fc2.astype(F32)
-    gate_two = pick(modulation[5], own_ids)
-    result_own = (residual_mid + gate_two * mlp_out).astype(BF16)
-    d_projected = attention.backward(d_attended, result_own).reshape(3 * features, rows)
+    d_attn_blocks, d_mid, mid_sums = call(
+        lambda *refs: middle_back_kernel(latents, *refs),
+        "middle_back",
+        meta,
+        (d_two_parts, residual_mid, attn_out, cotangent, mod_rows),
+        (((n_tensor, share, width), BF16), ((share, width), F32), ((3 * latents, width), F32)),
+    )
+    d_attn = exchange(d_attn_blocks, "tensor").reshape(rows, width)
+
+    d_spread, d_bias_proj = call(
+        spread_kernel,
+        "spread",
+        meta,
+        (d_attn, full_proj),
+        (((2 * heads, DH, rows // 2), BF16), ((1, width), F32)),
+    )
+    mlp_parts = parts_beside(after(mlp_part, d_spread), "tensor")
+    result_own, last_sums = call(
+        lambda *refs: result_kernel(latents, n_tensor, *refs),
+        "result",
+        meta,
+        (*mlp_parts, residual_mid, cotangent, mod_rows, b_fc2.reshape(1, -1)),
+        (((share, width), BF16), ((latents, width), F32)),
+    )
+    d_packed = attention.backward(d_spread, (result_own, late_grads))
     result = gather_beside(result_own, "tensor")
+    d_one_part, d_qk, d_vp = call(
+        unspread_kernel,
+        "unspread",
+        meta,
+        (d_packed, early_mine, early_other),
+        (((rows, width), BF16), ((rows, 2 * features), BF16), ((rows, 2 * features), BF16)),
+    )
+    d_one_parts = exchange_shares(d_one_part, "tensor")
+
+    left = jnp.concatenate([hidden_one, d_attn])
     blank = jnp.zeros((features, rows), BF16)
-    d_qk = d_projected[: 2 * features]
-    d_value = d_projected[2 * features :]
-    d_mine, d_other = choose(core, d_qk, jnp.concatenate([d_value, blank]))
-    d_one_part = lax.dot_general(
-        d_mine, early_mine, by_rows, preferred_element_type=F32
-    ) + lax.dot_general(d_other, early_other, by_rows, preferred_element_type=F32)
-    d_one_part = d_one_part.astype(BF16)
-    d_hidden_one = exchange_shares(d_one_part, "tensor")
-
-    left = jnp.concatenate([hidden_one, d_attn])
-    right_qk = jnp.concatenate([d_qk, jnp.zeros_like(d_qk)], axis=1)
-    right_vp = jnp.concatenate(
-        [jnp.concatenate([d_value, blank]), jnp.concatenate([blank, attended])], axis=1
-    )
+    right_qk = jnp.concatenate([d_qk, jnp.zeros_like(d_qk)])
+    right_vp = jnp.concatenate([d_vp, jnp.concatenate([blank, attended]).T])
     right_mine, right_other = choose(core, right_qk, right_vp)
-    right_mine, right_other = after((right_mine, right_other), d_one_part)
-    sent = lax.dot_general(left, right_other, by_rows, preferred_element_type=F32)
-    kept = lax.dot_general(left, right_mine, by_rows, preferred_element_type=F32)
+    sent = lax.dot_general(left, right_other, by_token, preferred_element_type=F32)
+    kept = lax.dot_general(left, right_mine, by_token, preferred_element_type=F32)
     early_total = pair_total(kept, sent)
     late_last = chip_share(after(late_total, d_one_part), n_dp // 2 - 1)
-    d_hidden_one, early_total = lax.optimization_barrier((d_hidden_one, early_total))
+    d_one_parts, early_total = lax.optimization_barrier((d_one_parts, early_total))
     early_grads = [chip_share(early_total, step) for step in range(n_dp // 2)]
 
-    d_hidden_one = jnp.sum(d_hidden_one.astype(F32), axis=0)
-    own_unit, own_inverse = own(unit_one), own(inverse_one)
-    scale_one = 1.0 + pick(modulation[1], own_ids)
-    grad_own = d_mid + norm_back(own_unit, own_inverse, d_hidden_one * scale_one)
-
-    d_float = d_projected.astype(F32).reshape(3, features, rows)
+    grad_own, d_mod_part = call(
+        lambda *refs: first_back_kernel(latents, *refs),
+        "first_back",
+        meta,
+        (d_one_parts, tokens, d_mid, mod_rows, mid_sums, last_sums),
+        (((share, width), BF16), ((n_tensor, 6 * latents, features), F32)),
+        [pltpu.VMEM((2 * latents, width), F32)],
+    )
     bias_part = jnp.concatenate(
         [
             jnp.sum(d_mlp.astype(F32), axis=0),
-            jnp.sum(d_attn.astype(F32), axis=0),
-            jnp.sum(d_pre.astype(F32), axis=0),
-            jnp.sum(d_float[0], axis=1),
-            jnp.sum(d_float[2], axis=1),
+            d_bias_proj[0],
+            d_bias_fc1[0],
+            jnp.sum(d_qk[:, :features].astype(F32), axis=0),
+            jnp.sum(d_vp[:, :features].astype(F32), axis=0),
         ]
     )
     bias_rows = bias_part.reshape(-1, features)
-
-    one_hot = (jnp.arange(latents, dtype=jnp.int32)[:, None] == own_ids[None, :]).astype(BF16)
-
-    def by_latent(parts):
-        joined = jnp.concatenate([part.astype(BF16) for part in parts], axis=1)
-        sums = jnp.dot(one_hot, joined, preferred_element_type=F32)
-        return sums.reshape(latents, len(parts), n_tensor, features)
-
-    d_mod_last = by_latent(
-        [d_mid * attn_out, d_hidden_two, d_hidden_two * unit_two, own_cotangent * mlp_out]
-    )
-    d_mod_first = by_latent([d_hidden_one, d_hidden_one * own_unit])
-    d_mod_part = jnp.concatenate([d_mod_first, d_mod_last], axis=1).transpose(2, 0, 1, 3)
-    d_mod_part = d_mod_part.reshape(n_tensor, latents * 6, features)
-    grad_tokens = gather_beside(after(grad_own.astype(BF16), d_mod_part), "tensor").astype(F32)
     d_mod_mine = jnp.sum(exchange(d_mod_part, "tensor"), axis=0)
+    grad_tokens = gather_beside(after(grad_own, d_mod_mine), "tensor").astype(F32)
     sums = jnp.sum(gather(jnp.concatenate([d_mod_mine, bias_rows]), "dp", n_dp), axis=0)
     d_mod = sums[: 6 * latents].reshape(latents, 6 * features)
     bias_total = sums[6 * latents :].reshape(-1)
@@ -590,7 +837,7 @@
     grad_cond = d_active * (gate * (1.0 + cond * (1.0 - gate)))
 
     grad_fc1, grad_fc2 = finish_pair(late_grads + [late_last])
-    grad_qk, grad_vp = finish_pair(early_grads)
+    grad_qk, grad_vp = finish_pair(after(early_grads, d_active))
     grad_qkv = jnp.concatenate([grad_qk, grad_vp[:, :features]], axis=1)
     grad_qkv = grad_qkv.reshape(share_width, 3, features)
 

time: 390 us -> 356 us (0.913)
  other arithmetic: 45.7 us -> 19.1 us
  Pallas kernels: 13 us -> 38 us
  waiting for transfers between devices: 132 us -> 112 us
  matrix products: 35.5 us -> 16.2 us
  blocking collectives: 8.1 us -> 25.9 us
  local copies, waits for them, and re-layouts: 67.5 us -> 54.8 us
  starting transfers between devices: 80.8 us -> 85.5 us
    pallas_call x0 -> x8, Pallas kernels: none -> 23.3 us  [call(): pl.pallas_call(body, out_shape=tuple((jax.ShapeDtypeStruct(shape, kind) f...]
    ppermute x29 -> x32, waiting for transfers between devices: 68.2 us -> 46.7 us  [swap(): return lax.ppermute(block, axis, route)]
    dot_general x13 -> x2, matrix products: 25 us -> 5.4 us  [the longest x1 3.37 us: local(): lax.dot_general(left, right_mine, by_token, preferred_element_type=F32)]
    all_to_all x1 -> x2, blocking collectives: 8.1 us -> 25.9 us  [exchange(): return lax.all_to_all(blocks, axis, 0, 0, tiled=True)]
    unnamed x187 -> x152, local copies, waits for them, and re-layouts: 7.79 us -> 25.5 us
    broadcast_in_dim x21 -> x0, local copies, waits for them, and re-layouts: 10.8 us -> none  [the longest x18 8.9 us: pick(): out = jnp.where(ids[:, None] == number, rows_by_latent[number][None], out)]
    reduce_sum x13 -> x3, other arithmetic: 9.01 us -> 0.21 us  [the longest x1 0.1 us: local(): jnp.sum(d_mlp.astype(F32), axis=0)]
    dynamic_update_slice x7 -> x4, local copies, waits for them, and re-layouts: 7.03 us -> 0.2 us  [assemble(): full = lax.dynamic_update_index_in_dim(full, part, chip ^ step, 0)]
  transfers between devices with their start and end apart: 42 -> 44, of which waited for: 19 -> 22; matrix products, arithmetic and copies ran while one was open for 25% -> 15% of each run, Pallas kernels for 2% -> 3%
where the time goes in v4:
time: 356 us; the launch traced here: 353 us
  waiting for transfers between devices  112 us (31%)
  starting transfers between devices  85.5 us (24%)
  local copies, waits for them, and re-layouts  54.8 us (15%)
  Pallas kernels  38 us (11%)
  blocking collectives  25.9 us (7%)
  other arithmetic  19.1 us (5%)
  matrix products  16.2 us (5%)
    all_to_all x12, waiting for transfers between devices, exchange(): return lax.all_to_all(blocks, axis, 0, 0, tiled=True)  65.4 us
    all_to_all x12, starting transfers between devices, exchange(): return lax.all_to_all(blocks, axis, 0, 0, tiled=True)  49.4 us
    ppermute x32, waiting for transfers between devices, swap(): return lax.ppermute(block, axis, route)  46.7 us
    ppermute x32, starting transfers between devices, swap(): return lax.ppermute(block, axis, route)  36.1 us
    all_to_all x2, blocking collectives, exchange(): return lax.all_to_all(blocks, axis, 0, 0, tiled=True)  25.9 us
    unnamed x152, local copies, waits for them, and re-layouts  25.5 us
    pallas_call x8, Pallas kernels, call(): pl.pallas_call(body, out_shape=tuple((jax.ShapeDtypeStruct(shape, kind) f...  23.3 us
    pallas_call x1, Pallas kernels, attend_backward(): pl.pallas_call(lambda *refs: backward_kernel(meta.shape[0] - 1, *refs), o...  7.79 us
  transfers between devices with their start and end apart: 44, of which 22 were waited for; matrix products, arithmetic and copies ran while one was open for 15% of the time, Pallas kernels for 3%

profile of v4, /device:TPU:0, one launch (start us, length us, event | category | flops | bytes accessed | tf_op | source)
XLA Modules:
  0.0 353.3 jit_solution(10034432870779471075)
XLA Ops:
  4.9 2.9 collective-permute-start.1
  10.4 4.2 %all-to-all-start = ((f32[8,18,288]{2,1,0:T(8,128)}), f32[8,18,288]{2,1,0:T(8,128)S(1)}, u32[]{:S(2)}, u32[]{:S(2)}) async-start(f32[8,18,288]{2,1,0:T(8,128)} %broadcast_in_dim.47), calls=%async_computation | async-start | bytes 589824 | tf_op jit(solution)/shard_map/all_to_all | solution.py:26
  14.6 14.6 %all-to-all-done = f32[8,18,288]{2,1,0:T(8,128)S(1)} async-done(((f32[8,18,288]{2,1,0:T(8,128)}), f32[8,18,288]{2,1,0:T(8,128)S(1)}, u32[]{:S(2)}, u32[]{:S(2)}) %all-to-all-start) | async-done | bytes 165920 | tf_op jit(solution)/shard_map/all_to_all | solution.py:26
  30.0 4.9 %all-to-all-start.1 = ((f32[4,18,288]{2,1,0:T(8,128)}), f32[4,18,288]{2,1,0:T(8,128)S(1)}, u32[]{:S(2)}, u32[]{:S(2)}) async-start(f32[4,18,288]{2,1,0:T(8,128)} %broadcast_in_dim.48), calls=%async_computation.1 | async-start | bytes 294912 | tf_op jit(solution)/shard_map/all_to_all | solution.py:26
  34.8 6.0 %all-to-all-done.1 = f32[4,18,288]{2,1,0:T(8,128)S(1)} async-done(((f32[4,18,288]{2,1,0:T(8,128)}), f32[4,18,288]{2,1,0:T(8,128)S(1)}, u32[]{:S(2)}, u32[]{:S(2)}) %all-to-all-start.1) | async-done | bytes 82976 | tf_op jit(solution)/shard_map/all_to_all | solution.py:26
  51.5 3.8 %project.1 = (bf16[256,1152]{1,0:T(8,128)(2,1)S(1)}, bf16[256,1152]{1,0:T(8,128)(2,1)S(1)}, bf16[8,72,640]{2,1,0:T(8,128)(2,1)S(1)}) custom-call(s32[7]{0:T(128)S(1)} %concatenate.48.refs_0_.meta_ref, bf16[256,1152]{1,0:T(8,128)(2,1)S(1)} %copy-done.2, bf16[256,1152]{1,0:T(8,128)(2,1)S(1)} %copy-done.5, f32[18,1152]{1,0:T(8,128)S(1)} %copy-done.8, ...), custom_call_target="tpu_custom_call" | custom-call | flops 1 | bytes 1 | tf_op jit(solution)/shard_map/project/pallas_call | solution.py:365
  57.0 4.2 %all-to-all-start.2 = ((bf16[8,72,640]{2,1,0:T(8,128)(2,1)}), bf16[8,72,640]{2,1,0:T(8,128)(2,1)}, u32[]{:S(2)}, u32[]{:S(2)}) async-start(bf16[8,72,640]{2,1,0:T(8,128)(2,1)} %copy-done.22), calls=%async_computation.2 | async-start | bytes 1474560 | tf_op jit(solution)/shard_map/all_to_all | solution.py:26
  73.3 6.9 %attend_forward.1 = (bf16[8,72,128]{2,1,0:T(8,128)(2,1)S(1)}, f32[8,72,128]{2,1,0:T(8,128)S(1)}, f32[8,1,128]{2,1,0:T(1,128)S(1)}) custom-call(s32[4]{0:T(128)S(1)} %pad_add_fusion.refs_0_, bf16[8,72,640]{2,1,0:T(8,128)(2,1)} %all-to-all-done.2.refs_1_), custom_call_target="tpu_custom_call" | custom-call | flops 1000000000 | bytes 4000000 | tf_op jit(solution)/shard_map/attend_forward/pallas_call | solution.py:215
  80.3 8.1 %all_to_all.70 = bf16[8,72,128]{2,1,0:T(8,128)(2,1)S(1)} all-to-all(bf16[8,72,128]{2,1,0:T(8,128)(2,1)S(1)} %get-tuple-element.75), channel_id=1, replica_groups=mesh['dp'=8,'tensor'=4] {'dp'}, dimensions={0} | all-to-all | bytes 294912 | tf_op jit(solution)/shard_map/all_to_all | solution.py:26
  89.9 4.2 %all-to-all-start.4 = ((bf16[4,64,1152]{2,1,0:T(8,128)(2,1)}), bf16[4,64,1152]{2,1,0:T(8,128)(2,1)}, u32[]{:S(2)}, u32[]{:S(2)}) async-start(bf16[4,64,1152]{2,1,0:T(8,128)(2,1)} %bitcast.118), calls=%async_computation.4 | async-start | bytes 1179648 | tf_op jit(solution)/shard_map/all_to_all | solution.py:26
  94.7 15.3 %all-to-all-done.4.refs_1_ = bf16[4,64,1152]{2,1,0:T(8,128)(2,1)} async-done(((bf16[4,64,1152]{2,1,0:T(8,128)(2,1)}), bf16[4,64,1152]{2,1,0:T(8,128)(2,1)}, u32[]{:S(2)}, u32[]{:S(2)}) %all-to-all-start.4) | async-done | bytes 589856 | tf_op jit(solution)/shard_map/all_to_all | solution.py:26
  115.9 4.3 %all-to-all-start.5 = ((bf16[4,64,1152]{2,1,0:T(8,128)(2,1)}), bf16[4,64,1152]{2,1,0:T(8,128)(2,1)}, u32[]{:S(2)}, u32[]{:S(2)}) async-start(bf16[4,64,1152]{2,1,0:T(8,128)(2,1)} %copy-done.24), calls=%async_computation.5 | async-start | bytes 1179648 | tf_op jit(solution)/shard_map/all_to_all | solution.py:26
  125.3 14.7 %collective-permute-done.6.refs_2_ = bf16[288,1152]{1,0:T(8,128)(2,1)} collective-permute-done((bf16[288,1152]{1,0:T(8,128)(2,1)}, bf16[288,1152]{1,0:T(8,128)(2,1)}, u32[]{:S(2)}, u32[]{:S(2)}) %collective-permute-start.6) | collective-permute-done | bytes 663584 | tf_op jit(solution)/shard_map/ppermute | solution.py:22
  140.0 12.6 %collective-permute-done.7.refs_3_ = bf16[288,1152]{1,0:T(8,128)(2,1)} collective-permute-done((bf16[288,1152]{1,0:T(8,128)(2,1)}, bf16[288,1152]{1,0:T(8,128)(2,1)}, u32[]{:S(2)}, u32[]{:S(2)}) %collective-permute-start.7) | collective-permute-done | bytes 663584 | tf_op jit(solution)/shard_map/ppermute | solution.py:22
  158.9 7.9 %mlp.1 = (bf16[256,1152]{1,0:T(8,128)(2,1)S(1)}, bf16[256,1152]{1,0:T(8,128)(2,1)S(1)}, bf16[256,1152]{1,0:T(8,128)(2,1)S(1)}, bf16[256,1152]{1,0:T(8,128)(2,1)S(1)}, f32[1,1152]{1,0:T(1,128)S(1)}) custom-call(s32[7]{0:T(128)S(1)} %concatenate.48.refs_0_.meta_ref, bf16[288,1152]{1,0:T(8,128)(2,1)S(1)} %copy-done.13, ...), custom_call_target="tpu_custom_call" | custom-call | flops 1 | bytes 1 | tf_op jit(solution)/shard_map/mlp/pallas_call | solution.py:365
  171.2 4.8 %all-to-all-start.6 = ((bf16[4,64,1152]{2,1,0:T(8,128)(2,1)}), bf16[4,64,1152]{2,1,0:T(8,128)(2,1)}, u32[]{:S(2)}, u32[]{:S(2)}) async-start(bf16[4,64,1152]{2,1,0:T(8,128)(2,1)} %bitcast.112), calls=%async_computation.6 | async-start | bytes 1179648 | tf_op jit(solution)/shard_map/all_to_all | solution.py:26
  176.1 4.7 %fusion = bf16[1152,1152]{1,0:T(8,128)(2,1)} fusion(bf16[1152,1152]{1,0:T(8,128)(2,1)} %collective-permute-done.13, bf16[256,1152]{1,0:T(8,128)(2,1)} %copy-done.15, bf16[256,1152]{1,0:T(8,128)(2,1)} %copy-done.14, bf16[256,1152]{1,0:T(8,128)(2,1)} %bitcast.17.refs_9_, bf16[256,1152]{1,0:T(8,128)(2,1)S(1)} %get-tuple-element.82.refs_10_, pred[]{:T(512)S(6)} %eq.9), kind=kOutput, calls=%fused_computation.2 | convolution fusion | flops 684048384 | bytes 7667713 | tf_op jit(solution)/shard_map/dot_general | solution.py:749
  180.8 11.4 %all-to-all-done.6.refs_1_ = bf16[4,64,1152]{2,1,0:T(8,128)(2,1)} async-done(((bf16[4,64,1152]{2,1,0:T(8,128)(2,1)}), bf16[4,64,1152]{2,1,0:T(8,128)(2,1)}, u32[]{:S(2)}, u32[]{:S(2)}) %all-to-all-start.6) | async-done | bytes 589856 | tf_op jit(solution)/shard_map/all_to_all | solution.py:26
  198.1 17.8 %all_to_all.71 = bf16[4,64,1152]{2,1,0:T(8,128)(2,1)S(1)} all-to-all(bf16[4,64,1152]{2,1,0:T(8,128)(2,1)S(1)} %get-tuple-element.90), channel_id=1, replica_groups=mesh['dp'=8,'tensor'=4] {'tensor'}, dimensions={0} | all-to-all | bytes 1179648 | tf_op jit(solution)/shard_map/all_to_all | solution.py:26
  218.4 4.0 %all-to-all-start.8 = ((bf16[8,72,128]{2,1,0:T(8,128)(2,1)}), bf16[8,72,128]{2,1,0:T(8,128)(2,1)}, u32[]{:S(2)}, u32[]{:S(2)}) async-start(bf16[8,72,128]{2,1,0:T(8,128)(2,1)} %copy-done.32), calls=%async_computation.8 | async-start | bytes 294912 | tf_op jit(solution)/shard_map/all_to_all | solution.py:26
  230.2 7.8 %attend_backward.1 = bf16[8,72,640]{2,1,0:T(8,128)(2,1)S(1)} custom-call(s32[4]{0:T(128)S(1)} %pad_add_fusion.refs_0_, bf16[8,72,640]{2,1,0:T(8,128)(2,1)} %all-to-all-done.2.refs_1_, bf16[8,72,128]{2,1,0:T(8,128)(2,1)} %all-to-all-done.8.refs_2_, f32[8,72,128]{2,1,0:T(8,128)S(1)} %copy-done.46, f32[8,1,128]{2,1,0:T(1,128)S(1)} %copy-done.48), custom_call_target="tpu_custom_call" | custom-call | flops 3000000000 | bytes 4000000 | tf_op jit(solution)/shard_map/attend_backward/pallas_call | solution.py:239
  238.9 4.3 %all-to-all-start.9 = ((bf16[8,72,640]{2,1,0:T(8,128)(2,1)}), bf16[8,72,640]{2,1,0:T(8,128)(2,1)}, u32[]{:S(2)}, u32[]{:S(2)}) async-start(bf16[8,72,640]{2,1,0:T(8,128)(2,1)} %copy-done.21), calls=%async_computation.9 | async-start | bytes 1474560 | tf_op jit(solution)/shard_map/all_to_all | solution.py:26
  249.0 3.7 %collective-permute-done.14.refs_2_ = bf16[64,1152]{1,0:T(8,128)(2,1)S(1)} collective-permute-done((bf16[64,1152]{1,0:T(8,128)(2,1)S(1)}, bf16[64,1152]{1,0:T(8,128)(2,1)S(1)}, u32[]{:S(2)}, u32[]{:S(2)}) %collective-permute-start.14) | collective-permute-done | bytes 147488 | tf_op jit(solution)/shard_map/ppermute | solution.py:22
  252.7 6.2 %collective-permute-done.15.refs_3_ = bf16[64,1152]{1,0:T(8,128)(2,1)S(1)} collective-permute-done((bf16[64,1152]{1,0:T(8,128)(2,1)S(1)}, bf16[64,1152]{1,0:T(8,128)(2,1)S(1)}, u32[]{:S(2)}, u32[]{:S(2)}) %collective-permute-start.15) | collective-permute-done | bytes 147488 | tf_op jit(solution)/shard_map/ppermute | solution.py:22
  262.0 4.0 %unspread.1 = (bf16[256,1152]{1,0:T(8,128)(2,1)}, bf16[256,576]{1,0:T(8,128)(2,1)S(1)}, bf16[256,576]{1,0:T(8,128)(2,1)S(1)}) custom-call(s32[7]{0:T(128)S(1)} %concatenate.48.refs_0_.meta_ref, bf16[8,72,640]{2,1,0:T(8,128)(2,1)} %all-to-all-done.9.parts_ref, bf16[1152,576]{1,0:T(8,128)(2,1)S(1)} %bitcast.107, bf16[1152,576]{1,0:T(8,128)(2,1)S(1)} %copy.82.refs_6_.other_ref), custom_call_target="tpu_custom_call" | custom-call | flops 1 | bytes 1 | tf_op jit(solution)/shard_map/unspread/pallas_call | solution.py:365
  280.1 3.6 %all-to-all-start.10 = ((bf16[4,64,1152]{2,1,0:T(8,128)(2,1)}), bf16[4,64,1152]{2,1,0:T(8,128)(2,1)S(1)}, u32[]{:S(2)}, u32[]{:S(2)}) async-start(bf16[4,64,1152]{2,1,0:T(8,128)(2,1)} %bitcast.37), calls=%async_computation.10 | async-start | bytes 1179648 | tf_op jit(solution)/shard_map/all_to_all | solution.py:26
  291.0 3.4 add_convert_fusion
  296.6 6.3 %all-to-all-done.10.refs_1_ = bf16[4,64,1152]{2,1,0:T(8,128)(2,1)S(1)} async-done(((bf16[4,64,1152]{2,1,0:T(8,128)(2,1)}), bf16[4,64,1152]{2,1,0:T(8,128)(2,1)S(1)}, u32[]{:S(2)}, u32[]{:S(2)}) %all-to-all-start.10) | async-done | bytes 589856 | tf_op jit(solution)/shard_map/all_to_all | solution.py:26
  304.8 5.0 %all-to-all-start.11 = ((f32[4,18,288]{2,1,0:T(8,128)}), f32[4,18,288]{2,1,0:T(8,128)S(1)}, u32[]{:S(2)}, u32[]{:S(2)}) async-start(f32[4,18,288]{2,1,0:T(8,128)} %get-tuple-element.107), calls=%async_computation.11 | async-start | bytes 294912 | tf_op jit(solution)/shard_map/all_to_all | solution.py:26
  311.9 4.1 %all-to-all-done.11 = f32[4,18,288]{2,1,0:T(8,128)S(1)} async-done(((f32[4,18,288]{2,1,0:T(8,128)}), f32[4,18,288]{2,1,0:T(8,128)S(1)}, u32[]{:S(2)}, u32[]{:S(2)}) %all-to-all-start.11) | async-done | bytes 82976 | tf_op jit(solution)/shard_map/all_to_all | solution.py:26
  323.7 3.5 all-to-all-start.12
  327.2 2.9 collective-permute-start.28
  (318 shorter events, 139.6 us)
Async XLA Ops:
  4.9 36.7 %collective-permute-start.1 = (bf16[288,576]{1,0:T(8,128)(2,1)S(1)}, bf16[288,576]{1,0:T(8,128)(2,1)S(1)}, u32[]{:S(2)}, u32[]{:S(2)}) collective-permute-start(bf16[288,576]{1,0:T(8,128)(2,1)S(1)} %pad_maximum_fusion.13), channel_id=1, source_target_pairs={{0,8},{4,12},{8,0},{12,4},{16,24},{20,28},{24,16},{28,20},{1,9},{5... | collective-permute-start | bytes 995336 | tf_op jit(solution)/shard_map/ppermute | solution.py:22
  7.8 33.8 %collective-permute-start.2 = (bf16[288,576]{1,0:T(8,128)(2,1)S(1)}, bf16[288,576]{1,0:T(8,128)(2,1)S(1)}, u32[]{:S(2)}, u32[]{:S(2)}) collective-permute-start(bf16[288,576]{1,0:T(8,128)(2,1)S(1)} %pad_maximum_fusion.13), channel_id=1, source_target_pairs={{0,16},{4,20},{8,24},{12,28},{16,0},{20,4},{24,8},{28,12},{1,17},{... | collective-permute-start | bytes 995336 | tf_op jit(solution)/shard_map/ppermute | solution.py:22
  9.4 32.3 %collective-permute-start.3 = (bf16[288,576]{1,0:T(8,128)(2,1)S(1)}, bf16[288,576]{1,0:T(8,128)(2,1)S(1)}, u32[]{:S(2)}, u32[]{:S(2)}) collective-permute-start(bf16[288,576]{1,0:T(8,128)(2,1)S(1)} %pad_maximum_fusion.13), channel_id=1, source_target_pairs={{0,24},{4,28},{8,16},{12,20},{16,8},{20,12},{24,0},{28,4},{1,25},{... | collective-permute-start | bytes 995336 | tf_op jit(solution)/shard_map/ppermute | solution.py:22
  10.4 18.8 %all-to-all-start = ((f32[8,18,288]{2,1,0:T(8,128)}), f32[8,18,288]{2,1,0:T(8,128)S(1)}, u32[]{:S(2)}, u32[]{:S(2)}) async-start(f32[8,18,288]{2,1,0:T(8,128)} %broadcast_in_dim.47), calls=%async_computation | async-start | bytes 589824 | tf_op jit(solution)/shard_map/all_to_all | solution.py:26
  30.0 10.8 %all-to-all-start.1 = ((f32[4,18,288]{2,1,0:T(8,128)}), f32[4,18,288]{2,1,0:T(8,128)S(1)}, u32[]{:S(2)}, u32[]{:S(2)}) async-start(f32[4,18,288]{2,1,0:T(8,128)} %broadcast_in_dim.48), calls=%async_computation.1 | async-start | bytes 294912 | tf_op jit(solution)/shard_map/all_to_all | solution.py:26
  57.0 16.3 %all-to-all-start.2 = ((bf16[8,72,640]{2,1,0:T(8,128)(2,1)}), bf16[8,72,640]{2,1,0:T(8,128)(2,1)}, u32[]{:S(2)}, u32[]{:S(2)}) async-start(bf16[8,72,640]{2,1,0:T(8,128)(2,1)} %copy-done.22), calls=%async_computation.2 | async-start | bytes 1474560 | tf_op jit(solution)/shard_map/all_to_all | solution.py:26
  89.9 20.2 %all-to-all-start.4 = ((bf16[4,64,1152]{2,1,0:T(8,128)(2,1)}), bf16[4,64,1152]{2,1,0:T(8,128)(2,1)}, u32[]{:S(2)}, u32[]{:S(2)}) async-start(bf16[4,64,1152]{2,1,0:T(8,128)(2,1)} %bitcast.118), calls=%async_computation.4 | async-start | bytes 1179648 | tf_op jit(solution)/shard_map/all_to_all | solution.py:26
  115.9 36.7 %all-to-all-start.5 = ((bf16[4,64,1152]{2,1,0:T(8,128)(2,1)}), bf16[4,64,1152]{2,1,0:T(8,128)(2,1)}, u32[]{:S(2)}, u32[]{:S(2)}) async-start(bf16[4,64,1152]{2,1,0:T(8,128)(2,1)} %copy-done.24), calls=%async_computation.5 | async-start | bytes 1179648 | tf_op jit(solution)/shard_map/all_to_all | solution.py:26
  121.8 18.2 %collective-permute-start.6 = (bf16[288,1152]{1,0:T(8,128)(2,1)}, bf16[288,1152]{1,0:T(8,128)(2,1)}, u32[]{:S(2)}, u32[]{:S(2)}) collective-permute-start(bf16[288,1152]{1,0:T(8,128)(2,1)} %pad_maximum_fusion.5.refs_1_), channel_id=1, source_target_pairs={{0,8},{4,12},{8,0},{12,4},{16,24},{20,28},{24,16},{28,20},{1,9},{5... | collective-permute-start | bytes 1990664 | tf_op jit(solution)/shard_map/ppermute | solution.py:22
  122.5 30.1 %collective-permute-start.7 = (bf16[288,1152]{1,0:T(8,128)(2,1)}, bf16[288,1152]{1,0:T(8,128)(2,1)}, u32[]{:S(2)}, u32[]{:S(2)}) collective-permute-start(bf16[288,1152]{1,0:T(8,128)(2,1)} %pad_maximum_fusion.5.refs_1_), channel_id=1, source_target_pairs={{0,16},{4,20},{8,24},{12,28},{16,0},{20,4},{24,8},{28,12},{1,17},{... | collective-permute-start | bytes 1990664 | tf_op jit(solution)/shard_map/ppermute | solution.py:22
  123.0 29.6 %collective-permute-start.8 = (bf16[288,1152]{1,0:T(8,128)(2,1)}, bf16[288,1152]{1,0:T(8,128)(2,1)}, u32[]{:S(2)}, u32[]{:S(2)}) collective-permute-start(bf16[288,1152]{1,0:T(8,128)(2,1)} %pad_maximum_fusion.5.refs_1_), channel_id=1, source_target_pairs={{0,24},{4,28},{8,16},{12,20},{16,8},{20,12},{24,0},{28,4},{1,25},{... | collective-permute-start | bytes 1990664 | tf_op jit(solution)/shard_map/ppermute | solution.py:22
  171.2 21.0 %all-to-all-start.6 = ((bf16[4,64,1152]{2,1,0:T(8,128)(2,1)}), bf16[4,64,1152]{2,1,0:T(8,128)(2,1)}, u32[]{:S(2)}, u32[]{:S(2)}) async-start(bf16[4,64,1152]{2,1,0:T(8,128)(2,1)} %bitcast.112), calls=%async_computation.6 | async-start | bytes 1179648 | tf_op jit(solution)/shard_map/all_to_all | solution.py:26
  225.2 36.8 %collective-permute-start.20 = (bf16[288,1152]{1,0:T(8,128)(2,1)}, bf16[288,1152]{1,0:T(8,128)(2,1)}, u32[]{:S(2)}, u32[]{:S(2)}) collective-permute-start(bf16[288,1152]{1,0:T(8,128)(2,1)} %get-tuple-element.187), channel_id=1, source_target_pairs={{0,8},{4,12},{8,0},{12,4},{16,24},{20,28},{24,16},{28,20},{1,9},{5... | collective-permute-start | bytes 1990664 | tf_op jit(solution)/shard_map/ppermute | solution.py:22
  227.1 34.9 %collective-permute-start.21 = (bf16[288,1152]{1,0:T(8,128)(2,1)}, bf16[288,1152]{1,0:T(8,128)(2,1)}, u32[]{:S(2)}, u32[]{:S(2)}) collective-permute-start(bf16[288,1152]{1,0:T(8,128)(2,1)} %get-tuple-element.186), channel_id=1, source_target_pairs={{0,16},{4,20},{8,24},{12,28},{16,0},{20,4},{24,8},{28,12},{1,17},{... | collective-permute-start | bytes 1990664 | tf_op jit(solution)/shard_map/ppermute | solution.py:22
  238.9 23.1 %all-to-all-start.9 = ((bf16[8,72,640]{2,1,0:T(8,128)(2,1)}), bf16[8,72,640]{2,1,0:T(8,128)(2,1)}, u32[]{:S(2)}, u32[]{:S(2)}) async-start(bf16[8,72,640]{2,1,0:T(8,128)(2,1)} %copy-done.21), calls=%async_computation.9 | async-start | bytes 1474560 | tf_op jit(solution)/shard_map/all_to_all | solution.py:26
  245.0 14.0 %collective-permute-start.15 = (bf16[64,1152]{1,0:T(8,128)(2,1)S(1)}, bf16[64,1152]{1,0:T(8,128)(2,1)S(1)}, u32[]{:S(2)}, u32[]{:S(2)}) collective-permute-start(bf16[64,1152]{1,0:T(8,128)(2,1)S(1)} %get-tuple-element.208), channel_id=1, source_target_pairs={{0,2},{1,3},{2,0},{3,1},{4,6},{5,7},{6,4},{7,5},{8,10},{9,11},{10,... | collective-permute-start | bytes 442376 | tf_op jit(solution)/shard_map/ppermute | solution.py:22
  246.6 12.3 %collective-permute-start.16 = (bf16[64,1152]{1,0:T(8,128)(2,1)S(1)}, bf16[64,1152]{1,0:T(8,128)(2,1)S(1)}, u32[]{:S(2)}, u32[]{:S(2)}) collective-permute-start(bf16[64,1152]{1,0:T(8,128)(2,1)S(1)} %get-tuple-element.207), channel_id=1, source_target_pairs={{0,3},{1,2},{2,1},{3,0},{4,7},{5,6},{6,5},{7,4},{8,11},{9,10},{10,... | collective-permute-start | bytes 442376 | tf_op jit(solution)/shard_map/ppermute | solution.py:22
  269.6 16.3 %collective-permute-start.30 = (bf16[288,1152]{1,0:T(8,128)(2,1)}, bf16[288,1152]{1,0:T(8,128)(2,1)}, u32[]{:S(2)}, u32[]{:S(2)}) collective-permute-start(bf16[288,1152]{1,0:T(8,128)(2,1)} %dynamic-slice_bitcast_fusion), channel_id=1, source_target_pairs={{0,24},{4,28},{8,16},{12,20},{16,8},{20,12},{24,0},{28,4},{1,25},{... | collective-permute-start | bytes 1990664 | tf_op jit(solution)/shard_map/ppermute | solution.py:22
  272.9 15.9 %collective-permute-start.17 = (bf16[64,1152]{1,0:T(8,128)(2,1)S(1)}, bf16[64,1152]{1,0:T(8,128)(2,1)S(1)}, u32[]{:S(2)}, u32[]{:S(2)}) collective-permute-start(bf16[64,1152]{1,0:T(8,128)(2,1)S(1)} %copy-done.31), channel_id=1, source_target_pairs={{0,1},{1,0},{2,3},{3,2},{4,5},{5,4},{6,7},{7,6},{8,9},{9,8},{10,11... | collective-permute-start | bytes 442376 | tf_op jit(solution)/shard_map/ppermute | solution.py:22
  275.6 13.2 %collective-permute-start.18 = (bf16[64,1152]{1,0:T(8,128)(2,1)S(1)}, bf16[64,1152]{1,0:T(8,128)(2,1)}, u32[]{:S(2)}, u32[]{:S(2)}) collective-permute-start(bf16[64,1152]{1,0:T(8,128)(2,1)S(1)} %copy-done.31), channel_id=1, source_target_pairs={{0,2},{1,3},{2,0},{3,1},{4,6},{5,7},{6,4},{7,5},{8,10},{9,11},{10,... | collective-permute-start | bytes 442376 | tf_op jit(solution)/shard_map/ppermute | solution.py:22
  275.7 13.1 %collective-permute-start.19 = (bf16[64,1152]{1,0:T(8,128)(2,1)S(1)}, bf16[64,1152]{1,0:T(8,128)(2,1)}, u32[]{:S(2)}, u32[]{:S(2)}) collective-permute-start(bf16[64,1152]{1,0:T(8,128)(2,1)S(1)} %copy-done.31), channel_id=1, source_target_pairs={{0,3},{1,2},{2,1},{3,0},{4,7},{5,6},{6,5},{7,4},{8,11},{9,10},{10,... | collective-permute-start | bytes 442376 | tf_op jit(solution)/shard_map/ppermute | solution.py:22
  280.1 10.9 %collective-permute-start.22 = (bf16[1152,576]{0,1:T(8,128)(2,1)}, bf16[1152,576]{0,1:T(8,128)(2,1)}, u32[]{:S(2)}, u32[]{:S(2)}) collective-permute-start(bf16[1152,576]{0,1:T(8,128)(2,1)} %convolution_convert_fusion.1), channel_id=1, source_target_pairs={{0,4},{4,0},{8,12},{12,8},{16,20},{20,16},{24,28},{28,24},{1,5},{5... | collective-permute-start | bytes 3981320 | tf_op jit(solution)/shard_map/ppermute | solution.py:22
  280.1 22.8 %all-to-all-start.10 = ((bf16[4,64,1152]{2,1,0:T(8,128)(2,1)}), bf16[4,64,1152]{2,1,0:T(8,128)(2,1)S(1)}, u32[]{:S(2)}, u32[]{:S(2)}) async-start(bf16[4,64,1152]{2,1,0:T(8,128)(2,1)} %bitcast.37), calls=%async_computation.10 | async-start | bytes 1179648 | tf_op jit(solution)/shard_map/all_to_all | solution.py:26
  288.8 29.5 %collective-permute-start.31 = (f32[144,1152]{1,0:T(8,128)}, f32[144,1152]{1,0:T(8,128)}, u32[]{:S(2)}, u32[]{:S(2)}) collective-permute-start(f32[144,1152]{1,0:T(8,128)} %slice_select_fusion.1), channel_id=1, source_target_pairs={{0,4},{4,0},{8,12},{12,8},{16,20},{20,16},{24,28},{28,24},{1,5},{5... | collective-permute-start | bytes 1990664 | tf_op jit(solution)/shard_map/ppermute | solution.py:22
  304.8 11.2 %all-to-all-start.11 = ((f32[4,18,288]{2,1,0:T(8,128)}), f32[4,18,288]{2,1,0:T(8,128)S(1)}, u32[]{:S(2)}, u32[]{:S(2)}) async-start(f32[4,18,288]{2,1,0:T(8,128)} %get-tuple-element.107), calls=%async_computation.11 | async-start | bytes 294912 | tf_op jit(solution)/shard_map/all_to_all | solution.py:26
  310.9 38.1 %collective-permute-start.26 = (bf16[288,576]{1,0:T(8,128)(2,1)}, bf16[288,576]{1,0:T(8,128)(2,1)S(1)}, u32[]{:S(2)}, u32[]{:S(2)}) collective-permute-start(bf16[288,576]{1,0:T(8,128)(2,1)} %get-tuple-element.193), channel_id=1, source_target_pairs={{0,8},{4,12},{8,0},{12,4},{16,24},{20,28},{24,16},{28,20},{1,9},{5... | collective-permute-start | bytes 995336 | tf_op jit(solution)/shard_map/ppermute | solution.py:22
  311.4 37.5 %collective-permute-start.27 = (bf16[288,576]{1,0:T(8,128)(2,1)}, bf16[288,576]{1,0:T(8,128)(2,1)S(1)}, u32[]{:S(2)}, u32[]{:S(2)}) collective-permute-start(bf16[288,576]{1,0:T(8,128)(2,1)} %get-tuple-element.192), channel_id=1, source_target_pairs={{0,16},{4,20},{8,24},{12,28},{16,0},{20,4},{24,8},{28,12},{1,17},{... | collective-permute-start | bytes 995336 | tf_op jit(solution)/shard_map/ppermute | solution.py:22
  316.0 11.2 %collective-permute-start.23 = (bf16[64,1152]{1,0:T(8,128)(2,1)S(1)}, bf16[64,1152]{1,0:T(8,128)(2,1)S(1)}, u32[]{:S(2)}, u32[]{:S(2)}) collective-permute-start(bf16[64,1152]{1,0:T(8,128)(2,1)S(1)} %get-tuple-element.108), channel_id=1, source_target_pairs={{0,1},{1,0},{2,3},{3,2},{4,5},{5,4},{6,7},{7,6},{8,9},{9,8},{10,11... | collective-permute-start | bytes 442376 | tf_op jit(solution)/shard_map/ppermute | solution.py:22
  318.2 11.9 %collective-permute-start.24 = (bf16[64,1152]{1,0:T(8,128)(2,1)S(1)}, bf16[64,1152]{1,0:T(8,128)(2,1)S(1)}, u32[]{:S(2)}, u32[]{:S(2)}) collective-permute-start(bf16[64,1152]{1,0:T(8,128)(2,1)S(1)} %get-tuple-element.108), channel_id=1, source_target_pairs={{0,2},{1,3},{2,0},{3,1},{4,6},{5,7},{6,4},{7,5},{8,10},{9,11},{10,... | collective-permute-start | bytes 442376 | tf_op jit(solution)/shard_map/ppermute | solution.py:22
  318.3 11.9 %collective-permute-start.25 = (bf16[64,1152]{1,0:T(8,128)(2,1)S(1)}, bf16[64,1152]{1,0:T(8,128)(2,1)}, u32[]{:S(2)}, u32[]{:S(2)}) collective-permute-start(bf16[64,1152]{1,0:T(8,128)(2,1)S(1)} %get-tuple-element.108), channel_id=1, source_target_pairs={{0,3},{1,2},{2,1},{3,0},{4,7},{5,6},{6,5},{7,4},{8,11},{9,10},{10,... | collective-permute-start | bytes 442376 | tf_op jit(solution)/shard_map/ppermute | solution.py:22
  323.7 12.2 %all-to-all-start.12 = ((f32[8,32,288]{2,1,0:T(8,128)}), f32[8,32,288]{2,1,0:T(8,128)S(1)}, u32[]{:S(2)}, u32[]{:S(2)}) async-start(f32[8,32,288]{2,1,0:T(8,128)} %broadcast_in_dim.55), calls=%async_computation.12 | async-start | bytes 786432 | tf_op jit(solution)/shard_map/all_to_all | solution.py:26
  327.2 21.7 %collective-permute-start.28 = (bf16[288,576]{1,0:T(8,128)(2,1)S(1)}, bf16[288,576]{1,0:T(8,128)(2,1)S(1)}, u32[]{:S(2)}, u32[]{:S(2)}) collective-permute-start(bf16[288,576]{1,0:T(8,128)(2,1)S(1)} %copy-done.62), channel_id=1, source_target_pairs={{0,24},{4,28},{8,16},{12,20},{16,8},{20,12},{24,0},{28,4},{1,25},{... | collective-permute-start | bytes 995336 | tf_op jit(solution)/shard_map/ppermute | solution.py:22
  (85 other events, 434.6 us)

commit v5 on v4

--- a/solution.py
+++ b/solution.py
@@ -12,7 +12,7 @@
 NORM_EPS = 1e-06
 NEGATIVE = -1e30
 SCALE = 1.0 / math.sqrt(DH)
-VMEM_BYTES = 40 * 1024 * 1024
+MIB = 1024 * 1024
 BF16 = jnp.bfloat16
 F32 = jnp.float32
 
@@ -49,25 +49,20 @@
     return [rows] + [swap(rows, "dp", 2 * step) for step in range(1, count)]
 
 
-def assemble(parts):
-    chip = lax.axis_index("dp") // 2
-    full = jnp.zeros((len(parts),) + parts[0].shape, parts[0].dtype)
-    for step, part in enumerate(parts):
-        full = lax.dynamic_update_index_in_dim(full, part, chip ^ step, 0)
-    mine = full.reshape(-1, parts[0].shape[1])
-    return mine, swap(mine, "dp", 1)
-
-
-def pair_total(mine, other):
-    count = lax.axis_size("dp") // 2
-    total = (mine + swap(other.astype(BF16), "dp", 1).astype(F32)).astype(BF16)
-    return total.reshape(count, total.shape[0] // count, total.shape[1])
-
-
-def chip_share(blocks, step):
-    chip = lax.axis_index("dp") // 2
-    sent = lax.dynamic_index_in_dim(blocks, chip ^ step, 0, keepdims=False)
-    return swap(sent, "dp", 2 * step) if step else sent
+def gather_chips(rows):
+    count = lax.axis_size("dp")
+    groups = [list(range(core, count, 2)) for core in range(2)]
+    return lax.all_gather(rows, "dp", axis=0, tiled=True, axis_index_groups=groups)
+
+
+def sum_chips(blocks):
+    if len(blocks) == 1:
+        count, chip = lax.axis_size("dp") // 2, lax.axis_index("dp") // 2
+        rows = blocks[0].reshape((count, -1) + blocks[0].shape[1:])
+        blocks = [
+            lax.dynamic_index_in_dim(rows, chip ^ step, 0, keepdims=False) for step in range(count)
+        ]
+    return [swap(block, "dp", 2 * step) if step else block for step, block in enumerate(blocks)]
 
 
 def finish_pair(parts):
@@ -228,7 +223,7 @@
             pltpu.VMEM((blocks, 256, DH), BF16),
             pltpu.VMEM((blocks, 256, 256), F32),
         ],
-        compiler_params=pltpu.CompilerParams(vmem_limit_bytes=VMEM_BYTES),
+        compiler_params=pltpu.CompilerParams(vmem_limit_bytes=10 * MIB),
         cost_estimate=pl.CostEstimate(flops=10**9, bytes_accessed=4 * 10**6, transcendentals=10**6),
         name="attend_forward",
     )(meta, packed)
@@ -248,7 +243,7 @@
             pltpu.VMEM((blocks, DH, 256), F32),
             pltpu.VMEM((blocks, DH, 256), F32),
         ],
-        compiler_params=pltpu.CompilerParams(vmem_limit_bytes=VMEM_BYTES),
+        compiler_params=pltpu.CompilerParams(vmem_limit_bytes=10 * MIB),
         cost_estimate=pl.CostEstimate(flops=3 * 10**9, bytes_accessed=4 * 10**6, transcendentals=10**6),
         name="attend_backward",
     )(meta, packed, grad, exact, log_total)
@@ -262,17 +257,12 @@
     def forward(self, packed, beside):
         self.packed = after(exchange(packed, "dp"), beside)
         out, self.exact, self.log_total = attend_forward(self.meta, self.packed)
-        return self.unsplit(exchange(out, "dp")).reshape(-1, self.rows)
-
-    def unsplit(self, parts):
-        heads = parts.shape[0] // 2
-        parts = parts.reshape(heads, 2, DH, self.rows // 2).transpose(0, 2, 1, 3)
-        return parts.reshape(heads, DH, self.rows)
+        return exchange(out, "dp")
 
     def backward(self, grad, beside):
         grad = exchange(grad, "dp")
         out = attend_backward(self.meta, self.packed, grad, self.exact, self.log_total)
-        return after(exchange(out, "dp"), beside)
+        return exchange(after(out, beside), "dp")
 
 
 class Window:
@@ -322,7 +312,8 @@
             return mixed.astype(BF16), (largest + jnp.log(totals))[:, 0]
 
         out, self.log_total = lax.map(one, self.operands)
-        return out.reshape(-1, self.rows)
+        out = out.reshape(-1, DH, 2, rows // 2).transpose(0, 2, 1, 3)
+        return out.reshape(-1, DH, rows // 2)
 
     def backward(self, grad, beside):
         rows, reach = self.rows, self.reach
@@ -361,7 +352,7 @@
     return [pl.BlockSpec(memory_space=pltpu.VMEM)] * count
 
 
-def call(body, name, meta, arrays, outs, scratch=(), anywhere=0):
+def call(body, name, meta, arrays, outs, scratch=(), anywhere=0, limit=8):
     return pl.pallas_call(
         body,
         out_shape=tuple(jax.ShapeDtypeStruct(shape, kind) for shape, kind in outs),
@@ -370,7 +361,7 @@
         + vmem(len(arrays) - anywhere),
         out_specs=tuple(vmem(len(outs))),
         scratch_shapes=list(scratch),
-        compiler_params=pltpu.CompilerParams(vmem_limit_bytes=VMEM_BYTES),
+        compiler_params=pltpu.CompilerParams(vmem_limit_bytes=limit * MIB),
         cost_estimate=pl.CostEstimate(flops=1, bytes_accessed=1, transcendentals=0),
         name=name,
     )(meta, *arrays)
@@ -416,11 +407,35 @@
         body(other, mine)
 
 
-def project_kernel(
-    latents, meta_ref, tokens_ref, cot_ref, mod_ref, bias_ref, mine_ref, other_ref,
-    hidden_ref, d_mlp_ref, packed_ref,
-):
+def place_rows(meta_ref, parts, whole, sems):
+    block = parts[0].shape[0]
+    copies = []
+    for step, part in enumerate(parts):
+        start = pl.multiple_of((meta_ref[3] ^ step) * block, 16)
+        copies.append(
+            pltpu.make_async_copy(part, whole.at[pl.ds(start, block), :], sems.at[step])
+        )
+    return copies
+
+
+def place_pair(meta_ref, mine, other, first_ref, second_ref, sems):
+    def body(first, second):
+        copies = place_rows(meta_ref, first, first_ref, sems.at[0])
+        copies += place_rows(meta_ref, second, second_ref, sems.at[1])
+        for copy in copies:
+            copy.start()
+        for copy in copies:
+            copy.wait()
+
+    on_core(meta_ref, body, mine, other)
+
+
+def project_kernel(latents, count, meta_ref, *refs):
+    mine, other = refs[:count], refs[count : 2 * count]
+    tokens_ref, cot_ref, mod_ref, bias_ref = refs[2 * count : 2 * count + 4]
+    hidden_ref, d_mlp_ref, packed_ref, qk_ref, vp_ref, sems = refs[2 * count + 4 :]
     rows, width = tokens_ref.shape
+    place_pair(meta_ref, mine, other, qk_ref, vp_ref, sems)
     masks = row_masks(meta_ref, latents, meta_ref[1], rows)
     unit, _ = normed(tokens_ref[...].astype(F32))
     hidden = unit * (1.0 + rows_of(mod_ref, masks, 1)) + rows_of(mod_ref, masks, 0)
@@ -428,26 +443,36 @@
     d_mlp_ref[...] = (cot_ref[...].astype(F32) * rows_of(mod_ref, masks, 5)).astype(BF16)
     heads = packed_ref.shape[0] // 2
     features = heads * DH
-
-    def body(qk_ref, vp_ref):
-        left = hidden_ref[...]
-        both = jnp.dot(left, qk_ref[...], preferred_element_type=F32) + bias_ref[0:1, :]
-        both = both.T
-        value = jnp.dot(left, vp_ref[...], preferred_element_type=F32) + bias_ref[1:2, :]
-        value = value.T
-        for head in range(heads):
-            start = head * DH
-            query = both[start : start + DH].astype(BF16)
-            key = both[features + start : features + start + DH].astype(BF16)
-            val = value[start : start + DH].astype(BF16)
-            for half in range(2):
-                packed_ref[2 * head + half, :, :rows] = key
-                packed_ref[2 * head + half, :, rows : 2 * rows] = val
-                packed_ref[2 * head + half, :, 2 * rows :] = query[
-                    :, half * (rows // 2) : (half + 1) * (rows // 2)
-                ]
-
-    on_core(meta_ref, body, mine_ref, other_ref)
+    left = hidden_ref[...]
+    both = jnp.dot(left, qk_ref[...], preferred_element_type=F32) + bias_ref[0:1, :]
+    both = both.T
+    value = jnp.dot(left, vp_ref[...], preferred_element_type=F32) + bias_ref[1:2, :]
+    value = value.T
+    for head in range(heads):
+        start = head * DH
+        query = both[start : start + DH].astype(BF16)
+        key = both[features + start : features + start + DH].astype(BF16)
+        val = value[start : start + DH].astype(BF16)
+        for half in range(2):
+            packed_ref[2 * head + half, :, :rows] = key
+            packed_ref[2 * head + half, :, rows : 2 * rows] = val
+            packed_ref[2 * head + half, :, 2 * rows :] = query[
+                :, half * (rows // 2) : (half + 1) * (rows // 2)
+            ]
+
+
+def attend_out_kernel(meta_ref, parts_ref, vp_ref, part_ref, attended_ref):
+    heads = parts_ref.shape[0] // 2
+    rows = part_ref.shape[0]
+    stacked = [jnp.zeros((heads * DH, rows), F32)]
+    for head in range(heads):
+        left = parts_ref[2 * head].astype(F32)
+        right = parts_ref[2 * head + 1].astype(F32)
+        stacked.append(jnp.concatenate([left, right], axis=1))
+    attended_ref[...] = jnp.concatenate(stacked, axis=0).T.astype(BF16)
+    part_ref[...] = lax.dot_general(
+        attended_ref[...], vp_ref[...], (((1,), (1,)), ((), ())), preferred_element_type=F32
+    ).astype(BF16)
 
 
 def middle_kernel(
@@ -467,49 +492,43 @@
         sent_ref[part] = hidden.astype(BF16)
 
 
-def mlp_kernel(count, meta_ref, *refs):
-    mine_parts, other_parts = refs[:count], refs[count : 2 * count]
-    hidden_ref, d_mlp_ref, bias_ref = refs[2 * count : 2 * count + 3]
-    d_two_ref, mlp_ref, gelu_ref, d_pre_ref, d_bias_ref = refs[2 * count + 3 : 2 * count + 8]
-    mine_ref, other_ref, d_two_sum, mlp_sum, sems = refs[2 * count + 8 :]
-    block = mine_parts[0].shape[0]
-    copies = []
-    for place, (parts, whole) in enumerate(((mine_parts, mine_ref), (other_parts, other_ref))):
-        for step, part in enumerate(parts):
-            start = pl.multiple_of((meta_ref[3] ^ step) * block, 16)
-            copies.append(
-                pltpu.make_async_copy(
-                    part, whole.at[pl.ds(start, block), :], sems.at[place * count + step]
-                )
-            )
-    for copy in copies:
-        copy.start()
-    for copy in copies:
-        copy.wait()
+def mlp_kernel(
+    meta_ref, mine_ref, other_ref, hidden_ref, d_mlp_ref, bias_ref,
+    d_two_ref, mlp_ref, gelu_ref, d_pre_ref, d_bias_ref,
+    fc1_ref, fc2_ref, d_two_sum, mlp_sum, sems,
+):
+    def load(first, second):
+        copies = [
+            pltpu.make_async_copy(first, fc1_ref, sems.at[0]),
+            pltpu.make_async_copy(second, fc2_ref, sems.at[1]),
+        ]
+        for copy in copies:
+            copy.start()
+        for copy in copies:
+            copy.wait()
+
+    on_core(meta_ref, load, mine_ref, other_ref)
     d_two_sum[...] = jnp.zeros_like(d_two_sum)
     mlp_sum[...] = jnp.zeros_like(mlp_sum)
     tile = 384
     by_last = (((1,), (1,)), ((), ()))
 
-    def body(fc1_ref, fc2_ref):
-        def step(number, carry):
-            units = pl.ds(pl.multiple_of(number * tile, tile), tile)
-            fc1, fc2 = fc1_ref[:, units], fc2_ref[:, units]
-            pre = jnp.dot(hidden_ref[...], fc1, preferred_element_type=F32)
-            gelu, slope = gelu_pair(pre + bias_ref[:, units].astype(F32))
-            grad = jnp.dot(d_mlp_ref[...], fc2, preferred_element_type=F32)
-            d_pre = (grad * slope).astype(BF16)
-            gelu = gelu.astype(BF16)
-            gelu_ref[:, units] = gelu
-            d_pre_ref[:, units] = d_pre
-            d_bias_ref[:, units] = jnp.sum(d_pre.astype(F32), axis=0, keepdims=True)
-            d_two_sum[...] += lax.dot_general(d_pre, fc1, by_last, preferred_element_type=F32)
-            mlp_sum[...] += lax.dot_general(gelu, fc2, by_last, preferred_element_type=F32)
-            return carry
-
-        lax.fori_loop(0, fc1_ref.shape[1] // tile, step, 0)
-
-    on_core(meta_ref, body, mine_ref, other_ref)
+    def step(number, carry):
+        units = pl.ds(pl.multiple_of(number * tile, tile), tile)
+        fc1, fc2 = fc1_ref[:, units], fc2_ref[:, units]
+        pre = jnp.dot(hidden_ref[...], fc1, preferred_element_type=F32)
+        gelu, slope = gelu_pair(pre + bias_ref[:, units].astype(F32))
+        grad = jnp.dot(d_mlp_ref[...], fc2, preferred_element_type=F32)
+        d_pre = (grad * slope).astype(BF16)
+        gelu = gelu.astype(BF16)
+        gelu_ref[:, units] = gelu
+        d_pre_ref[:, units] = d_pre
+        d_bias_ref[:, units] = jnp.sum(d_pre.astype(F32), axis=0, keepdims=True)
+        d_two_sum[...] += lax.dot_general(d_pre, fc1, by_last, preferred_element_type=F32)
+        mlp_sum[...] += lax.dot_general(gelu, fc2, by_last, preferred_element_type=F32)
+        return carry
+
+    lax.fori_loop(0, fc1_ref.shape[1] // tile, step, 0)
     d_two_ref[...] = d_two_sum[...].astype(BF16)
     mlp_ref[...] = mlp_sum[...].astype(BF16)
 
@@ -549,17 +568,18 @@
     latent_sums(sums_ref, masks, own_rows(meta_ref, cot_ref, share) * mlp, 0, 1)
 
 
-def spread_kernel(meta_ref, d_attn_ref, proj_ref, packed_ref, d_bias_ref):
-    grad = jnp.dot(d_attn_ref[...], proj_ref[...], preferred_element_type=F32).T
+def spread_kernel(meta_ref, d_attn_ref, vp_ref, packed_ref, d_bias_ref):
+    grad = jnp.dot(d_attn_ref[...], vp_ref[...], preferred_element_type=F32).T
     half = grad.shape[1] // 2
+    features = grad.shape[0] // 2
     for place in range(packed_ref.shape[0]):
-        start = place // 2 * DH
+        start = features + place // 2 * DH
         side = place % 2 * half
         packed_ref[place] = grad[start : start + DH, side : side + half].astype(BF16)
     d_bias_ref[...] = jnp.sum(d_attn_ref[...].astype(F32), axis=0, keepdims=True)
 
 
-def unspread_kernel(meta_ref, parts_ref, mine_ref, other_ref, d_one_ref, d_qk_ref, d_vp_ref):
+def unspread_kernel(meta_ref, parts_ref, qk_ref, vp_ref, d_one_ref, d_qk_ref, d_vp_ref):
     heads = parts_ref.shape[0] // 2
     rows = d_one_ref.shape[0]
     query, key, value = [], [], []
@@ -576,17 +596,40 @@
     tile = 384
     by_last = (((1,), (1,)), ((), ()))
 
-    def body(qk_ref, vp_ref):
+    def step(number, carry):
+        columns = pl.ds(pl.multiple_of(number * tile, tile), tile)
+        total = lax.dot_general(d_qk_ref[...], qk_ref[columns, :], by_last, preferred_element_type=F32)
+        total += lax.dot_general(d_vp_ref[...], vp_ref[columns, :], by_last, preferred_element_type=F32)
+        d_one_ref[:, columns] = total.astype(BF16)
+        return carry
+
+    lax.fori_loop(0, qk_ref.shape[0] // tile, step, 0)
+
+
+def weight_kernel(first_pairs, second_pairs, meta_ref, *refs):
+    operands = 1 + max(max(pair) for pair in first_pairs + second_pairs)
+    ins, outs, total = refs[:operands], refs[operands:-1], refs[-1]
+    tile = 384
+
+    def body(pairs):
         def step(number, carry):
             columns = pl.ds(pl.multiple_of(number * tile, tile), tile)
-            total = lax.dot_general(d_qk_ref[...], qk_ref[columns, :], by_last, preferred_element_type=F32)
-            total += lax.dot_general(d_vp_ref[...], vp_ref[columns, :], by_last, preferred_element_type=F32)
-            d_one_ref[:, columns] = total.astype(BF16)
+            block = jnp.zeros((tile, total.shape[1]), F32)
+            for left, right in pairs:
+                block += lax.dot_general(
+                    ins[left][:, columns], ins[right][...], (((0,), (0,)), ((), ())),
+                    preferred_element_type=F32,
+                )
+            total[columns, :] = block.astype(BF16)
             return carry
 
-        lax.fori_loop(0, qk_ref.shape[0] // tile, step, 0)
-
-    on_core(meta_ref, body, mine_ref, other_ref)
+        lax.fori_loop(0, total.shape[0] // tile, step, 0)
+
+    on_core(meta_ref, lambda pairs, _: body(pairs), first_pairs, second_pairs)
+    rows = outs[0].shape[0]
+    for step, out in enumerate(outs):
+        start = pl.multiple_of((meta_ref[3] ^ step) * rows, 16)
+        out[...] = total[pl.ds(start, rows), :]
 
 
 def first_back_kernel(
@@ -675,7 +718,7 @@
     core = my_dp % 2
     qk = w_qkv[:, :2].reshape(share_width, 2 * features)
     vp = jnp.concatenate([w_qkv[:, 2], w_proj.T], axis=1)
-    early_parts = chip_parts(pair_rows(qk, vp))
+    early_rows = pair_rows(qk, vp)
 
     cond = conditioning.astype(F32)
     gate = 1.0 / (1.0 + jnp.exp(-cond))
@@ -686,30 +729,44 @@
     mod_part = mod_part.reshape(latents * 6, features)
     mod_mine = jnp.sum(gather(mod_part, "dp", n_dp), axis=0)
     mod_mine = mod_mine + jnp.tile(b_ada.astype(F32), (latents, 1))
+    few_chips = n_dp // 2 <= 4
+    early_rows = after(early_rows, mod_mine)
+    early_parts = chip_parts(early_rows) if few_chips else [gather_chips(early_rows)]
     modulation = gather(mod_mine, "tensor", n_tensor).transpose(1, 0, 2).reshape(6 * latents, width)
 
     mod_rows, early_parts = lax.optimization_barrier((modulation, early_parts))
-    early_mine, early_other = assemble(early_parts)
+    early_parts += [swap(part, "dp", 1) for part in early_parts]
+    count = len(early_parts) // 2
     meta = jnp.stack([core, my_dp * rows, my_tensor, my_dp // 2]).astype(jnp.int32)
     meta = jnp.concatenate([meta, latent_len])
+    place_meta = meta if few_chips else meta.at[3].set(0)
     by_last = (((1,), (1,)), ((), ()))
     by_token = (((0,), (0,)), ((), ()))
-    by_rows = (((0,), (1,)), ((), ()))
     bias = jnp.concatenate([b_qv[0], jnp.zeros_like(b_qv[0]), b_qv[1], jnp.zeros_like(b_qv[0])])
-    hidden_one, d_mlp, packed = call(
-        lambda *refs: project_kernel(latents, *refs),
+    hidden_one, d_mlp, packed, full_qk, full_vp = call(
+        lambda *refs: project_kernel(latents, count, *refs),
         "project",
-        meta,
-        (tokens, cotangent, mod_rows, bias.astype(F32).reshape(2, -1), early_mine, early_other),
-        (((rows, width), BF16), ((rows, width), BF16), ((2 * heads, DH, rows * 5 // 2), BF16)),
-    )
-    full_proj = choose(core, after(early_other, packed), early_mine)[0][:, features:]
+        place_meta,
+        (*early_parts, tokens, cotangent, mod_rows, bias.astype(F32).reshape(2, -1)),
+        (((rows, width), BF16), ((rows, width), BF16), ((2 * heads, DH, rows * 5 // 2), BF16))
+        + (((width, 2 * features), BF16),) * 2,
+        [pltpu.SemaphoreType.DMA((2, count))],
+        2 * count,
+        12,
+    )
     late_rows = pair_rows(after(w_fc1, packed), after(w_fc2.T, packed))
+    hidden_other = swap(after(hidden_one, packed), "dp", 1)
     split = HeadSplit if 2 * heads == n_dp else Window
     attention = split(latent_len, rows)
-    attended = attention.forward(packed, (full_proj, late_rows))
-    attn_part = lax.dot_general(attended, full_proj, by_rows, preferred_element_type=F32).astype(BF16)
-    late_parts = chip_parts(after(late_rows, attended))
+    attended_parts = attention.forward(packed, late_rows)
+    late_mine = gather_chips(after(late_rows, attended_parts))
+    attn_part, attended = call(
+        attend_out_kernel,
+        "attend_out",
+        meta,
+        (attended_parts, full_vp),
+        (((rows, width), BF16), ((rows, 2 * features), BF16)),
+    )
     attn_parts = exchange_shares(attn_part, "tensor")
     hidden_blocks, attn_out, residual_mid = call(
         lambda *refs: middle_kernel(latents, *refs),
@@ -720,36 +777,37 @@
     )
     hidden_two = exchange(hidden_blocks, "tensor").reshape(rows, width)
 
-    late_parts = after(late_parts, hidden_two)
-    mlp_meta = meta
-    if len(late_parts) > 4:
-        late_mine, late_other = assemble(late_parts)
-        late_parts, swapped = [late_mine], [late_other]
-        mlp_meta = meta.at[3].set(0)
-    else:
-        swapped = [swap(part, "dp", 1) for part in late_parts]
-    count = len(late_parts)
+    late_other = swap(after(late_mine, hidden_two), "dp", 1)
     d_two_part, mlp_part, gelu_out, d_pre, d_bias_fc1 = call(
-        lambda *refs: mlp_kernel(count, *refs),
+        mlp_kernel,
         "mlp",
-        mlp_meta,
-        (*late_parts, *swapped, hidden_two, d_mlp, b_fc1.reshape(1, -1)),
+        meta,
+        (late_mine, late_other, hidden_two, d_mlp, b_fc1.reshape(1, -1)),
         (((rows, width), BF16), ((rows, width), BF16), ((rows, units), BF16), ((rows, units), BF16))
         + (((1, units), F32),),
         [pltpu.VMEM((width, units), BF16)] * 2
         + [pltpu.VMEM((rows, width), F32)] * 2
-        + [pltpu.SemaphoreType.DMA((2 * count,))],
-        2 * count,
+        + [pltpu.SemaphoreType.DMA((2,))],
+        2,
+        16,
     )
     d_two_parts = exchange_shares(d_two_part, "tensor")
 
-    left_mine, left_other = choose(core, hidden_two, d_mlp)
-    right_mine, right_other = choose(core, d_pre, gelu_out)
-    sent = lax.dot_general(left_other, right_other, by_token, preferred_element_type=F32)
-    kept = lax.dot_general(left_mine, right_mine, by_token, preferred_element_type=F32)
-    late_total = pair_total(kept, sent)
-    d_two_parts, late_total = lax.optimization_barrier((d_two_parts, late_total))
-    late_grads = [chip_share(late_total, step) for step in range(n_dp // 2 - 1)]
+    chips = n_dp // 2 if few_chips else 1
+    left_other = swap(choose(core, after(d_mlp, d_two_part), hidden_two)[0], "dp", 1)
+    right_other = swap(choose(core, after(gelu_out, d_two_part), d_pre)[0], "dp", 1)
+    late_blocks = call(
+        lambda *refs: weight_kernel([(0, 2), (4, 5)], [(1, 3), (4, 5)], *refs),
+        "late_weights",
+        place_meta,
+        (hidden_two, d_mlp, d_pre, gelu_out, left_other, right_other),
+        (((width // chips, units), BF16),) * chips,
+        [pltpu.VMEM((width, units), BF16)],
+        0,
+        12,
+    )
+    d_two_parts, late_blocks = lax.optimization_barrier((d_two_parts, late_blocks))
+    late_grads = sum_chips(late_blocks)
 
     d_attn_blocks, d_mid, mid_sums = call(
         lambda *refs: middle_back_kernel(latents, *refs),
@@ -764,10 +822,14 @@
         spread_kernel,
         "spread",
         meta,
-        (d_attn, full_proj),
+        (d_attn, full_vp),
         (((2 * heads, DH, rows // 2), BF16), ((1, width), F32)),
     )
     mlp_parts = parts_beside(after(mlp_part, d_spread), "tensor")
+    d_attn_other = swap(after(d_attn, d_spread), "dp", 1)
+    attended_other = swap(after(attended, d_spread), "dp", 1)
+    d_packed = attention.backward(d_spread, mlp_parts)
+    mlp_parts = after(mlp_parts, d_packed)
     result_own, last_sums = call(
         lambda *refs: result_kernel(latents, n_tensor, *refs),
         "result",
@@ -775,28 +837,32 @@
         (*mlp_parts, residual_mid, cotangent, mod_rows, b_fc2.reshape(1, -1)),
         (((share, width), BF16), ((latents, width), F32)),
     )
-    d_packed = attention.backward(d_spread, (result_own, late_grads))
-    result = gather_beside(result_own, "tensor")
     d_one_part, d_qk, d_vp = call(
         unspread_kernel,
         "unspread",
         meta,
-        (d_packed, early_mine, early_other),
+        (d_packed, full_qk, full_vp),
         (((rows, width), BF16), ((rows, 2 * features), BF16), ((rows, 2 * features), BF16)),
     )
     d_one_parts = exchange_shares(d_one_part, "tensor")
-
-    left = jnp.concatenate([hidden_one, d_attn])
-    blank = jnp.zeros((features, rows), BF16)
-    right_qk = jnp.concatenate([d_qk, jnp.zeros_like(d_qk)])
-    right_vp = jnp.concatenate([d_vp, jnp.concatenate([blank, attended]).T])
-    right_mine, right_other = choose(core, right_qk, right_vp)
-    sent = lax.dot_general(left, right_other, by_token, preferred_element_type=F32)
-    kept = lax.dot_general(left, right_mine, by_token, preferred_element_type=F32)
-    early_total = pair_total(kept, sent)
-    late_last = chip_share(after(late_total, d_one_part), n_dp // 2 - 1)
-    d_one_parts, early_total = lax.optimization_barrier((d_one_parts, early_total))
-    early_grads = [chip_share(early_total, step) for step in range(n_dp // 2)]
+    result = gather_beside(after(result_own, d_one_part), "tensor")
+
+    late_grads = late_grads[:-1] + [after(late_grads[-1], d_one_part)]
+    right_other = swap(choose(core, after(d_vp, d_one_part), d_qk)[0], "dp", 1)
+    early_blocks = call(
+        lambda *refs: weight_kernel(
+            [(0, 2), (5, 7)], [(0, 3), (1, 4), (5, 7), (6, 8)], *refs
+        ),
+        "early_weights",
+        place_meta,
+        (hidden_one, d_attn, d_qk, d_vp, attended, hidden_other, d_attn_other, right_other, attended_other),
+        (((width // chips, 2 * features), BF16),) * chips,
+        [pltpu.VMEM((width, 2 * features), BF16)],
+        0,
+        12,
+    )
+    d_one_parts, early_blocks = lax.optimization_barrier((d_one_parts, early_blocks))
+    early_grads = sum_chips(early_blocks)
 
     grad_own, d_mod_part = call(
         lambda *refs: first_back_kernel(latents, *refs),
@@ -836,7 +902,7 @@
     d_active = d_active.transpose(1, 0, 2).reshape(latents, width)
     grad_cond = d_active * (gate * (1.0 + cond * (1.0 - gate)))
 
-    grad_fc1, grad_fc2 = finish_pair(late_grads + [late_last])
+    grad_fc1, grad_fc2 = finish_pair(late_grads)
     grad_qk, grad_vp = finish_pair(after(early_grads, d_active))
     grad_qkv = jnp.concatenate([grad_qk, grad_vp[:, :features]], axis=1)
     grad_qkv = grad_qkv.reshape(share_width, 3, features)

time: 356 us -> 345 us (0.969)
  starting transfers between devices: 85.5 us -> 71 us
  matrix products: 16.2 us -> 2.18 us
  between operations: 1.72 us -> 15 us
  blocking collectives: 25.9 us -> 37.4 us
  waiting for transfers between devices: 112 us -> 105 us
  Pallas kernels: 38 us -> 44.9 us
  local copies, waits for them, and re-layouts: 54.8 us -> 48.5 us
    ppermute x32 -> x33, waiting for transfers between devices: 46.7 us -> 8.52 us  [swap(): return lax.ppermute(block, axis, route)]
    all_to_all x12 -> x11, waiting for transfers between devices: 65.4 us -> 96.4 us  [exchange(): return lax.all_to_all(blocks, axis, 0, 0, tiled=True)]
    dot_general x5 -> x0, matrix products: 14 us -> none  [the longest x1 4.66 us: local(): lax.dot_general(left_mine, right_mine, by_token, preferred_element_type=F32)]
    all_to_all x2 -> x3, blocking collectives: 25.9 us -> 37.4 us  [exchange(): return lax.all_to_all(blocks, axis, 0, 0, tiled=True)]
    unnamed x152 -> x147, local copies, waits for them, and re-layouts: 25.5 us -> 35.9 us
    all_to_all x12 -> x11, starting transfers between devices: 49.4 us -> 40.8 us  [exchange(): return lax.all_to_all(blocks, axis, 0, 0, tiled=True)]
    pallas_call x8 -> x11, Pallas kernels: 23.3 us -> 31.1 us  [call(): pl.pallas_call(body, out_shape=tuple((jax.ShapeDtypeStruct(shape, kind) f...]
    squeeze x3 -> x0, local copies, waits for them, and re-layouts: 6.09 us -> none  [chip_share(): sent = lax.dynamic_index_in_dim(blocks, chip ^ step, 0, keepdims=False)]
  transfers between devices with their start and end apart: 44 -> 45, of which waited for: 22 -> 15; matrix products, arithmetic and copies ran while one was open for 15% -> 8% of each run, Pallas kernels for 3% -> 7%
where the time goes in v5:
time: 345 us; the launch traced here: 343 us
  waiting for transfers between devices  105 us (30%)
  starting transfers between devices  71 us (21%)
  local copies, waits for them, and re-layouts  48.5 us (14%)
  Pallas kernels  44.9 us (13%)
  blocking collectives  37.4 us (11%)
  other arithmetic  19 us (6%)
  between operations  15 us (4%)
    all_to_all x11, waiting for transfers between devices, exchange(): return lax.all_to_all(blocks, axis, 0, 0, tiled=True)  96.4 us
    all_to_all x11, starting transfers between devices, exchange(): return lax.all_to_all(blocks, axis, 0, 0, tiled=True)  40.8 us
    all_to_all x3, blocking collectives, exchange(): return lax.all_to_all(blocks, axis, 0, 0, tiled=True)  37.4 us
    unnamed x147, local copies, waits for them, and re-layouts  35.9 us
    pallas_call x11, Pallas kernels, call(): pl.pallas_call(body, out_shape=tuple((jax.ShapeDtypeStruct(shape, kind) f...  31.1 us
    ppermute x33, starting transfers between devices, swap(): return lax.ppermute(block, axis, route)  30.1 us
    ppermute x33, waiting for transfers between devices, swap(): return lax.ppermute(block, axis, route)  8.52 us
    pallas_call x1, Pallas kernels, attend_backward(): pl.pallas_call(lambda *refs: backward_kernel(meta.shape[0] - 1, *refs), o...  7.58 us
  transfers between devices with their start and end apart: 45, of which 15 were waited for; matrix products, arithmetic and copies ran while one was open for 8% of the time, Pallas kernels for 7%

profile of v5, /device:TPU:0, one launch (start us, length us, event | category | flops | bytes accessed | tf_op | source)
XLA Modules:
  0.0 342.8 jit_solution(13698965280820755764)
XLA Ops:
  11.5 3.9 %collective-permute-start.3 = (bf16[288,576]{1,0:T(8,128)(2,1)S(1)}, bf16[288,576]{1,0:T(8,128)(2,1)S(1)}, u32[]{:S(2)}, u32[]{:S(2)}) collective-permute-start(bf16[288,576]{1,0:T(8,128)(2,1)S(1)} %pad_maximum_fusion.5.refs_1_), channel_id=1, source_target_pairs={{0,24},{4,28},{8,16},{12,20},{16,8},{20,12},{24,0},{28,4},{1,25},{... | collective-permute-start | bytes 995336 | tf_op jit(solution)/shard_map/ppermute | solution.py:22
  17.0 4.1 %all-to-all-start = ((f32[8,18,288]{2,1,0:T(8,128)}), f32[8,18,288]{2,1,0:T(8,128)S(1)}, u32[]{:S(2)}, u32[]{:S(2)}) async-start(f32[8,18,288]{2,1,0:T(8,128)} %broadcast_in_dim.13), calls=%async_computation | async-start | bytes 589824 | tf_op jit(solution)/shard_map/all_to_all | solution.py:26
  21.2 14.2 %all-to-all-done = f32[8,18,288]{2,1,0:T(8,128)S(1)} async-done(((f32[8,18,288]{2,1,0:T(8,128)}), f32[8,18,288]{2,1,0:T(8,128)S(1)}, u32[]{:S(2)}, u32[]{:S(2)}) %all-to-all-start) | async-done | bytes 165920 | tf_op jit(solution)/shard_map/all_to_all | solution.py:26
  35.4 11.5 %all_to_all.70 = f32[4,18,288]{2,1,0:T(8,128)S(1)} all-to-all(f32[4,18,288]{2,1,0:T(8,128)S(1)} %broadcast_in_dim.14), channel_id=1, replica_groups=mesh['dp'=8,'tensor'=4] {'tensor'}, dimensions={0} | all-to-all | bytes 165888 | tf_op jit(solution)/shard_map/all_to_all | solution.py:26
  56.4 4.9 %project.1 = (bf16[256,1152]{1,0:T(8,128)(2,1)}, bf16[256,1152]{1,0:T(8,128)(2,1)S(1)}, bf16[8,72,640]{2,1,0:T(8,128)(2,1)S(1)}, bf16[1152,576]{1,0:T(8,128)(2,1)S(1)}, bf16[1152,576]{1,0:T(8,128)(2,1)S(1)}) custom-call(s32[7]{0:T(128)S(1)} %concatenate.36.refs_0_.meta_ref, bf16[288,576]{1,0:T(8,128)(2,1)S(1)} %copy-done.10, ...), custom_call_target="tpu_custom_call" | custom-call | flops 1 | bytes 1 | tf_op jit(solution)/shard_map/project/pallas_call | solution.py:356
  63.5 3.5 %all-to-all-start.2 = ((bf16[8,72,640]{2,1,0:T(8,128)(2,1)}), bf16[8,72,640]{2,1,0:T(8,128)(2,1)S(1)}, u32[]{:S(2)}, u32[]{:S(2)}) async-start(bf16[8,72,640]{2,1,0:T(8,128)(2,1)} %copy-done.18), calls=%async_computation.2 | async-start | bytes 1474560 | tf_op jit(solution)/shard_map/all_to_all | solution.py:26
  69.2 9.9 %all-to-all-done.2.refs_1_ = bf16[8,72,640]{2,1,0:T(8,128)(2,1)S(1)} async-done(((bf16[8,72,640]{2,1,0:T(8,128)(2,1)}), bf16[8,72,640]{2,1,0:T(8,128)(2,1)S(1)}, u32[]{:S(2)}, u32[]{:S(2)}) %all-to-all-start.2) | async-done | bytes 737312 | tf_op jit(solution)/shard_map/all_to_all | solution.py:26
  79.1 6.2 %attend_forward.1 = (bf16[8,72,128]{2,1,0:T(8,128)(2,1)S(1)}, f32[8,72,128]{2,1,0:T(8,128)S(1)}, f32[8,1,128]{2,1,0:T(1,128)S(1)}) custom-call(s32[4]{0:T(128)S(1)} %pad_add_fusion.refs_0_, bf16[8,72,640]{2,1,0:T(8,128)(2,1)S(1)} %all-to-all-done.2.refs_1_), custom_call_target="tpu_custom_call" | custom-call | flops 1000000000 | bytes 4000000 | tf_op jit(solution)/shard_map/attend_forward/pallas_call | solution.py:210
  86.1 8.1 %all_to_all.71.parts_ref = bf16[8,72,128]{2,1,0:T(8,128)(2,1)S(1)} all-to-all(bf16[8,72,128]{2,1,0:T(8,128)(2,1)S(1)} %get-tuple-element.99), channel_id=1, replica_groups=mesh['dp'=8,'tensor'=4] {'dp'}, dimensions={0} | all-to-all | bytes 294912 | tf_op jit(solution)/shard_map/all_to_all | solution.py:26
  96.5 3.5 %all-to-all-start.4 = ((bf16[4,64,1152]{2,1,0:T(8,128)(2,1)}), bf16[4,64,1152]{2,1,0:T(8,128)(2,1)S(1)}, u32[]{:S(2)}, u32[]{:S(2)}) async-start(bf16[4,64,1152]{2,1,0:T(8,128)(2,1)} %bitcast.72), calls=%async_computation.4 | async-start | bytes 1179648 | tf_op jit(solution)/shard_map/all_to_all | solution.py:26
  100.0 15.9 %all-to-all-done.4.refs_1_ = bf16[4,64,1152]{2,1,0:T(8,128)(2,1)S(1)} async-done(((bf16[4,64,1152]{2,1,0:T(8,128)(2,1)}), bf16[4,64,1152]{2,1,0:T(8,128)(2,1)S(1)}, u32[]{:S(2)}, u32[]{:S(2)}) %all-to-all-start.4) | async-done | bytes 589856 | tf_op jit(solution)/shard_map/all_to_all | solution.py:26
  118.5 17.8 %all_to_all.72 = bf16[4,64,1152]{2,1,0:T(8,128)(2,1)S(1)} all-to-all(bf16[4,64,1152]{2,1,0:T(8,128)(2,1)S(1)} %get-tuple-element.103), channel_id=1, replica_groups=mesh['dp'=8,'tensor'=4] {'tensor'}, dimensions={0} | all-to-all | bytes 1179648 | tf_op jit(solution)/shard_map/all_to_all | solution.py:26
  136.3 5.1 %collective-permute-done.9.other_ref = bf16[1152,1152]{1,0:T(8,128)(2,1)S(1)} collective-permute-done((bf16[1152,1152]{1,0:T(8,128)(2,1)}, bf16[1152,1152]{1,0:T(8,128)(2,1)S(1)}, u32[]{:S(2)}, u32[]{:S(2)}) %collective-permute-start.9) | collective-permute-done | bytes 2654240 | tf_op jit(solution)/shard_map/ppermute | solution.py:22
  143.2 6.1 %mlp.1 = (bf16[256,1152]{1,0:T(8,128)(2,1)S(1)}, bf16[256,1152]{1,0:T(8,128)(2,1)S(1)}, bf16[256,1152]{1,0:T(8,128)(2,1)S(1)}, bf16[256,1152]{1,0:T(8,128)(2,1)S(1)}, f32[1,1152]{1,0:T(1,128)S(1)}) custom-call(s32[7]{0:T(128)S(1)} %concatenate.36.refs_0_.meta_ref, bf16[1152,1152]{1,0:T(8,128)(2,1)S(1)} %copy-done.4, ...), custom_call_target="tpu_custom_call" | custom-call | flops 1 | bytes 1 | tf_op jit(solution)/shard_map/mlp/pallas_call | solution.py:356
  152.6 4.2 %all-to-all-start.6 = ((bf16[4,64,1152]{2,1,0:T(8,128)(2,1)}), bf16[4,64,1152]{2,1,0:T(8,128)(2,1)}, u32[]{:S(2)}, u32[]{:S(2)}) async-start(bf16[4,64,1152]{2,1,0:T(8,128)(2,1)} %bitcast.71), calls=%async_computation.6 | async-start | bytes 1179648 | tf_op jit(solution)/shard_map/all_to_all | solution.py:26
  160.8 3.1 late_weights.1
  167.3 6.0 %all-to-all-done.6.refs_1_ = bf16[4,64,1152]{2,1,0:T(8,128)(2,1)} async-done(((bf16[4,64,1152]{2,1,0:T(8,128)(2,1)}), bf16[4,64,1152]{2,1,0:T(8,128)(2,1)}, u32[]{:S(2)}, u32[]{:S(2)}) %all-to-all-start.6) | async-done | bytes 589856 | tf_op jit(solution)/shard_map/all_to_all | solution.py:26
  180.1 4.2 %all-to-all-start.7 = ((bf16[4,64,1152]{2,1,0:T(8,128)(2,1)}), bf16[4,64,1152]{2,1,0:T(8,128)(2,1)}, u32[]{:S(2)}, u32[]{:S(2)}) async-start(bf16[4,64,1152]{2,1,0:T(8,128)(2,1)} %get-tuple-element.119), calls=%async_computation.7 | async-start | bytes 1179648 | tf_op jit(solution)/shard_map/all_to_all | solution.py:26
  184.2 15.7 %all-to-all-done.7 = bf16[4,64,1152]{2,1,0:T(8,128)(2,1)} async-done(((bf16[4,64,1152]{2,1,0:T(8,128)(2,1)}), bf16[4,64,1152]{2,1,0:T(8,128)(2,1)}, u32[]{:S(2)}, u32[]{:S(2)}) %all-to-all-start.7) | async-done | bytes 589856 | tf_op jit(solution)/shard_map/all_to_all | solution.py:26
  205.8 4.0 %all-to-all-start.8 = ((bf16[8,72,128]{2,1,0:T(8,128)(2,1)}), bf16[8,72,128]{2,1,0:T(8,128)(2,1)}, u32[]{:S(2)}, u32[]{:S(2)}) async-start(bf16[8,72,128]{2,1,0:T(8,128)(2,1)} %copy-done.41), calls=%async_computation.8 | async-start | bytes 294912 | tf_op jit(solution)/shard_map/all_to_all | solution.py:26
  213.3 2.9 collective-permute-start.12
  217.2 7.6 %attend_backward.1 = bf16[8,72,640]{2,1,0:T(8,128)(2,1)S(1)} custom-call(s32[4]{0:T(128)S(1)} %pad_add_fusion.refs_0_, bf16[8,72,640]{2,1,0:T(8,128)(2,1)S(1)} %copy-done.17, bf16[8,72,128]{2,1,0:T(8,128)(2,1)} %all-to-all-done.8.refs_2_, f32[8,72,128]{2,1,0:T(8,128)S(1)} %copy-done.54, f32[8,1,128]{2,1,0:T(1,128)S(1)} %get-tuple-element.123.refs_4_), custom_call_target="tpu_custom_call" | custom-call | flops 3000000000 | bytes 4000000 | tf_op jit(solution)/shard_map/attend_backward/pallas_call | solution.py:234
  225.7 4.2 %all-to-all-start.9 = ((bf16[8,72,640]{2,1,0:T(8,128)(2,1)}), bf16[8,72,640]{2,1,0:T(8,128)(2,1)}, u32[]{:S(2)}, u32[]{:S(2)}) async-start(bf16[8,72,640]{2,1,0:T(8,128)(2,1)} %copy-done.19), calls=%async_computation.9 | async-start | bytes 1474560 | tf_op jit(solution)/shard_map/all_to_all | solution.py:26
  230.5 21.4 %all-to-all-done.9.parts_ref = bf16[8,72,640]{2,1,0:T(8,128)(2,1)} async-done(((bf16[8,72,640]{2,1,0:T(8,128)(2,1)}), bf16[8,72,640]{2,1,0:T(8,128)(2,1)}, u32[]{:S(2)}, u32[]{:S(2)}) %all-to-all-start.9) | async-done | bytes 737312 | tf_op jit(solution)/shard_map/all_to_all | solution.py:26
  253.3 3.0 unspread.1
  257.1 3.8 %all-to-all-start.10 = ((bf16[4,64,1152]{2,1,0:T(8,128)(2,1)}), bf16[4,64,1152]{2,1,0:T(8,128)(2,1)S(1)}, u32[]{:S(2)}, u32[]{:S(2)}) async-start(bf16[4,64,1152]{2,1,0:T(8,128)(2,1)} %bitcast.69), calls=%async_computation.10 | async-start | bytes 1179648 | tf_op jit(solution)/shard_map/all_to_all | solution.py:26
  267.1 3.8 %collective-permute-start.17 = (bf16[64,1152]{1,0:T(8,128)(2,1)}, bf16[64,1152]{1,0:T(8,128)(2,1)}, u32[]{:S(2)}, u32[]{:S(2)}) collective-permute-start(bf16[64,1152]{1,0:T(8,128)(2,1)} %get-tuple-element.132), channel_id=1, source_target_pairs={{0,3},{1,2},{2,1},{3,0},{4,7},{5,6},{6,5},{7,4},{8,11},{9,10},{10,... | collective-permute-start | bytes 442376 | tf_op jit(solution)/shard_map/ppermute | solution.py:22
  273.1 3.4 early_weights.1
  278.7 4.3 %all-to-all-done.10.refs_1_ = bf16[4,64,1152]{2,1,0:T(8,128)(2,1)S(1)} async-done(((bf16[4,64,1152]{2,1,0:T(8,128)(2,1)}), bf16[4,64,1152]{2,1,0:T(8,128)(2,1)S(1)}, u32[]{:S(2)}, u32[]{:S(2)}) %all-to-all-start.10) | async-done | bytes 589856 | tf_op jit(solution)/shard_map/all_to_all | solution.py:26
  285.9 3.3 all-to-all-start.11
  291.3 3.9 %all-to-all-done.11 = f32[4,18,288]{2,1,0:T(8,128)S(1)} async-done(((f32[4,18,288]{2,1,0:T(8,128)}), f32[4,18,288]{2,1,0:T(8,128)S(1)}, u32[]{:S(2)}, u32[]{:S(2)}) %all-to-all-start.11) | async-done | bytes 82976 | tf_op jit(solution)/shard_map/all_to_all | solution.py:26
  305.2 3.5 %all-to-all-start.12 = ((f32[8,32,288]{2,1,0:T(8,128)}), f32[8,32,288]{2,1,0:T(8,128)S(1)}, u32[]{:S(2)}, u32[]{:S(2)}) async-start(f32[8,32,288]{2,1,0:T(8,128)} %broadcast_in_dim.32), calls=%async_computation.12 | async-start | bytes 786432 | tf_op jit(solution)/shard_map/all_to_all | solution.py:26
  (302 shorter events, 110.9 us)
Async XLA Ops:
  11.5 35.6 %collective-permute-start.3 = (bf16[288,576]{1,0:T(8,128)(2,1)S(1)}, bf16[288,576]{1,0:T(8,128)(2,1)S(1)}, u32[]{:S(2)}, u32[]{:S(2)}) collective-permute-start(bf16[288,576]{1,0:T(8,128)(2,1)S(1)} %pad_maximum_fusion.5.refs_1_), channel_id=1, source_target_pairs={{0,24},{4,28},{8,16},{12,20},{16,8},{20,12},{24,0},{28,4},{1,25},{... | collective-permute-start | bytes 995336 | tf_op jit(solution)/shard_map/ppermute | solution.py:22
  15.3 31.8 %collective-permute-start.2 = (bf16[288,576]{1,0:T(8,128)(2,1)S(1)}, bf16[288,576]{1,0:T(8,128)(2,1)S(1)}, u32[]{:S(2)}, u32[]{:S(2)}) collective-permute-start(bf16[288,576]{1,0:T(8,128)(2,1)S(1)} %pad_maximum_fusion.5.refs_1_), channel_id=1, source_target_pairs={{0,16},{4,20},{8,24},{12,28},{16,0},{20,4},{24,8},{28,12},{1,17},{... | collective-permute-start | bytes 995336 | tf_op jit(solution)/shard_map/ppermute | solution.py:22
  15.8 31.3 %collective-permute-start.1 = (bf16[288,576]{1,0:T(8,128)(2,1)S(1)}, bf16[288,576]{1,0:T(8,128)(2,1)S(1)}, u32[]{:S(2)}, u32[]{:S(2)}) collective-permute-start(bf16[288,576]{1,0:T(8,128)(2,1)S(1)} %pad_maximum_fusion.5.refs_1_), channel_id=1, source_target_pairs={{0,8},{4,12},{8,0},{12,4},{16,24},{20,28},{24,16},{28,20},{1,9},{5... | collective-permute-start | bytes 995336 | tf_op jit(solution)/shard_map/ppermute | solution.py:22
  17.0 18.3 %all-to-all-start = ((f32[8,18,288]{2,1,0:T(8,128)}), f32[8,18,288]{2,1,0:T(8,128)S(1)}, u32[]{:S(2)}, u32[]{:S(2)}) async-start(f32[8,18,288]{2,1,0:T(8,128)} %broadcast_in_dim.13), calls=%async_computation | async-start | bytes 589824 | tf_op jit(solution)/shard_map/all_to_all | solution.py:26
  63.5 15.6 %all-to-all-start.2 = ((bf16[8,72,640]{2,1,0:T(8,128)(2,1)}), bf16[8,72,640]{2,1,0:T(8,128)(2,1)S(1)}, u32[]{:S(2)}, u32[]{:S(2)}) async-start(bf16[8,72,640]{2,1,0:T(8,128)(2,1)} %copy-done.18), calls=%async_computation.2 | async-start | bytes 1474560 | tf_op jit(solution)/shard_map/all_to_all | solution.py:26
  67.1 69.2 %all-gather.2.cloned.1.call-start = ((), (), s32[]{:S(2)}) async-start(), calls=%async_computation.14 | async-start | bytes 3317760 | tf_op jit(solution)/shard_map/all_gather | solution.py:55
  96.5 19.5 %all-to-all-start.4 = ((bf16[4,64,1152]{2,1,0:T(8,128)(2,1)}), bf16[4,64,1152]{2,1,0:T(8,128)(2,1)S(1)}, u32[]{:S(2)}, u32[]{:S(2)}) async-start(bf16[4,64,1152]{2,1,0:T(8,128)(2,1)} %bitcast.72), calls=%async_computation.4 | async-start | bytes 1179648 | tf_op jit(solution)/shard_map/all_to_all | solution.py:26
  152.6 20.7 %all-to-all-start.6 = ((bf16[4,64,1152]{2,1,0:T(8,128)(2,1)}), bf16[4,64,1152]{2,1,0:T(8,128)(2,1)}, u32[]{:S(2)}, u32[]{:S(2)}) async-start(bf16[4,64,1152]{2,1,0:T(8,128)(2,1)} %bitcast.71), calls=%async_computation.6 | async-start | bytes 1179648 | tf_op jit(solution)/shard_map/all_to_all | solution.py:26
  180.1 19.9 %all-to-all-start.7 = ((bf16[4,64,1152]{2,1,0:T(8,128)(2,1)}), bf16[4,64,1152]{2,1,0:T(8,128)(2,1)}, u32[]{:S(2)}, u32[]{:S(2)}) async-start(bf16[4,64,1152]{2,1,0:T(8,128)(2,1)} %get-tuple-element.119), calls=%async_computation.7 | async-start | bytes 1179648 | tf_op jit(solution)/shard_map/all_to_all | solution.py:26
  205.8 10.5 %all-to-all-start.8 = ((bf16[8,72,128]{2,1,0:T(8,128)(2,1)}), bf16[8,72,128]{2,1,0:T(8,128)(2,1)}, u32[]{:S(2)}, u32[]{:S(2)}) async-start(bf16[8,72,128]{2,1,0:T(8,128)(2,1)} %copy-done.41), calls=%async_computation.8 | async-start | bytes 294912 | tf_op jit(solution)/shard_map/all_to_all | solution.py:26
  209.8 51.1 %collective-permute-start.29 = (bf16[288,1152]{1,0:T(8,128)(2,1)}, bf16[288,1152]{1,0:T(8,128)(2,1)}, u32[]{:S(2)}, u32[]{:S(2)}) collective-permute-start(bf16[288,1152]{1,0:T(8,128)(2,1)} %copy-done.45), channel_id=1, source_target_pairs={{0,8},{4,12},{8,0},{12,4},{16,24},{20,28},{24,16},{28,20},{1,9},{5... | collective-permute-start | bytes 1990664 | tf_op jit(solution)/shard_map/ppermute | solution.py:22
  211.7 49.2 %collective-permute-start.30 = (bf16[288,1152]{1,0:T(8,128)(2,1)}, bf16[288,1152]{1,0:T(8,128)(2,1)}, u32[]{:S(2)}, u32[]{:S(2)}) collective-permute-start(bf16[288,1152]{1,0:T(8,128)(2,1)} %copy-done.44), channel_id=1, source_target_pairs={{0,16},{4,20},{8,24},{12,28},{16,0},{20,4},{24,8},{28,12},{1,17},{... | collective-permute-start | bytes 1990664 | tf_op jit(solution)/shard_map/ppermute | solution.py:22
  213.2 47.7 %collective-permute-start.31 = (bf16[288,1152]{1,0:T(8,128)(2,1)}, bf16[288,1152]{1,0:T(8,128)(2,1)}, u32[]{:S(2)}, u32[]{:S(2)}) collective-permute-start(bf16[288,1152]{1,0:T(8,128)(2,1)} %copy-done.46), channel_id=1, source_target_pairs={{0,24},{4,28},{8,16},{12,20},{16,8},{20,12},{24,0},{28,4},{1,25},{... | collective-permute-start | bytes 1990664 | tf_op jit(solution)/shard_map/ppermute | solution.py:22
  213.3 12.4 %collective-permute-start.13 = (bf16[64,1152]{1,0:T(8,128)(2,1)}, bf16[64,1152]{1,0:T(8,128)(2,1)}, u32[]{:S(2)}, u32[]{:S(2)}) collective-permute-start(bf16[64,1152]{1,0:T(8,128)(2,1)} %get-tuple-element.264), channel_id=1, source_target_pairs={{0,2},{1,3},{2,0},{3,1},{4,6},{5,7},{6,4},{7,5},{8,10},{9,11},{10,... | collective-permute-start | bytes 442376 | tf_op jit(solution)/shard_map/ppermute | solution.py:22
  213.3 12.4 %collective-permute-start.12 = (bf16[64,1152]{1,0:T(8,128)(2,1)}, bf16[64,1152]{1,0:T(8,128)(2,1)}, u32[]{:S(2)}, u32[]{:S(2)}) collective-permute-start(bf16[64,1152]{1,0:T(8,128)(2,1)} %get-tuple-element.265), channel_id=1, source_target_pairs={{0,1},{1,0},{2,3},{3,2},{4,5},{5,4},{6,7},{7,6},{8,9},{9,8},{10,11... | collective-permute-start | bytes 442376 | tf_op jit(solution)/shard_map/ppermute | solution.py:22
  225.7 26.2 %all-to-all-start.9 = ((bf16[8,72,640]{2,1,0:T(8,128)(2,1)}), bf16[8,72,640]{2,1,0:T(8,128)(2,1)}, u32[]{:S(2)}, u32[]{:S(2)}) async-start(bf16[8,72,640]{2,1,0:T(8,128)(2,1)} %copy-done.19), calls=%async_computation.9 | async-start | bytes 1474560 | tf_op jit(solution)/shard_map/all_to_all | solution.py:26
  229.9 37.2 %collective-permute-start.18 = (bf16[256,1152]{1,0:T(8,128)(2,1)}, bf16[256,1152]{1,0:T(8,128)(2,1)}, u32[]{:S(2)}, u32[]{:S(2)}) collective-permute-start(bf16[256,1152]{1,0:T(8,128)(2,1)} %get-tuple-element.137.refs_1_), channel_id=1, source_target_pairs={{0,4},{4,0},{8,12},{12,8},{16,20},{20,16},{24,28},{28,24},{1,5},{5... | collective-permute-start | bytes 1769480 | tf_op jit(solution)/shard_map/ppermute | solution.py:22
  230.3 40.6 %collective-permute-start.21 = (bf16[256,576]{1,0:T(8,128)(2,1)}, bf16[256,576]{1,0:T(8,128)(2,1)}, u32[]{:S(2)}, u32[]{:S(2)}) collective-permute-start(bf16[256,576]{1,0:T(8,128)(2,1)} %get-tuple-element.140.refs_5_), channel_id=1, source_target_pairs={{0,4},{4,0},{8,12},{12,8},{16,20},{20,16},{24,28},{28,24},{1,5},{5... | collective-permute-start | bytes 884744 | tf_op jit(solution)/shard_map/ppermute | solution.py:22
  257.1 25.9 %all-to-all-start.10 = ((bf16[4,64,1152]{2,1,0:T(8,128)(2,1)}), bf16[4,64,1152]{2,1,0:T(8,128)(2,1)S(1)}, u32[]{:S(2)}, u32[]{:S(2)}) async-start(bf16[4,64,1152]{2,1,0:T(8,128)(2,1)} %bitcast.69), calls=%async_computation.10 | async-start | bytes 1179648 | tf_op jit(solution)/shard_map/all_to_all | solution.py:26
  260.9 10.0 %collective-permute-start.19 = (bf16[256,1152]{1,0:T(8,128)(2,1)}, bf16[256,1152]{1,0:T(8,128)(2,1)S(1)}, u32[]{:S(2)}, u32[]{:S(2)}) collective-permute-start(bf16[256,1152]{1,0:T(8,128)(2,1)} %bitcast.12.d_attn_ref.refs_2_), channel_id=1, source_target_pairs={{0,4},{4,0},{8,12},{12,8},{16,20},{20,16},{24,28},{28,24},{1,5},{5... | collective-permute-start | bytes 1769480 | tf_op jit(solution)/shard_map/ppermute | solution.py:22
  263.7 35.9 %collective-permute-start.32 = (f32[144,1152]{1,0:T(8,128)}, f32[144,1152]{1,0:T(8,128)}, u32[]{:S(2)}, u32[]{:S(2)}) collective-permute-start(f32[144,1152]{1,0:T(8,128)} %slice_select_fusion), channel_id=1, source_target_pairs={{0,4},{4,0},{8,12},{12,8},{16,20},{20,16},{24,28},{28,24},{1,5},{5... | collective-permute-start | bytes 1990664 | tf_op jit(solution)/shard_map/ppermute | solution.py:22
  267.1 22.1 %collective-permute-start.17 = (bf16[64,1152]{1,0:T(8,128)(2,1)}, bf16[64,1152]{1,0:T(8,128)(2,1)}, u32[]{:S(2)}, u32[]{:S(2)}) collective-permute-start(bf16[64,1152]{1,0:T(8,128)(2,1)} %get-tuple-element.132), channel_id=1, source_target_pairs={{0,3},{1,2},{2,1},{3,0},{4,7},{5,6},{6,5},{7,4},{8,11},{9,10},{10,... | collective-permute-start | bytes 442376 | tf_op jit(solution)/shard_map/ppermute | solution.py:22
  270.9 18.3 %collective-permute-start.16 = (bf16[64,1152]{1,0:T(8,128)(2,1)}, bf16[64,1152]{1,0:T(8,128)(2,1)}, u32[]{:S(2)}, u32[]{:S(2)}) collective-permute-start(bf16[64,1152]{1,0:T(8,128)(2,1)} %get-tuple-element.132), channel_id=1, source_target_pairs={{0,2},{1,3},{2,0},{3,1},{4,6},{5,7},{6,4},{7,5},{8,10},{9,11},{10,... | collective-permute-start | bytes 442376 | tf_op jit(solution)/shard_map/ppermute | solution.py:22
  270.9 18.3 %collective-permute-start.15 = (bf16[64,1152]{1,0:T(8,128)(2,1)}, bf16[64,1152]{1,0:T(8,128)(2,1)}, u32[]{:S(2)}, u32[]{:S(2)}) collective-permute-start(bf16[64,1152]{1,0:T(8,128)(2,1)} %get-tuple-element.132), channel_id=1, source_target_pairs={{0,1},{1,0},{2,3},{3,2},{4,5},{5,4},{6,7},{7,6},{8,9},{9,8},{10,11... | collective-permute-start | bytes 442376 | tf_op jit(solution)/shard_map/ppermute | solution.py:22
  295.2 13.5 %collective-permute-start.24 = (bf16[64,1152]{1,0:T(8,128)(2,1)S(1)}, bf16[64,1152]{1,0:T(8,128)(2,1)S(1)}, u32[]{:S(2)}, u32[]{:S(2)}) collective-permute-start(bf16[64,1152]{1,0:T(8,128)(2,1)S(1)} %get-tuple-element.151), channel_id=1, source_target_pairs={{0,3},{1,2},{2,1},{3,0},{4,7},{5,6},{6,5},{7,4},{8,11},{9,10},{10,... | collective-permute-start | bytes 442376 | tf_op jit(solution)/shard_map/ppermute | solution.py:22
  297.1 14.4 %collective-permute-start.23 = (bf16[64,1152]{1,0:T(8,128)(2,1)S(1)}, bf16[64,1152]{1,0:T(8,128)(2,1)S(1)}, u32[]{:S(2)}, u32[]{:S(2)}) collective-permute-start(bf16[64,1152]{1,0:T(8,128)(2,1)S(1)} %get-tuple-element.151), channel_id=1, source_target_pairs={{0,2},{1,3},{2,0},{3,1},{4,6},{5,7},{6,4},{7,5},{8,10},{9,11},{10,... | collective-permute-start | bytes 442376 | tf_op jit(solution)/shard_map/ppermute | solution.py:22
  298.2 13.4 %collective-permute-start.22 = (bf16[64,1152]{1,0:T(8,128)(2,1)S(1)}, bf16[64,1152]{1,0:T(8,128)(2,1)}, u32[]{:S(2)}, u32[]{:S(2)}) collective-permute-start(bf16[64,1152]{1,0:T(8,128)(2,1)S(1)} %get-tuple-element.151), channel_id=1, source_target_pairs={{0,1},{1,0},{2,3},{3,2},{4,5},{5,4},{6,7},{7,6},{8,9},{9,8},{10,11... | collective-permute-start | bytes 442376 | tf_op jit(solution)/shard_map/ppermute | solution.py:22
  302.0 28.5 %collective-permute-start.25 = (bf16[288,576]{1,0:T(8,128)(2,1)S(1)}, bf16[288,576]{1,0:T(8,128)(2,1)S(1)}, u32[]{:S(2)}, u32[]{:S(2)}) collective-permute-start(bf16[288,576]{1,0:T(8,128)(2,1)S(1)} %copy-done.52), channel_id=1, source_target_pairs={{0,8},{4,12},{8,0},{12,4},{16,24},{20,28},{24,16},{28,20},{1,9},{5... | collective-permute-start | bytes 995336 | tf_op jit(solution)/shard_map/ppermute | solution.py:22
  303.9 26.6 %collective-permute-start.26 = (bf16[288,576]{1,0:T(8,128)(2,1)S(1)}, bf16[288,576]{1,0:T(8,128)(2,1)}, u32[]{:S(2)}, u32[]{:S(2)}) collective-permute-start(bf16[288,576]{1,0:T(8,128)(2,1)S(1)} %copy-done.50), channel_id=1, source_target_pairs={{0,16},{4,20},{8,24},{12,28},{16,0},{20,4},{24,8},{28,12},{1,17},{... | collective-permute-start | bytes 995336 | tf_op jit(solution)/shard_map/ppermute | solution.py:22
  305.2 12.2 %all-to-all-start.12 = ((f32[8,32,288]{2,1,0:T(8,128)}), f32[8,32,288]{2,1,0:T(8,128)S(1)}, u32[]{:S(2)}, u32[]{:S(2)}) async-start(f32[8,32,288]{2,1,0:T(8,128)} %broadcast_in_dim.32), calls=%async_computation.12 | async-start | bytes 786432 | tf_op jit(solution)/shard_map/all_to_all | solution.py:26
  308.7 21.8 %collective-permute-start.27 = (bf16[288,576]{1,0:T(8,128)(2,1)S(1)}, bf16[288,576]{1,0:T(8,128)(2,1)}, u32[]{:S(2)}, u32[]{:S(2)}) collective-permute-start(bf16[288,576]{1,0:T(8,128)(2,1)S(1)} %copy-done.48), channel_id=1, source_target_pairs={{0,24},{4,28},{8,16},{12,20},{16,8},{20,12},{24,0},{28,4},{1,25},{... | collective-permute-start | bytes 995336 | tf_op jit(solution)/shard_map/ppermute | solution.py:22
  318.8 10.1 %all-to-all-start.13 = ((f32[32,1,432]{2,1,0:T(1,128)}), f32[32,1,432]{2,1,0:T(1,128)S(1)}, u32[]{:S(2)}, u32[]{:S(2)}) async-start(f32[32,1,432]{2,1,0:T(1,128)} %reshape.136), calls=%async_computation.13 | async-start | bytes 131072 | tf_op jit(solution)/shard_map/all_to_all | solution.py:26
  (84 other events, 448.9 us)
Sparse Core Ops, SparseCore 0:
  94.3 36.6 all-gather.1

commit v6 on v5

--- a/solution.py
+++ b/solution.py
@@ -12,7 +12,7 @@
 NORM_EPS = 1e-06
 NEGATIVE = -1e30
 SCALE = 1.0 / math.sqrt(DH)
-MIB = 1024 * 1024
+VMEM_BYTES = 58 * 1024 * 1024
 BF16 = jnp.bfloat16
 F32 = jnp.float32
 
@@ -30,8 +30,16 @@
     return exchange(jnp.broadcast_to(block[None], (count,) + block.shape), axis)
 
 
-def after(value, *others):
-    return lax.optimization_barrier((value,) + others)[0]
+def gate(value, *others):
+    return pl.pallas_call(
+        lambda *refs: None,
+        out_shape=jax.ShapeDtypeStruct(value.shape, value.dtype),
+        in_specs=[pl.BlockSpec(memory_space=pl.ANY)] * (1 + len(others)),
+        out_specs=pl.BlockSpec(memory_space=pl.ANY),
+        input_output_aliases={0: 0},
+        cost_estimate=pl.CostEstimate(flops=1, bytes_accessed=1, transcendentals=0),
+        name="gate",
+    )(value, *others)
 
 
 def choose(core, first, second):
@@ -71,16 +79,6 @@
     half = rows.shape[0] // 2
     keep, send = choose(core, rows[:half], rows[half:])
     return choose(core, keep, swap(send, "dp", 1))
-
-
-def parts_beside(partial, axis):
-    count, me = lax.axis_size(axis), lax.axis_index(axis)
-    blocks = partial.reshape((count, partial.shape[0] // count) + partial.shape[1:])
-    parts = [lax.dynamic_index_in_dim(blocks, me, 0, keepdims=False)]
-    for bits in range(1, count):
-        sent = lax.dynamic_index_in_dim(blocks, me ^ bits, 0, keepdims=False)
-        parts.append(swap(sent, axis, bits))
-    return parts
 
 
 def gather_beside(share, axis):
@@ -223,7 +221,7 @@
             pltpu.VMEM((blocks, 256, DH), BF16),
             pltpu.VMEM((blocks, 256, 256), F32),
         ],
-        compiler_params=pltpu.CompilerParams(vmem_limit_bytes=10 * MIB),
+        compiler_params=pltpu.CompilerParams(vmem_limit_bytes=VMEM_BYTES),
         cost_estimate=pl.CostEstimate(flops=10**9, bytes_accessed=4 * 10**6, transcendentals=10**6),
         name="attend_forward",
     )(meta, packed)
@@ -243,7 +241,7 @@
             pltpu.VMEM((blocks, DH, 256), F32),
             pltpu.VMEM((blocks, DH, 256), F32),
         ],
-        compiler_params=pltpu.CompilerParams(vmem_limit_bytes=10 * MIB),
+        compiler_params=pltpu.CompilerParams(vmem_limit_bytes=VMEM_BYTES),
         cost_estimate=pl.CostEstimate(flops=3 * 10**9, bytes_accessed=4 * 10**6, transcendentals=10**6),
         name="attend_backward",
     )(meta, packed, grad, exact, log_total)
@@ -254,15 +252,15 @@
         self.rows = rows
         self.meta = jnp.concatenate([lax.axis_index("dp").astype(jnp.int32)[None] % 2, latent_len])
 
-    def forward(self, packed, beside):
-        self.packed = after(exchange(packed, "dp"), beside)
+    def forward(self, packed):
+        self.packed = exchange(packed, "dp")
         out, self.exact, self.log_total = attend_forward(self.meta, self.packed)
         return exchange(out, "dp")
 
-    def backward(self, grad, beside):
+    def backward(self, grad, due):
         grad = exchange(grad, "dp")
         out = attend_backward(self.meta, self.packed, grad, self.exact, self.log_total)
-        return exchange(after(out, beside), "dp")
+        return exchange(gate(out, *due), "dp")
 
 
 class Window:
@@ -288,7 +286,7 @@
         raw = jnp.einsum("eq,ek->qk", query, key, preferred_element_type=F32) * SCALE
         return jnp.where(self.allowed, raw, NEGATIVE)
 
-    def forward(self, packed, beside):
+    def forward(self, packed):
         rows = self.rows
         split = packed.reshape(-1, 2, DH, rows * 5 // 2)
         query = jnp.concatenate([split[:, 0, :, 2 * rows :], split[:, 1, :, 2 * rows :]], axis=2)
@@ -315,7 +313,7 @@
         out = out.reshape(-1, DH, 2, rows // 2).transpose(0, 2, 1, 3)
         return out.reshape(-1, DH, rows // 2)
 
-    def backward(self, grad, beside):
+    def backward(self, grad, due):
         rows, reach = self.rows, self.reach
         halves = grad.reshape(-1, 2, DH, rows // 2)
         grads = jnp.concatenate([halves[:, 0], halves[:, 1]], axis=2)
@@ -352,19 +350,25 @@
     return [pl.BlockSpec(memory_space=pltpu.VMEM)] * count
 
 
-def call(body, name, meta, arrays, outs, scratch=(), anywhere=0, limit=8):
+def call(body, name, meta, arrays, outs, scratch=(), anywhere=0, due=()):
+    count = 1 + len(arrays)
+
+    def kernel(*refs):
+        body(*refs[:count], *refs[count + len(due) :])
+
     return pl.pallas_call(
-        body,
+        kernel,
         out_shape=tuple(jax.ShapeDtypeStruct(shape, kind) for shape, kind in outs),
         in_specs=[pl.BlockSpec(memory_space=pltpu.SMEM)]
         + [pl.BlockSpec(memory_space=pl.ANY)] * anywhere
-        + vmem(len(arrays) - anywhere),
+        + vmem(len(arrays) - anywhere)
+        + [pl.BlockSpec(memory_space=pl.ANY)] * len(due),
         out_specs=tuple(vmem(len(outs))),
         scratch_shapes=list(scratch),
-        compiler_params=pltpu.CompilerParams(vmem_limit_bytes=limit * MIB),
+        compiler_params=pltpu.CompilerParams(vmem_limit_bytes=VMEM_BYTES),
         cost_estimate=pl.CostEstimate(flops=1, bytes_accessed=1, transcendentals=0),
         name=name,
-    )(meta, *arrays)
+    )(meta, *arrays, *due)
 
 
 def row_masks(meta_ref, latents, first, rows):
@@ -492,22 +496,13 @@
         sent_ref[part] = hidden.astype(BF16)
 
 
-def mlp_kernel(
-    meta_ref, mine_ref, other_ref, hidden_ref, d_mlp_ref, bias_ref,
-    d_two_ref, mlp_ref, gelu_ref, d_pre_ref, d_bias_ref,
-    fc1_ref, fc2_ref, d_two_sum, mlp_sum, sems,
-):
-    def load(first, second):
-        copies = [
-            pltpu.make_async_copy(first, fc1_ref, sems.at[0]),
-            pltpu.make_async_copy(second, fc2_ref, sems.at[1]),
-        ]
-        for copy in copies:
-            copy.start()
-        for copy in copies:
-            copy.wait()
-
-    on_core(meta_ref, load, mine_ref, other_ref)
+def mlp_kernel(count, meta_ref, *refs):
+    mine, other = refs[:count], refs[count : 2 * count]
+    hidden_ref, d_mlp_ref, bias_ref = refs[2 * count : 2 * count + 3]
+    d_two_ref, gelu_ref, d_pre_ref, d_bias_ref = refs[2 * count + 3 : 2 * count + 7]
+    mlp_refs = refs[2 * count + 7 : -5]
+    fc1_ref, fc2_ref, d_two_sum, mlp_sum, sems = refs[-5:]
+    place_pair(meta_ref, mine, other, fc1_ref, fc2_ref, sems)
     d_two_sum[...] = jnp.zeros_like(d_two_sum)
     mlp_sum[...] = jnp.zeros_like(mlp_sum)
     tile = 384
@@ -530,7 +525,10 @@
 
     lax.fori_loop(0, fc1_ref.shape[1] // tile, step, 0)
     d_two_ref[...] = d_two_sum[...].astype(BF16)
-    mlp_ref[...] = mlp_sum[...].astype(BF16)
+    share = mlp_refs[0].shape[0]
+    for step, mlp_ref in enumerate(mlp_refs):
+        start = pl.multiple_of((meta_ref[2] ^ step) * share, share)
+        mlp_ref[...] = mlp_sum[pl.ds(start, share), :].astype(BF16)
 
 
 def middle_back_kernel(
@@ -721,20 +719,20 @@
     early_rows = pair_rows(qk, vp)
 
     cond = conditioning.astype(F32)
-    gate = 1.0 / (1.0 + jnp.exp(-cond))
-    activated = (cond * gate).astype(BF16)
+    sigmoid = 1.0 / (1.0 + jnp.exp(-cond))
+    activated = (cond * sigmoid).astype(BF16)
     own_activated = lax.dynamic_slice_in_dim(activated, my_dp * share_width, share_width, 1)
     flat_ada = w_ada.reshape(share_width, 6 * features)
     mod_part = jnp.dot(own_activated, flat_ada, preferred_element_type=F32)
     mod_part = mod_part.reshape(latents * 6, features)
     mod_mine = jnp.sum(gather(mod_part, "dp", n_dp), axis=0)
     mod_mine = mod_mine + jnp.tile(b_ada.astype(F32), (latents, 1))
-    few_chips = n_dp // 2 <= 4
-    early_rows = after(early_rows, mod_mine)
+    few_chips = n_dp // 2 == 4
+    early_rows = gate(early_rows, mod_mine)
     early_parts = chip_parts(early_rows) if few_chips else [gather_chips(early_rows)]
     modulation = gather(mod_mine, "tensor", n_tensor).transpose(1, 0, 2).reshape(6 * latents, width)
 
-    mod_rows, early_parts = lax.optimization_barrier((modulation, early_parts))
+    mod_rows = modulation
     early_parts += [swap(part, "dp", 1) for part in early_parts]
     count = len(early_parts) // 2
     meta = jnp.stack([core, my_dp * rows, my_tensor, my_dp // 2]).astype(jnp.int32)
@@ -752,14 +750,14 @@
         + (((width, 2 * features), BF16),) * 2,
         [pltpu.SemaphoreType.DMA((2, count))],
         2 * count,
-        12,
-    )
-    late_rows = pair_rows(after(w_fc1, packed), after(w_fc2.T, packed))
-    hidden_other = swap(after(hidden_one, packed), "dp", 1)
+    )
+    late_rows = pair_rows(w_fc1, w_fc2.T)
+    hidden_other = swap(hidden_one, "dp", 1)
     split = HeadSplit if 2 * heads == n_dp else Window
     attention = split(latent_len, rows)
-    attended_parts = attention.forward(packed, late_rows)
-    late_mine = gather_chips(after(late_rows, attended_parts))
+    attended_parts = attention.forward(packed)
+    late_rows = gate(late_rows, attended_parts)
+    late_parts = chip_parts(late_rows)[:-1] if few_chips else [gather_chips(late_rows)]
     attn_part, attended = call(
         attend_out_kernel,
         "attend_out",
@@ -774,28 +772,31 @@
         meta,
         (attn_parts, tokens, mod_rows, b_proj.reshape(1, -1)),
         (((n_tensor, share, width), BF16), ((share, width), F32), ((share, width), F32)),
+        due=late_parts[1:],
     )
     hidden_two = exchange(hidden_blocks, "tensor").reshape(rows, width)
-
-    late_other = swap(after(late_mine, hidden_two), "dp", 1)
-    d_two_part, mlp_part, gelu_out, d_pre, d_bias_fc1 = call(
-        mlp_kernel,
+    if few_chips:
+        last_part = swap(gate(late_rows, attn_out), "dp", n_dp - 2)
+        late_parts.append(gate(last_part, hidden_two))
+    late_other = [swap(part, "dp", 1) for part in late_parts]
+
+    d_two_part, gelu_out, d_pre, d_bias_fc1, *mlp_blocks = call(
+        lambda *refs: mlp_kernel(count, *refs),
         "mlp",
-        meta,
-        (late_mine, late_other, hidden_two, d_mlp, b_fc1.reshape(1, -1)),
-        (((rows, width), BF16), ((rows, width), BF16), ((rows, units), BF16), ((rows, units), BF16))
-        + (((1, units), F32),),
+        place_meta,
+        (*late_parts, *late_other, hidden_two, d_mlp, b_fc1.reshape(1, -1)),
+        (((rows, width), BF16), ((rows, units), BF16), ((rows, units), BF16), ((1, units), F32))
+        + (((share, width), BF16),) * n_tensor,
         [pltpu.VMEM((width, units), BF16)] * 2
         + [pltpu.VMEM((rows, width), F32)] * 2
-        + [pltpu.SemaphoreType.DMA((2,))],
-        2,
-        16,
+        + [pltpu.SemaphoreType.DMA((2, count))],
+        2 * count,
     )
     d_two_parts = exchange_shares(d_two_part, "tensor")
 
     chips = n_dp // 2 if few_chips else 1
-    left_other = swap(choose(core, after(d_mlp, d_two_part), hidden_two)[0], "dp", 1)
-    right_other = swap(choose(core, after(gelu_out, d_two_part), d_pre)[0], "dp", 1)
+    left_other = swap(choose(core, d_mlp, hidden_two)[0], "dp", 1)
+    right_other = swap(choose(core, gelu_out, d_pre)[0], "dp", 1)
     late_blocks = call(
         lambda *refs: weight_kernel([(0, 2), (4, 5)], [(1, 3), (4, 5)], *refs),
         "late_weights",
@@ -803,11 +804,8 @@
         (hidden_two, d_mlp, d_pre, gelu_out, left_other, right_other),
         (((width // chips, units), BF16),) * chips,
         [pltpu.VMEM((width, units), BF16)],
-        0,
-        12,
-    )
-    d_two_parts, late_blocks = lax.optimization_barrier((d_two_parts, late_blocks))
-    late_grads = sum_chips(late_blocks)
+    )
+    late_grads = sum_chips(late_blocks[:-1]) if few_chips else sum_chips(late_blocks)
 
     d_attn_blocks, d_mid, mid_sums = call(
         lambda *refs: middle_back_kernel(latents, *refs),
@@ -815,6 +813,7 @@
         meta,
         (d_two_parts, residual_mid, attn_out, cotangent, mod_rows),
         (((n_tensor, share, width), BF16), ((share, width), F32), ((3 * latents, width), F32)),
+        due=late_blocks,
     )
     d_attn = exchange(d_attn_blocks, "tensor").reshape(rows, width)
 
@@ -824,12 +823,16 @@
         meta,
         (d_attn, full_vp),
         (((2 * heads, DH, rows // 2), BF16), ((1, width), F32)),
-    )
-    mlp_parts = parts_beside(after(mlp_part, d_spread), "tensor")
-    d_attn_other = swap(after(d_attn, d_spread), "dp", 1)
-    attended_other = swap(after(attended, d_spread), "dp", 1)
-    d_packed = attention.backward(d_spread, mlp_parts)
-    mlp_parts = after(mlp_parts, d_packed)
+        due=late_grads[1:],
+    )
+    mlp_parts = mlp_blocks[:1] + [
+        swap(gate(block, d_spread), "tensor", step)
+        for step, block in enumerate(mlp_blocks)
+        if step
+    ]
+    d_attn_other = swap(d_attn, "dp", 1)
+    attended_other = swap(attended, "dp", 1)
+    d_packed = attention.backward(d_spread, mlp_parts[1:])
     result_own, last_sums = call(
         lambda *refs: result_kernel(latents, n_tensor, *refs),
         "result",
@@ -845,10 +848,11 @@
         (((rows, width), BF16), ((rows, 2 * features), BF16), ((rows, 2 * features), BF16)),
     )
     d_one_parts = exchange_shares(d_one_part, "tensor")
-    result = gather_beside(after(result_own, d_one_part), "tensor")
-
-    late_grads = late_grads[:-1] + [after(late_grads[-1], d_one_part)]
-    right_other = swap(choose(core, after(d_vp, d_one_part), d_qk)[0], "dp", 1)
+    result = gather_beside(result_own, "tensor")
+
+    if few_chips:
+        late_grads.append(swap(gate(late_blocks[-1], d_one_part), "dp", n_dp - 2))
+    right_other = swap(choose(core, d_vp, d_qk)[0], "dp", 1)
     early_blocks = call(
         lambda *refs: weight_kernel(
             [(0, 2), (5, 7)], [(0, 3), (1, 4), (5, 7), (6, 8)], *refs
@@ -858,10 +862,7 @@
         (hidden_one, d_attn, d_qk, d_vp, attended, hidden_other, d_attn_other, right_other, attended_other),
         (((width // chips, 2 * features), BF16),) * chips,
         [pltpu.VMEM((width, 2 * features), BF16)],
-        0,
-        12,
-    )
-    d_one_parts, early_blocks = lax.optimization_barrier((d_one_parts, early_blocks))
+    )
     early_grads = sum_chips(early_blocks)
 
     grad_own, d_mod_part = call(
@@ -871,6 +872,7 @@
         (d_one_parts, tokens, d_mid, mod_rows, mid_sums, last_sums),
         (((share, width), BF16), ((n_tensor, 6 * latents, features), F32)),
         [pltpu.VMEM((2 * latents, width), F32)],
+        due=early_blocks,
     )
     bias_part = jnp.concatenate(
         [
@@ -883,7 +885,7 @@
     )
     bias_rows = bias_part.reshape(-1, features)
     d_mod_mine = jnp.sum(exchange(d_mod_part, "tensor"), axis=0)
-    grad_tokens = gather_beside(after(grad_own, d_mod_mine), "tensor").astype(F32)
+    grad_tokens = gather_beside(gate(grad_own, d_mod_mine), "tensor").astype(F32)
     sums = jnp.sum(gather(jnp.concatenate([d_mod_mine, bias_rows]), "dp", n_dp), axis=0)
     d_mod = sums[: 6 * latents].reshape(latents, 6 * features)
     bias_total = sums[6 * latents :].reshape(-1)
@@ -897,13 +899,14 @@
         jnp.concatenate([high, low]), flat_ada, by_last, preferred_element_type=F32
     )
     d_active = d_active[:latents] + d_active[latents:]
+    d_active = gate(d_active, *early_grads[1:]) if few_chips else d_active
     d_active = gather(d_active, ("dp", "tensor"), n_dp * n_tensor)
     d_active = jnp.sum(d_active.reshape(n_dp, n_tensor, latents, share_width), axis=1)
     d_active = d_active.transpose(1, 0, 2).reshape(latents, width)
-    grad_cond = d_active * (gate * (1.0 + cond * (1.0 - gate)))
+    grad_cond = d_active * (sigmoid * (1.0 + cond * (1.0 - sigmoid)))
 
     grad_fc1, grad_fc2 = finish_pair(late_grads)
-    grad_qk, grad_vp = finish_pair(after(early_grads, d_active))
+    grad_qk, grad_vp = finish_pair(early_grads)
     grad_qkv = jnp.concatenate([grad_qk, grad_vp[:, :features]], axis=1)
     grad_qkv = grad_qkv.reshape(share_width, 3, features)
 

time: 345 us -> 352 us (1.020)
  blocking collectives: 37.4 us -> 0 us
  waiting for transfers between devices: 105 us -> 140 us
  Pallas kernels: 44.9 us -> 64.4 us
  local copies, waits for them, and re-layouts: 48.5 us -> 33.2 us
  starting transfers between devices: 71 us -> 85.6 us
  between operations: 15 us -> 1.44 us
  other arithmetic: 19 us -> 23.9 us
    ppermute x33 -> x39, waiting for transfers between devices: 8.52 us -> 83.4 us  [swap(): return lax.ppermute(block, axis, route)]
    all_to_all x11 -> x14, waiting for transfers between devices: 96.4 us -> 56.2 us  [exchange(): return lax.all_to_all(blocks, axis, 0, 0, tiled=True)]
    all_to_all x3 -> x0, blocking collectives: 37.4 us -> none  [exchange(): return lax.all_to_all(blocks, axis, 0, 0, tiled=True)]
    unnamed x147 -> x134, local copies, waits for them, and re-layouts: 35.9 us -> 15.9 us
    pallas_call x11 -> x22, Pallas kernels: 31.1 us -> 48 us  [the longest x11 48 us: call(): pl.pallas_call(kernel, out_shape=tuple((jax.ShapeDtypeStruct(shape, kind)...]
    all_to_all x11 -> x14, starting transfers between devices: 40.8 us -> 55.9 us  [exchange(): return lax.all_to_all(blocks, axis, 0, 0, tiled=True)]
    ppermute x33 -> x39, starting transfers between devices: 30.1 us -> 29.7 us  [swap(): return lax.ppermute(block, axis, route)]
  transfers between devices with their start and end apart: 45 -> 53, of which waited for: 15 -> 24; matrix products, arithmetic and copies ran while one was open for 8% -> 12% of each run, Pallas kernels for 7% -> 13%
where the time goes in v6:
time: 352 us; the launch traced here: 350 us
  waiting for transfers between devices  140 us (40%)
  starting transfers between devices  85.6 us (24%)
  Pallas kernels  64.4 us (18%)
  local copies, waits for them, and re-layouts  33.2 us (9%)
  other arithmetic  23.9 us (7%)
    ppermute x39, waiting for transfers between devices, swap(): return lax.ppermute(block, axis, route)  83.4 us
    all_to_all x14, waiting for transfers between devices, exchange(): return lax.all_to_all(blocks, axis, 0, 0, tiled=True)  56.2 us
    all_to_all x14, starting transfers between devices, exchange(): return lax.all_to_all(blocks, axis, 0, 0, tiled=True)  55.9 us
    pallas_call x11, Pallas kernels, call(): pl.pallas_call(kernel, out_shape=tuple((jax.ShapeDtypeStruct(shape, kind)...  48 us
    ppermute x39, starting transfers between devices, swap(): return lax.ppermute(block, axis, route)  29.7 us
    unnamed x134, local copies, waits for them, and re-layouts  15.9 us
    pallas_call x1, Pallas kernels, attend_backward(): pl.pallas_call(lambda *refs: backward_kernel(meta.shape[0] - 1, *refs), o...  8.79 us
    pallas_call x1, Pallas kernels, attend_forward(): pl.pallas_call(lambda *refs: forward_kernel(meta.shape[0] - 1, *refs), ou...  7.59 us
  transfers between devices with their start and end apart: 53, of which 24 were waited for; matrix products, arithmetic and copies ran while one was open for 12% of the time, Pallas kernels for 13%

profile of v6, /device:TPU:0, one launch (start us, length us, event | category | flops | bytes accessed | tf_op | source)
XLA Modules:
  0.0 350.3 jit_solution(1111778561433347031)
XLA Ops:
  5.6 4.8 %all-to-all-start = ((f32[8,18,288]{2,1,0:T(8,128)}), f32[8,18,288]{2,1,0:T(8,128)S(1)}, u32[]{:S(2)}, u32[]{:S(2)}) async-start(f32[8,18,288]{2,1,0:T(8,128)} %broadcast_in_dim.14), calls=%async_computation | async-start | bytes 589824 | tf_op jit(solution)/shard_map/all_to_all | solution.py:26
  10.4 7.3 %all-to-all-done = f32[8,18,288]{2,1,0:T(8,128)S(1)} async-done(((f32[8,18,288]{2,1,0:T(8,128)}), f32[8,18,288]{2,1,0:T(8,128)S(1)}, u32[]{:S(2)}, u32[]{:S(2)}) %all-to-all-start) | async-done | bytes 165920 | tf_op jit(solution)/shard_map/all_to_all | solution.py:26
  22.8 8.2 %collective-permute-done.2.refs_2_ = bf16[288,576]{1,0:T(8,128)(2,1)S(1)} collective-permute-done((bf16[288,576]{1,0:T(8,128)(2,1)}, bf16[288,576]{1,0:T(8,128)(2,1)S(1)}, u32[]{:S(2)}, u32[]{:S(2)}) %collective-permute-start.2) | collective-permute-done | bytes 331808 | tf_op jit(solution)/shard_map/ppermute | solution.py:22
  31.0 7.1 %collective-permute-done.3.refs_3_ = bf16[288,576]{1,0:T(8,128)(2,1)S(1)} collective-permute-done((bf16[288,576]{1,0:T(8,128)(2,1)}, bf16[288,576]{1,0:T(8,128)(2,1)S(1)}, u32[]{:S(2)}, u32[]{:S(2)}) %collective-permute-start.3) | collective-permute-done | bytes 331808 | tf_op jit(solution)/shard_map/ppermute | solution.py:22
  39.4 4.9 %all-to-all-start.1 = ((f32[4,18,288]{2,1,0:T(8,128)}), f32[4,18,288]{2,1,0:T(8,128)S(1)}, u32[]{:S(2)}, u32[]{:S(2)}) async-start(f32[4,18,288]{2,1,0:T(8,128)} %broadcast_in_dim.15), calls=%async_computation.1 | async-start | bytes 294912 | tf_op jit(solution)/shard_map/all_to_all | solution.py:26
  45.7 5.0 %all-to-all-done.1 = f32[4,18,288]{2,1,0:T(8,128)S(1)} async-done(((f32[4,18,288]{2,1,0:T(8,128)}), f32[4,18,288]{2,1,0:T(8,128)S(1)}, u32[]{:S(2)}, u32[]{:S(2)}) %all-to-all-start.1) | async-done | bytes 82976 | tf_op jit(solution)/shard_map/all_to_all | solution.py:26
  53.2 5.9 %project.1 = (bf16[256,1152]{1,0:T(8,128)(2,1)}, bf16[256,1152]{1,0:T(8,128)(2,1)}, bf16[8,72,640]{2,1,0:T(8,128)(2,1)}, bf16[1152,576]{1,0:T(8,128)(2,1)}, bf16[1152,576]{1,0:T(8,128)(2,1)}) custom-call(s32[7]{0:T(128)} %concatenate.36.refs_0_, bf16[288,576]{1,0:T(8,128)(2,1)} %gate.11.refs_1_, bf16[288,576]{1,0:T(8,128)(2,1)} %copy-done.43, ...), custom_call_target="tpu_custom_call" | custom-call | flops 1 | bytes 1 | tf_op jit(solution)/shard_map/project/pallas_call | solution.py:359
  59.2 3.7 %all-to-all-start.2 = ((bf16[8,72,640]{2,1,0:T(8,128)(2,1)}), bf16[8,72,640]{2,1,0:T(8,128)(2,1)S(1)}, u32[]{:S(2)}, u32[]{:S(2)}) async-start(bf16[8,72,640]{2,1,0:T(8,128)(2,1)} %get-tuple-element.54), calls=%async_computation.2 | async-start | bytes 1474560 | tf_op jit(solution)/shard_map/all_to_all | solution.py:26
  64.0 10.9 %all-to-all-done.2.refs_1_ = bf16[8,72,640]{2,1,0:T(8,128)(2,1)S(1)} async-done(((bf16[8,72,640]{2,1,0:T(8,128)(2,1)}), bf16[8,72,640]{2,1,0:T(8,128)(2,1)S(1)}, u32[]{:S(2)}, u32[]{:S(2)}) %all-to-all-start.2) | async-done | bytes 737312 | tf_op jit(solution)/shard_map/all_to_all | solution.py:26
  75.7 7.6 %attend_forward.1 = (bf16[8,72,128]{2,1,0:T(8,128)(2,1)}, f32[8,72,128]{2,1,0:T(8,128)}, f32[8,1,128]{2,1,0:T(1,128)}) custom-call(s32[4]{0:T(128)} %pad_add_fusion.refs_0_, bf16[8,72,640]{2,1,0:T(8,128)(2,1)} %copy-done.29), custom_call_target="tpu_custom_call" | custom-call | flops 1000000000 | bytes 4000000 | tf_op jit(solution)/shard_map/attend_forward/pallas_call | solution.py:208
  86.8 5.5 %all-to-all-done.3.refs_1_ = bf16[8,72,128]{2,1,0:T(8,128)(2,1)S(1)} async-done(((bf16[8,72,128]{2,1,0:T(8,128)(2,1)}), bf16[8,72,128]{2,1,0:T(8,128)(2,1)S(1)}, u32[]{:S(2)}, u32[]{:S(2)}) %all-to-all-start.3) | async-done | bytes 147488 | tf_op jit(solution)/shard_map/all_to_all | solution.py:26
  102.1 14.9 %collective-permute-done.10.refs_6_.refs_3_ = bf16[288,1152]{1,0:T(8,128)(2,1)S(1)} collective-permute-done((bf16[288,1152]{1,0:T(8,128)(2,1)}, bf16[288,1152]{1,0:T(8,128)(2,1)S(1)}, u32[]{:S(2)}, u32[]{:S(2)}) %collective-permute-start.10) | collective-permute-done | bytes 663584 | tf_op jit(solution)/shard_map/ppermute | solution.py:22
  121.6 4.8 %all-to-all-start.5 = ((bf16[4,64,1152]{2,1,0:T(8,128)(2,1)}), bf16[4,64,1152]{2,1,0:T(8,128)(2,1)S(1)}, u32[]{:S(2)}, u32[]{:S(2)}) async-start(bf16[4,64,1152]{2,1,0:T(8,128)(2,1)} %get-tuple-element.59), calls=%async_computation.5 | async-start | bytes 1179648 | tf_op jit(solution)/shard_map/all_to_all | solution.py:26
  129.3 14.1 %collective-permute-done.11.refs_0_ = bf16[288,1152]{1,0:T(8,128)(2,1)} collective-permute-done((bf16[288,1152]{1,0:T(8,128)(2,1)}, bf16[288,1152]{1,0:T(8,128)(2,1)}, u32[]{:S(2)}, u32[]{:S(2)}) %collective-permute-start.11) | collective-permute-done | bytes 663584 | tf_op jit(solution)/shard_map/ppermute | solution.py:22
  148.3 9.9 %mlp.1 = (bf16[256,1152]{1,0:T(8,128)(2,1)}, bf16[256,1152]{1,0:T(8,128)(2,1)}, bf16[256,1152]{1,0:T(8,128)(2,1)}, f32[1,1152]{1,0:T(1,128)}, bf16[64,1152]{1,0:...) custom-call(s32[7]{0:T(128)} %concatenate.36.refs_0_, ...), custom_call_target="tpu_custom_call" | custom-call | flops 1 | bytes 1 | tf_op jit(solution)/shard_map/mlp/pallas_call | solution.py:359
  158.2 5.0 %all-to-all-start.6 = ((bf16[4,64,1152]{2,1,0:T(8,128)(2,1)}), bf16[4,64,1152]{2,1,0:T(8,128)(2,1)S(1)}, u32[]{:S(2)}, u32[]{:S(2)}) async-start(bf16[4,64,1152]{2,1,0:T(8,128)(2,1)} %bitcast.71), calls=%async_computation.6 | async-start | bytes 1179648 | tf_op jit(solution)/shard_map/all_to_all | solution.py:26
  166.1 6.0 %late_weights.1 = (bf16[288,1152]{1,0:T(8,128)(2,1)}, bf16[288,1152]{1,0:T(8,128)(2,1)}, bf16[288,1152]{1,0:T(8,128)(2,1)}, bf16[288,1152]{1,0:T(8,128)(2,1)}) custom-call(s32[7]{0:T(128)} %concatenate.36.refs_0_, bf16[256,1152]{1,0:T(8,128)(2,1)} %bitcast.66, bf16[256,1152]{1,0:T(8,128)(2,1)} %get-tuple-element.60.refs_10_.refs_2_, ...), custom_call_target="tpu_custom_call" | custom-call | flops 1 | bytes 1 | tf_op jit(solution)/shard_map/late_weights/pallas_call | solution.py:359
  172.1 7.1 %all-to-all-done.6.refs_1_ = bf16[4,64,1152]{2,1,0:T(8,128)(2,1)S(1)} async-done(((bf16[4,64,1152]{2,1,0:T(8,128)(2,1)}), bf16[4,64,1152]{2,1,0:T(8,128)(2,1)S(1)}, u32[]{:S(2)}, u32[]{:S(2)}) %all-to-all-start.6) | async-done | bytes 589856 | tf_op jit(solution)/shard_map/all_to_all | solution.py:26
  188.6 14.1 %collective-permute-done.18.refs_3_ = bf16[288,1152]{1,0:T(8,128)(2,1)S(1)} collective-permute-done((bf16[288,1152]{1,0:T(8,128)(2,1)}, bf16[288,1152]{1,0:T(8,128)(2,1)S(1)}, u32[]{:S(2)}, u32[]{:S(2)}) %collective-permute-start.18) | collective-permute-done | bytes 663584 | tf_op jit(solution)/shard_map/ppermute | solution.py:22
  210.3 3.5 %collective-permute-start.22 = (bf16[64,1152]{1,0:T(8,128)(2,1)}, bf16[64,1152]{1,0:T(8,128)(2,1)S(1)}, u32[]{:S(2)}, u32[]{:S(2)}) collective-permute-start(bf16[64,1152]{1,0:T(8,128)(2,1)} %gate.17), channel_id=1, source_target_pairs={{0,3},{1,2},{2,1},{3,0},{4,7},{5,6},{6,5},{7,4},{8,11},{9,10},{10,... | collective-permute-start | bytes 442376 | tf_op jit(solution)/shard_map/ppermute | solution.py:22
  216.6 8.8 %attend_backward.1.refs_0_ = bf16[8,72,640]{2,1,0:T(8,128)(2,1)} custom-call(s32[4]{0:T(128)} %pad_add_fusion.refs_0_, bf16[8,72,640]{2,1,0:T(8,128)(2,1)} %copy-done.29, bf16[8,72,128]{2,1,0:T(8,128)(2,1)} %copy-done.54, f32[8,72,128]{2,1,0:T(8,128)} %get-tuple-element.76.refs_3_, f32[8,1,128]{2,1,0:T(1,128)} %get-tuple-element.77.refs_4_), custom_call_target="tpu_custom_call" | custom-call | flops 3000000000 | bytes 4000000 | tf_op jit(solution)/shard_map/attend_backward/pallas_call | solution.py:232
  228.5 3.9 %all-to-all-start.9 = ((bf16[8,72,640]{2,1,0:T(8,128)(2,1)}), bf16[8,72,640]{2,1,0:T(8,128)(2,1)S(1)}, u32[]{:S(2)}, u32[]{:S(2)}) async-start(bf16[8,72,640]{2,1,0:T(8,128)(2,1)} %gate.18), calls=%async_computation.9 | async-start | bytes 1474560 | tf_op jit(solution)/shard_map/all_to_all | solution.py:26
  233.4 11.1 %all-to-all-done.9.refs_1_ = bf16[8,72,640]{2,1,0:T(8,128)(2,1)S(1)} async-done(((bf16[8,72,640]{2,1,0:T(8,128)(2,1)}), bf16[8,72,640]{2,1,0:T(8,128)(2,1)S(1)}, u32[]{:S(2)}, u32[]{:S(2)}) %all-to-all-start.9) | async-done | bytes 737312 | tf_op jit(solution)/shard_map/all_to_all | solution.py:26
  245.3 4.7 %unspread.1 = (bf16[256,1152]{1,0:T(8,128)(2,1)}, bf16[256,576]{1,0:T(8,128)(2,1)}, bf16[256,576]{1,0:T(8,128)(2,1)}) custom-call(s32[7]{0:T(128)} %concatenate.36.refs_0_, bf16[8,72,640]{2,1,0:T(8,128)(2,1)} %copy-done.6, bf16[1152,576]{1,0:T(8,128)(2,1)} %get-tuple-element.78.refs_2_, bf16[1152,576]{1,0:T(8,128)(2,1)} %get-tuple-element.56.refs_2_.refs_3_), custom_call_target="tpu_custom_call" | custom-call | flops 1 | bytes 1 | tf_op jit(solution)/shard_map/unspread/pallas_call | solution.py:359
  260.1 4.9 %early_weights.1 = (bf16[288,576]{1,0:T(8,128)(2,1)}, bf16[288,576]{1,0:T(8,128)(2,1)}, bf16[288,576]{1,0:T(8,128)(2,1)}, bf16[288,576]{1,0:T(8,128)(2,1)}) custom-call(s32[7]{0:T(128)} %concatenate.36.refs_0_, bf16[256,1152]{1,0:T(8,128)(2,1)} %get-tuple-element.83.refs_1_, bf16[256,1152]{1,0:T(8,128)(2,1)} %bitcast.68, ...), custom_call_target="tpu_custom_call" | custom-call | flops 1 | bytes 1 | tf_op jit(solution)/shard_map/early_weights/pallas_call | solution.py:359
  270.0 4.9 %all-to-all-start.10 = ((bf16[4,64,1152]{2,1,0:T(8,128)(2,1)}), bf16[4,64,1152]{2,1,0:T(8,128)(2,1)}, u32[]{:S(2)}, u32[]{:S(2)}) async-start(bf16[4,64,1152]{2,1,0:T(8,128)(2,1)} %bitcast.21), calls=%async_computation.10 | async-start | bytes 1179648 | tf_op jit(solution)/shard_map/all_to_all | solution.py:26
  274.9 10.6 %collective-permute-done.33.refs_1_ = bf16[288,576]{1,0:T(8,128)(2,1)S(1)} collective-permute-done((bf16[288,576]{1,0:T(8,128)(2,1)}, bf16[288,576]{1,0:T(8,128)(2,1)S(1)}, u32[]{:S(2)}, u32[]{:S(2)}) %collective-permute-start.33) | collective-permute-done | bytes 331808 | tf_op jit(solution)/shard_map/ppermute | solution.py:22
  286.3 6.6 %collective-permute-done.35.refs_3_ = bf16[288,576]{1,0:T(8,128)(2,1)S(1)} collective-permute-done((bf16[288,576]{1,0:T(8,128)(2,1)}, bf16[288,576]{1,0:T(8,128)(2,1)S(1)}, u32[]{:S(2)}, u32[]{:S(2)}) %collective-permute-start.35) | collective-permute-done | bytes 331808 | tf_op jit(solution)/shard_map/ppermute | solution.py:22
  301.3 3.6 %all-to-all-start.11 = ((f32[4,18,288]{2,1,0:T(8,128)}), f32[4,18,288]{2,1,0:T(8,128)S(1)}, u32[]{:S(2)}, u32[]{:S(2)}) async-start(f32[4,18,288]{2,1,0:T(8,128)} %get-tuple-element.92), calls=%async_computation.11 | async-start | bytes 294912 | tf_op jit(solution)/shard_map/all_to_all | solution.py:26
  307.6 3.7 %all-to-all-done.11 = f32[4,18,288]{2,1,0:T(8,128)S(1)} async-done(((f32[4,18,288]{2,1,0:T(8,128)}), f32[4,18,288]{2,1,0:T(8,128)S(1)}, u32[]{:S(2)}, u32[]{:S(2)}) %all-to-all-start.11) | async-done | bytes 82976 | tf_op jit(solution)/shard_map/all_to_all | solution.py:26
  320.5 4.1 %all-to-all-start.12 = ((f32[8,32,288]{2,1,0:T(8,128)}), f32[8,32,288]{2,1,0:T(8,128)}, u32[]{:S(2)}, u32[]{:S(2)}) async-start(f32[8,32,288]{2,1,0:T(8,128)} %broadcast_in_dim.32), calls=%async_computation.12 | async-start | bytes 786432 | tf_op jit(solution)/shard_map/all_to_all | solution.py:26
  329.1 3.9 %all-to-all-done.12 = f32[8,32,288]{2,1,0:T(8,128)} async-done(((f32[8,32,288]{2,1,0:T(8,128)}), f32[8,32,288]{2,1,0:T(8,128)}, u32[]{:S(2)}, u32[]{:S(2)}) %all-to-all-start.12) | async-done | bytes 294944 | tf_op jit(solution)/shard_map/all_to_all | solution.py:26
  (311 shorter events, 127.8 us)
Async XLA Ops:
  3.1 15.2 %collective-permute-start.1 = (bf16[144,576]{1,0:T(8,128)(2,1)S(1)}, bf16[144,576]{1,0:T(8,128)(2,1)S(1)}, u32[]{:S(2)}, u32[]{:S(2)}) collective-permute-start(bf16[144,576]{1,0:T(8,128)(2,1)S(1)} %broadcast_select_fusion.10), channel_id=1, source_target_pairs={{0,4},{4,0},{8,12},{12,8},{16,20},{20,16},{24,28},{28,24},{1,5},{5... | collective-permute-start | bytes 497672 | tf_op jit(solution)/shard_map/ppermute | solution.py:22
  19.9 18.3 %collective-permute-start.3 = (bf16[288,576]{1,0:T(8,128)(2,1)}, bf16[288,576]{1,0:T(8,128)(2,1)S(1)}, u32[]{:S(2)}, u32[]{:S(2)}) collective-permute-start(bf16[288,576]{1,0:T(8,128)(2,1)} %gate.11.refs_1_), channel_id=1, source_target_pairs={{0,16},{4,20},{8,24},{12,28},{16,0},{20,4},{24,8},{28,12},{1,17},{... | collective-permute-start | bytes 995336 | tf_op jit(solution)/shard_map/ppermute | solution.py:22
  20.4 17.7 %collective-permute-start.4 = (bf16[288,576]{1,0:T(8,128)(2,1)}, bf16[288,576]{1,0:T(8,128)(2,1)S(1)}, u32[]{:S(2)}, u32[]{:S(2)}) collective-permute-start(bf16[288,576]{1,0:T(8,128)(2,1)} %gate.11.refs_1_), channel_id=1, source_target_pairs={{0,24},{4,28},{8,16},{12,20},{16,8},{20,12},{24,0},{28,4},{1,25},{... | collective-permute-start | bytes 995336 | tf_op jit(solution)/shard_map/ppermute | solution.py:22
  22.8 28.6 %collective-permute-start.5 = (bf16[288,576]{1,0:T(8,128)(2,1)}, bf16[288,576]{1,0:T(8,128)(2,1)S(1)}, u32[]{:S(2)}, u32[]{:S(2)}) collective-permute-start(bf16[288,576]{1,0:T(8,128)(2,1)} %gate.11.refs_1_), channel_id=1, source_target_pairs={{0,4},{4,0},{8,12},{12,8},{16,20},{20,16},{24,28},{28,24},{1,5},{5... | collective-permute-start | bytes 995336 | tf_op jit(solution)/shard_map/ppermute | solution.py:22
  31.0 20.4 %collective-permute-start.6 = (bf16[288,576]{1,0:T(8,128)(2,1)S(1)}, bf16[288,576]{1,0:T(8,128)(2,1)S(1)}, u32[]{:S(2)}, u32[]{:S(2)}) collective-permute-start(bf16[288,576]{1,0:T(8,128)(2,1)S(1)} %collective-permute-done.2.refs_2_), channel_id=1, source_target_pairs={{0,4},{4,0},{8,12},{12,8},{16,20},{20,16},{24,28},{28,24},{1,5},{5... | collective-permute-start | bytes 995336 | tf_op jit(solution)/shard_map/ppermute | solution.py:22
  59.2 15.7 %all-to-all-start.2 = ((bf16[8,72,640]{2,1,0:T(8,128)(2,1)}), bf16[8,72,640]{2,1,0:T(8,128)(2,1)S(1)}, u32[]{:S(2)}, u32[]{:S(2)}) async-start(bf16[8,72,640]{2,1,0:T(8,128)(2,1)} %get-tuple-element.54), calls=%async_computation.2 | async-start | bytes 1474560 | tf_op jit(solution)/shard_map/all_to_all | solution.py:26
  62.9 23.8 %collective-permute-start = (bf16[144,1152]{1,0:T(8,128)(2,1)S(1)}, bf16[144,1152]{1,0:T(8,128)(2,1)S(1)}, u32[]{:S(2)}, u32[]{:S(2)}) collective-permute-start(bf16[144,1152]{1,0:T(8,128)(2,1)S(1)} %bitcast_select_fusion), channel_id=1, source_target_pairs={{0,4},{4,0},{8,12},{12,8},{16,20},{20,16},{24,28},{28,24},{1,5},{5... | collective-permute-start | bytes 995336 | tf_op jit(solution)/shard_map/ppermute | solution.py:22
  96.0 21.3 %all-to-all-start.4 = ((bf16[4,64,1152]{2,1,0:T(8,128)(2,1)}), bf16[4,64,1152]{2,1,0:T(8,128)(2,1)S(1)}, u32[]{:S(2)}, u32[]{:S(2)}) async-start(bf16[4,64,1152]{2,1,0:T(8,128)(2,1)} %bitcast.72), calls=%async_computation.4 | async-start | bytes 1179648 | tf_op jit(solution)/shard_map/all_to_all | solution.py:26
  100.4 16.7 %collective-permute-start.10 = (bf16[288,1152]{1,0:T(8,128)(2,1)}, bf16[288,1152]{1,0:T(8,128)(2,1)S(1)}, u32[]{:S(2)}, u32[]{:S(2)}) collective-permute-start(bf16[288,1152]{1,0:T(8,128)(2,1)} %gate.12.refs_1_), channel_id=1, source_target_pairs={{0,16},{4,20},{8,24},{12,28},{16,0},{20,4},{24,8},{28,12},{1,17},{... | collective-permute-start | bytes 1990664 | tf_op jit(solution)/shard_map/ppermute | solution.py:22
  100.9 16.4 %collective-permute-start.9 = (bf16[288,1152]{1,0:T(8,128)(2,1)}, bf16[288,1152]{1,0:T(8,128)(2,1)S(1)}, u32[]{:S(2)}, u32[]{:S(2)}) collective-permute-start(bf16[288,1152]{1,0:T(8,128)(2,1)} %gate.12.refs_1_), channel_id=1, source_target_pairs={{0,8},{4,12},{8,0},{12,4},{16,24},{20,28},{24,16},{28,20},{1,9},{5... | collective-permute-start | bytes 1990664 | tf_op jit(solution)/shard_map/ppermute | solution.py:22
  121.6 21.8 %all-to-all-start.5 = ((bf16[4,64,1152]{2,1,0:T(8,128)(2,1)}), bf16[4,64,1152]{2,1,0:T(8,128)(2,1)S(1)}, u32[]{:S(2)}, u32[]{:S(2)}) async-start(bf16[4,64,1152]{2,1,0:T(8,128)(2,1)} %get-tuple-element.59), calls=%async_computation.5 | async-start | bytes 1179648 | tf_op jit(solution)/shard_map/all_to_all | solution.py:26
  127.3 16.1 %collective-permute-start.11 = (bf16[288,1152]{1,0:T(8,128)(2,1)}, bf16[288,1152]{1,0:T(8,128)(2,1)}, u32[]{:S(2)}, u32[]{:S(2)}) collective-permute-start(bf16[288,1152]{1,0:T(8,128)(2,1)} %gate.13), channel_id=1, source_target_pairs={{0,24},{4,28},{8,16},{12,20},{16,8},{20,12},{24,0},{28,4},{1,25},{... | collective-permute-start | bytes 1990664 | tf_op jit(solution)/shard_map/ppermute | solution.py:22
  128.8 18.6 %collective-permute-start.12 = (bf16[288,1152]{1,0:T(8,128)(2,1)S(1)}, bf16[288,1152]{1,0:T(8,128)(2,1)}, u32[]{:S(2)}, u32[]{:S(2)}) collective-permute-start(bf16[288,1152]{1,0:T(8,128)(2,1)S(1)} %copy-done.1), channel_id=1, source_target_pairs={{0,4},{4,0},{8,12},{12,8},{16,20},{20,16},{24,28},{28,24},{1,5},{5... | collective-permute-start | bytes 1990664 | tf_op jit(solution)/shard_map/ppermute | solution.py:22
  128.8 18.6 %collective-permute-start.13 = (bf16[288,1152]{1,0:T(8,128)(2,1)}, bf16[288,1152]{1,0:T(8,128)(2,1)}, u32[]{:S(2)}, u32[]{:S(2)}) collective-permute-start(bf16[288,1152]{1,0:T(8,128)(2,1)} %copy-done.9), channel_id=1, source_target_pairs={{0,4},{4,0},{8,12},{12,8},{16,20},{20,16},{24,28},{28,24},{1,5},{5... | collective-permute-start | bytes 1990664 | tf_op jit(solution)/shard_map/ppermute | solution.py:22
  129.3 18.1 %collective-permute-start.14 = (bf16[288,1152]{1,0:T(8,128)(2,1)S(1)}, bf16[288,1152]{1,0:T(8,128)(2,1)}, u32[]{:S(2)}, u32[]{:S(2)}) collective-permute-start(bf16[288,1152]{1,0:T(8,128)(2,1)S(1)} %copy-done.8), channel_id=1, source_target_pairs={{0,4},{4,0},{8,12},{12,8},{16,20},{20,16},{24,28},{28,24},{1,5},{5... | collective-permute-start | bytes 1990664 | tf_op jit(solution)/shard_map/ppermute | solution.py:22
  146.9 16.4 %collective-permute-start.16 = (bf16[256,1152]{1,0:T(8,128)(2,1)}, bf16[256,1152]{1,0:T(8,128)(2,1)S(1)}, u32[]{:S(2)}, u32[]{:S(2)}) collective-permute-start(bf16[256,1152]{1,0:T(8,128)(2,1)} %broadcast_select_fusion.1), channel_id=1, source_target_pairs={{0,4},{4,0},{8,12},{12,8},{16,20},{20,16},{24,28},{28,24},{1,5},{5... | collective-permute-start | bytes 1769480 | tf_op jit(solution)/shard_map/ppermute | solution.py:22
  158.2 21.0 %all-to-all-start.6 = ((bf16[4,64,1152]{2,1,0:T(8,128)(2,1)}), bf16[4,64,1152]{2,1,0:T(8,128)(2,1)S(1)}, u32[]{:S(2)}, u32[]{:S(2)}) async-start(bf16[4,64,1152]{2,1,0:T(8,128)(2,1)} %bitcast.71), calls=%async_computation.6 | async-start | bytes 1179648 | tf_op jit(solution)/shard_map/all_to_all | solution.py:26
  183.1 19.9 %all-to-all-start.7 = ((bf16[4,64,1152]{2,1,0:T(8,128)(2,1)}), bf16[4,64,1152]{2,1,0:T(8,128)(2,1)S(1)}, u32[]{:S(2)}, u32[]{:S(2)}) async-start(bf16[4,64,1152]{2,1,0:T(8,128)(2,1)} %get-tuple-element.71), calls=%async_computation.7 | async-start | bytes 1179648 | tf_op jit(solution)/shard_map/all_to_all | solution.py:26
  186.6 16.2 %collective-permute-start.18 = (bf16[288,1152]{1,0:T(8,128)(2,1)}, bf16[288,1152]{1,0:T(8,128)(2,1)S(1)}, u32[]{:S(2)}, u32[]{:S(2)}) collective-permute-start(bf16[288,1152]{1,0:T(8,128)(2,1)} %get-tuple-element.68.refs_7_), channel_id=1, source_target_pairs={{0,8},{4,12},{8,0},{12,4},{16,24},{20,28},{24,16},{28,20},{1,9},{5... | collective-permute-start | bytes 1990664 | tf_op jit(solution)/shard_map/ppermute | solution.py:22
  187.4 15.6 %collective-permute-start.19 = (bf16[288,1152]{1,0:T(8,128)(2,1)S(1)}, bf16[288,1152]{1,0:T(8,128)(2,1)S(1)}, u32[]{:S(2)}, u32[]{:S(2)}) collective-permute-start(bf16[288,1152]{1,0:T(8,128)(2,1)S(1)} %copy-done.32), channel_id=1, source_target_pairs={{0,16},{4,20},{8,24},{12,28},{16,0},{20,4},{24,8},{28,12},{1,17},{... | collective-permute-start | bytes 1990664 | tf_op jit(solution)/shard_map/ppermute | solution.py:22
  210.3 15.1 %collective-permute-start.22 = (bf16[64,1152]{1,0:T(8,128)(2,1)}, bf16[64,1152]{1,0:T(8,128)(2,1)S(1)}, u32[]{:S(2)}, u32[]{:S(2)}) collective-permute-start(bf16[64,1152]{1,0:T(8,128)(2,1)} %gate.17), channel_id=1, source_target_pairs={{0,3},{1,2},{2,1},{3,0},{4,7},{5,6},{6,5},{7,4},{8,11},{9,10},{10,... | collective-permute-start | bytes 442376 | tf_op jit(solution)/shard_map/ppermute | solution.py:22
  228.5 15.9 %all-to-all-start.9 = ((bf16[8,72,640]{2,1,0:T(8,128)(2,1)}), bf16[8,72,640]{2,1,0:T(8,128)(2,1)S(1)}, u32[]{:S(2)}, u32[]{:S(2)}) async-start(bf16[8,72,640]{2,1,0:T(8,128)(2,1)} %gate.18), calls=%async_computation.9 | async-start | bytes 1474560 | tf_op jit(solution)/shard_map/all_to_all | solution.py:26
  232.4 22.4 %collective-permute-start.26 = (bf16[256,1152]{1,0:T(8,128)(2,1)S(1)}, bf16[256,1152]{1,0:T(8,128)(2,1)S(1)}, u32[]{:S(2)}, u32[]{:S(2)}) collective-permute-start(bf16[256,1152]{1,0:T(8,128)(2,1)S(1)} %copy-done.34), channel_id=1, source_target_pairs={{0,4},{4,0},{8,12},{12,8},{16,20},{20,16},{24,28},{28,24},{1,5},{5... | collective-permute-start | bytes 1769480 | tf_op jit(solution)/shard_map/ppermute | solution.py:22
  232.9 26.5 %collective-permute-start.27 = (bf16[256,1152]{1,0:T(8,128)(2,1)S(1)}, bf16[256,1152]{1,0:T(8,128)(2,1)}, u32[]{:S(2)}, u32[]{:S(2)}) collective-permute-start(bf16[256,1152]{1,0:T(8,128)(2,1)S(1)} %bitcast.69), channel_id=1, source_target_pairs={{0,4},{4,0},{8,12},{12,8},{16,20},{20,16},{24,28},{28,24},{1,5},{5... | collective-permute-start | bytes 1769480 | tf_op jit(solution)/shard_map/ppermute | solution.py:22
  233.0 24.8 %collective-permute-start.29 = (bf16[256,576]{1,0:T(8,128)(2,1)}, bf16[256,576]{1,0:T(8,128)(2,1)S(1)}, u32[]{:S(2)}, u32[]{:S(2)}) collective-permute-start(bf16[256,576]{1,0:T(8,128)(2,1)} %get-tuple-element.86.refs_5_), channel_id=1, source_target_pairs={{0,4},{4,0},{8,12},{12,8},{16,20},{20,16},{24,28},{28,24},{1,5},{5... | collective-permute-start | bytes 884744 | tf_op jit(solution)/shard_map/ppermute | solution.py:22
  254.9 14.2 %collective-permute-start.24 = (bf16[64,1152]{1,0:T(8,128)(2,1)}, bf16[64,1152]{1,0:T(8,128)(2,1)S(1)}, u32[]{:S(2)}, u32[]{:S(2)}) collective-permute-start(bf16[64,1152]{1,0:T(8,128)(2,1)} %get-tuple-element.75), channel_id=1, source_target_pairs={{0,2},{1,3},{2,0},{3,1},{4,6},{5,7},{6,4},{7,5},{8,10},{9,11},{10,... | collective-permute-start | bytes 442376 | tf_op jit(solution)/shard_map/ppermute | solution.py:22
  259.4 36.3 %collective-permute-start.37 = (bf16[288,1152]{1,0:T(8,128)(2,1)}, bf16[288,1152]{1,0:T(8,128)(2,1)}, u32[]{:S(2)}, u32[]{:S(2)}) collective-permute-start(bf16[288,1152]{1,0:T(8,128)(2,1)} %gate.21), channel_id=1, source_target_pairs={{0,24},{4,28},{8,16},{12,20},{16,8},{20,12},{24,0},{28,4},{1,25},{... | collective-permute-start | bytes 1990664 | tf_op jit(solution)/shard_map/ppermute | solution.py:22
  265.0 20.5 %collective-permute-start.33 = (bf16[288,576]{1,0:T(8,128)(2,1)}, bf16[288,576]{1,0:T(8,128)(2,1)S(1)}, u32[]{:S(2)}, u32[]{:S(2)}) collective-permute-start(bf16[288,576]{1,0:T(8,128)(2,1)} %get-tuple-element.88.refs_8_), channel_id=1, source_target_pairs={{0,8},{4,12},{8,0},{12,4},{16,24},{20,28},{24,16},{28,20},{1,9},{5... | collective-permute-start | bytes 995336 | tf_op jit(solution)/shard_map/ppermute | solution.py:22
  266.5 19.8 %collective-permute-start.34 = (bf16[288,576]{1,0:T(8,128)(2,1)}, bf16[288,576]{1,0:T(8,128)(2,1)S(1)}, u32[]{:S(2)}, u32[]{:S(2)}) collective-permute-start(bf16[288,576]{1,0:T(8,128)(2,1)} %get-tuple-element.89.refs_9_), channel_id=1, source_target_pairs={{0,16},{4,20},{8,24},{12,28},{16,0},{20,4},{24,8},{28,12},{1,17},{... | collective-permute-start | bytes 995336 | tf_op jit(solution)/shard_map/ppermute | solution.py:22
  269.0 23.9 %collective-permute-start.35 = (bf16[288,576]{1,0:T(8,128)(2,1)}, bf16[288,576]{1,0:T(8,128)(2,1)S(1)}, u32[]{:S(2)}, u32[]{:S(2)}) collective-permute-start(bf16[288,576]{1,0:T(8,128)(2,1)} %get-tuple-element.90.refs_10_), channel_id=1, source_target_pairs={{0,24},{4,28},{8,16},{12,20},{16,8},{20,12},{24,0},{28,4},{1,25},{... | collective-permute-start | bytes 995336 | tf_op jit(solution)/shard_map/ppermute | solution.py:22
  270.0 28.6 %all-to-all-start.10 = ((bf16[4,64,1152]{2,1,0:T(8,128)(2,1)}), bf16[4,64,1152]{2,1,0:T(8,128)(2,1)}, u32[]{:S(2)}, u32[]{:S(2)}) async-start(bf16[4,64,1152]{2,1,0:T(8,128)(2,1)} %bitcast.21), calls=%async_computation.10 | async-start | bytes 1179648 | tf_op jit(solution)/shard_map/all_to_all | solution.py:26
  298.1 47.1 %collective-permute-start.38 = (f32[144,1152]{1,0:T(8,128)}, f32[144,1152]{1,0:T(8,128)}, u32[]{:S(2)}, u32[]{:S(2)}) collective-permute-start(f32[144,1152]{1,0:T(8,128)} %slice_select_fusion), channel_id=1, source_target_pairs={{0,4},{4,0},{8,12},{12,8},{16,20},{20,16},{24,28},{28,24},{1,5},{5... | collective-permute-start | bytes 1990664 | tf_op jit(solution)/shard_map/ppermute | solution.py:22
  (85 other events, 616.3 us)

commit v7 on v6

--- a/solution.py
+++ b/solution.py
@@ -30,16 +30,21 @@
     return exchange(jnp.broadcast_to(block[None], (count,) + block.shape), axis)
 
 
-def gate(value, *others):
+def gate_all(values, *others):
+    anywhere = pl.BlockSpec(memory_space=pl.ANY)
     return pl.pallas_call(
         lambda *refs: None,
-        out_shape=jax.ShapeDtypeStruct(value.shape, value.dtype),
-        in_specs=[pl.BlockSpec(memory_space=pl.ANY)] * (1 + len(others)),
-        out_specs=pl.BlockSpec(memory_space=pl.ANY),
-        input_output_aliases={0: 0},
+        out_shape=tuple(jax.ShapeDtypeStruct(value.shape, value.dtype) for value in values),
+        in_specs=[anywhere] * (len(values) + len(others)),
+        out_specs=(anywhere,) * len(values),
+        input_output_aliases={place: place for place in range(len(values))},
         cost_estimate=pl.CostEstimate(flops=1, bytes_accessed=1, transcendentals=0),
         name="gate",
-    )(value, *others)
+    )(*values, *others)
+
+
+def gate(value, *others):
+    return gate_all((value,), *others)[0]
 
 
 def choose(core, first, second):
@@ -81,10 +86,12 @@
     return choose(core, keep, swap(send, "dp", 1))
 
 
-def gather_beside(share, axis):
-    count, me = lax.axis_size(axis), lax.axis_index(axis)
-    parts = jnp.stack([share] + [swap(share, axis, bits) for bits in range(1, count)])
-    ordered = [lax.dynamic_index_in_dim(parts, me ^ place, 0, keepdims=False) for place in range(count)]
+def in_order(parts, axis):
+    me = lax.axis_index(axis)
+    stacked = jnp.stack(parts)
+    ordered = [
+        lax.dynamic_index_in_dim(stacked, me ^ place, 0, keepdims=False) for place in range(len(parts))
+    ]
     return jnp.concatenate(ordered)
 
 
@@ -437,14 +444,16 @@
 def project_kernel(latents, count, meta_ref, *refs):
     mine, other = refs[:count], refs[count : 2 * count]
     tokens_ref, cot_ref, mod_ref, bias_ref = refs[2 * count : 2 * count + 4]
-    hidden_ref, d_mlp_ref, packed_ref, qk_ref, vp_ref, sems = refs[2 * count + 4 :]
+    hidden_ref, d_mlp_ref, packed_ref, qk_ref, vp_ref, d_bias_ref, sems = refs[2 * count + 4 :]
     rows, width = tokens_ref.shape
     place_pair(meta_ref, mine, other, qk_ref, vp_ref, sems)
     masks = row_masks(meta_ref, latents, meta_ref[1], rows)
     unit, _ = normed(tokens_ref[...].astype(F32))
     hidden = unit * (1.0 + rows_of(mod_ref, masks, 1)) + rows_of(mod_ref, masks, 0)
     hidden_ref[...] = hidden.astype(BF16)
-    d_mlp_ref[...] = (cot_ref[...].astype(F32) * rows_of(mod_ref, masks, 5)).astype(BF16)
+    d_mlp = (cot_ref[...].astype(F32) * rows_of(mod_ref, masks, 5)).astype(BF16)
+    d_mlp_ref[...] = d_mlp
+    d_bias_ref[...] = jnp.sum(d_mlp.astype(F32), axis=0, keepdims=True)
     heads = packed_ref.shape[0] // 2
     features = heads * DH
     left = hidden_ref[...]
@@ -499,8 +508,8 @@
 def mlp_kernel(count, meta_ref, *refs):
     mine, other = refs[:count], refs[count : 2 * count]
     hidden_ref, d_mlp_ref, bias_ref = refs[2 * count : 2 * count + 3]
-    d_two_ref, gelu_ref, d_pre_ref, d_bias_ref = refs[2 * count + 3 : 2 * count + 7]
-    mlp_refs = refs[2 * count + 7 : -5]
+    d_two_ref, gelu_ref, d_pre_ref, d_bias_ref, left_ref, right_ref = refs[2 * count + 3 : 2 * count + 9]
+    mlp_refs = refs[2 * count + 9 : -5]
     fc1_ref, fc2_ref, d_two_sum, mlp_sum, sems = refs[-5:]
     place_pair(meta_ref, mine, other, fc1_ref, fc2_ref, sems)
     d_two_sum[...] = jnp.zeros_like(d_two_sum)
@@ -525,6 +534,11 @@
 
     lax.fori_loop(0, fc1_ref.shape[1] // tile, step, 0)
     d_two_ref[...] = d_two_sum[...].astype(BF16)
+    def sent(left, right):
+        left_ref[...] = left[0][...]
+        right_ref[...] = left[1][...]
+
+    on_core(meta_ref, sent, (d_mlp_ref, gelu_ref), (hidden_ref, d_pre_ref))
     share = mlp_refs[0].shape[0]
     for step, mlp_ref in enumerate(mlp_refs):
         start = pl.multiple_of((meta_ref[2] ^ step) * share, share)
@@ -577,7 +591,9 @@
     d_bias_ref[...] = jnp.sum(d_attn_ref[...].astype(F32), axis=0, keepdims=True)
 
 
-def unspread_kernel(meta_ref, parts_ref, qk_ref, vp_ref, d_one_ref, d_qk_ref, d_vp_ref):
+def unspread_kernel(
+    meta_ref, parts_ref, qk_ref, vp_ref, d_one_ref, d_qk_ref, d_vp_ref, sent_ref, d_bias_ref
+):
     heads = parts_ref.shape[0] // 2
     rows = d_one_ref.shape[0]
     query, key, value = [], [], []
@@ -603,6 +619,13 @@
 
     lax.fori_loop(0, qk_ref.shape[0] // tile, step, 0)
 
+    def sent(first, second):
+        sent_ref[...] = first[...]
+
+    on_core(meta_ref, sent, d_vp_ref, d_qk_ref)
+    d_bias_ref[0:1, :] = jnp.sum(d_qk_ref[...].astype(F32), axis=0, keepdims=True)
+    d_bias_ref[1:2, :] = jnp.sum(d_vp_ref[...].astype(F32), axis=0, keepdims=True)
+
 
 def weight_kernel(first_pairs, second_pairs, meta_ref, *refs):
     operands = 1 + max(max(pair) for pair in first_pairs + second_pairs)
@@ -632,7 +655,7 @@
 
 def first_back_kernel(
     latents, meta_ref, parts_ref, tokens_ref, d_mid_ref, mod_ref, mid_sums_ref, last_sums_ref,
-    grad_ref, sent_ref, first_sums,
+    fc2_bias_ref, proj_bias_ref, fc1_bias_ref, qv_bias_ref, grad_ref, sent_ref, bias_ref, first_sums,
 ):
     copies, share, width = parts_ref.shape
     masks = row_masks(meta_ref, latents, meta_ref[1] + meta_ref[2] * share, share)
@@ -657,6 +680,12 @@
             place = number * 6 + feature
             for part in range(copies):
                 sent_ref[part, place : place + 1, :] = row[:, part * columns : (part + 1) * columns]
+    place = 0
+    for ref in (fc2_bias_ref, proj_bias_ref, fc1_bias_ref):
+        for start in range(0, ref.shape[1], columns):
+            bias_ref[place : place + 1, :] = ref[:, start : start + columns]
+            place += 1
+    bias_ref[place : place + 2, :] = qv_bias_ref[:, :columns]
 
 
 def latent_index(latent_len, first_row, row_count, token_total):
@@ -733,6 +762,7 @@
     modulation = gather(mod_mine, "tensor", n_tensor).transpose(1, 0, 2).reshape(6 * latents, width)
 
     mod_rows = modulation
+    early_parts = list(gate_all(early_parts, modulation))
     early_parts += [swap(part, "dp", 1) for part in early_parts]
     count = len(early_parts) // 2
     meta = jnp.stack([core, my_dp * rows, my_tensor, my_dp // 2]).astype(jnp.int32)
@@ -741,13 +771,14 @@
     by_last = (((1,), (1,)), ((), ()))
     by_token = (((0,), (0,)), ((), ()))
     bias = jnp.concatenate([b_qv[0], jnp.zeros_like(b_qv[0]), b_qv[1], jnp.zeros_like(b_qv[0])])
-    hidden_one, d_mlp, packed, full_qk, full_vp = call(
+    hidden_one, d_mlp, packed, full_qk, full_vp, d_bias_fc2 = call(
         lambda *refs: project_kernel(latents, count, *refs),
         "project",
         place_meta,
         (*early_parts, tokens, cotangent, mod_rows, bias.astype(F32).reshape(2, -1)),
         (((rows, width), BF16), ((rows, width), BF16), ((2 * heads, DH, rows * 5 // 2), BF16))
-        + (((width, 2 * features), BF16),) * 2,
+        + (((width, 2 * features), BF16),) * 2
+        + (((1, width), F32),),
         [pltpu.SemaphoreType.DMA((2, count))],
         2 * count,
     )
@@ -780,12 +811,13 @@
         late_parts.append(gate(last_part, hidden_two))
     late_other = [swap(part, "dp", 1) for part in late_parts]
 
-    d_two_part, gelu_out, d_pre, d_bias_fc1, *mlp_blocks = call(
+    d_two_part, gelu_out, d_pre, d_bias_fc1, left_sent, right_sent, *mlp_blocks = call(
         lambda *refs: mlp_kernel(count, *refs),
         "mlp",
         place_meta,
         (*late_parts, *late_other, hidden_two, d_mlp, b_fc1.reshape(1, -1)),
         (((rows, width), BF16), ((rows, units), BF16), ((rows, units), BF16), ((1, units), F32))
+        + (((rows, width), BF16), ((rows, units), BF16))
         + (((share, width), BF16),) * n_tensor,
         [pltpu.VMEM((width, units), BF16)] * 2
         + [pltpu.VMEM((rows, width), F32)] * 2
@@ -795,8 +827,8 @@
     d_two_parts = exchange_shares(d_two_part, "tensor")
 
     chips = n_dp // 2 if few_chips else 1
-    left_other = swap(choose(core, d_mlp, hidden_two)[0], "dp", 1)
-    right_other = swap(choose(core, gelu_out, d_pre)[0], "dp", 1)
+    left_other = swap(left_sent, "dp", 1)
+    right_other = swap(right_sent, "dp", 1)
     late_blocks = call(
         lambda *refs: weight_kernel([(0, 2), (4, 5)], [(1, 3), (4, 5)], *refs),
         "late_weights",
@@ -840,19 +872,33 @@
         (*mlp_parts, residual_mid, cotangent, mod_rows, b_fc2.reshape(1, -1)),
         (((share, width), BF16), ((latents, width), F32)),
     )
-    d_one_part, d_qk, d_vp = call(
+    result_parts = [result_own] + [swap(result_own, "tensor", bits) for bits in range(1, n_tensor)]
+    d_one_part, d_qk, d_vp, d_sent, d_bias_qv = call(
         unspread_kernel,
         "unspread",
         meta,
         (d_packed, full_qk, full_vp),
-        (((rows, width), BF16), ((rows, 2 * features), BF16), ((rows, 2 * features), BF16)),
+        (((rows, width), BF16),)
+        + (((rows, 2 * features), BF16),) * 3
+        + (((2, 2 * features), F32),),
+        due=result_parts[1:],
     )
     d_one_parts = exchange_shares(d_one_part, "tensor")
-    result = gather_beside(result_own, "tensor")
-
+    result = in_order(result_parts, "tensor")
+
+    grad_own, d_mod_part, bias_rows = call(
+        lambda *refs: first_back_kernel(latents, *refs),
+        "first_back",
+        meta,
+        (d_one_parts, tokens, d_mid, mod_rows, mid_sums, last_sums)
+        + (d_bias_fc2, d_bias_proj, d_bias_fc1, d_bias_qv),
+        (((share, width), BF16), ((n_tensor, 6 * latents, features), F32))
+        + (((2 * (width // features) + units // features + 2, features), F32),),
+        [pltpu.VMEM((2 * latents, width), F32)],
+    )
     if few_chips:
         late_grads.append(swap(gate(late_blocks[-1], d_one_part), "dp", n_dp - 2))
-    right_other = swap(choose(core, d_vp, d_qk)[0], "dp", 1)
+    right_other = swap(gate(d_sent, d_one_parts), "dp", 1)
     early_blocks = call(
         lambda *refs: weight_kernel(
             [(0, 2), (5, 7)], [(0, 3), (1, 4), (5, 7), (6, 8)], *refs
@@ -862,31 +908,16 @@
         (hidden_one, d_attn, d_qk, d_vp, attended, hidden_other, d_attn_other, right_other, attended_other),
         (((width // chips, 2 * features), BF16),) * chips,
         [pltpu.VMEM((width, 2 * features), BF16)],
+        due=[d_mod_part],
     )
     early_grads = sum_chips(early_blocks)
 
-    grad_own, d_mod_part = call(
-        lambda *refs: first_back_kernel(latents, *refs),
-        "first_back",
-        meta,
-        (d_one_parts, tokens, d_mid, mod_rows, mid_sums, last_sums),
-        (((share, width), BF16), ((n_tensor, 6 * latents, features), F32)),
-        [pltpu.VMEM((2 * latents, width), F32)],
-        due=early_blocks,
-    )
-    bias_part = jnp.concatenate(
-        [
-            jnp.sum(d_mlp.astype(F32), axis=0),
-            d_bias_proj[0],
-            d_bias_fc1[0],
-            jnp.sum(d_qk[:, :features].astype(F32), axis=0),
-            jnp.sum(d_vp[:, :features].astype(F32), axis=0),
-        ]
-    )
-    bias_rows = bias_part.reshape(-1, features)
-    d_mod_mine = jnp.sum(exchange(d_mod_part, "tensor"), axis=0)
-    grad_tokens = gather_beside(gate(grad_own, d_mod_mine), "tensor").astype(F32)
-    sums = jnp.sum(gather(jnp.concatenate([d_mod_mine, bias_rows]), "dp", n_dp), axis=0)
+    d_mod_mine = jnp.sum(gate(exchange(d_mod_part, "tensor"), early_blocks[-1]), axis=0)
+    grad_own = gate(grad_own, d_mod_mine)
+    grad_parts = [grad_own] + [swap(grad_own, "tensor", bits) for bits in range(1, n_tensor)]
+    sums = gather(jnp.concatenate([d_mod_mine, bias_rows]), "dp", n_dp)
+    sums = jnp.sum(gate(sums, *early_grads[1:]) if few_chips else sums, axis=0)
+    grad_tokens = in_order(gate_all(grad_parts, sums), "tensor").astype(F32)
     d_mod = sums[: 6 * latents].reshape(latents, 6 * features)
     bias_total = sums[6 * latents :].reshape(-1)
     grad_b_ada = jnp.sum(d_mod, axis=0).reshape(6, features)
@@ -899,7 +930,6 @@
         jnp.concatenate([high, low]), flat_ada, by_last, preferred_element_type=F32
     )
     d_active = d_active[:latents] + d_active[latents:]
-    d_active = gate(d_active, *early_grads[1:]) if few_chips else d_active
     d_active = gather(d_active, ("dp", "tensor"), n_dp * n_tensor)
     d_active = jnp.sum(d_active.reshape(n_dp, n_tensor, latents, share_width), axis=1)
     d_active = d_active.transpose(1, 0, 2).reshape(latents, width)

time: 352 us -> 343 us (0.974)
  waiting for transfers between devices: 140 us -> 114 us
  blocking collectives: 0 us -> 11.3 us
  Pallas kernels: 64.4 us -> 71.1 us
    all_to_all x14 -> x13, waiting for transfers between devices: 56.2 us -> 35.5 us  [exchange(): return lax.all_to_all(blocks, axis, 0, 0, tiled=True)]
    all_to_all x0 -> x1, blocking collectives: none -> 11.3 us  [exchange(): return lax.all_to_all(blocks, axis, 0, 0, tiled=True)]
    ppermute x39, starting transfers between devices: 29.7 us -> 36.1 us  [swap(): return lax.ppermute(block, axis, route)]
    all_to_all x14 -> x13, starting transfers between devices: 55.9 us -> 50.9 us  [exchange(): return lax.all_to_all(blocks, axis, 0, 0, tiled=True)]
    ppermute x39, waiting for transfers between devices: 83.4 us -> 78.6 us  [swap(): return lax.ppermute(block, axis, route)]
    select_n x6 -> x3, other arithmetic: 5.92 us -> 1.31 us  [choose(): jnp.where(core == 0, first, second)]
    unnamed x134 -> x122, local copies, waits for them, and re-layouts: 15.9 us -> 19.4 us
  transfers between devices with their start and end apart: 53 -> 52, of which waited for: 24 -> 22; matrix products, arithmetic and copies ran while one was open for 12% -> 10% of each run, Pallas kernels for 13% -> 11%
where the time goes in v7:
time: 343 us
  waiting for transfers between devices  114 us (33%)
  starting transfers between devices  87 us (25%)
  Pallas kernels  71.1 us (21%)
  local copies, waits for them, and re-layouts  34.9 us (10%)
  other arithmetic  21.1 us (6%)
  blocking collectives  11.3 us (3%)
    ppermute x39, waiting for transfers between devices, swap(): return lax.ppermute(block, axis, route)  78.6 us
    all_to_all x13, starting transfers between devices, exchange(): return lax.all_to_all(blocks, axis, 0, 0, tiled=True)  50.9 us
    pallas_call x11, Pallas kernels, call(): pl.pallas_call(kernel, out_shape=tuple((jax.ShapeDtypeStruct(shape, kind)...  49.4 us
    ppermute x39, starting transfers between devices, swap(): return lax.ppermute(block, axis, route)  36.1 us
    all_to_all x13, waiting for transfers between devices, exchange(): return lax.all_to_all(blocks, axis, 0, 0, tiled=True)  35.5 us
    unnamed x122, local copies, waits for them, and re-layouts  19.4 us
    pallas_call x1, Pallas kernels, attend_backward(): pl.pallas_call(lambda *refs: backward_kernel(meta.shape[0] - 1, *refs), o...  11.6 us
    all_to_all x1, blocking collectives, exchange(): return lax.all_to_all(blocks, axis, 0, 0, tiled=True)  11.3 us
  transfers between devices with their start and end apart: 52, of which 22 were waited for; matrix products, arithmetic and copies ran while one was open for 10% of the time, Pallas kernels for 11%

profile of v7, /device:TPU:0, one launch (start us, length us, event | category | flops | bytes accessed | tf_op | source)
XLA Modules:
  0.0 343.1 jit_solution(17149769114538435985)
XLA Ops:
  5.6 4.8 %all-to-all-start = ((f32[8,18,288]{2,1,0:T(8,128)}), f32[8,18,288]{2,1,0:T(8,128)S(1)}, u32[]{:S(2)}, u32[]{:S(2)}) async-start(f32[8,18,288]{2,1,0:T(8,128)} %broadcast_in_dim.14), calls=%async_computation | async-start | bytes 589824 | tf_op jit(solution)/shard_map/all_to_all | solution.py:26
  10.4 7.3 %all-to-all-done = f32[8,18,288]{2,1,0:T(8,128)S(1)} async-done(((f32[8,18,288]{2,1,0:T(8,128)}), f32[8,18,288]{2,1,0:T(8,128)S(1)}, u32[]{:S(2)}, u32[]{:S(2)}) %all-to-all-start) | async-done | bytes 165920 | tf_op jit(solution)/shard_map/all_to_all | solution.py:26
  22.8 11.3 %all_to_all.70 = f32[4,18,288]{2,1,0:T(8,128)S(1)} all-to-all(f32[4,18,288]{2,1,0:T(8,128)S(1)} %broadcast_in_dim.15), channel_id=1, replica_groups=mesh['dp'=8,'tensor'=4] {'tensor'}, dimensions={0} | all-to-all | bytes 165888 | tf_op jit(solution)/shard_map/all_to_all | solution.py:26
  44.1 6.0 %project.1 = (bf16[256,1152]{1,0:T(8,128)(2,1)}, bf16[256,1152]{1,0:T(8,128)(2,1)}, bf16[8,72,640]{2,1,0:T(8,128)(2,1)}, bf16[1152,576]{1,0:T(8,128)(2,1)}, bf16...) custom-call(s32[7]{0:T(128)} %concatenate.33.refs_0_, bf16[288,576]{1,0:T(8,128)(2,1)} %get-tuple-element.68.refs_1_, ...), custom_call_target="tpu_custom_call" | custom-call | flops 1 | bytes 1 | tf_op jit(solution)/shard_map/project/pallas_call | solution.py:366
  50.1 3.7 %all-to-all-start.2 = ((bf16[8,72,640]{2,1,0:T(8,128)(2,1)}), bf16[8,72,640]{2,1,0:T(8,128)(2,1)S(1)}, u32[]{:S(2)}, u32[]{:S(2)}) async-start(bf16[8,72,640]{2,1,0:T(8,128)(2,1)} %get-tuple-element.72), calls=%async_computation.2 | async-start | bytes 1474560 | tf_op jit(solution)/shard_map/all_to_all | solution.py:26
  54.9 10.9 %all-to-all-done.2.refs_1_ = bf16[8,72,640]{2,1,0:T(8,128)(2,1)S(1)} async-done(((bf16[8,72,640]{2,1,0:T(8,128)(2,1)}), bf16[8,72,640]{2,1,0:T(8,128)(2,1)S(1)}, u32[]{:S(2)}, u32[]{:S(2)}) %all-to-all-start.2) | async-done | bytes 737312 | tf_op jit(solution)/shard_map/all_to_all | solution.py:26
  66.6 10.1 %attend_forward.1 = (bf16[8,72,128]{2,1,0:T(8,128)(2,1)}, f32[8,72,128]{2,1,0:T(8,128)}, f32[8,1,128]{2,1,0:T(1,128)}) custom-call(s32[4]{0:T(128)} %pad_add_fusion.refs_0_, bf16[8,72,640]{2,1,0:T(8,128)(2,1)} %copy-done.25), custom_call_target="tpu_custom_call" | custom-call | flops 1000000000 | bytes 4000000 | tf_op jit(solution)/shard_map/attend_forward/pallas_call | solution.py:215
  76.7 3.4 all-to-all-start.3
  80.2 5.5 %all-to-all-done.3.refs_1_ = bf16[8,72,128]{2,1,0:T(8,128)(2,1)S(1)} async-done(((bf16[8,72,128]{2,1,0:T(8,128)(2,1)}), bf16[8,72,128]{2,1,0:T(8,128)(2,1)S(1)}, u32[]{:S(2)}, u32[]{:S(2)}) %all-to-all-start.3) | async-done | bytes 147488 | tf_op jit(solution)/shard_map/all_to_all | solution.py:26
  89.4 4.9 %all-to-all-start.4 = ((bf16[4,64,1152]{2,1,0:T(8,128)(2,1)}), bf16[4,64,1152]{2,1,0:T(8,128)(2,1)S(1)}, u32[]{:S(2)}, u32[]{:S(2)}) async-start(bf16[4,64,1152]{2,1,0:T(8,128)(2,1)} %bitcast.76), calls=%async_computation.4 | async-start | bytes 1179648 | tf_op jit(solution)/shard_map/all_to_all | solution.py:26
  96.9 14.7 %collective-permute-done.10.refs_6_.refs_3_ = bf16[288,1152]{1,0:T(8,128)(2,1)S(1)} collective-permute-done((bf16[288,1152]{1,0:T(8,128)(2,1)}, bf16[288,1152]{1,0:T(8,128)(2,1)S(1)}, u32[]{:S(2)}, u32[]{:S(2)}) %collective-permute-start.10) | collective-permute-done | bytes 663584 | tf_op jit(solution)/shard_map/ppermute | solution.py:22
  116.2 4.8 %all-to-all-start.5 = ((bf16[4,64,1152]{2,1,0:T(8,128)(2,1)}), bf16[4,64,1152]{2,1,0:T(8,128)(2,1)S(1)}, u32[]{:S(2)}, u32[]{:S(2)}) async-start(bf16[4,64,1152]{2,1,0:T(8,128)(2,1)} %get-tuple-element.77), calls=%async_computation.5 | async-start | bytes 1179648 | tf_op jit(solution)/shard_map/all_to_all | solution.py:26
  124.0 13.7 %collective-permute-done.11.refs_0_ = bf16[288,1152]{1,0:T(8,128)(2,1)} collective-permute-done((bf16[288,1152]{1,0:T(8,128)(2,1)}, bf16[288,1152]{1,0:T(8,128)(2,1)}, u32[]{:S(2)}, u32[]{:S(2)}) %collective-permute-start.11) | collective-permute-done | bytes 663584 | tf_op jit(solution)/shard_map/ppermute | solution.py:22
  141.8 10.7 %mlp.1 = (bf16[256,1152]{1,0:T(8,128)(2,1)}, bf16[256,1152]{1,0:T(8,128)(2,1)}, bf16[256,1152]{1,0:T(8,128)(2,1)}, f32[1,1152]{1,0:T(1,128)}, bf16[256,1152]{1,0...) custom-call(s32[7]{0:T(128)} %concatenate.33.refs_0_, ...), custom_call_target="tpu_custom_call" | custom-call | flops 1 | bytes 1 | tf_op jit(solution)/shard_map/mlp/pallas_call | solution.py:366
  152.5 4.8 %all-to-all-start.6 = ((bf16[4,64,1152]{2,1,0:T(8,128)(2,1)}), bf16[4,64,1152]{2,1,0:T(8,128)(2,1)S(1)}, u32[]{:S(2)}, u32[]{:S(2)}) async-start(bf16[4,64,1152]{2,1,0:T(8,128)(2,1)} %bitcast.75), calls=%async_computation.6 | async-start | bytes 1179648 | tf_op jit(solution)/shard_map/all_to_all | solution.py:26
  161.2 6.0 %late_weights.1 = (bf16[288,1152]{1,0:T(8,128)(2,1)}, bf16[288,1152]{1,0:T(8,128)(2,1)}, bf16[288,1152]{1,0:T(8,128)(2,1)}, bf16[288,1152]{1,0:T(8,128)(2,1)}) custom-call(s32[7]{0:T(128)} %concatenate.33.refs_0_, bf16[256,1152]{1,0:T(8,128)(2,1)} %bitcast.65, bf16[256,1152]{1,0:T(8,128)(2,1)} %get-tuple-element.78.refs_10_.refs_2_, ...), custom_call_target="tpu_custom_call" | custom-call | flops 1 | bytes 1 | tf_op jit(solution)/shard_map/late_weights/pallas_call | solution.py:366
  167.2 6.4 %all-to-all-done.6.refs_1_ = bf16[4,64,1152]{2,1,0:T(8,128)(2,1)S(1)} async-done(((bf16[4,64,1152]{2,1,0:T(8,128)(2,1)}), bf16[4,64,1152]{2,1,0:T(8,128)(2,1)S(1)}, u32[]{:S(2)}, u32[]{:S(2)}) %all-to-all-start.6) | async-done | bytes 589856 | tf_op jit(solution)/shard_map/all_to_all | solution.py:26
  177.4 3.5 %all-to-all-start.7 = ((bf16[4,64,1152]{2,1,0:T(8,128)(2,1)}), bf16[4,64,1152]{2,1,0:T(8,128)(2,1)S(1)}, u32[]{:S(2)}, u32[]{:S(2)}) async-start(bf16[4,64,1152]{2,1,0:T(8,128)(2,1)} %get-tuple-element.91), calls=%async_computation.7 | async-start | bytes 1179648 | tf_op jit(solution)/shard_map/all_to_all | solution.py:26
  182.9 14.2 %collective-permute-done.18.refs_3_ = bf16[288,1152]{1,0:T(8,128)(2,1)S(1)} collective-permute-done((bf16[288,1152]{1,0:T(8,128)(2,1)}, bf16[288,1152]{1,0:T(8,128)(2,1)S(1)}, u32[]{:S(2)}, u32[]{:S(2)}) %collective-permute-start.18) | collective-permute-done | bytes 663584 | tf_op jit(solution)/shard_map/ppermute | solution.py:22
  204.6 3.5 %collective-permute-start.22 = (bf16[64,1152]{1,0:T(8,128)(2,1)}, bf16[64,1152]{1,0:T(8,128)(2,1)S(1)}, u32[]{:S(2)}, u32[]{:S(2)}) collective-permute-start(bf16[64,1152]{1,0:T(8,128)(2,1)} %gate.22), channel_id=1, source_target_pairs={{0,3},{1,2},{2,1},{3,0},{4,7},{5,6},{6,5},{7,4},{8,11},{9,10},{10,... | collective-permute-start | bytes 442376 | tf_op jit(solution)/shard_map/ppermute | solution.py:22
  210.8 11.6 %attend_backward.1.refs_0_ = bf16[8,72,640]{2,1,0:T(8,128)(2,1)} custom-call(s32[4]{0:T(128)} %pad_add_fusion.refs_0_, bf16[8,72,640]{2,1,0:T(8,128)(2,1)} %copy-done.25, bf16[8,72,128]{2,1,0:T(8,128)(2,1)} %copy-done.49, f32[8,72,128]{2,1,0:T(8,128)} %get-tuple-element.96.refs_3_, f32[8,1,128]{2,1,0:T(1,128)} %get-tuple-element.97.refs_4_), custom_call_target="tpu_custom_call" | custom-call | flops 3000000000 | bytes 4000000 | tf_op jit(solution)/shard_map/attend_backward/pallas_call | solution.py:239
  223.9 3.5 %all-to-all-start.9 = ((bf16[8,72,640]{2,1,0:T(8,128)(2,1)}), bf16[8,72,640]{2,1,0:T(8,128)(2,1)S(1)}, u32[]{:S(2)}, u32[]{:S(2)}) async-start(bf16[8,72,640]{2,1,0:T(8,128)(2,1)} %gate.23), calls=%async_computation.9 | async-start | bytes 1474560 | tf_op jit(solution)/shard_map/all_to_all | solution.py:26
  234.7 4.6 %collective-permute-done.23.refs_4_ = bf16[64,1152]{1,0:T(8,128)(2,1)S(1)} collective-permute-done((bf16[64,1152]{1,0:T(8,128)(2,1)}, bf16[64,1152]{1,0:T(8,128)(2,1)S(1)}, u32[]{:S(2)}, u32[]{:S(2)}) %collective-permute-start.23) | collective-permute-done | bytes 147488 | tf_op jit(solution)/shard_map/ppermute | solution.py:22
  239.4 6.8 %collective-permute-done.24.refs_5_ = bf16[64,1152]{1,0:T(8,128)(2,1)S(1)} collective-permute-done((bf16[64,1152]{1,0:T(8,128)(2,1)}, bf16[64,1152]{1,0:T(8,128)(2,1)S(1)}, u32[]{:S(2)}, u32[]{:S(2)}) %collective-permute-start.24) | collective-permute-done | bytes 147488 | tf_op jit(solution)/shard_map/ppermute | solution.py:22
  247.1 5.1 %unspread.1 = (bf16[256,1152]{1,0:T(8,128)(2,1)}, bf16[256,576]{1,0:T(8,128)(2,1)}, bf16[256,576]{1,0:T(8,128)(2,1)}, bf16[256,576]{1,0:T(8,128)(2,1)}, f32[2,576]{1,0:T(2,128)}) custom-call(s32[7]{0:T(128)} %concatenate.33.refs_0_, bf16[8,72,640]{2,1,0:T(8,128)(2,1)} %copy-done.6, bf16[1152,576]{1,0:T(8,128)(2,1)} %get-tuple-element.98.refs_2_, ...), custom_call_target="tpu_custom_call" | custom-call | flops 1 | bytes 1 | tf_op jit(solution)/shard_map/unspread/pallas_call | solution.py:366
  255.6 4.8 %all-to-all-start.10 = ((bf16[4,64,1152]{2,1,0:T(8,128)(2,1)}), bf16[4,64,1152]{2,1,0:T(8,128)(2,1)S(1)}, u32[]{:S(2)}, u32[]{:S(2)}) async-start(bf16[4,64,1152]{2,1,0:T(8,128)(2,1)} %bitcast.21), calls=%async_computation.10 | async-start | bytes 1179648 | tf_op jit(solution)/shard_map/all_to_all | solution.py:26
  260.3 8.4 %collective-permute-done.37 = bf16[288,1152]{1,0:T(8,128)(2,1)} collective-permute-done((bf16[288,1152]{1,0:T(8,128)(2,1)}, bf16[288,1152]{1,0:T(8,128)(2,1)}, u32[]{:S(2)}, u32[]{:S(2)}) %collective-permute-start.37) | collective-permute-done | bytes 663584 | tf_op jit(solution)/shard_map/ppermute | solution.py:22
  272.1 4.2 %all-to-all-done.10.refs_1_ = bf16[4,64,1152]{2,1,0:T(8,128)(2,1)S(1)} async-done(((bf16[4,64,1152]{2,1,0:T(8,128)(2,1)}), bf16[4,64,1152]{2,1,0:T(8,128)(2,1)S(1)}, u32[]{:S(2)}, u32[]{:S(2)}) %all-to-all-start.10) | async-done | bytes 589856 | tf_op jit(solution)/shard_map/all_to_all | solution.py:26
  284.6 4.9 %early_weights.1 = (bf16[288,576]{1,0:T(8,128)(2,1)}, bf16[288,576]{1,0:T(8,128)(2,1)}, bf16[288,576]{1,0:T(8,128)(2,1)}, bf16[288,576]{1,0:T(8,128)(2,1)}) custom-call(s32[7]{0:T(128)} %concatenate.33.refs_0_, bf16[256,1152]{1,0:T(8,128)(2,1)} %get-tuple-element.109.refs_1_, bf16[256,1152]{1,0:T(8,128)(2,1)} %bitcast.67, ...), custom_call_target="tpu_custom_call" | custom-call | flops 1 | bytes 1 | tf_op jit(solution)/shard_map/early_weights/pallas_call | solution.py:366
  299.6 3.5 %all-to-all-start.12 = ((f32[8,32,288]{2,1,0:T(8,128)}), f32[8,32,288]{2,1,0:T(8,128)S(1)}, u32[]{:S(2)}, u32[]{:S(2)}) async-start(f32[8,32,288]{2,1,0:T(8,128)} %broadcast_in_dim.32), calls=%async_computation.12 | async-start | bytes 786432 | tf_op jit(solution)/shard_map/all_to_all | solution.py:26
  308.9 3.8 %collective-permute-start.32 = (bf16[64,1152]{1,0:T(8,128)(2,1)S(1)}, bf16[64,1152]{1,0:T(8,128)(2,1)S(1)}, u32[]{:S(2)}, u32[]{:S(2)}) collective-permute-start(bf16[64,1152]{1,0:T(8,128)(2,1)S(1)} %copy-done.21), channel_id=1, source_target_pairs={{0,3},{1,2},{2,1},{3,0},{4,7},{5,6},{6,5},{7,4},{8,11},{9,10},{10,... | collective-permute-start | bytes 442376 | tf_op jit(solution)/shard_map/ppermute | solution.py:22
  312.7 5.6 %collective-permute-done.34.refs_2_ = bf16[288,576]{1,0:T(8,128)(2,1)S(1)} collective-permute-done((bf16[288,576]{1,0:T(8,128)(2,1)}, bf16[288,576]{1,0:T(8,128)(2,1)S(1)}, u32[]{:S(2)}, u32[]{:S(2)}) %collective-permute-start.34) | collective-permute-done | bytes 331808 | tf_op jit(solution)/shard_map/ppermute | solution.py:22
  (293 shorter events, 124.8 us)
Async XLA Ops:
  3.1 15.2 %collective-permute-start.1 = (bf16[144,576]{1,0:T(8,128)(2,1)S(1)}, bf16[144,576]{1,0:T(8,128)(2,1)S(1)}, u32[]{:S(2)}, u32[]{:S(2)}) collective-permute-start(bf16[144,576]{1,0:T(8,128)(2,1)S(1)} %broadcast_select_fusion.7), channel_id=1, source_target_pairs={{0,4},{4,0},{8,12},{12,8},{16,20},{20,16},{24,28},{28,24},{1,5},{5... | collective-permute-start | bytes 497672 | tf_op jit(solution)/shard_map/ppermute | solution.py:22
  19.3 15.6 %collective-permute-start.2 = (bf16[288,576]{1,0:T(8,128)(2,1)}, bf16[288,576]{1,0:T(8,128)(2,1)S(1)}, u32[]{:S(2)}, u32[]{:S(2)}) collective-permute-start(bf16[288,576]{1,0:T(8,128)(2,1)} %gate.15.refs_0_), channel_id=1, source_target_pairs={{0,8},{4,12},{8,0},{12,4},{16,24},{20,28},{24,16},{28,20},{1,9},{5... | collective-permute-start | bytes 995336 | tf_op jit(solution)/shard_map/ppermute | solution.py:22
  19.9 18.3 %collective-permute-start.3 = (bf16[288,576]{1,0:T(8,128)(2,1)}, bf16[288,576]{1,0:T(8,128)(2,1)S(1)}, u32[]{:S(2)}, u32[]{:S(2)}) collective-permute-start(bf16[288,576]{1,0:T(8,128)(2,1)} %gate.15.refs_0_), channel_id=1, source_target_pairs={{0,16},{4,20},{8,24},{12,28},{16,0},{20,4},{24,8},{28,12},{1,17},{... | collective-permute-start | bytes 995336 | tf_op jit(solution)/shard_map/ppermute | solution.py:22
  20.4 17.7 %collective-permute-start.4 = (bf16[288,576]{1,0:T(8,128)(2,1)}, bf16[288,576]{1,0:T(8,128)(2,1)S(1)}, u32[]{:S(2)}, u32[]{:S(2)}) collective-permute-start(bf16[288,576]{1,0:T(8,128)(2,1)} %gate.15.refs_0_), channel_id=1, source_target_pairs={{0,24},{4,28},{8,16},{12,20},{16,8},{20,12},{24,0},{28,4},{1,25},{... | collective-permute-start | bytes 995336 | tf_op jit(solution)/shard_map/ppermute | solution.py:22
  50.1 15.7 %all-to-all-start.2 = ((bf16[8,72,640]{2,1,0:T(8,128)(2,1)}), bf16[8,72,640]{2,1,0:T(8,128)(2,1)S(1)}, u32[]{:S(2)}, u32[]{:S(2)}) async-start(bf16[8,72,640]{2,1,0:T(8,128)(2,1)} %get-tuple-element.72), calls=%async_computation.2 | async-start | bytes 1474560 | tf_op jit(solution)/shard_map/all_to_all | solution.py:26
  53.8 26.3 %collective-permute-start = (bf16[144,1152]{1,0:T(8,128)(2,1)S(1)}, bf16[144,1152]{1,0:T(8,128)(2,1)S(1)}, u32[]{:S(2)}, u32[]{:S(2)}) collective-permute-start(bf16[144,1152]{1,0:T(8,128)(2,1)S(1)} %bitcast_select_fusion), channel_id=1, source_target_pairs={{0,4},{4,0},{8,12},{12,8},{16,20},{20,16},{24,28},{28,24},{1,5},{5... | collective-permute-start | bytes 995336 | tf_op jit(solution)/shard_map/ppermute | solution.py:22
  89.4 22.4 %all-to-all-start.4 = ((bf16[4,64,1152]{2,1,0:T(8,128)(2,1)}), bf16[4,64,1152]{2,1,0:T(8,128)(2,1)S(1)}, u32[]{:S(2)}, u32[]{:S(2)}) async-start(bf16[4,64,1152]{2,1,0:T(8,128)(2,1)} %bitcast.76), calls=%async_computation.4 | async-start | bytes 1179648 | tf_op jit(solution)/shard_map/all_to_all | solution.py:26
  95.2 16.4 %collective-permute-start.10 = (bf16[288,1152]{1,0:T(8,128)(2,1)}, bf16[288,1152]{1,0:T(8,128)(2,1)S(1)}, u32[]{:S(2)}, u32[]{:S(2)}) collective-permute-start(bf16[288,1152]{1,0:T(8,128)(2,1)} %gate.17.refs_1_), channel_id=1, source_target_pairs={{0,16},{4,20},{8,24},{12,28},{16,0},{20,4},{24,8},{28,12},{1,17},{... | collective-permute-start | bytes 1990664 | tf_op jit(solution)/shard_map/ppermute | solution.py:22
  95.7 16.1 %collective-permute-start.9 = (bf16[288,1152]{1,0:T(8,128)(2,1)}, bf16[288,1152]{1,0:T(8,128)(2,1)S(1)}, u32[]{:S(2)}, u32[]{:S(2)}) collective-permute-start(bf16[288,1152]{1,0:T(8,128)(2,1)} %gate.17.refs_1_), channel_id=1, source_target_pairs={{0,8},{4,12},{8,0},{12,4},{16,24},{20,28},{24,16},{28,20},{1,9},{5... | collective-permute-start | bytes 1990664 | tf_op jit(solution)/shard_map/ppermute | solution.py:22
  116.2 21.5 %all-to-all-start.5 = ((bf16[4,64,1152]{2,1,0:T(8,128)(2,1)}), bf16[4,64,1152]{2,1,0:T(8,128)(2,1)S(1)}, u32[]{:S(2)}, u32[]{:S(2)}) async-start(bf16[4,64,1152]{2,1,0:T(8,128)(2,1)} %get-tuple-element.77), calls=%async_computation.5 | async-start | bytes 1179648 | tf_op jit(solution)/shard_map/all_to_all | solution.py:26
  121.9 15.9 %collective-permute-start.11 = (bf16[288,1152]{1,0:T(8,128)(2,1)}, bf16[288,1152]{1,0:T(8,128)(2,1)}, u32[]{:S(2)}, u32[]{:S(2)}) collective-permute-start(bf16[288,1152]{1,0:T(8,128)(2,1)} %gate.18), channel_id=1, source_target_pairs={{0,24},{4,28},{8,16},{12,20},{16,8},{20,12},{24,0},{28,4},{1,25},{... | collective-permute-start | bytes 1990664 | tf_op jit(solution)/shard_map/ppermute | solution.py:22
  123.4 15.8 %collective-permute-start.12 = (bf16[288,1152]{1,0:T(8,128)(2,1)S(1)}, bf16[288,1152]{1,0:T(8,128)(2,1)}, u32[]{:S(2)}, u32[]{:S(2)}) collective-permute-start(bf16[288,1152]{1,0:T(8,128)(2,1)S(1)} %copy-done), channel_id=1, source_target_pairs={{0,4},{4,0},{8,12},{12,8},{16,20},{20,16},{24,28},{28,24},{1,5},{5... | collective-permute-start | bytes 1990664 | tf_op jit(solution)/shard_map/ppermute | solution.py:22
  123.4 15.8 %collective-permute-start.13 = (bf16[288,1152]{1,0:T(8,128)(2,1)S(1)}, bf16[288,1152]{1,0:T(8,128)(2,1)}, u32[]{:S(2)}, u32[]{:S(2)}) collective-permute-start(bf16[288,1152]{1,0:T(8,128)(2,1)S(1)} %copy-done.10), channel_id=1, source_target_pairs={{0,4},{4,0},{8,12},{12,8},{16,20},{20,16},{24,28},{28,24},{1,5},{5... | collective-permute-start | bytes 1990664 | tf_op jit(solution)/shard_map/ppermute | solution.py:22
  123.9 15.3 %collective-permute-start.14 = (bf16[288,1152]{1,0:T(8,128)(2,1)S(1)}, bf16[288,1152]{1,0:T(8,128)(2,1)}, u32[]{:S(2)}, u32[]{:S(2)}) collective-permute-start(bf16[288,1152]{1,0:T(8,128)(2,1)S(1)} %copy-done.8), channel_id=1, source_target_pairs={{0,4},{4,0},{8,12},{12,8},{16,20},{20,16},{24,28},{28,24},{1,5},{5... | collective-permute-start | bytes 1990664 | tf_op jit(solution)/shard_map/ppermute | solution.py:22
  152.5 21.0 %all-to-all-start.6 = ((bf16[4,64,1152]{2,1,0:T(8,128)(2,1)}), bf16[4,64,1152]{2,1,0:T(8,128)(2,1)S(1)}, u32[]{:S(2)}, u32[]{:S(2)}) async-start(bf16[4,64,1152]{2,1,0:T(8,128)(2,1)} %bitcast.75), calls=%async_computation.6 | async-start | bytes 1179648 | tf_op jit(solution)/shard_map/all_to_all | solution.py:26
  177.4 19.9 %all-to-all-start.7 = ((bf16[4,64,1152]{2,1,0:T(8,128)(2,1)}), bf16[4,64,1152]{2,1,0:T(8,128)(2,1)S(1)}, u32[]{:S(2)}, u32[]{:S(2)}) async-start(bf16[4,64,1152]{2,1,0:T(8,128)(2,1)} %get-tuple-element.91), calls=%async_computation.7 | async-start | bytes 1179648 | tf_op jit(solution)/shard_map/all_to_all | solution.py:26
  180.9 16.2 %collective-permute-start.18 = (bf16[288,1152]{1,0:T(8,128)(2,1)}, bf16[288,1152]{1,0:T(8,128)(2,1)S(1)}, u32[]{:S(2)}, u32[]{:S(2)}) collective-permute-start(bf16[288,1152]{1,0:T(8,128)(2,1)} %get-tuple-element.88.refs_7_), channel_id=1, source_target_pairs={{0,8},{4,12},{8,0},{12,4},{16,24},{20,28},{24,16},{28,20},{1,9},{5... | collective-permute-start | bytes 1990664 | tf_op jit(solution)/shard_map/ppermute | solution.py:22
  181.7 15.6 %collective-permute-start.19 = (bf16[288,1152]{1,0:T(8,128)(2,1)S(1)}, bf16[288,1152]{1,0:T(8,128)(2,1)S(1)}, u32[]{:S(2)}, u32[]{:S(2)}) collective-permute-start(bf16[288,1152]{1,0:T(8,128)(2,1)S(1)} %copy-done.28), channel_id=1, source_target_pairs={{0,16},{4,20},{8,24},{12,28},{16,0},{20,4},{24,8},{28,12},{1,17},{... | collective-permute-start | bytes 1990664 | tf_op jit(solution)/shard_map/ppermute | solution.py:22
  204.6 17.9 %collective-permute-start.22 = (bf16[64,1152]{1,0:T(8,128)(2,1)}, bf16[64,1152]{1,0:T(8,128)(2,1)S(1)}, u32[]{:S(2)}, u32[]{:S(2)}) collective-permute-start(bf16[64,1152]{1,0:T(8,128)(2,1)} %gate.22), channel_id=1, source_target_pairs={{0,3},{1,2},{2,1},{3,0},{4,7},{5,6},{6,5},{7,4},{8,11},{9,10},{10,... | collective-permute-start | bytes 442376 | tf_op jit(solution)/shard_map/ppermute | solution.py:22
  223.9 22.3 %all-to-all-start.9 = ((bf16[8,72,640]{2,1,0:T(8,128)(2,1)}), bf16[8,72,640]{2,1,0:T(8,128)(2,1)S(1)}, u32[]{:S(2)}, u32[]{:S(2)}) async-start(bf16[8,72,640]{2,1,0:T(8,128)(2,1)} %gate.23), calls=%async_computation.9 | async-start | bytes 1474560 | tf_op jit(solution)/shard_map/all_to_all | solution.py:26
  252.2 16.5 %collective-permute-start.37 = (bf16[288,1152]{1,0:T(8,128)(2,1)}, bf16[288,1152]{1,0:T(8,128)(2,1)}, u32[]{:S(2)}, u32[]{:S(2)}) collective-permute-start(bf16[288,1152]{1,0:T(8,128)(2,1)} %gate.29), channel_id=1, source_target_pairs={{0,24},{4,28},{8,16},{12,20},{16,8},{20,12},{24,0},{28,4},{1,25},{... | collective-permute-start | bytes 1990664 | tf_op jit(solution)/shard_map/ppermute | solution.py:22
  255.0 29.5 %collective-permute-start.26 = (bf16[256,1152]{1,0:T(8,128)(2,1)}, bf16[256,1152]{1,0:T(8,128)(2,1)}, u32[]{:S(2)}, u32[]{:S(2)}) collective-permute-start(bf16[256,1152]{1,0:T(8,128)(2,1)} %get-tuple-element.109.refs_1_), channel_id=1, source_target_pairs={{0,4},{4,0},{8,12},{12,8},{16,20},{20,16},{24,28},{28,24},{1,5},{5... | collective-permute-start | bytes 1769480 | tf_op jit(solution)/shard_map/ppermute | solution.py:22
  255.0 29.5 %collective-permute-start.27 = (bf16[256,1152]{1,0:T(8,128)(2,1)S(1)}, bf16[256,1152]{1,0:T(8,128)(2,1)}, u32[]{:S(2)}, u32[]{:S(2)}) collective-permute-start(bf16[256,1152]{1,0:T(8,128)(2,1)S(1)} %bitcast.68), channel_id=1, source_target_pairs={{0,4},{4,0},{8,12},{12,8},{16,20},{20,16},{24,28},{28,24},{1,5},{5... | collective-permute-start | bytes 1769480 | tf_op jit(solution)/shard_map/ppermute | solution.py:22
  255.6 20.8 %all-to-all-start.10 = ((bf16[4,64,1152]{2,1,0:T(8,128)(2,1)}), bf16[4,64,1152]{2,1,0:T(8,128)(2,1)S(1)}, u32[]{:S(2)}, u32[]{:S(2)}) async-start(bf16[4,64,1152]{2,1,0:T(8,128)(2,1)} %bitcast.21), calls=%async_computation.10 | async-start | bytes 1179648 | tf_op jit(solution)/shard_map/all_to_all | solution.py:26
  271.6 31.4 %collective-permute-start.38 = (f32[144,1152]{1,0:T(8,128)}, f32[144,1152]{1,0:T(8,128)}, u32[]{:S(2)}, u32[]{:S(2)}) collective-permute-start(f32[144,1152]{1,0:T(8,128)} %slice_select_fusion), channel_id=1, source_target_pairs={{0,4},{4,0},{8,12},{12,8},{16,20},{20,16},{24,28},{28,24},{1,5},{5... | collective-permute-start | bytes 1990664 | tf_op jit(solution)/shard_map/ppermute | solution.py:22
  289.5 28.8 %collective-permute-start.35 = (bf16[288,576]{1,0:T(8,128)(2,1)}, bf16[288,576]{1,0:T(8,128)(2,1)S(1)}, u32[]{:S(2)}, u32[]{:S(2)}) collective-permute-start(bf16[288,576]{1,0:T(8,128)(2,1)} %get-tuple-element.114.refs_1_), channel_id=1, source_target_pairs={{0,24},{4,28},{8,16},{12,20},{16,8},{20,12},{24,0},{28,4},{1,25},{... | collective-permute-start | bytes 995336 | tf_op jit(solution)/shard_map/ppermute | solution.py:22
  292.7 35.4 %collective-permute-start.30 = (bf16[64,1152]{1,0:T(8,128)(2,1)}, bf16[64,1152]{1,0:T(8,128)(2,1)S(1)}, u32[]{:S(2)}, u32[]{:S(2)}) collective-permute-start(bf16[64,1152]{1,0:T(8,128)(2,1)} %gate.26.refs_0_), channel_id=1, source_target_pairs={{0,1},{1,0},{2,3},{3,2},{4,5},{5,4},{6,7},{7,6},{8,9},{9,8},{10,11... | collective-permute-start | bytes 442376 | tf_op jit(solution)/shard_map/ppermute | solution.py:22
  294.7 33.4 %collective-permute-start.31 = (bf16[64,1152]{1,0:T(8,128)(2,1)}, bf16[64,1152]{1,0:T(8,128)(2,1)}, u32[]{:S(2)}, u32[]{:S(2)}) collective-permute-start(bf16[64,1152]{1,0:T(8,128)(2,1)} %gate.26.refs_0_), channel_id=1, source_target_pairs={{0,2},{1,3},{2,0},{3,1},{4,6},{5,7},{6,4},{7,5},{8,10},{9,11},{10,... | collective-permute-start | bytes 442376 | tf_op jit(solution)/shard_map/ppermute | solution.py:22
  299.6 21.0 %all-to-all-start.12 = ((f32[8,32,288]{2,1,0:T(8,128)}), f32[8,32,288]{2,1,0:T(8,128)S(1)}, u32[]{:S(2)}, u32[]{:S(2)}) async-start(f32[8,32,288]{2,1,0:T(8,128)} %broadcast_in_dim.32), calls=%async_computation.12 | async-start | bytes 786432 | tf_op jit(solution)/shard_map/all_to_all | solution.py:26
  303.1 15.2 %collective-permute-start.34 = (bf16[288,576]{1,0:T(8,128)(2,1)}, bf16[288,576]{1,0:T(8,128)(2,1)S(1)}, u32[]{:S(2)}, u32[]{:S(2)}) collective-permute-start(bf16[288,576]{1,0:T(8,128)(2,1)} %get-tuple-element.117), channel_id=1, source_target_pairs={{0,16},{4,20},{8,24},{12,28},{16,0},{20,4},{24,8},{28,12},{1,17},{... | collective-permute-start | bytes 995336 | tf_op jit(solution)/shard_map/ppermute | solution.py:22
  308.9 19.2 %collective-permute-start.32 = (bf16[64,1152]{1,0:T(8,128)(2,1)S(1)}, bf16[64,1152]{1,0:T(8,128)(2,1)S(1)}, u32[]{:S(2)}, u32[]{:S(2)}) collective-permute-start(bf16[64,1152]{1,0:T(8,128)(2,1)S(1)} %copy-done.21), channel_id=1, source_target_pairs={{0,3},{1,2},{2,1},{3,0},{4,7},{5,6},{6,5},{7,4},{8,11},{9,10},{10,... | collective-permute-start | bytes 442376 | tf_op jit(solution)/shard_map/ppermute | solution.py:22
  320.5 19.2 %collective-permute-start.36 = (f32[144,576]{1,0:T(8,128)}, f32[144,576]{1,0:T(8,128)}, u32[]{:S(2)}, u32[]{:S(2)}) collective-permute-start(f32[144,576]{1,0:T(8,128)} %slice_select_fusion.2), channel_id=1, source_target_pairs={{0,4},{4,0},{8,12},{12,8},{16,20},{20,16},{24,28},{28,24},{1,5},{5... | collective-permute-start | bytes 995336 | tf_op jit(solution)/shard_map/ppermute | solution.py:22
  (78 other events, 393.8 us)

commit v8 on v7

--- a/solution.py
+++ b/solution.py
@@ -357,7 +357,7 @@
     return [pl.BlockSpec(memory_space=pltpu.VMEM)] * count
 
 
-def call(body, name, meta, arrays, outs, scratch=(), anywhere=0, due=()):
+def call(body, name, meta, arrays, outs, scratch=(), anywhere=0, due=(), flops=1):
     count = 1 + len(arrays)
 
     def kernel(*refs):
@@ -373,7 +373,7 @@
         out_specs=tuple(vmem(len(outs))),
         scratch_shapes=list(scratch),
         compiler_params=pltpu.CompilerParams(vmem_limit_bytes=VMEM_BYTES),
-        cost_estimate=pl.CostEstimate(flops=1, bytes_accessed=1, transcendentals=0),
+        cost_estimate=pl.CostEstimate(flops=flops, bytes_accessed=1, transcendentals=0),
         name=name,
     )(meta, *arrays, *due)
 
@@ -443,10 +443,17 @@
 
 def project_kernel(latents, count, meta_ref, *refs):
     mine, other = refs[:count], refs[count : 2 * count]
-    tokens_ref, cot_ref, mod_ref, bias_ref = refs[2 * count : 2 * count + 4]
-    hidden_ref, d_mlp_ref, packed_ref, qk_ref, vp_ref, d_bias_ref, sems = refs[2 * count + 4 :]
+    tokens_ref, cot_ref, mod_parts_ref, bias_ref = refs[2 * count : 2 * count + 4]
+    hidden_ref, d_mlp_ref, packed_ref, qk_ref, vp_ref, d_bias_ref, mod_ref, sems = refs[2 * count + 4 :]
     rows, width = tokens_ref.shape
     place_pair(meta_ref, mine, other, qk_ref, vp_ref, sems)
+    columns = mod_parts_ref.shape[2]
+    pieces = width // columns
+    for piece in range(pieces):
+        total = mod_parts_ref[piece].astype(F32)
+        for part in range(piece + pieces, mod_parts_ref.shape[0], pieces):
+            total = total + mod_parts_ref[part].astype(F32)
+        mod_ref[:, piece * columns : (piece + 1) * columns] = total
     masks = row_masks(meta_ref, latents, meta_ref[1], rows)
     unit, _ = normed(tokens_ref[...].astype(F32))
     hidden = unit * (1.0 + rows_of(mod_ref, masks, 1)) + rows_of(mod_ref, masks, 0)
@@ -688,6 +695,43 @@
     bias_ref[place : place + 2, :] = qv_bias_ref[:, :columns]
 
 
+def finish_kernel(
+    latents, meta_ref, sums_ref, active_ref, w_ada_ref,
+    w_grad_ref, b_grad_ref, d_active_ref, fc2_ref, proj_ref, fc1_ref, qv_ref, total_ref,
+):
+    total = sums_ref[0]
+    for part in range(1, sums_ref.shape[0]):
+        total = total + sums_ref[part]
+    total_ref[...] = total
+    by_last = (((1,), (1,)), ((), ()))
+    d_active = jnp.zeros(d_active_ref.shape, F32)
+    for feature in range(6):
+        rows = [
+            total_ref[number * 6 + feature : number * 6 + feature + 1, :] for number in range(latents)
+        ]
+        grad = active_ref[:, 0:1] * rows[0]
+        bias = rows[0]
+        for number in range(1, latents):
+            grad = grad + active_ref[:, number : number + 1] * rows[number]
+            bias = bias + rows[number]
+        w_grad_ref[feature] = grad
+        b_grad_ref[feature : feature + 1, :] = bias
+        wide = jnp.concatenate(rows, axis=0)
+        high = wide.astype(BF16)
+        low = (wide - high.astype(F32)).astype(BF16)
+        weight = w_ada_ref[feature]
+        d_active += lax.dot_general(high, weight, by_last, preferred_element_type=F32)
+        d_active += lax.dot_general(low, weight, by_last, preferred_element_type=F32)
+    d_active_ref[...] = d_active
+    columns = total_ref.shape[1]
+    place = 6 * latents
+    for ref in (fc2_ref, proj_ref, fc1_ref):
+        for start in range(0, ref.shape[1], columns):
+            ref[:, start : start + columns] = total_ref[place : place + 1, :]
+            place += 1
+    qv_ref[...] = total_ref[place : place + 2, :]
+
+
 def latent_index(latent_len, first_row, row_count, token_total):
     positions = first_row + jnp.arange(row_count, dtype=jnp.int32)
     ends = jnp.cumsum(latent_len, dtype=jnp.int32)
@@ -754,15 +798,14 @@
     flat_ada = w_ada.reshape(share_width, 6 * features)
     mod_part = jnp.dot(own_activated, flat_ada, preferred_element_type=F32)
     mod_part = mod_part.reshape(latents * 6, features)
-    mod_mine = jnp.sum(gather(mod_part, "dp", n_dp), axis=0)
-    mod_mine = mod_mine + jnp.tile(b_ada.astype(F32), (latents, 1))
+    bias_ada = jnp.tile(b_ada.astype(F32), (latents, 1))
     few_chips = n_dp // 2 == 4
-    early_rows = gate(early_rows, mod_mine)
+    early_rows = gate(early_rows, mod_part)
+    mod_mine = jnp.sum(gather(mod_part, "dp", n_dp), axis=0) + bias_ada
+    mod_parts = gather(mod_mine, "tensor", n_tensor)
     early_parts = chip_parts(early_rows) if few_chips else [gather_chips(early_rows)]
-    modulation = gather(mod_mine, "tensor", n_tensor).transpose(1, 0, 2).reshape(6 * latents, width)
-
-    mod_rows = modulation
-    early_parts = list(gate_all(early_parts, modulation))
+
+    early_parts = list(gate_all(early_parts, mod_parts))
     early_parts += [swap(part, "dp", 1) for part in early_parts]
     count = len(early_parts) // 2
     meta = jnp.stack([core, my_dp * rows, my_tensor, my_dp // 2]).astype(jnp.int32)
@@ -771,14 +814,14 @@
     by_last = (((1,), (1,)), ((), ()))
     by_token = (((0,), (0,)), ((), ()))
     bias = jnp.concatenate([b_qv[0], jnp.zeros_like(b_qv[0]), b_qv[1], jnp.zeros_like(b_qv[0])])
-    hidden_one, d_mlp, packed, full_qk, full_vp, d_bias_fc2 = call(
+    hidden_one, d_mlp, packed, full_qk, full_vp, d_bias_fc2, mod_rows = call(
         lambda *refs: project_kernel(latents, count, *refs),
         "project",
         place_meta,
-        (*early_parts, tokens, cotangent, mod_rows, bias.astype(F32).reshape(2, -1)),
+        (*early_parts, tokens, cotangent, mod_parts, bias.astype(F32).reshape(2, -1)),
         (((rows, width), BF16), ((rows, width), BF16), ((2 * heads, DH, rows * 5 // 2), BF16))
         + (((width, 2 * features), BF16),) * 2
-        + (((1, width), F32),),
+        + (((1, width), F32), ((6 * latents, width), F32)),
         [pltpu.SemaphoreType.DMA((2, count))],
         2 * count,
     )
@@ -872,7 +915,6 @@
         (*mlp_parts, residual_mid, cotangent, mod_rows, b_fc2.reshape(1, -1)),
         (((share, width), BF16), ((latents, width), F32)),
     )
-    result_parts = [result_own] + [swap(result_own, "tensor", bits) for bits in range(1, n_tensor)]
     d_one_part, d_qk, d_vp, d_sent, d_bias_qv = call(
         unspread_kernel,
         "unspread",
@@ -881,11 +923,25 @@
         (((rows, width), BF16),)
         + (((rows, 2 * features), BF16),) * 3
         + (((2, 2 * features), F32),),
-        due=result_parts[1:],
-    )
+        flops=2 * 10**10,
+    )
+    result_parts = [result_own] + [swap(result_own, "tensor", bits) for bits in range(1, n_tensor)]
+    d_one_part = gate(d_one_part, *result_parts[1:])
     d_one_parts = exchange_shares(d_one_part, "tensor")
-    result = in_order(result_parts, "tensor")
-
+
+    if few_chips:
+        late_grads.append(swap(gate(late_blocks[-1], d_one_part), "dp", n_dp - 2))
+    right_other = swap(d_sent, "dp", 1)
+    early_blocks = call(
+        lambda *refs: weight_kernel(
+            [(0, 2), (5, 7)], [(0, 3), (1, 4), (5, 7), (6, 8)], *refs
+        ),
+        "early_weights",
+        place_meta,
+        (hidden_one, d_attn, d_qk, d_vp, attended, hidden_other, d_attn_other, right_other, attended_other),
+        (((width // chips, 2 * features), BF16),) * chips,
+        [pltpu.VMEM((width, 2 * features), BF16)],
+    )
     grad_own, d_mod_part, bias_rows = call(
         lambda *refs: first_back_kernel(latents, *refs),
         "first_back",
@@ -895,41 +951,26 @@
         (((share, width), BF16), ((n_tensor, 6 * latents, features), F32))
         + (((2 * (width // features) + units // features + 2, features), F32),),
         [pltpu.VMEM((2 * latents, width), F32)],
-    )
-    if few_chips:
-        late_grads.append(swap(gate(late_blocks[-1], d_one_part), "dp", n_dp - 2))
-    right_other = swap(gate(d_sent, d_one_parts), "dp", 1)
-    early_blocks = call(
-        lambda *refs: weight_kernel(
-            [(0, 2), (5, 7)], [(0, 3), (1, 4), (5, 7), (6, 8)], *refs
-        ),
-        "early_weights",
-        place_meta,
-        (hidden_one, d_attn, d_qk, d_vp, attended, hidden_other, d_attn_other, right_other, attended_other),
-        (((width // chips, 2 * features), BF16),) * chips,
-        [pltpu.VMEM((width, 2 * features), BF16)],
-        due=[d_mod_part],
-    )
-    early_grads = sum_chips(early_blocks)
-
-    d_mod_mine = jnp.sum(gate(exchange(d_mod_part, "tensor"), early_blocks[-1]), axis=0)
+        due=early_blocks,
+    )
+    early_grads = sum_chips(gate_all(early_blocks, d_mod_part))
+    d_mod_mine = exchange(d_mod_part, "tensor")
+    d_mod_mine = jnp.sum(gate(d_mod_mine, *early_grads[1:3]) if few_chips else d_mod_mine, axis=0)
     grad_own = gate(grad_own, d_mod_mine)
     grad_parts = [grad_own] + [swap(grad_own, "tensor", bits) for bits in range(1, n_tensor)]
     sums = gather(jnp.concatenate([d_mod_mine, bias_rows]), "dp", n_dp)
-    sums = jnp.sum(gate(sums, *early_grads[1:]) if few_chips else sums, axis=0)
+    sums = gate(sums, early_grads[3]) if few_chips else sums
     grad_tokens = in_order(gate_all(grad_parts, sums), "tensor").astype(F32)
-    d_mod = sums[: 6 * latents].reshape(latents, 6 * features)
-    bias_total = sums[6 * latents :].reshape(-1)
-    grad_b_ada = jnp.sum(d_mod, axis=0).reshape(6, features)
-    grad_w_ada = lax.dot_general(
-        own_activated.astype(F32), d_mod, by_token, precision=lax.Precision.HIGHEST
-    ).reshape(share_width, 6, features)
-    high = d_mod.astype(BF16)
-    low = (d_mod - high.astype(F32)).astype(BF16)
-    d_active = lax.dot_general(
-        jnp.concatenate([high, low]), flat_ada, by_last, preferred_element_type=F32
-    )
-    d_active = d_active[:latents] + d_active[latents:]
+    result = in_order(gate_all(result_parts, sums), "tensor")
+    grad_w_ada, grad_b_ada, d_active, sum_b_fc2, sum_b_proj, sum_b_fc1, sum_b_qv = call(
+        lambda *refs: finish_kernel(latents, *refs),
+        "finish",
+        meta,
+        (sums, own_activated.astype(F32).T, w_ada.transpose(1, 0, 2)),
+        (((6, share_width, features), F32), ((6, features), F32), ((latents, share_width), F32))
+        + (((1, width), F32), ((1, width), F32), ((1, units), F32), ((2, features), F32)),
+        [pltpu.VMEM(sums.shape[1:], F32)],
+    )
     d_active = gather(d_active, ("dp", "tensor"), n_dp * n_tensor)
     d_active = jnp.sum(d_active.reshape(n_dp, n_tensor, latents, share_width), axis=1)
     d_active = d_active.transpose(1, 0, 2).reshape(latents, width)
@@ -944,16 +985,16 @@
         result,
         grad_tokens,
         grad_cond,
-        grad_w_ada,
+        grad_w_ada.transpose(1, 0, 2),
         grad_b_ada,
         grad_qkv,
-        bias_total[2 * width + units :].reshape(2, features),
+        sum_b_qv,
         grad_vp[:, features:].T,
-        bias_total[width : 2 * width],
+        sum_b_proj[0],
         grad_fc1,
-        bias_total[2 * width : 2 * width + units],
+        sum_b_fc1[0],
         grad_fc2.T,
-        bias_total[:width],
+        sum_b_fc2[0],
     )
 
 

time: 343 us -> 343 us (level)
  waiting for transfers between devices: 114 us -> 123 us
  starting transfers between devices: 87 us -> 83.4 us
    all_to_all x13, waiting for transfers between devices: 35.5 us -> 58.5 us  [exchange(): return lax.all_to_all(blocks, axis, 0, 0, tiled=True)]
    ppermute x39, waiting for transfers between devices: 78.6 us -> 65 us  [swap(): return lax.ppermute(block, axis, route)]
    ppermute x39, starting transfers between devices: 36.1 us -> 31.7 us  [swap(): return lax.ppermute(block, axis, route)]
    slice x6 -> x0, local copies, waits for them, and re-layouts: 4.14 us -> none  [the longest x2 1.5 us: local(): bias_total[:width]]
    pallas_call x11 -> x12, Pallas kernels: 49.4 us -> 52.5 us  [call(): pl.pallas_call(kernel, out_shape=tuple((jax.ShapeDtypeStruct(shape, kind)...]
    unnamed x122 -> x130, local copies, waits for them, and re-layouts: 19.4 us -> 19.2 us
  transfers between devices with their start and end apart: 52 -> 52, of which waited for: 22 -> 23; matrix products, arithmetic and copies ran while one was open for 10% -> 9% of each run, Pallas kernels for 11% -> 12%
where the time goes in v8:
time: 343 us; the launch traced here: 341 us
  waiting for transfers between devices  123 us (36%)
  starting transfers between devices  83.4 us (24%)
  Pallas kernels  69.7 us (20%)
  local copies, waits for them, and re-layouts  31.8 us (9%)
  other arithmetic  20 us (6%)
  blocking collectives  11.4 us (3%)
    ppermute x39, waiting for transfers between devices, swap(): return lax.ppermute(block, axis, route)  65 us
    all_to_all x13, waiting for transfers between devices, exchange(): return lax.all_to_all(blocks, axis, 0, 0, tiled=True)  58.5 us
    pallas_call x12, Pallas kernels, call(): pl.pallas_call(kernel, out_shape=tuple((jax.ShapeDtypeStruct(shape, kind)...  52.5 us
    all_to_all x13, starting transfers between devices, exchange(): return lax.all_to_all(blocks, axis, 0, 0, tiled=True)  51.7 us
    ppermute x39, starting transfers between devices, swap(): return lax.ppermute(block, axis, route)  31.7 us
    unnamed x130, local copies, waits for them, and re-layouts  19.2 us
    all_to_all x1, blocking collectives, exchange(): return lax.all_to_all(blocks, axis, 0, 0, tiled=True)  11.4 us
    pallas_call x1, Pallas kernels, attend_backward(): pl.pallas_call(lambda *refs: backward_kernel(meta.shape[0] - 1, *refs), o...  9.2 us
  transfers between devices with their start and end apart: 52, of which 23 were waited for; matrix products, arithmetic and copies ran while one was open for 9% of the time, Pallas kernels for 12%

profile of v8, /device:TPU:0, one launch (start us, length us, event | category | flops | bytes accessed | tf_op | source)
XLA Modules:
  0.0 341.4 jit_solution(7736569440210430689)
XLA Ops:
  12.9 4.2 %all-to-all-start = ((f32[8,18,288]{2,1,0:T(8,128)}), f32[8,18,288]{2,1,0:T(8,128)S(1)}, u32[]{:S(2)}, u32[]{:S(2)}) async-start(f32[8,18,288]{2,1,0:T(8,128)} %broadcast_in_dim.11), calls=%async_computation | async-start | bytes 589824 | tf_op jit(solution)/shard_map/all_to_all | solution.py:26
  17.1 15.5 %all-to-all-done = f32[8,18,288]{2,1,0:T(8,128)S(1)} async-done(((f32[8,18,288]{2,1,0:T(8,128)}), f32[8,18,288]{2,1,0:T(8,128)S(1)}, u32[]{:S(2)}, u32[]{:S(2)}) %all-to-all-start) | async-done | bytes 165920 | tf_op jit(solution)/shard_map/all_to_all | solution.py:26
  32.7 11.4 %all_to_all.70.refs_4_.refs_11_ = f32[4,18,288]{2,1,0:T(8,128)} all-to-all(f32[4,18,288]{2,1,0:T(8,128)S(1)} %broadcast_in_dim.12), channel_id=1, replica_groups=mesh['dp'=8,'tensor'=4] {'tensor'}, dimensions={0} | all-to-all | bytes 165888 | tf_op jit(solution)/shard_map/all_to_all | solution.py:26
  50.1 6.1 %project.1 = (bf16[256,1152]{1,0:T(8,128)(2,1)}, bf16[256,1152]{1,0:T(8,128)(2,1)}, bf16[8,72,640]{2,1,0:T(8,128)(2,1)}, bf16[1152,576]{1,0:T(8,128)(2,1)}, bf16...) custom-call(s32[7]{0:T(128)} %concatenate.30.refs_0_, bf16[288,576]{1,0:T(8,128)(2,1)} %get-tuple-element.84.refs_1_, ...), custom_call_target="tpu_custom_call" | custom-call | flops 1 | bytes 1 | tf_op jit(solution)/shard_map/project/pallas_call | solution.py:366
  56.3 3.7 %all-to-all-start.2 = ((bf16[8,72,640]{2,1,0:T(8,128)(2,1)}), bf16[8,72,640]{2,1,0:T(8,128)(2,1)S(1)}, u32[]{:S(2)}, u32[]{:S(2)}) async-start(bf16[8,72,640]{2,1,0:T(8,128)(2,1)} %get-tuple-element.88), calls=%async_computation.2 | async-start | bytes 1474560 | tf_op jit(solution)/shard_map/all_to_all | solution.py:26
  61.1 10.9 %all-to-all-done.2.refs_1_ = bf16[8,72,640]{2,1,0:T(8,128)(2,1)S(1)} async-done(((bf16[8,72,640]{2,1,0:T(8,128)(2,1)}), bf16[8,72,640]{2,1,0:T(8,128)(2,1)S(1)}, u32[]{:S(2)}, u32[]{:S(2)}) %all-to-all-start.2) | async-done | bytes 737312 | tf_op jit(solution)/shard_map/all_to_all | solution.py:26
  72.9 7.9 %attend_forward.1 = (bf16[8,72,128]{2,1,0:T(8,128)(2,1)}, f32[8,72,128]{2,1,0:T(8,128)}, f32[8,1,128]{2,1,0:T(1,128)}) custom-call(s32[4]{0:T(128)} %pad_add_fusion.refs_0_, bf16[8,72,640]{2,1,0:T(8,128)(2,1)} %copy-done.33), custom_call_target="tpu_custom_call" | custom-call | flops 1000000000 | bytes 4000000 | tf_op jit(solution)/shard_map/attend_forward/pallas_call | solution.py:215
  84.3 5.5 %all-to-all-done.3.refs_1_ = bf16[8,72,128]{2,1,0:T(8,128)(2,1)S(1)} async-done(((bf16[8,72,128]{2,1,0:T(8,128)(2,1)}), bf16[8,72,128]{2,1,0:T(8,128)(2,1)S(1)}, u32[]{:S(2)}, u32[]{:S(2)}) %all-to-all-start.3) | async-done | bytes 147488 | tf_op jit(solution)/shard_map/all_to_all | solution.py:26
  93.5 3.5 %all-to-all-start.4 = ((bf16[4,64,1152]{2,1,0:T(8,128)(2,1)}), bf16[4,64,1152]{2,1,0:T(8,128)(2,1)S(1)}, u32[]{:S(2)}, u32[]{:S(2)}) async-start(bf16[4,64,1152]{2,1,0:T(8,128)(2,1)} %bitcast.74), calls=%async_computation.4 | async-start | bytes 1179648 | tf_op jit(solution)/shard_map/all_to_all | solution.py:26
  99.6 14.9 %collective-permute-done.10.refs_6_.refs_3_ = bf16[288,1152]{1,0:T(8,128)(2,1)S(1)} collective-permute-done((bf16[288,1152]{1,0:T(8,128)(2,1)}, bf16[288,1152]{1,0:T(8,128)(2,1)S(1)}, u32[]{:S(2)}, u32[]{:S(2)}) %collective-permute-start.10) | collective-permute-done | bytes 663584 | tf_op jit(solution)/shard_map/ppermute | solution.py:22
  118.6 4.8 %all-to-all-start.5 = ((bf16[4,64,1152]{2,1,0:T(8,128)(2,1)}), bf16[4,64,1152]{2,1,0:T(8,128)(2,1)S(1)}, u32[]{:S(2)}, u32[]{:S(2)}) async-start(bf16[4,64,1152]{2,1,0:T(8,128)(2,1)} %get-tuple-element.94), calls=%async_computation.5 | async-start | bytes 1179648 | tf_op jit(solution)/shard_map/all_to_all | solution.py:26
  126.4 14.0 %collective-permute-done.11.refs_0_ = bf16[288,1152]{1,0:T(8,128)(2,1)} collective-permute-done((bf16[288,1152]{1,0:T(8,128)(2,1)}, bf16[288,1152]{1,0:T(8,128)(2,1)}, u32[]{:S(2)}, u32[]{:S(2)}) %collective-permute-start.11) | collective-permute-done | bytes 663584 | tf_op jit(solution)/shard_map/ppermute | solution.py:22
  144.5 10.7 %mlp.1 = (bf16[256,1152]{1,0:T(8,128)(2,1)}, bf16[256,1152]{1,0:T(8,128)(2,1)}, bf16[256,1152]{1,0:T(8,128)(2,1)}, f32[1,1152]{1,0:T(1,128)}, bf16[256,1152]{1,0...) custom-call(s32[7]{0:T(128)} %concatenate.30.refs_0_, ...), custom_call_target="tpu_custom_call" | custom-call | flops 1 | bytes 1 | tf_op jit(solution)/shard_map/mlp/pallas_call | solution.py:366
  155.2 4.8 %all-to-all-start.6 = ((bf16[4,64,1152]{2,1,0:T(8,128)(2,1)}), bf16[4,64,1152]{2,1,0:T(8,128)(2,1)S(1)}, u32[]{:S(2)}, u32[]{:S(2)}) async-start(bf16[4,64,1152]{2,1,0:T(8,128)(2,1)} %bitcast.73), calls=%async_computation.6 | async-start | bytes 1179648 | tf_op jit(solution)/shard_map/all_to_all | solution.py:26
  163.9 6.0 %late_weights.1 = (bf16[288,1152]{1,0:T(8,128)(2,1)}, bf16[288,1152]{1,0:T(8,128)(2,1)}, bf16[288,1152]{1,0:T(8,128)(2,1)}, bf16[288,1152]{1,0:T(8,128)(2,1)}) custom-call(s32[7]{0:T(128)} %concatenate.30.refs_0_, bf16[256,1152]{1,0:T(8,128)(2,1)} %bitcast.63, bf16[256,1152]{1,0:T(8,128)(2,1)} %get-tuple-element.95.refs_10_.refs_2_, ...), custom_call_target="tpu_custom_call" | custom-call | flops 1 | bytes 1 | tf_op jit(solution)/shard_map/late_weights/pallas_call | solution.py:366
  169.9 6.3 %all-to-all-done.6.refs_1_ = bf16[4,64,1152]{2,1,0:T(8,128)(2,1)S(1)} async-done(((bf16[4,64,1152]{2,1,0:T(8,128)(2,1)}), bf16[4,64,1152]{2,1,0:T(8,128)(2,1)S(1)}, u32[]{:S(2)}, u32[]{:S(2)}) %all-to-all-start.6) | async-done | bytes 589856 | tf_op jit(solution)/shard_map/all_to_all | solution.py:26
  180.1 3.5 %all-to-all-start.7 = ((bf16[4,64,1152]{2,1,0:T(8,128)(2,1)}), bf16[4,64,1152]{2,1,0:T(8,128)(2,1)S(1)}, u32[]{:S(2)}, u32[]{:S(2)}) async-start(bf16[4,64,1152]{2,1,0:T(8,128)(2,1)} %get-tuple-element.108), calls=%async_computation.7 | async-start | bytes 1179648 | tf_op jit(solution)/shard_map/all_to_all | solution.py:26
  185.6 14.2 %collective-permute-done.18.refs_3_ = bf16[288,1152]{1,0:T(8,128)(2,1)S(1)} collective-permute-done((bf16[288,1152]{1,0:T(8,128)(2,1)}, bf16[288,1152]{1,0:T(8,128)(2,1)S(1)}, u32[]{:S(2)}, u32[]{:S(2)}) %collective-permute-start.18) | collective-permute-done | bytes 663584 | tf_op jit(solution)/shard_map/ppermute | solution.py:22
  207.3 3.5 %collective-permute-start.22 = (bf16[64,1152]{1,0:T(8,128)(2,1)}, bf16[64,1152]{1,0:T(8,128)(2,1)S(1)}, u32[]{:S(2)}, u32[]{:S(2)}) collective-permute-start(bf16[64,1152]{1,0:T(8,128)(2,1)} %gate.24), channel_id=1, source_target_pairs={{0,3},{1,2},{2,1},{3,0},{4,7},{5,6},{6,5},{7,4},{8,11},{9,10},{10,... | collective-permute-start | bytes 442376 | tf_op jit(solution)/shard_map/ppermute | solution.py:22
  213.6 9.2 %attend_backward.1.refs_0_ = bf16[8,72,640]{2,1,0:T(8,128)(2,1)} custom-call(s32[4]{0:T(128)} %pad_add_fusion.refs_0_, bf16[8,72,640]{2,1,0:T(8,128)(2,1)} %copy-done.33, bf16[8,72,128]{2,1,0:T(8,128)(2,1)} %copy-done.50, f32[8,72,128]{2,1,0:T(8,128)} %get-tuple-element.113.refs_3_, f32[8,1,128]{2,1,0:T(1,128)} %get-tuple-element.114.refs_4_), custom_call_target="tpu_custom_call" | custom-call | flops 3000000000 | bytes 4000000 | tf_op jit(solution)/shard_map/attend_backward/pallas_call | solution.py:239
  225.5 3.9 %all-to-all-start.9 = ((bf16[8,72,640]{2,1,0:T(8,128)(2,1)}), bf16[8,72,640]{2,1,0:T(8,128)(2,1)S(1)}, u32[]{:S(2)}, u32[]{:S(2)}) async-start(bf16[8,72,640]{2,1,0:T(8,128)(2,1)} %gate.25), calls=%async_computation.9 | async-start | bytes 1474560 | tf_op jit(solution)/shard_map/all_to_all | solution.py:26
  236.7 4.8 %all-to-all-done.9.refs_1_ = bf16[8,72,640]{2,1,0:T(8,128)(2,1)S(1)} async-done(((bf16[8,72,640]{2,1,0:T(8,128)(2,1)}), bf16[8,72,640]{2,1,0:T(8,128)(2,1)S(1)}, u32[]{:S(2)}, u32[]{:S(2)}) %all-to-all-start.9) | async-done | bytes 737312 | tf_op jit(solution)/shard_map/all_to_all | solution.py:26
  242.4 5.1 %unspread.1 = (bf16[256,1152]{1,0:T(8,128)(2,1)}, bf16[256,576]{1,0:T(8,128)(2,1)}, bf16[256,576]{1,0:T(8,128)(2,1)}, bf16[256,576]{1,0:T(8,128)(2,1)}, f32[2,576]{1,0:T(2,128)}) custom-call(s32[7]{0:T(128)} %concatenate.30.refs_0_, bf16[8,72,640]{2,1,0:T(8,128)(2,1)} %copy-done.34, bf16[1152,576]{1,0:T(8,128)(2,1)} %get-tuple-element.115.refs_2_, ...), custom_call_target="tpu_custom_call" | custom-call | flops 20000000000 | bytes 1 | tf_op jit(solution)/shard_map/unspread/pallas_call | solution.py:366
  251.5 5.1 %all-to-all-start.10 = ((bf16[4,64,1152]{2,1,0:T(8,128)(2,1)}), bf16[4,64,1152]{2,1,0:T(8,128)(2,1)S(1)}, u32[]{:S(2)}, u32[]{:S(2)}) async-start(bf16[4,64,1152]{2,1,0:T(8,128)(2,1)} %bitcast.12), calls=%async_computation.10 | async-start | bytes 1179648 | tf_op jit(solution)/shard_map/all_to_all | solution.py:26
  256.7 5.0 %early_weights.1 = (bf16[288,576]{1,0:T(8,128)(2,1)}, bf16[288,576]{1,0:T(8,128)(2,1)}, bf16[288,576]{1,0:T(8,128)(2,1)}, bf16[288,576]{1,0:T(8,128)(2,1)}) custom-call(s32[7]{0:T(128)} %concatenate.30.refs_0_, bf16[256,1152]{1,0:T(8,128)(2,1)} %get-tuple-element.124.refs_1_, bf16[256,1152]{1,0:T(8,128)(2,1)} %bitcast.65, ...), custom_call_target="tpu_custom_call" | custom-call | flops 1 | bytes 1 | tf_op jit(solution)/shard_map/early_weights/pallas_call | solution.py:366
  265.6 7.1 %all-to-all-done.10.refs_1_ = bf16[4,64,1152]{2,1,0:T(8,128)(2,1)S(1)} async-done(((bf16[4,64,1152]{2,1,0:T(8,128)(2,1)}), bf16[4,64,1152]{2,1,0:T(8,128)(2,1)S(1)}, u32[]{:S(2)}, u32[]{:S(2)}) %all-to-all-start.10) | async-done | bytes 589856 | tf_op jit(solution)/shard_map/all_to_all | solution.py:26
  276.3 4.1 %all-to-all-start.11 = ((f32[4,18,288]{2,1,0:T(8,128)}), f32[4,18,288]{2,1,0:T(8,128)}, u32[]{:S(2)}, u32[]{:S(2)}) async-start(f32[4,18,288]{2,1,0:T(8,128)} %get-tuple-element.133.refs_4_), calls=%async_computation.11 | async-start | bytes 294912 | tf_op jit(solution)/shard_map/all_to_all | solution.py:26
  286.6 5.7 %collective-permute-done.30.refs_1_ = bf16[288,576]{1,0:T(8,128)(2,1)S(1)} collective-permute-done((bf16[288,576]{1,0:T(8,128)(2,1)}, bf16[288,576]{1,0:T(8,128)(2,1)S(1)}, u32[]{:S(2)}, u32[]{:S(2)}) %collective-permute-start.30) | collective-permute-done | bytes 331808 | tf_op jit(solution)/shard_map/ppermute | solution.py:22
  292.2 6.2 %collective-permute-done.31.refs_2_ = bf16[288,576]{1,0:T(8,128)(2,1)S(1)} collective-permute-done((bf16[288,576]{1,0:T(8,128)(2,1)}, bf16[288,576]{1,0:T(8,128)(2,1)S(1)}, u32[]{:S(2)}, u32[]{:S(2)}) %collective-permute-start.31) | collective-permute-done | bytes 331808 | tf_op jit(solution)/shard_map/ppermute | solution.py:22
  308.2 3.7 %all-to-all-start.12 = ((f32[8,32,288]{2,1,0:T(8,128)}), f32[8,32,288]{2,1,0:T(8,128)S(1)}, u32[]{:S(2)}, u32[]{:S(2)}) async-start(f32[8,32,288]{2,1,0:T(8,128)} %broadcast_in_dim.13), calls=%async_computation.12 | async-start | bytes 786432 | tf_op jit(solution)/shard_map/all_to_all | solution.py:26
  314.2 5.8 %all-to-all-done.12.refs_0_ = f32[8,32,288]{2,1,0:T(8,128)S(1)} async-done(((f32[8,32,288]{2,1,0:T(8,128)}), f32[8,32,288]{2,1,0:T(8,128)S(1)}, u32[]{:S(2)}, u32[]{:S(2)}) %all-to-all-start.12) | async-done | bytes 294944 | tf_op jit(solution)/shard_map/all_to_all | solution.py:26
  325.1 3.8 %all-to-all-start.13 = ((f32[32,1,432]{2,1,0:T(1,128)}), f32[32,1,432]{2,1,0:T(1,128)S(1)}, u32[]{:S(2)}, u32[]{:S(2)}) async-start(f32[32,1,432]{2,1,0:T(1,128)} %reshape.110), calls=%async_computation.13 | async-start | bytes 131072 | tf_op jit(solution)/shard_map/all_to_all | solution.py:26
  (294 shorter events, 119.2 us)
Async XLA Ops:
  8.1 36.0 %collective-permute-start.2 = (bf16[288,576]{1,0:T(8,128)(2,1)}, bf16[288,576]{1,0:T(8,128)(2,1)S(1)}, u32[]{:S(2)}, u32[]{:S(2)}) collective-permute-start(bf16[288,576]{1,0:T(8,128)(2,1)} %gate.17.refs_0_), channel_id=1, source_target_pairs={{0,8},{4,12},{8,0},{12,4},{16,24},{20,28},{24,16},{28,20},{1,9},{5... | collective-permute-start | bytes 995336 | tf_op jit(solution)/shard_map/ppermute | solution.py:22
  10.6 33.5 %collective-permute-start.3 = (bf16[288,576]{1,0:T(8,128)(2,1)}, bf16[288,576]{1,0:T(8,128)(2,1)S(1)}, u32[]{:S(2)}, u32[]{:S(2)}) collective-permute-start(bf16[288,576]{1,0:T(8,128)(2,1)} %gate.17.refs_0_), channel_id=1, source_target_pairs={{0,16},{4,20},{8,24},{12,28},{16,0},{20,4},{24,8},{28,12},{1,17},{... | collective-permute-start | bytes 995336 | tf_op jit(solution)/shard_map/ppermute | solution.py:22
  12.1 32.0 %collective-permute-start.4 = (bf16[288,576]{1,0:T(8,128)(2,1)}, bf16[288,576]{1,0:T(8,128)(2,1)S(1)}, u32[]{:S(2)}, u32[]{:S(2)}) collective-permute-start(bf16[288,576]{1,0:T(8,128)(2,1)} %gate.17.refs_0_), channel_id=1, source_target_pairs={{0,24},{4,28},{8,16},{12,20},{16,8},{20,12},{24,0},{28,4},{1,25},{... | collective-permute-start | bytes 995336 | tf_op jit(solution)/shard_map/ppermute | solution.py:22
  12.9 19.7 %all-to-all-start = ((f32[8,18,288]{2,1,0:T(8,128)}), f32[8,18,288]{2,1,0:T(8,128)S(1)}, u32[]{:S(2)}, u32[]{:S(2)}) async-start(f32[8,18,288]{2,1,0:T(8,128)} %broadcast_in_dim.11), calls=%async_computation | async-start | bytes 589824 | tf_op jit(solution)/shard_map/all_to_all | solution.py:26
  56.3 15.7 %all-to-all-start.2 = ((bf16[8,72,640]{2,1,0:T(8,128)(2,1)}), bf16[8,72,640]{2,1,0:T(8,128)(2,1)S(1)}, u32[]{:S(2)}, u32[]{:S(2)}) async-start(bf16[8,72,640]{2,1,0:T(8,128)(2,1)} %get-tuple-element.88), calls=%async_computation.2 | async-start | bytes 1474560 | tf_op jit(solution)/shard_map/all_to_all | solution.py:26
  60.1 24.1 %collective-permute-start = (bf16[144,1152]{1,0:T(8,128)(2,1)S(1)}, bf16[144,1152]{1,0:T(8,128)(2,1)S(1)}, u32[]{:S(2)}, u32[]{:S(2)}) collective-permute-start(bf16[144,1152]{1,0:T(8,128)(2,1)S(1)} %bitcast_select_fusion), channel_id=1, source_target_pairs={{0,4},{4,0},{8,12},{12,8},{16,20},{20,16},{24,28},{28,24},{1,5},{5... | collective-permute-start | bytes 995336 | tf_op jit(solution)/shard_map/ppermute | solution.py:22
  93.5 21.3 %all-to-all-start.4 = ((bf16[4,64,1152]{2,1,0:T(8,128)(2,1)}), bf16[4,64,1152]{2,1,0:T(8,128)(2,1)S(1)}, u32[]{:S(2)}, u32[]{:S(2)}) async-start(bf16[4,64,1152]{2,1,0:T(8,128)(2,1)} %bitcast.74), calls=%async_computation.4 | async-start | bytes 1179648 | tf_op jit(solution)/shard_map/all_to_all | solution.py:26
  97.9 16.7 %collective-permute-start.10 = (bf16[288,1152]{1,0:T(8,128)(2,1)}, bf16[288,1152]{1,0:T(8,128)(2,1)S(1)}, u32[]{:S(2)}, u32[]{:S(2)}) collective-permute-start(bf16[288,1152]{1,0:T(8,128)(2,1)} %gate.19.refs_1_), channel_id=1, source_target_pairs={{0,16},{4,20},{8,24},{12,28},{16,0},{20,4},{24,8},{28,12},{1,17},{... | collective-permute-start | bytes 1990664 | tf_op jit(solution)/shard_map/ppermute | solution.py:22
  98.4 16.4 %collective-permute-start.9 = (bf16[288,1152]{1,0:T(8,128)(2,1)}, bf16[288,1152]{1,0:T(8,128)(2,1)S(1)}, u32[]{:S(2)}, u32[]{:S(2)}) collective-permute-start(bf16[288,1152]{1,0:T(8,128)(2,1)} %gate.19.refs_1_), channel_id=1, source_target_pairs={{0,8},{4,12},{8,0},{12,4},{16,24},{20,28},{24,16},{28,20},{1,9},{5... | collective-permute-start | bytes 1990664 | tf_op jit(solution)/shard_map/ppermute | solution.py:22
  118.6 21.8 %all-to-all-start.5 = ((bf16[4,64,1152]{2,1,0:T(8,128)(2,1)}), bf16[4,64,1152]{2,1,0:T(8,128)(2,1)S(1)}, u32[]{:S(2)}, u32[]{:S(2)}) async-start(bf16[4,64,1152]{2,1,0:T(8,128)(2,1)} %get-tuple-element.94), calls=%async_computation.5 | async-start | bytes 1179648 | tf_op jit(solution)/shard_map/all_to_all | solution.py:26
  124.3 16.1 %collective-permute-start.11 = (bf16[288,1152]{1,0:T(8,128)(2,1)}, bf16[288,1152]{1,0:T(8,128)(2,1)}, u32[]{:S(2)}, u32[]{:S(2)}) collective-permute-start(bf16[288,1152]{1,0:T(8,128)(2,1)} %gate.20), channel_id=1, source_target_pairs={{0,24},{4,28},{8,16},{12,20},{16,8},{20,12},{24,0},{28,4},{1,25},{... | collective-permute-start | bytes 1990664 | tf_op jit(solution)/shard_map/ppermute | solution.py:22
  125.8 16.1 %collective-permute-start.12 = (bf16[288,1152]{1,0:T(8,128)(2,1)S(1)}, bf16[288,1152]{1,0:T(8,128)(2,1)}, u32[]{:S(2)}, u32[]{:S(2)}) collective-permute-start(bf16[288,1152]{1,0:T(8,128)(2,1)S(1)} %copy-done), channel_id=1, source_target_pairs={{0,4},{4,0},{8,12},{12,8},{16,20},{20,16},{24,28},{28,24},{1,5},{5... | collective-permute-start | bytes 1990664 | tf_op jit(solution)/shard_map/ppermute | solution.py:22
  125.8 16.1 %collective-permute-start.13 = (bf16[288,1152]{1,0:T(8,128)(2,1)S(1)}, bf16[288,1152]{1,0:T(8,128)(2,1)}, u32[]{:S(2)}, u32[]{:S(2)}) collective-permute-start(bf16[288,1152]{1,0:T(8,128)(2,1)S(1)} %copy-done.9), channel_id=1, source_target_pairs={{0,4},{4,0},{8,12},{12,8},{16,20},{20,16},{24,28},{28,24},{1,5},{5... | collective-permute-start | bytes 1990664 | tf_op jit(solution)/shard_map/ppermute | solution.py:22
  126.3 15.6 %collective-permute-start.14 = (bf16[288,1152]{1,0:T(8,128)(2,1)S(1)}, bf16[288,1152]{1,0:T(8,128)(2,1)}, u32[]{:S(2)}, u32[]{:S(2)}) collective-permute-start(bf16[288,1152]{1,0:T(8,128)(2,1)S(1)} %copy-done.7), channel_id=1, source_target_pairs={{0,4},{4,0},{8,12},{12,8},{16,20},{20,16},{24,28},{28,24},{1,5},{5... | collective-permute-start | bytes 1990664 | tf_op jit(solution)/shard_map/ppermute | solution.py:22
  155.2 21.0 %all-to-all-start.6 = ((bf16[4,64,1152]{2,1,0:T(8,128)(2,1)}), bf16[4,64,1152]{2,1,0:T(8,128)(2,1)S(1)}, u32[]{:S(2)}, u32[]{:S(2)}) async-start(bf16[4,64,1152]{2,1,0:T(8,128)(2,1)} %bitcast.73), calls=%async_computation.6 | async-start | bytes 1179648 | tf_op jit(solution)/shard_map/all_to_all | solution.py:26
  180.1 19.9 %all-to-all-start.7 = ((bf16[4,64,1152]{2,1,0:T(8,128)(2,1)}), bf16[4,64,1152]{2,1,0:T(8,128)(2,1)S(1)}, u32[]{:S(2)}, u32[]{:S(2)}) async-start(bf16[4,64,1152]{2,1,0:T(8,128)(2,1)} %get-tuple-element.108), calls=%async_computation.7 | async-start | bytes 1179648 | tf_op jit(solution)/shard_map/all_to_all | solution.py:26
  183.6 16.2 %collective-permute-start.18 = (bf16[288,1152]{1,0:T(8,128)(2,1)}, bf16[288,1152]{1,0:T(8,128)(2,1)S(1)}, u32[]{:S(2)}, u32[]{:S(2)}) collective-permute-start(bf16[288,1152]{1,0:T(8,128)(2,1)} %get-tuple-element.105.refs_7_), channel_id=1, source_target_pairs={{0,8},{4,12},{8,0},{12,4},{16,24},{20,28},{24,16},{28,20},{1,9},{5... | collective-permute-start | bytes 1990664 | tf_op jit(solution)/shard_map/ppermute | solution.py:22
  184.4 15.6 %collective-permute-start.19 = (bf16[288,1152]{1,0:T(8,128)(2,1)S(1)}, bf16[288,1152]{1,0:T(8,128)(2,1)S(1)}, u32[]{:S(2)}, u32[]{:S(2)}) collective-permute-start(bf16[288,1152]{1,0:T(8,128)(2,1)S(1)} %copy-done.36), channel_id=1, source_target_pairs={{0,16},{4,20},{8,24},{12,28},{16,0},{20,4},{24,8},{28,12},{1,17},{... | collective-permute-start | bytes 1990664 | tf_op jit(solution)/shard_map/ppermute | solution.py:22
  207.3 15.5 %collective-permute-start.22 = (bf16[64,1152]{1,0:T(8,128)(2,1)}, bf16[64,1152]{1,0:T(8,128)(2,1)S(1)}, u32[]{:S(2)}, u32[]{:S(2)}) collective-permute-start(bf16[64,1152]{1,0:T(8,128)(2,1)} %gate.24), channel_id=1, source_target_pairs={{0,3},{1,2},{2,1},{3,0},{4,7},{5,6},{6,5},{7,4},{8,11},{9,10},{10,... | collective-permute-start | bytes 442376 | tf_op jit(solution)/shard_map/ppermute | solution.py:22
  225.5 15.9 %all-to-all-start.9 = ((bf16[8,72,640]{2,1,0:T(8,128)(2,1)}), bf16[8,72,640]{2,1,0:T(8,128)(2,1)S(1)}, u32[]{:S(2)}, u32[]{:S(2)}) async-start(bf16[8,72,640]{2,1,0:T(8,128)(2,1)} %gate.25), calls=%async_computation.9 | async-start | bytes 1474560 | tf_op jit(solution)/shard_map/all_to_all | solution.py:26
  232.3 15.1 %collective-permute-start.23 = (bf16[64,1152]{1,0:T(8,128)(2,1)}, bf16[64,1152]{1,0:T(8,128)(2,1)S(1)}, u32[]{:S(2)}, u32[]{:S(2)}) collective-permute-start(bf16[64,1152]{1,0:T(8,128)(2,1)} %get-tuple-element.112.refs_0_), channel_id=1, source_target_pairs={{0,1},{1,0},{2,3},{3,2},{4,5},{5,4},{6,7},{7,6},{8,9},{9,8},{10,11... | collective-permute-start | bytes 442376 | tf_op jit(solution)/shard_map/ppermute | solution.py:22
  232.3 15.1 %collective-permute-start.24 = (bf16[64,1152]{1,0:T(8,128)(2,1)}, bf16[64,1152]{1,0:T(8,128)(2,1)S(1)}, u32[]{:S(2)}, u32[]{:S(2)}) collective-permute-start(bf16[64,1152]{1,0:T(8,128)(2,1)} %get-tuple-element.112.refs_0_), channel_id=1, source_target_pairs={{0,2},{1,3},{2,0},{3,1},{4,6},{5,7},{6,4},{7,5},{8,10},{9,11},{10,... | collective-permute-start | bytes 442376 | tf_op jit(solution)/shard_map/ppermute | solution.py:22
  248.2 16.2 %collective-permute-start.37 = (bf16[288,1152]{1,0:T(8,128)(2,1)}, bf16[288,1152]{1,0:T(8,128)(2,1)S(1)}, u32[]{:S(2)}, u32[]{:S(2)}) collective-permute-start(bf16[288,1152]{1,0:T(8,128)(2,1)} %gate.33), channel_id=1, source_target_pairs={{0,24},{4,28},{8,16},{12,20},{16,8},{20,12},{24,0},{28,4},{1,25},{... | collective-permute-start | bytes 1990664 | tf_op jit(solution)/shard_map/ppermute | solution.py:22
  251.5 21.2 %all-to-all-start.10 = ((bf16[4,64,1152]{2,1,0:T(8,128)(2,1)}), bf16[4,64,1152]{2,1,0:T(8,128)(2,1)S(1)}, u32[]{:S(2)}, u32[]{:S(2)}) async-start(bf16[4,64,1152]{2,1,0:T(8,128)(2,1)} %bitcast.12), calls=%async_computation.10 | async-start | bytes 1179648 | tf_op jit(solution)/shard_map/all_to_all | solution.py:26
  265.6 46.3 %collective-permute-start.38 = (f32[144,1152]{1,0:T(8,128)}, f32[144,1152]{1,0:T(8,128)}, u32[]{:S(2)}, u32[]{:S(2)}) collective-permute-start(f32[144,1152]{1,0:T(8,128)} %slice_select_fusion), channel_id=1, source_target_pairs={{0,4},{4,0},{8,12},{12,8},{16,20},{20,16},{24,28},{28,24},{1,5},{5... | collective-permute-start | bytes 1990664 | tf_op jit(solution)/shard_map/ppermute | solution.py:22
  281.1 17.4 %collective-permute-start.31 = (bf16[288,576]{1,0:T(8,128)(2,1)}, bf16[288,576]{1,0:T(8,128)(2,1)S(1)}, u32[]{:S(2)}, u32[]{:S(2)}) collective-permute-start(bf16[288,576]{1,0:T(8,128)(2,1)} %get-tuple-element.135), channel_id=1, source_target_pairs={{0,16},{4,20},{8,24},{12,28},{16,0},{20,4},{24,8},{28,12},{1,17},{... | collective-permute-start | bytes 995336 | tf_op jit(solution)/shard_map/ppermute | solution.py:22
  282.0 23.2 %collective-permute-start.32 = (bf16[288,576]{1,0:T(8,128)(2,1)}, bf16[288,576]{1,0:T(8,128)(2,1)S(1)}, u32[]{:S(2)}, u32[]{:S(2)}) collective-permute-start(bf16[288,576]{1,0:T(8,128)(2,1)} %get-tuple-element.137), channel_id=1, source_target_pairs={{0,24},{4,28},{8,16},{12,20},{16,8},{20,12},{24,0},{28,4},{1,25},{... | collective-permute-start | bytes 995336 | tf_op jit(solution)/shard_map/ppermute | solution.py:22
  300.8 29.3 %collective-permute-start.33 = (bf16[64,1152]{1,0:T(8,128)(2,1)}, bf16[64,1152]{1,0:T(8,128)(2,1)}, u32[]{:S(2)}, u32[]{:S(2)}) collective-permute-start(bf16[64,1152]{1,0:T(8,128)(2,1)} %gate.31.refs_0_), channel_id=1, source_target_pairs={{0,1},{1,0},{2,3},{3,2},{4,5},{5,4},{6,7},{7,6},{8,9},{9,8},{10,11... | collective-permute-start | bytes 442376 | tf_op jit(solution)/shard_map/ppermute | solution.py:22
  302.4 27.7 %collective-permute-start.34 = (bf16[64,1152]{1,0:T(8,128)(2,1)}, bf16[64,1152]{1,0:T(8,128)(2,1)}, u32[]{:S(2)}, u32[]{:S(2)}) collective-permute-start(bf16[64,1152]{1,0:T(8,128)(2,1)} %gate.31.refs_0_), channel_id=1, source_target_pairs={{0,2},{1,3},{2,0},{3,1},{4,6},{5,7},{6,4},{7,5},{8,10},{9,11},{10,... | collective-permute-start | bytes 442376 | tf_op jit(solution)/shard_map/ppermute | solution.py:22
  304.8 25.4 %collective-permute-start.35 = (bf16[64,1152]{1,0:T(8,128)(2,1)}, bf16[64,1152]{1,0:T(8,128)(2,1)}, u32[]{:S(2)}, u32[]{:S(2)}) collective-permute-start(bf16[64,1152]{1,0:T(8,128)(2,1)} %gate.31.refs_0_), channel_id=1, source_target_pairs={{0,3},{1,2},{2,1},{3,0},{4,7},{5,6},{6,5},{7,4},{8,11},{9,10},{10,... | collective-permute-start | bytes 442376 | tf_op jit(solution)/shard_map/ppermute | solution.py:22
  307.4 27.9 %collective-permute-start.36 = (f32[144,576]{1,0:T(8,128)}, f32[144,576]{1,0:T(8,128)}, u32[]{:S(2)}, u32[]{:S(2)}) collective-permute-start(f32[144,576]{1,0:T(8,128)} %slice_select_fusion.2), channel_id=1, source_target_pairs={{0,4},{4,0},{8,12},{12,8},{16,20},{20,16},{24,28},{28,24},{1,5},{5... | collective-permute-start | bytes 995336 | tf_op jit(solution)/shard_map/ppermute | solution.py:22
  325.1 13.6 %all-to-all-start.13 = ((f32[32,1,432]{2,1,0:T(1,128)}), f32[32,1,432]{2,1,0:T(1,128)S(1)}, u32[]{:S(2)}, u32[]{:S(2)}) async-start(f32[32,1,432]{2,1,0:T(1,128)} %reshape.110), calls=%async_computation.13 | async-start | bytes 131072 | tf_op jit(solution)/shard_map/all_to_all | solution.py:26
  (82 other events, 378.1 us)

commit v9 on v8

--- a/solution.py
+++ b/solution.py
@@ -84,15 +84,6 @@
     half = rows.shape[0] // 2
     keep, send = choose(core, rows[:half], rows[half:])
     return choose(core, keep, swap(send, "dp", 1))
-
-
-def in_order(parts, axis):
-    me = lax.axis_index(axis)
-    stacked = jnp.stack(parts)
-    ordered = [
-        lax.dynamic_index_in_dim(stacked, me ^ place, 0, keepdims=False) for place in range(len(parts))
-    ]
-    return jnp.concatenate(ordered)
 
 
 def exchange_shares(partial, axis):
@@ -264,10 +255,11 @@
         out, self.exact, self.log_total = attend_forward(self.meta, self.packed)
         return exchange(out, "dp")
 
-    def backward(self, grad, due):
+    def backward(self, grad, due, beside):
         grad = exchange(grad, "dp")
+        beside = swap(gate(beside, grad), "dp", lax.axis_size("dp") - 2)
         out = attend_backward(self.meta, self.packed, grad, self.exact, self.log_total)
-        return exchange(gate(out, *due), "dp")
+        return exchange(gate(out, beside, *due), "dp"), beside
 
 
 class Window:
@@ -320,7 +312,7 @@
         out = out.reshape(-1, DH, 2, rows // 2).transpose(0, 2, 1, 3)
         return out.reshape(-1, DH, rows // 2)
 
-    def backward(self, grad, due):
+    def backward(self, grad, due, beside):
         rows, reach = self.rows, self.reach
         halves = grad.reshape(-1, 2, DH, rows // 2)
         grads = jnp.concatenate([halves[:, 0], halves[:, 1]], axis=2)
@@ -347,7 +339,7 @@
         wide = jnp.stack([wide, jnp.zeros_like(wide)], axis=1)
         halves = d_query.reshape(-1, DH, 2, rows // 2).transpose(0, 2, 1, 3)
         packed = jnp.concatenate([wide, halves], axis=3).astype(BF16)
-        return packed.reshape(-1, DH, rows * 5 // 2)
+        return packed.reshape(-1, DH, rows * 5 // 2), beside
 
 
 META = 4
@@ -695,6 +687,15 @@
     bias_ref[place : place + 2, :] = qv_bias_ref[:, :columns]
 
 
+def order_kernel(count, meta_ref, *refs):
+    result_ref, grad_ref = refs[2 * count :]
+    share = refs[0].shape[0]
+    for step in range(count):
+        start = pl.multiple_of((meta_ref[2] ^ step) * share, share)
+        result_ref[pl.ds(start, share), :] = refs[step][...]
+        grad_ref[pl.ds(start, share), :] = refs[count + step][...].astype(F32)
+
+
 def finish_kernel(
     latents, meta_ref, sums_ref, active_ref, w_ada_ref,
     w_grad_ref, b_grad_ref, d_active_ref, fc2_ref, proj_ref, fc1_ref, qv_ref, total_ref,
@@ -800,8 +801,8 @@
     mod_part = mod_part.reshape(latents * 6, features)
     bias_ada = jnp.tile(b_ada.astype(F32), (latents, 1))
     few_chips = n_dp // 2 == 4
-    early_rows = gate(early_rows, mod_part)
     mod_mine = jnp.sum(gather(mod_part, "dp", n_dp), axis=0) + bias_ada
+    early_rows = gate(early_rows, mod_mine)
     mod_parts = gather(mod_mine, "tensor", n_tensor)
     early_parts = chip_parts(early_rows) if few_chips else [gather_chips(early_rows)]
 
@@ -907,7 +908,7 @@
     ]
     d_attn_other = swap(d_attn, "dp", 1)
     attended_other = swap(attended, "dp", 1)
-    d_packed = attention.backward(d_spread, mlp_parts[1:])
+    d_packed, last_grad = attention.backward(d_spread, mlp_parts[1:], late_blocks[-1])
     result_own, last_sums = call(
         lambda *refs: result_kernel(latents, n_tensor, *refs),
         "result",
@@ -930,7 +931,7 @@
     d_one_parts = exchange_shares(d_one_part, "tensor")
 
     if few_chips:
-        late_grads.append(swap(gate(late_blocks[-1], d_one_part), "dp", n_dp - 2))
+        late_grads.append(last_grad)
     right_other = swap(d_sent, "dp", 1)
     early_blocks = call(
         lambda *refs: weight_kernel(
@@ -942,6 +943,8 @@
         (((width // chips, 2 * features), BF16),) * chips,
         [pltpu.VMEM((width, 2 * features), BF16)],
     )
+    early_grads = sum_chips(early_blocks[:3] if few_chips else early_blocks)
+
     grad_own, d_mod_part, bias_rows = call(
         lambda *refs: first_back_kernel(latents, *refs),
         "first_back",
@@ -951,17 +954,26 @@
         (((share, width), BF16), ((n_tensor, 6 * latents, features), F32))
         + (((2 * (width // features) + units // features + 2, features), F32),),
         [pltpu.VMEM((2 * latents, width), F32)],
-        due=early_blocks,
-    )
-    early_grads = sum_chips(gate_all(early_blocks, d_mod_part))
-    d_mod_mine = exchange(d_mod_part, "tensor")
-    d_mod_mine = jnp.sum(gate(d_mod_mine, *early_grads[1:3]) if few_chips else d_mod_mine, axis=0)
-    grad_own = gate(grad_own, d_mod_mine)
+        due=early_grads[1:3],
+    )
+    if few_chips:
+        last_block = gate(early_blocks[3], d_mod_part)
+        early_grads.append(swap(last_block, "dp", n_dp - 2))
+    d_mod_mine = jnp.sum(exchange(d_mod_part, "tensor"), axis=0)
+    d_mod_rows = jnp.concatenate([d_mod_mine, bias_rows])
+    d_mod_rows = gate(jnp.broadcast_to(d_mod_rows[None], (n_dp,) + d_mod_rows.shape))
+    grad_own = gate(grad_own, d_mod_rows)
     grad_parts = [grad_own] + [swap(grad_own, "tensor", bits) for bits in range(1, n_tensor)]
-    sums = gather(jnp.concatenate([d_mod_mine, bias_rows]), "dp", n_dp)
+    sums = exchange(d_mod_rows, "dp")
     sums = gate(sums, early_grads[3]) if few_chips else sums
-    grad_tokens = in_order(gate_all(grad_parts, sums), "tensor").astype(F32)
-    result = in_order(gate_all(result_parts, sums), "tensor")
+    grad_parts = gate_all(grad_parts, sums)
+    result, grad_tokens = call(
+        lambda *refs: order_kernel(n_tensor, *refs),
+        "order",
+        meta,
+        (*result_parts, *grad_parts),
+        (((rows, width), BF16), ((rows, width), F32)),
+    )
     grad_w_ada, grad_b_ada, d_active, sum_b_fc2, sum_b_proj, sum_b_fc1, sum_b_qv = call(
         lambda *refs: finish_kernel(latents, *refs),
         "finish",
@@ -990,11 +1002,11 @@
         grad_qkv,
         sum_b_qv,
         grad_vp[:, features:].T,
-        sum_b_proj[0],
+        sum_b_proj.reshape(width),
         grad_fc1,
-        sum_b_fc1[0],
+        sum_b_fc1.reshape(units),
         grad_fc2.T,
-        sum_b_fc2[0],
+        sum_b_fc2.reshape(width),
     )
 
 

time: 343 us -> 328 us (0.956)
  waiting for transfers between devices: 123 us -> 105 us
  blocking collectives: 11.4 us -> 21.1 us
  Pallas kernels: 69.7 us -> 76 us
  other arithmetic: 20 us -> 14.5 us
    all_to_all x13 -> x12, waiting for transfers between devices: 58.5 us -> 39.8 us  [exchange(): return lax.all_to_all(blocks, axis, 0, 0, tiled=True)]
    all_to_all x1 -> x2, blocking collectives: 11.4 us -> 21.1 us  [exchange(): return lax.all_to_all(blocks, axis, 0, 0, tiled=True)]
    pallas_call x12 -> x13, Pallas kernels: 52.5 us -> 55.1 us  [call(): pl.pallas_call(kernel, out_shape=tuple((jax.ShapeDtypeStruct(shape, kind)...]
    all_to_all x13 -> x12, starting transfers between devices: 51.7 us -> 49.9 us  [exchange(): return lax.all_to_all(blocks, axis, 0, 0, tiled=True)]
    unnamed x130 -> x126, local copies, waits for them, and re-layouts: 19.2 us -> 17.5 us
  transfers between devices with their start and end apart: 52 -> 51, of which waited for: 23 -> 24; matrix products, arithmetic and copies ran while one was open for 9% -> 7% of each run, Pallas kernels for 12% -> 15%
where the time goes in v9:
time: 328 us; the launch traced here: 327 us
  waiting for transfers between devices  105 us (32%)
  starting transfers between devices  80.3 us (24%)
  Pallas kernels  76 us (23%)
  local copies, waits for them, and re-layouts  28.5 us (9%)
  blocking collectives  21.1 us (6%)
  other arithmetic  14.5 us (4%)
    ppermute x39, waiting for transfers between devices, swap(): return lax.ppermute(block, axis, route)  65.3 us
    pallas_call x13, Pallas kernels, call(): pl.pallas_call(kernel, out_shape=tuple((jax.ShapeDtypeStruct(shape, kind)...  55.1 us
    all_to_all x12, starting transfers between devices, exchange(): return lax.all_to_all(blocks, axis, 0, 0, tiled=True)  49.9 us
    all_to_all x12, waiting for transfers between devices, exchange(): return lax.all_to_all(blocks, axis, 0, 0, tiled=True)  39.8 us
    ppermute x39, starting transfers between devices, swap(): return lax.ppermute(block, axis, route)  30.4 us
    all_to_all x2, blocking collectives, exchange(): return lax.all_to_all(blocks, axis, 0, 0, tiled=True)  21.1 us
    unnamed x126, local copies, waits for them, and re-layouts  17.5 us
    pallas_call x1, Pallas kernels, attend_backward(): pl.pallas_call(lambda *refs: backward_kernel(meta.shape[0] - 1, *refs), o...  11.2 us
  transfers between devices with their start and end apart: 51, of which 24 were waited for; matrix products, arithmetic and copies ran while one was open for 7% of the time, Pallas kernels for 15%

profile of v9, /device:TPU:0, one launch (start us, length us, event | category | flops | bytes accessed | tf_op | source)
XLA Modules:
  0.0 327.2 jit_solution(17895363873157573698)
XLA Ops:
  7.3 4.8 %all-to-all-start = ((f32[8,18,288]{2,1,0:T(8,128)}), f32[8,18,288]{2,1,0:T(8,128)S(1)}, u32[]{:S(2)}, u32[]{:S(2)}) async-start(f32[8,18,288]{2,1,0:T(8,128)} %broadcast_in_dim.14), calls=%async_computation | async-start | bytes 589824 | tf_op jit(solution)/shard_map/all_to_all | solution.py:26
  12.1 7.3 %all-to-all-done = f32[8,18,288]{2,1,0:T(8,128)S(1)} async-done(((f32[8,18,288]{2,1,0:T(8,128)}), f32[8,18,288]{2,1,0:T(8,128)S(1)}, u32[]{:S(2)}, u32[]{:S(2)}) %all-to-all-start) | async-done | bytes 165920 | tf_op jit(solution)/shard_map/all_to_all | solution.py:26
  24.5 11.4 %all_to_all.70.refs_4_.refs_11_ = f32[4,18,288]{2,1,0:T(8,128)} all-to-all(f32[4,18,288]{2,1,0:T(8,128)S(1)} %broadcast_in_dim.15), channel_id=1, replica_groups=mesh['dp'=8,'tensor'=4] {'tensor'}, dimensions={0} | all-to-all | bytes 165888 | tf_op jit(solution)/shard_map/all_to_all | solution.py:26
  36.0 3.9 %collective-permute-done.3.refs_2_ = bf16[288,576]{1,0:T(8,128)(2,1)S(1)} collective-permute-done((bf16[288,576]{1,0:T(8,128)(2,1)}, bf16[288,576]{1,0:T(8,128)(2,1)S(1)}, u32[]{:S(2)}, u32[]{:S(2)}) %collective-permute-start.3) | collective-permute-done | bytes 331808 | tf_op jit(solution)/shard_map/ppermute | solution.py:22
  45.8 6.1 %project.1 = (bf16[256,1152]{1,0:T(8,128)(2,1)}, bf16[256,1152]{1,0:T(8,128)(2,1)}, bf16[8,72,640]{2,1,0:T(8,128)(2,1)}, bf16[1152,576]{1,0:T(8,128)(2,1)}, bf16...) custom-call(s32[7]{0:T(128)} %concatenate.24.refs_0_, bf16[288,576]{1,0:T(8,128)(2,1)} %get-tuple-element.78.refs_1_, ...), custom_call_target="tpu_custom_call" | custom-call | flops 1 | bytes 1 | tf_op jit(solution)/shard_map/project/pallas_call | solution.py:358
  51.9 3.7 %all-to-all-start.2 = ((bf16[8,72,640]{2,1,0:T(8,128)(2,1)}), bf16[8,72,640]{2,1,0:T(8,128)(2,1)S(1)}, u32[]{:S(2)}, u32[]{:S(2)}) async-start(bf16[8,72,640]{2,1,0:T(8,128)(2,1)} %get-tuple-element.82), calls=%async_computation.2 | async-start | bytes 1474560 | tf_op jit(solution)/shard_map/all_to_all | solution.py:26
  56.8 10.9 %all-to-all-done.2.refs_1_ = bf16[8,72,640]{2,1,0:T(8,128)(2,1)S(1)} async-done(((bf16[8,72,640]{2,1,0:T(8,128)(2,1)}), bf16[8,72,640]{2,1,0:T(8,128)(2,1)S(1)}, u32[]{:S(2)}, u32[]{:S(2)}) %all-to-all-start.2) | async-done | bytes 737312 | tf_op jit(solution)/shard_map/all_to_all | solution.py:26
  68.5 9.8 %attend_forward.1 = (bf16[8,72,128]{2,1,0:T(8,128)(2,1)}, f32[8,72,128]{2,1,0:T(8,128)}, f32[8,1,128]{2,1,0:T(1,128)}) custom-call(s32[4]{0:T(128)} %pad_add_fusion.refs_0_, bf16[8,72,640]{2,1,0:T(8,128)(2,1)} %copy-done.30), custom_call_target="tpu_custom_call" | custom-call | flops 1000000000 | bytes 4000000 | tf_op jit(solution)/shard_map/attend_forward/pallas_call | solution.py:206
  78.3 3.4 %all-to-all-start.3 = ((bf16[8,72,128]{2,1,0:T(8,128)(2,1)}), bf16[8,72,128]{2,1,0:T(8,128)(2,1)S(1)}, u32[]{:S(2)}, u32[]{:S(2)}) async-start(bf16[8,72,128]{2,1,0:T(8,128)(2,1)} %get-tuple-element.83), calls=%async_computation.3 | async-start | bytes 294912 | tf_op jit(solution)/shard_map/all_to_all | solution.py:26
  81.8 5.5 %all-to-all-done.3.refs_1_ = bf16[8,72,128]{2,1,0:T(8,128)(2,1)S(1)} async-done(((bf16[8,72,128]{2,1,0:T(8,128)(2,1)}), bf16[8,72,128]{2,1,0:T(8,128)(2,1)S(1)}, u32[]{:S(2)}, u32[]{:S(2)}) %all-to-all-start.3) | async-done | bytes 147488 | tf_op jit(solution)/shard_map/all_to_all | solution.py:26
  91.0 4.9 %all-to-all-start.4 = ((bf16[4,64,1152]{2,1,0:T(8,128)(2,1)}), bf16[4,64,1152]{2,1,0:T(8,128)(2,1)S(1)}, u32[]{:S(2)}, u32[]{:S(2)}) async-start(bf16[4,64,1152]{2,1,0:T(8,128)(2,1)} %bitcast.46), calls=%async_computation.4 | async-start | bytes 1179648 | tf_op jit(solution)/shard_map/all_to_all | solution.py:26
  98.4 14.7 %collective-permute-done.10.refs_6_.refs_3_ = bf16[288,1152]{1,0:T(8,128)(2,1)S(1)} collective-permute-done((bf16[288,1152]{1,0:T(8,128)(2,1)}, bf16[288,1152]{1,0:T(8,128)(2,1)S(1)}, u32[]{:S(2)}, u32[]{:S(2)}) %collective-permute-start.10) | collective-permute-done | bytes 663584 | tf_op jit(solution)/shard_map/ppermute | solution.py:22
  117.2 4.8 %all-to-all-start.5 = ((bf16[4,64,1152]{2,1,0:T(8,128)(2,1)}), bf16[4,64,1152]{2,1,0:T(8,128)(2,1)S(1)}, u32[]{:S(2)}, u32[]{:S(2)}) async-start(bf16[4,64,1152]{2,1,0:T(8,128)(2,1)} %get-tuple-element.88), calls=%async_computation.5 | async-start | bytes 1179648 | tf_op jit(solution)/shard_map/all_to_all | solution.py:26
  125.0 13.7 %collective-permute-done.11.refs_0_ = bf16[288,1152]{1,0:T(8,128)(2,1)} collective-permute-done((bf16[288,1152]{1,0:T(8,128)(2,1)}, bf16[288,1152]{1,0:T(8,128)(2,1)}, u32[]{:S(2)}, u32[]{:S(2)}) %collective-permute-start.11) | collective-permute-done | bytes 663584 | tf_op jit(solution)/shard_map/ppermute | solution.py:22
  142.7 10.7 %mlp.1 = (bf16[256,1152]{1,0:T(8,128)(2,1)}, bf16[256,1152]{1,0:T(8,128)(2,1)}, bf16[256,1152]{1,0:T(8,128)(2,1)}, f32[1,1152]{1,0:T(1,128)}, bf16[256,1152]{1,0...) custom-call(s32[7]{0:T(128)} %concatenate.24.refs_0_, ...), custom_call_target="tpu_custom_call" | custom-call | flops 1 | bytes 1 | tf_op jit(solution)/shard_map/mlp/pallas_call | solution.py:358
  153.5 4.8 %all-to-all-start.6 = ((bf16[4,64,1152]{2,1,0:T(8,128)(2,1)}), bf16[4,64,1152]{2,1,0:T(8,128)(2,1)S(1)}, u32[]{:S(2)}, u32[]{:S(2)}) async-start(bf16[4,64,1152]{2,1,0:T(8,128)(2,1)} %bitcast.45), calls=%async_computation.6 | async-start | bytes 1179648 | tf_op jit(solution)/shard_map/all_to_all | solution.py:26
  162.2 6.0 %late_weights.1 = (bf16[288,1152]{1,0:T(8,128)(2,1)}, bf16[288,1152]{1,0:T(8,128)(2,1)}, bf16[288,1152]{1,0:T(8,128)(2,1)}, bf16[288,1152]{1,0:T(8,128)(2,1)}) custom-call(s32[7]{0:T(128)} %concatenate.24.refs_0_, bf16[256,1152]{1,0:T(8,128)(2,1)} %bitcast.39, bf16[256,1152]{1,0:T(8,128)(2,1)} %get-tuple-element.89.refs_10_.refs_2_, ...), custom_call_target="tpu_custom_call" | custom-call | flops 1 | bytes 1 | tf_op jit(solution)/shard_map/late_weights/pallas_call | solution.py:358
  168.1 6.4 %all-to-all-done.6.refs_1_ = bf16[4,64,1152]{2,1,0:T(8,128)(2,1)S(1)} async-done(((bf16[4,64,1152]{2,1,0:T(8,128)(2,1)}), bf16[4,64,1152]{2,1,0:T(8,128)(2,1)S(1)}, u32[]{:S(2)}, u32[]{:S(2)}) %all-to-all-start.6) | async-done | bytes 589856 | tf_op jit(solution)/shard_map/all_to_all | solution.py:26
  175.3 3.0 middle_back.1
  178.4 3.5 %all-to-all-start.7 = ((bf16[4,64,1152]{2,1,0:T(8,128)(2,1)}), bf16[4,64,1152]{2,1,0:T(8,128)(2,1)S(1)}, u32[]{:S(2)}, u32[]{:S(2)}) async-start(bf16[4,64,1152]{2,1,0:T(8,128)(2,1)} %get-tuple-element.102), calls=%async_computation.7 | async-start | bytes 1179648 | tf_op jit(solution)/shard_map/all_to_all | solution.py:26
  183.9 14.2 %collective-permute-done.18.refs_3_ = bf16[288,1152]{1,0:T(8,128)(2,1)S(1)} collective-permute-done((bf16[288,1152]{1,0:T(8,128)(2,1)}, bf16[288,1152]{1,0:T(8,128)(2,1)S(1)}, u32[]{:S(2)}, u32[]{:S(2)}) %collective-permute-start.18) | collective-permute-done | bytes 663584 | tf_op jit(solution)/shard_map/ppermute | solution.py:22
  202.1 9.7 %all_to_all.71.refs_2_.refs_1_ = bf16[8,72,128]{2,1,0:T(8,128)(2,1)} all-to-all(bf16[8,72,128]{2,1,0:T(8,128)(2,1)} %get-tuple-element.103.refs_1_), channel_id=1, replica_groups=mesh['dp'=8,'tensor'=4] {'dp'}, dimensions={0} | all-to-all | bytes 294912 | tf_op jit(solution)/shard_map/all_to_all | solution.py:26
  212.4 3.4 %collective-permute-start.22 = (bf16[64,1152]{1,0:T(8,128)(2,1)}, bf16[64,1152]{1,0:T(8,128)(2,1)S(1)}, u32[]{:S(2)}, u32[]{:S(2)}) collective-permute-start(bf16[64,1152]{1,0:T(8,128)(2,1)} %gate.23), channel_id=1, source_target_pairs={{0,3},{1,2},{2,1},{3,0},{4,7},{5,6},{6,5},{7,4},{8,11},{9,10},{10,... | collective-permute-start | bytes 442376 | tf_op jit(solution)/shard_map/ppermute | solution.py:22
  216.8 11.2 %attend_backward.1.refs_0_ = bf16[8,72,640]{2,1,0:T(8,128)(2,1)} custom-call(s32[4]{0:T(128)} %pad_add_fusion.refs_0_, bf16[8,72,640]{2,1,0:T(8,128)(2,1)} %copy-done.30, bf16[8,72,128]{2,1,0:T(8,128)(2,1)} %all_to_all.71.refs_2_.refs_1_, f32[8,72,128]{2,1,0:T(8,128)} %get-tuple-element.107.refs_3_, f32[8,1,128]{2,1,0:T(1,128)} %get-tuple-element.108.refs_4_), custom_call_target="tpu_custom_call" | custom-call | flops 3000000000 | bytes 4000000 | tf_op jit(solution)/shard_map/attend_backward/pallas_call | solution.py:230
  230.3 4.3 %all-to-all-start.9 = ((bf16[8,72,640]{2,1,0:T(8,128)(2,1)}), bf16[8,72,640]{2,1,0:T(8,128)(2,1)}, u32[]{:S(2)}, u32[]{:S(2)}) async-start(bf16[8,72,640]{2,1,0:T(8,128)(2,1)} %gate.25), calls=%async_computation.9 | async-start | bytes 1474560 | tf_op jit(solution)/shard_map/all_to_all | solution.py:26
  242.8 3.9 %all-to-all-done.9.refs_1_ = bf16[8,72,640]{2,1,0:T(8,128)(2,1)} async-done(((bf16[8,72,640]{2,1,0:T(8,128)(2,1)}), bf16[8,72,640]{2,1,0:T(8,128)(2,1)}, u32[]{:S(2)}, u32[]{:S(2)}) %all-to-all-start.9) | async-done | bytes 737312 | tf_op jit(solution)/shard_map/all_to_all | solution.py:26
  246.7 5.2 %unspread.1 = (bf16[256,1152]{1,0:T(8,128)(2,1)}, bf16[256,576]{1,0:T(8,128)(2,1)}, bf16[256,576]{1,0:T(8,128)(2,1)}, bf16[256,576]{1,0:T(8,128)(2,1)}, f32[2,576]{1,0:T(2,128)}) custom-call(s32[7]{0:T(128)} %concatenate.24.refs_0_, bf16[8,72,640]{2,1,0:T(8,128)(2,1)} %all-to-all-done.9.refs_1_, bf16[1152,576]{1,0:T(8,128)(2,1)} %get-tuple-element.109.refs_2_, ...), custom_call_target="tpu_custom_call" | custom-call | flops 20000000000 | bytes 1 | tf_op jit(solution)/shard_map/unspread/pallas_call | solution.py:358
  254.6 4.6 %all-to-all-start.10 = ((bf16[4,64,1152]{2,1,0:T(8,128)(2,1)}), bf16[4,64,1152]{2,1,0:T(8,128)(2,1)}, u32[]{:S(2)}, u32[]{:S(2)}) async-start(bf16[4,64,1152]{2,1,0:T(8,128)(2,1)} %bitcast.44), calls=%async_computation.10 | async-start | bytes 1179648 | tf_op jit(solution)/shard_map/all_to_all | solution.py:26
  260.3 4.9 %early_weights.1 = (bf16[288,576]{1,0:T(8,128)(2,1)}, bf16[288,576]{1,0:T(8,128)(2,1)}, bf16[288,576]{1,0:T(8,128)(2,1)}, bf16[288,576]{1,0:T(8,128)(2,1)}) custom-call(s32[7]{0:T(128)} %concatenate.24.refs_0_, bf16[256,1152]{1,0:T(8,128)(2,1)} %get-tuple-element.118.refs_1_, bf16[256,1152]{1,0:T(8,128)(2,1)} %bitcast.41, ...), custom_call_target="tpu_custom_call" | custom-call | flops 1 | bytes 1 | tf_op jit(solution)/shard_map/early_weights/pallas_call | solution.py:358
  268.6 7.8 %collective-permute-done.31.refs_11_ = bf16[288,576]{1,0:T(8,128)(2,1)S(1)} collective-permute-done((bf16[288,576]{1,0:T(8,128)(2,1)}, bf16[288,576]{1,0:T(8,128)(2,1)S(1)}, u32[]{:S(2)}, u32[]{:S(2)}) %collective-permute-start.31) | collective-permute-done | bytes 331808 | tf_op jit(solution)/shard_map/ppermute | solution.py:22
  281.8 5.1 %all-to-all-start.11 = ((f32[4,18,288]{2,1,0:T(8,128)}), f32[4,18,288]{2,1,0:T(8,128)S(1)}, u32[]{:S(2)}, u32[]{:S(2)}) async-start(f32[4,18,288]{2,1,0:T(8,128)} %get-tuple-element.126.refs_1_), calls=%async_computation.11 | async-start | bytes 294912 | tf_op jit(solution)/shard_map/all_to_all | solution.py:26
  294.2 3.5 %all-to-all-start.12 = ((f32[8,32,288]{2,1,0:T(8,128)}), f32[8,32,288]{2,1,0:T(8,128)S(1)}, u32[]{:S(2)}, u32[]{:S(2)}) async-start(f32[8,32,288]{2,1,0:T(8,128)} %gate.27.refs_1_), calls=%async_computation.12 | async-start | bytes 786432 | tf_op jit(solution)/shard_map/all_to_all | solution.py:26
  (284 shorter events, 108.9 us)
Async XLA Ops:
  3.1 17.0 %collective-permute-start.1 = (bf16[144,576]{1,0:T(8,128)(2,1)S(1)}, bf16[144,576]{1,0:T(8,128)(2,1)S(1)}, u32[]{:S(2)}, u32[]{:S(2)}) collective-permute-start(bf16[144,576]{1,0:T(8,128)(2,1)S(1)} %broadcast_select_fusion.7), channel_id=1, source_target_pairs={{0,4},{4,0},{8,12},{12,8},{16,20},{20,16},{24,28},{28,24},{1,5},{5... | collective-permute-start | bytes 497672 | tf_op jit(solution)/shard_map/ppermute | solution.py:22
  21.0 15.0 %collective-permute-start.2 = (bf16[288,576]{1,0:T(8,128)(2,1)}, bf16[288,576]{1,0:T(8,128)(2,1)S(1)}, u32[]{:S(2)}, u32[]{:S(2)}) collective-permute-start(bf16[288,576]{1,0:T(8,128)(2,1)} %gate.16.refs_0_), channel_id=1, source_target_pairs={{0,8},{4,12},{8,0},{12,4},{16,24},{20,28},{24,16},{28,20},{1,9},{5... | collective-permute-start | bytes 995336 | tf_op jit(solution)/shard_map/ppermute | solution.py:22
  21.6 18.3 %collective-permute-start.3 = (bf16[288,576]{1,0:T(8,128)(2,1)}, bf16[288,576]{1,0:T(8,128)(2,1)S(1)}, u32[]{:S(2)}, u32[]{:S(2)}) collective-permute-start(bf16[288,576]{1,0:T(8,128)(2,1)} %gate.16.refs_0_), channel_id=1, source_target_pairs={{0,16},{4,20},{8,24},{12,28},{16,0},{20,4},{24,8},{28,12},{1,17},{... | collective-permute-start | bytes 995336 | tf_op jit(solution)/shard_map/ppermute | solution.py:22
  22.1 17.7 %collective-permute-start.4 = (bf16[288,576]{1,0:T(8,128)(2,1)}, bf16[288,576]{1,0:T(8,128)(2,1)S(1)}, u32[]{:S(2)}, u32[]{:S(2)}) collective-permute-start(bf16[288,576]{1,0:T(8,128)(2,1)} %gate.16.refs_0_), channel_id=1, source_target_pairs={{0,24},{4,28},{8,16},{12,20},{16,8},{20,12},{24,0},{28,4},{1,25},{... | collective-permute-start | bytes 995336 | tf_op jit(solution)/shard_map/ppermute | solution.py:22
  51.9 15.7 %all-to-all-start.2 = ((bf16[8,72,640]{2,1,0:T(8,128)(2,1)}), bf16[8,72,640]{2,1,0:T(8,128)(2,1)S(1)}, u32[]{:S(2)}, u32[]{:S(2)}) async-start(bf16[8,72,640]{2,1,0:T(8,128)(2,1)} %get-tuple-element.82), calls=%async_computation.2 | async-start | bytes 1474560 | tf_op jit(solution)/shard_map/all_to_all | solution.py:26
  55.7 25.9 %collective-permute-start = (bf16[144,1152]{1,0:T(8,128)(2,1)S(1)}, bf16[144,1152]{1,0:T(8,128)(2,1)S(1)}, u32[]{:S(2)}, u32[]{:S(2)}) collective-permute-start(bf16[144,1152]{1,0:T(8,128)(2,1)S(1)} %bitcast_select_fusion), channel_id=1, source_target_pairs={{0,4},{4,0},{8,12},{12,8},{16,20},{20,16},{24,28},{28,24},{1,5},{5... | collective-permute-start | bytes 995336 | tf_op jit(solution)/shard_map/ppermute | solution.py:22
  91.0 22.4 %all-to-all-start.4 = ((bf16[4,64,1152]{2,1,0:T(8,128)(2,1)}), bf16[4,64,1152]{2,1,0:T(8,128)(2,1)S(1)}, u32[]{:S(2)}, u32[]{:S(2)}) async-start(bf16[4,64,1152]{2,1,0:T(8,128)(2,1)} %bitcast.46), calls=%async_computation.4 | async-start | bytes 1179648 | tf_op jit(solution)/shard_map/all_to_all | solution.py:26
  96.7 16.4 %collective-permute-start.10 = (bf16[288,1152]{1,0:T(8,128)(2,1)}, bf16[288,1152]{1,0:T(8,128)(2,1)S(1)}, u32[]{:S(2)}, u32[]{:S(2)}) collective-permute-start(bf16[288,1152]{1,0:T(8,128)(2,1)} %gate.18.refs_1_), channel_id=1, source_target_pairs={{0,16},{4,20},{8,24},{12,28},{16,0},{20,4},{24,8},{28,12},{1,17},{... | collective-permute-start | bytes 1990664 | tf_op jit(solution)/shard_map/ppermute | solution.py:22
  97.3 16.1 %collective-permute-start.9 = (bf16[288,1152]{1,0:T(8,128)(2,1)}, bf16[288,1152]{1,0:T(8,128)(2,1)S(1)}, u32[]{:S(2)}, u32[]{:S(2)}) collective-permute-start(bf16[288,1152]{1,0:T(8,128)(2,1)} %gate.18.refs_1_), channel_id=1, source_target_pairs={{0,8},{4,12},{8,0},{12,4},{16,24},{20,28},{24,16},{28,20},{1,9},{5... | collective-permute-start | bytes 1990664 | tf_op jit(solution)/shard_map/ppermute | solution.py:22
  117.2 21.5 %all-to-all-start.5 = ((bf16[4,64,1152]{2,1,0:T(8,128)(2,1)}), bf16[4,64,1152]{2,1,0:T(8,128)(2,1)S(1)}, u32[]{:S(2)}, u32[]{:S(2)}) async-start(bf16[4,64,1152]{2,1,0:T(8,128)(2,1)} %get-tuple-element.88), calls=%async_computation.5 | async-start | bytes 1179648 | tf_op jit(solution)/shard_map/all_to_all | solution.py:26
  122.8 15.9 %collective-permute-start.11 = (bf16[288,1152]{1,0:T(8,128)(2,1)}, bf16[288,1152]{1,0:T(8,128)(2,1)}, u32[]{:S(2)}, u32[]{:S(2)}) collective-permute-start(bf16[288,1152]{1,0:T(8,128)(2,1)} %gate.19), channel_id=1, source_target_pairs={{0,24},{4,28},{8,16},{12,20},{16,8},{20,12},{24,0},{28,4},{1,25},{... | collective-permute-start | bytes 1990664 | tf_op jit(solution)/shard_map/ppermute | solution.py:22
  124.4 15.8 %collective-permute-start.12 = (bf16[288,1152]{1,0:T(8,128)(2,1)S(1)}, bf16[288,1152]{1,0:T(8,128)(2,1)}, u32[]{:S(2)}, u32[]{:S(2)}) collective-permute-start(bf16[288,1152]{1,0:T(8,128)(2,1)S(1)} %copy-done), channel_id=1, source_target_pairs={{0,4},{4,0},{8,12},{12,8},{16,20},{20,16},{24,28},{28,24},{1,5},{5... | collective-permute-start | bytes 1990664 | tf_op jit(solution)/shard_map/ppermute | solution.py:22
  124.4 15.8 %collective-permute-start.13 = (bf16[288,1152]{1,0:T(8,128)(2,1)S(1)}, bf16[288,1152]{1,0:T(8,128)(2,1)}, u32[]{:S(2)}, u32[]{:S(2)}) collective-permute-start(bf16[288,1152]{1,0:T(8,128)(2,1)S(1)} %copy-done.8), channel_id=1, source_target_pairs={{0,4},{4,0},{8,12},{12,8},{16,20},{20,16},{24,28},{28,24},{1,5},{5... | collective-permute-start | bytes 1990664 | tf_op jit(solution)/shard_map/ppermute | solution.py:22
  124.9 15.3 %collective-permute-start.14 = (bf16[288,1152]{1,0:T(8,128)(2,1)S(1)}, bf16[288,1152]{1,0:T(8,128)(2,1)}, u32[]{:S(2)}, u32[]{:S(2)}) collective-permute-start(bf16[288,1152]{1,0:T(8,128)(2,1)S(1)} %copy-done.6), channel_id=1, source_target_pairs={{0,4},{4,0},{8,12},{12,8},{16,20},{20,16},{24,28},{28,24},{1,5},{5... | collective-permute-start | bytes 1990664 | tf_op jit(solution)/shard_map/ppermute | solution.py:22
  153.5 21.0 %all-to-all-start.6 = ((bf16[4,64,1152]{2,1,0:T(8,128)(2,1)}), bf16[4,64,1152]{2,1,0:T(8,128)(2,1)S(1)}, u32[]{:S(2)}, u32[]{:S(2)}) async-start(bf16[4,64,1152]{2,1,0:T(8,128)(2,1)} %bitcast.45), calls=%async_computation.6 | async-start | bytes 1179648 | tf_op jit(solution)/shard_map/all_to_all | solution.py:26
  178.4 19.9 %all-to-all-start.7 = ((bf16[4,64,1152]{2,1,0:T(8,128)(2,1)}), bf16[4,64,1152]{2,1,0:T(8,128)(2,1)S(1)}, u32[]{:S(2)}, u32[]{:S(2)}) async-start(bf16[4,64,1152]{2,1,0:T(8,128)(2,1)} %get-tuple-element.102), calls=%async_computation.7 | async-start | bytes 1179648 | tf_op jit(solution)/shard_map/all_to_all | solution.py:26
  181.8 16.2 %collective-permute-start.18 = (bf16[288,1152]{1,0:T(8,128)(2,1)}, bf16[288,1152]{1,0:T(8,128)(2,1)S(1)}, u32[]{:S(2)}, u32[]{:S(2)}) collective-permute-start(bf16[288,1152]{1,0:T(8,128)(2,1)} %get-tuple-element.99.refs_7_), channel_id=1, source_target_pairs={{0,8},{4,12},{8,0},{12,4},{16,24},{20,28},{24,16},{28,20},{1,9},{5... | collective-permute-start | bytes 1990664 | tf_op jit(solution)/shard_map/ppermute | solution.py:22
  182.6 15.6 %collective-permute-start.19 = (bf16[288,1152]{1,0:T(8,128)(2,1)S(1)}, bf16[288,1152]{1,0:T(8,128)(2,1)S(1)}, u32[]{:S(2)}, u32[]{:S(2)}) collective-permute-start(bf16[288,1152]{1,0:T(8,128)(2,1)S(1)} %copy-done.32), channel_id=1, source_target_pairs={{0,16},{4,20},{8,24},{12,28},{16,0},{20,4},{24,8},{28,12},{1,17},{... | collective-permute-start | bytes 1990664 | tf_op jit(solution)/shard_map/ppermute | solution.py:22
  211.8 17.6 %collective-permute-start.26 = (bf16[288,1152]{1,0:T(8,128)(2,1)}, bf16[288,1152]{1,0:T(8,128)(2,1)S(1)}, u32[]{:S(2)}, u32[]{:S(2)}) collective-permute-start(bf16[288,1152]{1,0:T(8,128)(2,1)} %gate.24), channel_id=1, source_target_pairs={{0,24},{4,28},{8,16},{12,20},{16,8},{20,12},{24,0},{28,4},{1,25},{... | collective-permute-start | bytes 1990664 | tf_op jit(solution)/shard_map/ppermute | solution.py:22
  212.4 15.6 %collective-permute-start.22 = (bf16[64,1152]{1,0:T(8,128)(2,1)}, bf16[64,1152]{1,0:T(8,128)(2,1)S(1)}, u32[]{:S(2)}, u32[]{:S(2)}) collective-permute-start(bf16[64,1152]{1,0:T(8,128)(2,1)} %gate.23), channel_id=1, source_target_pairs={{0,3},{1,2},{2,1},{3,0},{4,7},{5,6},{6,5},{7,4},{8,11},{9,10},{10,... | collective-permute-start | bytes 442376 | tf_op jit(solution)/shard_map/ppermute | solution.py:22
  215.8 12.5 %collective-permute-start.20 = (bf16[64,1152]{1,0:T(8,128)(2,1)}, bf16[64,1152]{1,0:T(8,128)(2,1)S(1)}, u32[]{:S(2)}, u32[]{:S(2)}) collective-permute-start(bf16[64,1152]{1,0:T(8,128)(2,1)} %gate.21), channel_id=1, source_target_pairs={{0,1},{1,0},{2,3},{3,2},{4,5},{5,4},{6,7},{7,6},{8,9},{9,8},{10,11... | collective-permute-start | bytes 442376 | tf_op jit(solution)/shard_map/ppermute | solution.py:22
  230.3 16.4 %all-to-all-start.9 = ((bf16[8,72,640]{2,1,0:T(8,128)(2,1)}), bf16[8,72,640]{2,1,0:T(8,128)(2,1)}, u32[]{:S(2)}, u32[]{:S(2)}) async-start(bf16[8,72,640]{2,1,0:T(8,128)(2,1)} %gate.25), calls=%async_computation.9 | async-start | bytes 1474560 | tf_op jit(solution)/shard_map/all_to_all | solution.py:26
  235.2 25.1 %collective-permute-start.27 = (bf16[256,1152]{1,0:T(8,128)(2,1)}, bf16[256,1152]{1,0:T(8,128)(2,1)}, u32[]{:S(2)}, u32[]{:S(2)}) collective-permute-start(bf16[256,1152]{1,0:T(8,128)(2,1)} %get-tuple-element.118.refs_1_), channel_id=1, source_target_pairs={{0,4},{4,0},{8,12},{12,8},{16,20},{20,16},{24,28},{28,24},{1,5},{5... | collective-permute-start | bytes 1769480 | tf_op jit(solution)/shard_map/ppermute | solution.py:22
  235.6 24.7 %collective-permute-start.30 = (bf16[256,576]{1,0:T(8,128)(2,1)}, bf16[256,576]{1,0:T(8,128)(2,1)}, u32[]{:S(2)}, u32[]{:S(2)}) collective-permute-start(bf16[256,576]{1,0:T(8,128)(2,1)} %get-tuple-element.121.refs_5_), channel_id=1, source_target_pairs={{0,4},{4,0},{8,12},{12,8},{16,20},{20,16},{24,28},{28,24},{1,5},{5... | collective-permute-start | bytes 884744 | tf_op jit(solution)/shard_map/ppermute | solution.py:22
  238.1 13.8 %collective-permute-start.23 = (bf16[64,1152]{1,0:T(8,128)(2,1)}, bf16[64,1152]{1,0:T(8,128)(2,1)S(1)}, u32[]{:S(2)}, u32[]{:S(2)}) collective-permute-start(bf16[64,1152]{1,0:T(8,128)(2,1)} %get-tuple-element.106.refs_1_), channel_id=1, source_target_pairs={{0,1},{1,0},{2,3},{3,2},{4,5},{5,4},{6,7},{7,6},{8,9},{9,8},{10,11... | collective-permute-start | bytes 442376 | tf_op jit(solution)/shard_map/ppermute | solution.py:22
  239.7 14.2 %collective-permute-start.24 = (bf16[64,1152]{1,0:T(8,128)(2,1)}, bf16[64,1152]{1,0:T(8,128)(2,1)S(1)}, u32[]{:S(2)}, u32[]{:S(2)}) collective-permute-start(bf16[64,1152]{1,0:T(8,128)(2,1)} %get-tuple-element.106.refs_1_), channel_id=1, source_target_pairs={{0,2},{1,3},{2,0},{3,1},{4,6},{5,7},{6,4},{7,5},{8,10},{9,11},{10,... | collective-permute-start | bytes 442376 | tf_op jit(solution)/shard_map/ppermute | solution.py:22
  254.6 23.7 %all-to-all-start.10 = ((bf16[4,64,1152]{2,1,0:T(8,128)(2,1)}), bf16[4,64,1152]{2,1,0:T(8,128)(2,1)}, u32[]{:S(2)}, u32[]{:S(2)}) async-start(bf16[4,64,1152]{2,1,0:T(8,128)(2,1)} %bitcast.44), calls=%async_computation.10 | async-start | bytes 1179648 | tf_op jit(solution)/shard_map/all_to_all | solution.py:26
  260.1 28.3 %collective-permute-start.38 = (f32[144,1152]{1,0:T(8,128)}, f32[144,1152]{1,0:T(8,128)}, u32[]{:S(2)}, u32[]{:S(2)}) collective-permute-start(f32[144,1152]{1,0:T(8,128)} %slice_select_fusion), channel_id=1, source_target_pairs={{0,4},{4,0},{8,12},{12,8},{16,20},{20,16},{24,28},{28,24},{1,5},{5... | collective-permute-start | bytes 1990664 | tf_op jit(solution)/shard_map/ppermute | solution.py:22
  286.9 15.2 %collective-permute-start.36 = (bf16[288,576]{1,0:T(8,128)(2,1)}, bf16[288,576]{1,0:T(8,128)(2,1)}, u32[]{:S(2)}, u32[]{:S(2)}) collective-permute-start(bf16[288,576]{1,0:T(8,128)(2,1)} %gate.29), channel_id=1, source_target_pairs={{0,24},{4,28},{8,16},{12,20},{16,8},{20,12},{24,0},{28,4},{1,25},{... | collective-permute-start | bytes 995336 | tf_op jit(solution)/shard_map/ppermute | solution.py:22
  297.6 16.9 %collective-permute-start.33 = (bf16[64,1152]{1,0:T(8,128)(2,1)}, bf16[64,1152]{1,0:T(8,128)(2,1)S(1)}, u32[]{:S(2)}, u32[]{:S(2)}) collective-permute-start(bf16[64,1152]{1,0:T(8,128)(2,1)} %gate.28.refs_0_), channel_id=1, source_target_pairs={{0,1},{1,0},{2,3},{3,2},{4,5},{5,4},{6,7},{7,6},{8,9},{9,8},{10,11... | collective-permute-start | bytes 442376 | tf_op jit(solution)/shard_map/ppermute | solution.py:22
  298.7 15.9 %collective-permute-start.34 = (bf16[64,1152]{1,0:T(8,128)(2,1)}, bf16[64,1152]{1,0:T(8,128)(2,1)S(1)}, u32[]{:S(2)}, u32[]{:S(2)}) collective-permute-start(bf16[64,1152]{1,0:T(8,128)(2,1)} %gate.28.refs_0_), channel_id=1, source_target_pairs={{0,2},{1,3},{2,0},{3,1},{4,6},{5,7},{6,4},{7,5},{8,10},{9,11},{10,... | collective-permute-start | bytes 442376 | tf_op jit(solution)/shard_map/ppermute | solution.py:22
  300.0 14.5 %collective-permute-start.35 = (bf16[64,1152]{1,0:T(8,128)(2,1)}, bf16[64,1152]{1,0:T(8,128)(2,1)S(1)}, u32[]{:S(2)}, u32[]{:S(2)}) collective-permute-start(bf16[64,1152]{1,0:T(8,128)(2,1)} %gate.28.refs_0_), channel_id=1, source_target_pairs={{0,3},{1,2},{2,1},{3,0},{4,7},{5,6},{6,5},{7,4},{8,11},{9,10},{10,... | collective-permute-start | bytes 442376 | tf_op jit(solution)/shard_map/ppermute | solution.py:22
  (79 other events, 378.2 us)

commit v10 on v9

--- a/solution.py
+++ b/solution.py
@@ -12,7 +12,7 @@
 NORM_EPS = 1e-06
 NEGATIVE = -1e30
 SCALE = 1.0 / math.sqrt(DH)
-VMEM_BYTES = 58 * 1024 * 1024
+VMEM_BYTES = 64 * 1024 * 1024
 BF16 = jnp.bfloat16
 F32 = jnp.float32
 
@@ -801,12 +801,16 @@
     mod_part = mod_part.reshape(latents * 6, features)
     bias_ada = jnp.tile(b_ada.astype(F32), (latents, 1))
     few_chips = n_dp // 2 == 4
-    mod_mine = jnp.sum(gather(mod_part, "dp", n_dp), axis=0) + bias_ada
-    early_rows = gate(early_rows, mod_mine)
-    mod_parts = gather(mod_mine, "tensor", n_tensor)
+    if few_chips:
+        mod_part = mod_part + jnp.where(my_dp == 0, bias_ada, 0.0)
+        mod_wide = gather(mod_part, "tensor", n_tensor)
+        mod_parts = gather(mod_wide, "dp", n_dp).reshape((-1,) + mod_part.shape)
+    else:
+        mod_wide = jnp.sum(gather(mod_part, "dp", n_dp), axis=0) + bias_ada
+        mod_parts = gather(mod_wide, "tensor", n_tensor)
     early_parts = chip_parts(early_rows) if few_chips else [gather_chips(early_rows)]
 
-    early_parts = list(gate_all(early_parts, mod_parts))
+    early_parts = list(gate_all(early_parts, mod_wide))
     early_parts += [swap(part, "dp", 1) for part in early_parts]
     count = len(early_parts) // 2
     meta = jnp.stack([core, my_dp * rows, my_tensor, my_dp // 2]).astype(jnp.int32)

time: 328 us -> 328 us (level)
  other arithmetic: 14.5 us -> 26.7 us
  blocking collectives: 21.1 us -> 9.69 us
  starting transfers between devices: 80.3 us -> 88.6 us
  local copies, waits for them, and re-layouts: 28.5 us -> 23 us
    all_to_all x2 -> x1, blocking collectives: 21.1 us -> 9.69 us  [exchange(): return lax.all_to_all(blocks, axis, 0, 0, tiled=True)]
    unnamed x126 -> x72, local copies, waits for them, and re-layouts: 17.5 us -> 8.38 us
    all_to_all x12 -> x13, starting transfers between devices: 49.9 us -> 58.3 us  [exchange(): return lax.all_to_all(blocks, axis, 0, 0, tiled=True)]
    all_to_all x12 -> x13, waiting for transfers between devices: 39.8 us -> 34.5 us  [exchange(): return lax.all_to_all(blocks, axis, 0, 0, tiled=True)]
    add x2, other arithmetic: 1.58 us -> 5.38 us  [finish_pair(): rows = sum((part.astype(F32) for part in parts))]
  transfers between devices with their start and end apart: 51 -> 52, of which waited for: 24 -> 24; matrix products, arithmetic and copies ran while one was open for 7% -> 12% of each run, Pallas kernels for 15% -> 14%
where the time goes in v10:
time: 328 us; the launch traced here: 326 us
  waiting for transfers between devices  103 us (31%)
  starting transfers between devices  88.6 us (27%)
  Pallas kernels  73.9 us (23%)
  other arithmetic  26.7 us (8%)
  local copies, waits for them, and re-layouts  23 us (7%)
  blocking collectives  9.69 us (3%)
    ppermute x39, waiting for transfers between devices, swap(): return lax.ppermute(block, axis, route)  68.1 us
    all_to_all x13, starting transfers between devices, exchange(): return lax.all_to_all(blocks, axis, 0, 0, tiled=True)  58.3 us
    pallas_call x13, Pallas kernels, call(): pl.pallas_call(kernel, out_shape=tuple((jax.ShapeDtypeStruct(shape, kind)...  55.2 us
    all_to_all x13, waiting for transfers between devices, exchange(): return lax.all_to_all(blocks, axis, 0, 0, tiled=True)  34.5 us
    ppermute x39, starting transfers between devices, swap(): return lax.ppermute(block, axis, route)  30.3 us
    pallas_call x1, Pallas kernels, attend_backward(): pl.pallas_call(lambda *refs: backward_kernel(meta.shape[0] - 1, *refs), o...  10 us
    all_to_all x1, blocking collectives, exchange(): return lax.all_to_all(blocks, axis, 0, 0, tiled=True)  9.69 us
    pallas_call x1, Pallas kernels, attend_forward(): pl.pallas_call(lambda *refs: forward_kernel(meta.shape[0] - 1, *refs), ou...  8.68 us
  transfers between devices with their start and end apart: 52, of which 24 were waited for; matrix products, arithmetic and copies ran while one was open for 12% of the time, Pallas kernels for 14%

profile of v10, /device:TPU:0, one launch (start us, length us, event | category | flops | bytes accessed | tf_op | source)
XLA Modules:
  0.0 326.0 jit_solution(3986540365351877089)
XLA Ops:
  7.9 5.9 %all-to-all-start = ((f32[4,18,288]{2,1,0:T(8,128)}), f32[4,18,288]{2,1,0:T(8,128)S(1)}, u32[]{:S(2)}, u32[]{:S(2)}) async-start(f32[4,18,288]{2,1,0:T(8,128)} %broadcast_in_dim.16), calls=%async_computation | async-start | bytes 294912 | tf_op jit(solution)/shard_map/all_to_all | solution.py:26
  21.6 3.9 %all-to-all-start.1 = ((f32[8,4,18,288]{3,1,2,0:T(4,128)}), f32[8,4,18,288]{3,1,2,0:T(4,128)S(1)}, u32[]{:S(2)}, u32[]{:S(2)}) async-start(f32[8,4,18,288]{3,1,2,0:T(4,128)} %broadcast_in_dim.17), calls=%async_computation.1 | async-start | bytes 1769472 | tf_op jit(solution)/shard_map/all_to_all | solution.py:26
  25.5 8.5 %collective-permute-done.3.refs_2_ = bf16[288,576]{1,0:T(8,128)(2,1)S(1)} collective-permute-done((bf16[288,576]{1,0:T(8,128)(2,1)S(1)}, bf16[288,576]{1,0:T(8,128)(2,1)S(1)}, u32[]{:S(2)}, u32[]{:S(2)}) %collective-permute-start.3) | collective-permute-done | bytes 331808 | tf_op jit(solution)/shard_map/ppermute | solution.py:22
  38.0 5.4 %all-to-all-done.1 = f32[8,4,18,288]{3,1,2,0:T(4,128)S(1)} async-done(((f32[8,4,18,288]{3,1,2,0:T(4,128)}), f32[8,4,18,288]{3,1,2,0:T(4,128)S(1)}, u32[]{:S(2)}, u32[]{:S(2)}) %all-to-all-start.1) | async-done | bytes 663584 | tf_op jit(solution)/shard_map/all_to_all | solution.py:26
  44.5 6.5 %project.1 = (bf16[256,1152]{1,0:T(8,128)(2,1)}, bf16[256,1152]{1,0:T(8,128)(2,1)}, bf16[8,72,640]{2,1,0:T(8,128)(2,1)}, bf16[1152,576]{1,0:T(8,128)(2,1)}, bf16...) custom-call(s32[7]{0:T(128)} %concatenate.24.refs_0_, bf16[288,576]{1,0:T(8,128)(2,1)} %get-tuple-element.78.refs_1_, ...), custom_call_target="tpu_custom_call" | custom-call | flops 1 | bytes 1 | tf_op jit(solution)/shard_map/project/pallas_call | solution.py:358
  51.1 4.4 %all-to-all-start.2 = ((bf16[8,72,640]{2,1,0:T(8,128)(2,1)}), bf16[8,72,640]{2,1,0:T(8,128)(2,1)}, u32[]{:S(2)}, u32[]{:S(2)}) async-start(bf16[8,72,640]{2,1,0:T(8,128)(2,1)} %get-tuple-element.82), calls=%async_computation.2 | async-start | bytes 1474560 | tf_op jit(solution)/shard_map/all_to_all | solution.py:26
  57.2 10.3 %all-to-all-done.2.refs_1_ = bf16[8,72,640]{2,1,0:T(8,128)(2,1)} async-done(((bf16[8,72,640]{2,1,0:T(8,128)(2,1)}), bf16[8,72,640]{2,1,0:T(8,128)(2,1)}, u32[]{:S(2)}, u32[]{:S(2)}) %all-to-all-start.2) | async-done | bytes 737312 | tf_op jit(solution)/shard_map/all_to_all | solution.py:26
  67.5 8.7 %attend_forward.1 = (bf16[8,72,128]{2,1,0:T(8,128)(2,1)}, f32[8,72,128]{2,1,0:T(8,128)}, f32[8,1,128]{2,1,0:T(1,128)}) custom-call(s32[4]{0:T(128)} %pad_add_fusion.refs_0_, bf16[8,72,640]{2,1,0:T(8,128)(2,1)} %all-to-all-done.2.refs_1_), custom_call_target="tpu_custom_call" | custom-call | flops 1000000000 | bytes 4000000 | tf_op jit(solution)/shard_map/attend_forward/pallas_call | solution.py:206
  76.2 4.0 %all-to-all-start.3 = ((bf16[8,72,128]{2,1,0:T(8,128)(2,1)}), bf16[8,72,128]{2,1,0:T(8,128)(2,1)}, u32[]{:S(2)}, u32[]{:S(2)}) async-start(bf16[8,72,128]{2,1,0:T(8,128)(2,1)} %get-tuple-element.83), calls=%async_computation.3 | async-start | bytes 294912 | tf_op jit(solution)/shard_map/all_to_all | solution.py:26
  82.3 3.6 %all-to-all-done.3.refs_1_ = bf16[8,72,128]{2,1,0:T(8,128)(2,1)} async-done(((bf16[8,72,128]{2,1,0:T(8,128)(2,1)}), bf16[8,72,128]{2,1,0:T(8,128)(2,1)}, u32[]{:S(2)}, u32[]{:S(2)}) %all-to-all-start.3) | async-done | bytes 147488 | tf_op jit(solution)/shard_map/all_to_all | solution.py:26
  89.0 4.9 %all-to-all-start.4 = ((bf16[4,64,1152]{2,1,0:T(8,128)(2,1)}), bf16[4,64,1152]{2,1,0:T(8,128)(2,1)}, u32[]{:S(2)}, u32[]{:S(2)}) async-start(bf16[4,64,1152]{2,1,0:T(8,128)(2,1)} %bitcast.45), calls=%async_computation.4 | async-start | bytes 1179648 | tf_op jit(solution)/shard_map/all_to_all | solution.py:26
  96.5 14.8 %collective-permute-done.10.refs_6_.refs_3_ = bf16[288,1152]{1,0:T(8,128)(2,1)} collective-permute-done((bf16[288,1152]{1,0:T(8,128)(2,1)}, bf16[288,1152]{1,0:T(8,128)(2,1)}, u32[]{:S(2)}, u32[]{:S(2)}) %collective-permute-start.10) | collective-permute-done | bytes 663584 | tf_op jit(solution)/shard_map/ppermute | solution.py:22
  114.2 4.9 %all-to-all-start.5 = ((bf16[4,64,1152]{2,1,0:T(8,128)(2,1)}), bf16[4,64,1152]{2,1,0:T(8,128)(2,1)S(1)}, u32[]{:S(2)}, u32[]{:S(2)}) async-start(bf16[4,64,1152]{2,1,0:T(8,128)(2,1)} %get-tuple-element.88), calls=%async_computation.5 | async-start | bytes 1179648 | tf_op jit(solution)/shard_map/all_to_all | solution.py:26
  122.0 13.5 %collective-permute-done.11.refs_0_ = bf16[288,1152]{1,0:T(8,128)(2,1)S(1)} collective-permute-done((bf16[288,1152]{1,0:T(8,128)(2,1)}, bf16[288,1152]{1,0:T(8,128)(2,1)S(1)}, u32[]{:S(2)}, u32[]{:S(2)}) %collective-permute-start.11) | collective-permute-done | bytes 663584 | tf_op jit(solution)/shard_map/ppermute | solution.py:22
  139.0 10.7 %mlp.1 = (bf16[256,1152]{1,0:T(8,128)(2,1)}, bf16[256,1152]{1,0:T(8,128)(2,1)}, bf16[256,1152]{1,0:T(8,128)(2,1)}, f32[1,1152]{1,0:T(1,128)}, bf16[256,1152]{1,0...) custom-call(s32[7]{0:T(128)} %concatenate.24.refs_0_, ...), custom_call_target="tpu_custom_call" | custom-call | flops 1 | bytes 1 | tf_op jit(solution)/shard_map/mlp/pallas_call | solution.py:358
  149.7 4.8 %all-to-all-start.6 = ((bf16[4,64,1152]{2,1,0:T(8,128)(2,1)}), bf16[4,64,1152]{2,1,0:T(8,128)(2,1)}, u32[]{:S(2)}, u32[]{:S(2)}) async-start(bf16[4,64,1152]{2,1,0:T(8,128)(2,1)} %bitcast.44), calls=%async_computation.6 | async-start | bytes 1179648 | tf_op jit(solution)/shard_map/all_to_all | solution.py:26
  157.7 6.0 %late_weights.1 = (bf16[288,1152]{1,0:T(8,128)(2,1)}, bf16[288,1152]{1,0:T(8,128)(2,1)}, bf16[288,1152]{1,0:T(8,128)(2,1)}, bf16[288,1152]{1,0:T(8,128)(2,1)}) custom-call(s32[7]{0:T(128)} %concatenate.24.refs_0_, bf16[256,1152]{1,0:T(8,128)(2,1)} %bitcast.40, bf16[256,1152]{1,0:T(8,128)(2,1)} %get-tuple-element.89.refs_10_.refs_2_, ...), custom_call_target="tpu_custom_call" | custom-call | flops 1 | bytes 1 | tf_op jit(solution)/shard_map/late_weights/pallas_call | solution.py:358
  163.7 7.4 %all-to-all-done.6.refs_1_ = bf16[4,64,1152]{2,1,0:T(8,128)(2,1)} async-done(((bf16[4,64,1152]{2,1,0:T(8,128)(2,1)}), bf16[4,64,1152]{2,1,0:T(8,128)(2,1)}, u32[]{:S(2)}, u32[]{:S(2)}) %all-to-all-start.6) | async-done | bytes 589856 | tf_op jit(solution)/shard_map/all_to_all | solution.py:26
  174.1 4.2 %all-to-all-start.7 = ((bf16[4,64,1152]{2,1,0:T(8,128)(2,1)}), bf16[4,64,1152]{2,1,0:T(8,128)(2,1)}, u32[]{:S(2)}, u32[]{:S(2)}) async-start(bf16[4,64,1152]{2,1,0:T(8,128)(2,1)} %get-tuple-element.102), calls=%async_computation.7 | async-start | bytes 1179648 | tf_op jit(solution)/shard_map/all_to_all | solution.py:26
  180.5 14.2 %collective-permute-done.18.refs_3_ = bf16[288,1152]{1,0:T(8,128)(2,1)} collective-permute-done((bf16[288,1152]{1,0:T(8,128)(2,1)}, bf16[288,1152]{1,0:T(8,128)(2,1)}, u32[]{:S(2)}, u32[]{:S(2)}) %collective-permute-start.18) | collective-permute-done | bytes 663584 | tf_op jit(solution)/shard_map/ppermute | solution.py:22
  197.9 9.7 %all_to_all.70.refs_2_.refs_1_ = bf16[8,72,128]{2,1,0:T(8,128)(2,1)} all-to-all(bf16[8,72,128]{2,1,0:T(8,128)(2,1)} %get-tuple-element.103.refs_1_), channel_id=1, replica_groups=mesh['dp'=8,'tensor'=4] {'dp'}, dimensions={0} | all-to-all | bytes 294912 | tf_op jit(solution)/shard_map/all_to_all | solution.py:26
  208.2 3.4 %collective-permute-start.22 = (bf16[64,1152]{1,0:T(8,128)(2,1)}, bf16[64,1152]{1,0:T(8,128)(2,1)}, u32[]{:S(2)}, u32[]{:S(2)}) collective-permute-start(bf16[64,1152]{1,0:T(8,128)(2,1)} %gate.21), channel_id=1, source_target_pairs={{0,3},{1,2},{2,1},{3,0},{4,7},{5,6},{6,5},{7,4},{8,11},{9,10},{10,... | collective-permute-start | bytes 442376 | tf_op jit(solution)/shard_map/ppermute | solution.py:22
  212.6 10.0 %attend_backward.1.refs_0_ = bf16[8,72,640]{2,1,0:T(8,128)(2,1)} custom-call(s32[4]{0:T(128)} %pad_add_fusion.refs_0_, bf16[8,72,640]{2,1,0:T(8,128)(2,1)} %all-to-all-done.2.refs_1_, bf16[8,72,128]{2,1,0:T(8,128)(2,1)} %all_to_all.70.refs_2_.refs_1_, f32[8,72,128]{2,1,0:T(8,128)} %get-tuple-element.107.refs_3_, f32[8,1,128]{2,1,0:T(1,128)} %get-tuple-element.108.refs_4_), custom_call_target="tpu_custom_call" | custom-call | flops 3000000000 | bytes 4000000 | tf_op jit(solution)/shard_map/attend_backward/pallas_call | solution.py:230
  225.3 4.3 %all-to-all-start.9 = ((bf16[8,72,640]{2,1,0:T(8,128)(2,1)}), bf16[8,72,640]{2,1,0:T(8,128)(2,1)}, u32[]{:S(2)}, u32[]{:S(2)}) async-start(bf16[8,72,640]{2,1,0:T(8,128)(2,1)} %gate.23), calls=%async_computation.9 | async-start | bytes 1474560 | tf_op jit(solution)/shard_map/all_to_all | solution.py:26
  237.5 3.1 convert_add_fusion
  241.7 5.1 %unspread.1 = (bf16[256,1152]{1,0:T(8,128)(2,1)}, bf16[256,576]{1,0:T(8,128)(2,1)}, bf16[256,576]{1,0:T(8,128)(2,1)}, bf16[256,576]{1,0:T(8,128)(2,1)}, f32[2,576]{1,0:T(2,128)}) custom-call(s32[7]{0:T(128)} %concatenate.24.refs_0_, bf16[8,72,640]{2,1,0:T(8,128)(2,1)} %all-to-all-done.9.refs_1_, bf16[1152,576]{1,0:T(8,128)(2,1)} %get-tuple-element.109.refs_2_, ...), custom_call_target="tpu_custom_call" | custom-call | flops 20000000000 | bytes 1 | tf_op jit(solution)/shard_map/unspread/pallas_call | solution.py:358
  249.0 5.1 %all-to-all-start.10 = ((bf16[4,64,1152]{2,1,0:T(8,128)(2,1)}), bf16[4,64,1152]{2,1,0:T(8,128)(2,1)}, u32[]{:S(2)}, u32[]{:S(2)}) async-start(bf16[4,64,1152]{2,1,0:T(8,128)(2,1)} %bitcast.43), calls=%async_computation.10 | async-start | bytes 1179648 | tf_op jit(solution)/shard_map/all_to_all | solution.py:26
  255.9 4.9 %early_weights.1 = (bf16[288,576]{1,0:T(8,128)(2,1)}, bf16[288,576]{1,0:T(8,128)(2,1)}, bf16[288,576]{1,0:T(8,128)(2,1)}, bf16[288,576]{1,0:T(8,128)(2,1)}) custom-call(s32[7]{0:T(128)} %concatenate.24.refs_0_, bf16[256,1152]{1,0:T(8,128)(2,1)} %get-tuple-element.118.refs_1_, bf16[256,1152]{1,0:T(8,128)(2,1)} %bitcast.12.refs_1_.refs_2_, ...), custom_call_target="tpu_custom_call" | custom-call | flops 1 | bytes 1 | tf_op jit(solution)/shard_map/early_weights/pallas_call | solution.py:358
  265.8 6.3 %collective-permute-done.31.refs_11_ = bf16[288,576]{1,0:T(8,128)(2,1)} collective-permute-done((bf16[288,576]{1,0:T(8,128)(2,1)}, bf16[288,576]{1,0:T(8,128)(2,1)}, u32[]{:S(2)}, u32[]{:S(2)}) %collective-permute-start.31) | collective-permute-done | bytes 331808 | tf_op jit(solution)/shard_map/ppermute | solution.py:22
  276.8 5.1 %all-to-all-start.11 = ((f32[4,18,288]{2,1,0:T(8,128)}), f32[4,18,288]{2,1,0:T(8,128)S(1)}, u32[]{:S(2)}, u32[]{:S(2)}) async-start(f32[4,18,288]{2,1,0:T(8,128)} %get-tuple-element.126.refs_1_), calls=%async_computation.11 | async-start | bytes 294912 | tf_op jit(solution)/shard_map/all_to_all | solution.py:26
  289.1 3.5 %all-to-all-start.12 = ((f32[8,32,288]{2,1,0:T(8,128)}), f32[8,32,288]{2,1,0:T(8,128)S(1)}, u32[]{:S(2)}, u32[]{:S(2)}) async-start(f32[8,32,288]{2,1,0:T(8,128)} %gate.25.refs_1_), calls=%async_computation.12 | async-start | bytes 786432 | tf_op jit(solution)/shard_map/all_to_all | solution.py:26
  306.0 3.3 %all-to-all-start.13 = ((f32[32,1,432]{2,1,0:T(1,128)}), f32[32,1,432]{2,1,0:T(1,128)}, u32[]{:S(2)}, u32[]{:S(2)}) async-start(f32[32,1,432]{2,1,0:T(1,128)} %reshape.132), calls=%async_computation.13 | async-start | bytes 131072 | tf_op jit(solution)/shard_map/all_to_all | solution.py:26
  (232 shorter events, 114.5 us)
Async XLA Ops:
  15.6 18.5 %collective-permute-start.3 = (bf16[288,576]{1,0:T(8,128)(2,1)S(1)}, bf16[288,576]{1,0:T(8,128)(2,1)S(1)}, u32[]{:S(2)}, u32[]{:S(2)}) collective-permute-start(bf16[288,576]{1,0:T(8,128)(2,1)S(1)} %pad_maximum_fusion.2.refs_0_), channel_id=1, source_target_pairs={{0,16},{4,20},{8,24},{12,28},{16,0},{20,4},{24,8},{28,12},{1,17},{... | collective-permute-start | bytes 995336 | tf_op jit(solution)/shard_map/ppermute | solution.py:22
  17.1 17.3 %collective-permute-start.4 = (bf16[288,576]{1,0:T(8,128)(2,1)S(1)}, bf16[288,576]{1,0:T(8,128)(2,1)S(1)}, u32[]{:S(2)}, u32[]{:S(2)}) collective-permute-start(bf16[288,576]{1,0:T(8,128)(2,1)S(1)} %pad_maximum_fusion.2.refs_0_), channel_id=1, source_target_pairs={{0,24},{4,28},{8,16},{12,20},{16,8},{20,12},{24,0},{28,4},{1,25},{... | collective-permute-start | bytes 995336 | tf_op jit(solution)/shard_map/ppermute | solution.py:22
  21.6 21.8 %all-to-all-start.1 = ((f32[8,4,18,288]{3,1,2,0:T(4,128)}), f32[8,4,18,288]{3,1,2,0:T(4,128)S(1)}, u32[]{:S(2)}, u32[]{:S(2)}) async-start(f32[8,4,18,288]{3,1,2,0:T(4,128)} %broadcast_in_dim.17), calls=%async_computation.1 | async-start | bytes 1769472 | tf_op jit(solution)/shard_map/all_to_all | solution.py:26
  51.1 16.4 %all-to-all-start.2 = ((bf16[8,72,640]{2,1,0:T(8,128)(2,1)}), bf16[8,72,640]{2,1,0:T(8,128)(2,1)}, u32[]{:S(2)}, u32[]{:S(2)}) async-start(bf16[8,72,640]{2,1,0:T(8,128)(2,1)} %get-tuple-element.82), calls=%async_computation.2 | async-start | bytes 1474560 | tf_op jit(solution)/shard_map/all_to_all | solution.py:26
  56.2 24.0 %collective-permute-start = (bf16[144,1152]{1,0:T(8,128)(2,1)}, bf16[144,1152]{1,0:T(8,128)(2,1)}, u32[]{:S(2)}, u32[]{:S(2)}) collective-permute-start(bf16[144,1152]{1,0:T(8,128)(2,1)} %bitcast_select_fusion), channel_id=1, source_target_pairs={{0,4},{4,0},{8,12},{12,8},{16,20},{20,16},{24,28},{28,24},{1,5},{5... | collective-permute-start | bytes 995336 | tf_op jit(solution)/shard_map/ppermute | solution.py:22
  89.0 22.6 %all-to-all-start.4 = ((bf16[4,64,1152]{2,1,0:T(8,128)(2,1)}), bf16[4,64,1152]{2,1,0:T(8,128)(2,1)}, u32[]{:S(2)}, u32[]{:S(2)}) async-start(bf16[4,64,1152]{2,1,0:T(8,128)(2,1)} %bitcast.45), calls=%async_computation.4 | async-start | bytes 1179648 | tf_op jit(solution)/shard_map/all_to_all | solution.py:26
  94.8 16.5 %collective-permute-start.10 = (bf16[288,1152]{1,0:T(8,128)(2,1)}, bf16[288,1152]{1,0:T(8,128)(2,1)}, u32[]{:S(2)}, u32[]{:S(2)}) collective-permute-start(bf16[288,1152]{1,0:T(8,128)(2,1)} %gate.16.refs_1_), channel_id=1, source_target_pairs={{0,16},{4,20},{8,24},{12,28},{16,0},{20,4},{24,8},{28,12},{1,17},{... | collective-permute-start | bytes 1990664 | tf_op jit(solution)/shard_map/ppermute | solution.py:22
  95.3 16.2 %collective-permute-start.9 = (bf16[288,1152]{1,0:T(8,128)(2,1)}, bf16[288,1152]{1,0:T(8,128)(2,1)}, u32[]{:S(2)}, u32[]{:S(2)}) collective-permute-start(bf16[288,1152]{1,0:T(8,128)(2,1)} %gate.16.refs_1_), channel_id=1, source_target_pairs={{0,8},{4,12},{8,0},{12,4},{16,24},{20,28},{24,16},{28,20},{1,9},{5... | collective-permute-start | bytes 1990664 | tf_op jit(solution)/shard_map/ppermute | solution.py:22
  114.2 21.3 %all-to-all-start.5 = ((bf16[4,64,1152]{2,1,0:T(8,128)(2,1)}), bf16[4,64,1152]{2,1,0:T(8,128)(2,1)S(1)}, u32[]{:S(2)}, u32[]{:S(2)}) async-start(bf16[4,64,1152]{2,1,0:T(8,128)(2,1)} %get-tuple-element.88), calls=%async_computation.5 | async-start | bytes 1179648 | tf_op jit(solution)/shard_map/all_to_all | solution.py:26
  120.0 15.5 %collective-permute-start.11 = (bf16[288,1152]{1,0:T(8,128)(2,1)}, bf16[288,1152]{1,0:T(8,128)(2,1)S(1)}, u32[]{:S(2)}, u32[]{:S(2)}) collective-permute-start(bf16[288,1152]{1,0:T(8,128)(2,1)} %gate.17), channel_id=1, source_target_pairs={{0,24},{4,28},{8,16},{12,20},{16,8},{20,12},{24,0},{28,4},{1,25},{... | collective-permute-start | bytes 1990664 | tf_op jit(solution)/shard_map/ppermute | solution.py:22
  121.5 15.6 %collective-permute-start.12 = (bf16[288,1152]{1,0:T(8,128)(2,1)S(1)}, bf16[288,1152]{1,0:T(8,128)(2,1)S(1)}, u32[]{:S(2)}, u32[]{:S(2)}) collective-permute-start(bf16[288,1152]{1,0:T(8,128)(2,1)S(1)} %copy-done.1), channel_id=1, source_target_pairs={{0,4},{4,0},{8,12},{12,8},{16,20},{20,16},{24,28},{28,24},{1,5},{5... | collective-permute-start | bytes 1990664 | tf_op jit(solution)/shard_map/ppermute | solution.py:22
  121.5 16.5 %collective-permute-start.13 = (bf16[288,1152]{1,0:T(8,128)(2,1)}, bf16[288,1152]{1,0:T(8,128)(2,1)S(1)}, u32[]{:S(2)}, u32[]{:S(2)}) collective-permute-start(bf16[288,1152]{1,0:T(8,128)(2,1)} %collective-permute-done.9.refs_5_.refs_2_), channel_id=1, source_target_pairs={{0,4},{4,0},{8,12},{12,8},{16,20},{20,16},{24,28},{28,24},{1,5},{5... | collective-permute-start | bytes 1990664 | tf_op jit(solution)/shard_map/ppermute | solution.py:22
  122.0 16.8 %collective-permute-start.14 = (bf16[288,1152]{1,0:T(8,128)(2,1)}, bf16[288,1152]{1,0:T(8,128)(2,1)}, u32[]{:S(2)}, u32[]{:S(2)}) collective-permute-start(bf16[288,1152]{1,0:T(8,128)(2,1)} %collective-permute-done.10.refs_6_.refs_3_), channel_id=1, source_target_pairs={{0,4},{4,0},{8,12},{12,8},{16,20},{20,16},{24,28},{28,24},{1,5},{5... | collective-permute-start | bytes 1990664 | tf_op jit(solution)/shard_map/ppermute | solution.py:22
  149.7 21.4 %all-to-all-start.6 = ((bf16[4,64,1152]{2,1,0:T(8,128)(2,1)}), bf16[4,64,1152]{2,1,0:T(8,128)(2,1)}, u32[]{:S(2)}, u32[]{:S(2)}) async-start(bf16[4,64,1152]{2,1,0:T(8,128)(2,1)} %bitcast.44), calls=%async_computation.6 | async-start | bytes 1179648 | tf_op jit(solution)/shard_map/all_to_all | solution.py:26
  174.1 21.0 %all-to-all-start.7 = ((bf16[4,64,1152]{2,1,0:T(8,128)(2,1)}), bf16[4,64,1152]{2,1,0:T(8,128)(2,1)}, u32[]{:S(2)}, u32[]{:S(2)}) async-start(bf16[4,64,1152]{2,1,0:T(8,128)(2,1)} %get-tuple-element.102), calls=%async_computation.7 | async-start | bytes 1179648 | tf_op jit(solution)/shard_map/all_to_all | solution.py:26
  178.2 16.4 %collective-permute-start.18 = (bf16[288,1152]{1,0:T(8,128)(2,1)}, bf16[288,1152]{1,0:T(8,128)(2,1)}, u32[]{:S(2)}, u32[]{:S(2)}) collective-permute-start(bf16[288,1152]{1,0:T(8,128)(2,1)} %get-tuple-element.99.refs_7_), channel_id=1, source_target_pairs={{0,8},{4,12},{8,0},{12,4},{16,24},{20,28},{24,16},{28,20},{1,9},{5... | collective-permute-start | bytes 1990664 | tf_op jit(solution)/shard_map/ppermute | solution.py:22
  179.0 16.1 %collective-permute-start.19 = (bf16[288,1152]{1,0:T(8,128)(2,1)}, bf16[288,1152]{1,0:T(8,128)(2,1)}, u32[]{:S(2)}, u32[]{:S(2)}) collective-permute-start(bf16[288,1152]{1,0:T(8,128)(2,1)} %get-tuple-element.100.refs_8_), channel_id=1, source_target_pairs={{0,16},{4,20},{8,24},{12,28},{16,0},{20,4},{24,8},{28,12},{1,17},{... | collective-permute-start | bytes 1990664 | tf_op jit(solution)/shard_map/ppermute | solution.py:22
  207.6 17.7 %collective-permute-start.26 = (bf16[288,1152]{1,0:T(8,128)(2,1)}, bf16[288,1152]{1,0:T(8,128)(2,1)}, u32[]{:S(2)}, u32[]{:S(2)}) collective-permute-start(bf16[288,1152]{1,0:T(8,128)(2,1)} %gate.22), channel_id=1, source_target_pairs={{0,24},{4,28},{8,16},{12,20},{16,8},{20,12},{24,0},{28,4},{1,25},{... | collective-permute-start | bytes 1990664 | tf_op jit(solution)/shard_map/ppermute | solution.py:22
  208.2 14.4 %collective-permute-start.22 = (bf16[64,1152]{1,0:T(8,128)(2,1)}, bf16[64,1152]{1,0:T(8,128)(2,1)}, u32[]{:S(2)}, u32[]{:S(2)}) collective-permute-start(bf16[64,1152]{1,0:T(8,128)(2,1)} %gate.21), channel_id=1, source_target_pairs={{0,3},{1,2},{2,1},{3,0},{4,7},{5,6},{6,5},{7,4},{8,11},{9,10},{10,... | collective-permute-start | bytes 442376 | tf_op jit(solution)/shard_map/ppermute | solution.py:22
  211.6 12.6 %collective-permute-start.21 = (bf16[64,1152]{1,0:T(8,128)(2,1)}, bf16[64,1152]{1,0:T(8,128)(2,1)}, u32[]{:S(2)}, u32[]{:S(2)}) collective-permute-start(bf16[64,1152]{1,0:T(8,128)(2,1)} %gate.20), channel_id=1, source_target_pairs={{0,2},{1,3},{2,0},{3,1},{4,6},{5,7},{6,4},{7,5},{8,10},{9,11},{10,... | collective-permute-start | bytes 442376 | tf_op jit(solution)/shard_map/ppermute | solution.py:22
  211.6 12.6 %collective-permute-start.20 = (bf16[64,1152]{1,0:T(8,128)(2,1)}, bf16[64,1152]{1,0:T(8,128)(2,1)}, u32[]{:S(2)}, u32[]{:S(2)}) collective-permute-start(bf16[64,1152]{1,0:T(8,128)(2,1)} %gate.19), channel_id=1, source_target_pairs={{0,1},{1,0},{2,3},{3,2},{4,5},{5,4},{6,7},{7,6},{8,9},{9,8},{10,11... | collective-permute-start | bytes 442376 | tf_op jit(solution)/shard_map/ppermute | solution.py:22
  225.3 16.4 %all-to-all-start.9 = ((bf16[8,72,640]{2,1,0:T(8,128)(2,1)}), bf16[8,72,640]{2,1,0:T(8,128)(2,1)}, u32[]{:S(2)}, u32[]{:S(2)}) async-start(bf16[8,72,640]{2,1,0:T(8,128)(2,1)} %gate.23), calls=%async_computation.9 | async-start | bytes 1474560 | tf_op jit(solution)/shard_map/all_to_all | solution.py:26
  230.2 25.7 %collective-permute-start.27 = (bf16[256,1152]{1,0:T(8,128)(2,1)}, bf16[256,1152]{1,0:T(8,128)(2,1)}, u32[]{:S(2)}, u32[]{:S(2)}) collective-permute-start(bf16[256,1152]{1,0:T(8,128)(2,1)} %get-tuple-element.118.refs_1_), channel_id=1, source_target_pairs={{0,4},{4,0},{8,12},{12,8},{16,20},{20,16},{24,28},{28,24},{1,5},{5... | collective-permute-start | bytes 1769480 | tf_op jit(solution)/shard_map/ppermute | solution.py:22
  230.6 25.3 %collective-permute-start.30 = (bf16[256,576]{1,0:T(8,128)(2,1)}, bf16[256,576]{1,0:T(8,128)(2,1)}, u32[]{:S(2)}, u32[]{:S(2)}) collective-permute-start(bf16[256,576]{1,0:T(8,128)(2,1)} %get-tuple-element.121.refs_5_), channel_id=1, source_target_pairs={{0,4},{4,0},{8,12},{12,8},{16,20},{20,16},{24,28},{28,24},{1,5},{5... | collective-permute-start | bytes 884744 | tf_op jit(solution)/shard_map/ppermute | solution.py:22
  233.1 13.7 %collective-permute-start.23 = (bf16[64,1152]{1,0:T(8,128)(2,1)}, bf16[64,1152]{1,0:T(8,128)(2,1)}, u32[]{:S(2)}, u32[]{:S(2)}) collective-permute-start(bf16[64,1152]{1,0:T(8,128)(2,1)} %get-tuple-element.106.refs_1_), channel_id=1, source_target_pairs={{0,1},{1,0},{2,3},{3,2},{4,5},{5,4},{6,7},{7,6},{8,9},{9,8},{10,11... | collective-permute-start | bytes 442376 | tf_op jit(solution)/shard_map/ppermute | solution.py:22
  234.7 14.3 %collective-permute-start.24 = (bf16[64,1152]{1,0:T(8,128)(2,1)}, bf16[64,1152]{1,0:T(8,128)(2,1)}, u32[]{:S(2)}, u32[]{:S(2)}) collective-permute-start(bf16[64,1152]{1,0:T(8,128)(2,1)} %get-tuple-element.106.refs_1_), channel_id=1, source_target_pairs={{0,2},{1,3},{2,0},{3,1},{4,6},{5,7},{6,4},{7,5},{8,10},{9,11},{10,... | collective-permute-start | bytes 442376 | tf_op jit(solution)/shard_map/ppermute | solution.py:22
  249.0 25.0 %all-to-all-start.10 = ((bf16[4,64,1152]{2,1,0:T(8,128)(2,1)}), bf16[4,64,1152]{2,1,0:T(8,128)(2,1)}, u32[]{:S(2)}, u32[]{:S(2)}) async-start(bf16[4,64,1152]{2,1,0:T(8,128)(2,1)} %bitcast.43), calls=%async_computation.10 | async-start | bytes 1179648 | tf_op jit(solution)/shard_map/all_to_all | solution.py:26
  255.1 28.3 %collective-permute-start.38 = (f32[144,1152]{1,0:T(8,128)}, f32[144,1152]{1,0:T(8,128)}, u32[]{:S(2)}, u32[]{:S(2)}) collective-permute-start(f32[144,1152]{1,0:T(8,128)} %slice_select_fusion), channel_id=1, source_target_pairs={{0,4},{4,0},{8,12},{12,8},{16,20},{20,16},{24,28},{28,24},{1,5},{5... | collective-permute-start | bytes 1990664 | tf_op jit(solution)/shard_map/ppermute | solution.py:22
  281.9 15.2 %collective-permute-start.36 = (bf16[288,576]{1,0:T(8,128)(2,1)}, bf16[288,576]{1,0:T(8,128)(2,1)S(1)}, u32[]{:S(2)}, u32[]{:S(2)}) collective-permute-start(bf16[288,576]{1,0:T(8,128)(2,1)} %gate.27), channel_id=1, source_target_pairs={{0,24},{4,28},{8,16},{12,20},{16,8},{20,12},{24,0},{28,4},{1,25},{... | collective-permute-start | bytes 995336 | tf_op jit(solution)/shard_map/ppermute | solution.py:22
  292.6 18.6 %collective-permute-start.33 = (bf16[64,1152]{1,0:T(8,128)(2,1)}, bf16[64,1152]{1,0:T(8,128)(2,1)}, u32[]{:S(2)}, u32[]{:S(2)}) collective-permute-start(bf16[64,1152]{1,0:T(8,128)(2,1)} %gate.26.refs_0_), channel_id=1, source_target_pairs={{0,1},{1,0},{2,3},{3,2},{4,5},{5,4},{6,7},{7,6},{8,9},{9,8},{10,11... | collective-permute-start | bytes 442376 | tf_op jit(solution)/shard_map/ppermute | solution.py:22
  293.6 17.6 %collective-permute-start.34 = (bf16[64,1152]{1,0:T(8,128)(2,1)}, bf16[64,1152]{1,0:T(8,128)(2,1)}, u32[]{:S(2)}, u32[]{:S(2)}) collective-permute-start(bf16[64,1152]{1,0:T(8,128)(2,1)} %gate.26.refs_0_), channel_id=1, source_target_pairs={{0,2},{1,3},{2,0},{3,1},{4,6},{5,7},{6,4},{7,5},{8,10},{9,11},{10,... | collective-permute-start | bytes 442376 | tf_op jit(solution)/shard_map/ppermute | solution.py:22
  295.0 16.2 %collective-permute-start.35 = (bf16[64,1152]{1,0:T(8,128)(2,1)}, bf16[64,1152]{1,0:T(8,128)(2,1)}, u32[]{:S(2)}, u32[]{:S(2)}) collective-permute-start(bf16[64,1152]{1,0:T(8,128)(2,1)} %gate.26.refs_0_), channel_id=1, source_target_pairs={{0,3},{1,2},{2,1},{3,0},{4,7},{5,6},{6,5},{7,4},{8,11},{9,10},{10,... | collective-permute-start | bytes 442376 | tf_op jit(solution)/shard_map/ppermute | solution.py:22
  (53 other events, 340.1 us)

commit v11 on v10

--- a/solution.py
+++ b/solution.py
@@ -9,10 +9,11 @@
 
 DH = 72
 SEQ = 1024
+STEP = 512
 NORM_EPS = 1e-06
 NEGATIVE = -1e30
 SCALE = 1.0 / math.sqrt(DH)
-VMEM_BYTES = 64 * 1024 * 1024
+VMEM_BYTES = 255 * 256 * 1024
 BF16 = jnp.bfloat16
 F32 = jnp.float32
 
@@ -110,7 +111,7 @@
         low = jnp.where((first >= start) & (first < end), start, low)
         high = jnp.where((last >= start) & (last < end), end, high)
         start = end
-    return begin, finish, low // 256, (high + 255) // 256
+    return begin, finish, low // STEP, (high + STEP - 1) // STEP
 
 
 def pair(ref, tile, start):
@@ -119,16 +120,22 @@
     return jnp.concatenate([left, right], axis=1)
 
 
+def wide(packed_ref, block, start):
+    left = packed_ref[2 * block, :, start : start + 256]
+    right = packed_ref[2 * block + 1, :, start : start + 256]
+    return jnp.concatenate([left, right], axis=1)
+
+
 def key_mask(block, begin, finish):
-    place = block * 256 + lax.broadcasted_iota(jnp.int32, (256, 256), 0)
+    place = block * STEP + lax.broadcasted_iota(jnp.int32, (STEP, 256), 0)
     return (place >= begin) & (place < finish)
 
 
 def forward_kernel(latents, meta_ref, packed_ref, out_ref, exact_ref, log_ref, keys, scores):
     blocks = packed_ref.shape[0]
     core = meta_ref[0]
-    for block in range(blocks):
-        keys[block] = packed_ref[block, :, :256].astype(F32).T.astype(BF16)
+    for block in range(blocks // 2):
+        keys[block] = wide(packed_ref, block, 0).astype(F32).T.astype(BF16)
     for tile in range(blocks // 2):
         begin, finish, low, high = tile_range(meta_ref, latents, tile, core)
         query = pair(packed_ref, tile, 512)
@@ -145,7 +152,7 @@
             total, mixed = carry
             weights = jnp.exp(scores[block] - largest)
             total = total + jnp.sum(weights, axis=0, keepdims=True)
-            values = packed_ref[block, :, 256:512]
+            values = wide(packed_ref, block, 256)
             mixed = mixed + jnp.dot(values, weights.astype(BF16), preferred_element_type=F32)
             return total, mixed
 
@@ -166,9 +173,9 @@
 ):
     blocks = packed_ref.shape[0]
     core = meta_ref[0]
-    for block in range(blocks):
-        keys[block] = packed_ref[block, :, :256].astype(F32).T.astype(BF16)
-        values[block] = packed_ref[block, :, 256:512].astype(F32).T.astype(BF16)
+    for block in range(blocks // 2):
+        keys[block] = wide(packed_ref, block, 0).astype(F32).T.astype(BF16)
+        values[block] = wide(packed_ref, block, 256).astype(F32).T.astype(BF16)
     d_keys[...] = jnp.zeros_like(d_keys)
     d_values[...] = jnp.zeros_like(d_values)
     by_query = (((1,), (1,)), ((), ()))
@@ -188,7 +195,7 @@
                 grad, probs.astype(BF16), by_query, preferred_element_type=F32
             )
             d_keys[block] += lax.dot_general(query, d_scores, by_query, preferred_element_type=F32)
-            key_rows = packed_ref[block, :, :256]
+            key_rows = wide(packed_ref, block, 0)
             return d_query + jnp.dot(key_rows, d_scores, preferred_element_type=F32)
 
         d_query = lax.fori_loop(low, high, step, jnp.zeros((DH, 256), F32)) * SCALE
@@ -196,8 +203,9 @@
             part = d_query[:, half * 128 : half * 128 + 128]
             out_ref[2 * tile + half, :, 512:640] = part.astype(BF16)
     for block in range(blocks):
-        out_ref[block, :, :256] = (d_keys[block] * SCALE).astype(BF16)
-        out_ref[block, :, 256:512] = d_values[block].astype(BF16)
+        half = slice(block % 2 * 256, block % 2 * 256 + 256)
+        out_ref[block, :, :256] = (d_keys[block // 2, :, half] * SCALE).astype(BF16)
+        out_ref[block, :, 256:512] = d_values[block // 2, :, half].astype(BF16)
 
 
 def attend_forward(meta, packed):
@@ -216,8 +224,8 @@
         ],
         out_specs=tuple([pl.BlockSpec(memory_space=pltpu.VMEM)] * 3),
         scratch_shapes=[
-            pltpu.VMEM((blocks, 256, DH), BF16),
-            pltpu.VMEM((blocks, 256, 256), F32),
+            pltpu.VMEM((blocks // 2, STEP, DH), BF16),
+            pltpu.VMEM((blocks // 2, STEP, 256), F32),
         ],
         compiler_params=pltpu.CompilerParams(vmem_limit_bytes=VMEM_BYTES),
         cost_estimate=pl.CostEstimate(flops=10**9, bytes_accessed=4 * 10**6, transcendentals=10**6),
@@ -234,10 +242,10 @@
         + [pl.BlockSpec(memory_space=pltpu.VMEM)] * 4,
         out_specs=pl.BlockSpec(memory_space=pltpu.VMEM),
         scratch_shapes=[
-            pltpu.VMEM((blocks, 256, DH), BF16),
-            pltpu.VMEM((blocks, 256, DH), BF16),
-            pltpu.VMEM((blocks, DH, 256), F32),
-            pltpu.VMEM((blocks, DH, 256), F32),
+            pltpu.VMEM((blocks // 2, STEP, DH), BF16),
+            pltpu.VMEM((blocks // 2, STEP, DH), BF16),
+            pltpu.VMEM((blocks // 2, DH, STEP), F32),
+            pltpu.VMEM((blocks // 2, DH, STEP), F32),
         ],
         compiler_params=pltpu.CompilerParams(vmem_limit_bytes=VMEM_BYTES),
         cost_estimate=pl.CostEstimate(flops=3 * 10**9, bytes_accessed=4 * 10**6, transcendentals=10**6),
@@ -802,7 +810,7 @@
     bias_ada = jnp.tile(b_ada.astype(F32), (latents, 1))
     few_chips = n_dp // 2 == 4
     if few_chips:
-        mod_part = mod_part + jnp.where(my_dp == 0, bias_ada, 0.0)
+        mod_part = gate(mod_part + jnp.where(my_dp == 0, bias_ada, 0.0), early_rows)
         mod_wide = gather(mod_part, "tensor", n_tensor)
         mod_parts = gather(mod_wide, "dp", n_dp).reshape((-1,) + mod_part.shape)
     else:

time: 328 us -> 326 us (level)
    unnamed x72 -> x82, local copies, waits for them, and re-layouts: 8.38 us -> 9.87 us
  transfers between devices with their start and end apart: 52 -> 52, of which waited for: 24 -> 24; matrix products, arithmetic and copies ran while one was open for 12% -> 11% of each run, Pallas kernels for 14% -> 13%
where the time goes in v11:
time: 326 us; the launch traced here: 325 us
  waiting for transfers between devices  104 us (32%)
  starting transfers between devices  88.4 us (27%)
  Pallas kernels  72.3 us (22%)
  local copies, waits for them, and re-layouts  24.6 us (8%)
  other arithmetic  24.6 us (8%)
  blocking collectives  9.69 us (3%)
    ppermute x39, waiting for transfers between devices, swap(): return lax.ppermute(block, axis, route)  69.4 us
    all_to_all x13, starting transfers between devices, exchange(): return lax.all_to_all(blocks, axis, 0, 0, tiled=True)  58 us
    pallas_call x13, Pallas kernels, call(): pl.pallas_call(kernel, out_shape=tuple((jax.ShapeDtypeStruct(shape, kind)...  55 us
    all_to_all x13, waiting for transfers between devices, exchange(): return lax.all_to_all(blocks, axis, 0, 0, tiled=True)  34.7 us
    ppermute x39, starting transfers between devices, swap(): return lax.ppermute(block, axis, route)  30.4 us
    unnamed x82, local copies, waits for them, and re-layouts  9.87 us
    all_to_all x1, blocking collectives, exchange(): return lax.all_to_all(blocks, axis, 0, 0, tiled=True)  9.69 us
    pallas_call x1, Pallas kernels, attend_backward(): pl.pallas_call(lambda *refs: backward_kernel(meta.shape[0] - 1, *refs), o...  9.39 us
  transfers between devices with their start and end apart: 52, of which 24 were waited for; matrix products, arithmetic and copies ran while one was open for 11% of the time, Pallas kernels for 13%

profile of v11, /device:TPU:0, one launch (start us, length us, event | category | flops | bytes accessed | tf_op | source)
XLA Modules:
  0.0 325.0 jit_solution(15994479105725743020)
XLA Ops:
  9.6 5.9 %all-to-all-start = ((f32[4,18,288]{2,1,0:T(8,128)}), f32[4,18,288]{2,1,0:T(8,128)S(1)}, u32[]{:S(2)}, u32[]{:S(2)}) async-start(f32[4,18,288]{2,1,0:T(8,128)} %broadcast_in_dim.16), calls=%async_computation | async-start | bytes 294912 | tf_op jit(solution)/shard_map/all_to_all | solution.py:27
  19.0 3.2 all-to-all-done.refs_4_
  23.3 3.9 %all-to-all-start.1 = ((f32[8,4,18,288]{3,1,2,0:T(4,128)}), f32[8,4,18,288]{3,1,2,0:T(4,128)S(1)}, u32[]{:S(2)}, u32[]{:S(2)}) async-start(f32[8,4,18,288]{3,1,2,0:T(4,128)} %broadcast_in_dim.17), calls=%async_computation.1 | async-start | bytes 1769472 | tf_op jit(solution)/shard_map/all_to_all | solution.py:27
  27.2 8.7 %collective-permute-done.3.refs_2_ = bf16[288,576]{1,0:T(8,128)(2,1)S(1)} collective-permute-done((bf16[288,576]{1,0:T(8,128)(2,1)}, bf16[288,576]{1,0:T(8,128)(2,1)S(1)}, u32[]{:S(2)}, u32[]{:S(2)}) %collective-permute-start.3) | collective-permute-done | bytes 331808 | tf_op jit(solution)/shard_map/ppermute | solution.py:23
  39.8 5.2 %all-to-all-done.1 = f32[8,4,18,288]{3,1,2,0:T(4,128)S(1)} async-done(((f32[8,4,18,288]{3,1,2,0:T(4,128)}), f32[8,4,18,288]{3,1,2,0:T(4,128)S(1)}, u32[]{:S(2)}, u32[]{:S(2)}) %all-to-all-start.1) | async-done | bytes 663584 | tf_op jit(solution)/shard_map/all_to_all | solution.py:27
  46.2 6.5 %project.1 = (bf16[256,1152]{1,0:T(8,128)(2,1)}, bf16[256,1152]{1,0:T(8,128)(2,1)}, bf16[8,72,640]{2,1,0:T(8,128)(2,1)}, bf16[1152,576]{1,0:T(8,128)(2,1)}, bf16...) custom-call(s32[7]{0:T(128)} %concatenate.24.refs_0_, bf16[288,576]{1,0:T(8,128)(2,1)} %get-tuple-element.78.refs_1_, ...), custom_call_target="tpu_custom_call" | custom-call | flops 1 | bytes 1 | tf_op jit(solution)/shard_map/project/pallas_call | solution.py:366
  52.7 4.4 %all-to-all-start.2 = ((bf16[8,72,640]{2,1,0:T(8,128)(2,1)}), bf16[8,72,640]{2,1,0:T(8,128)(2,1)}, u32[]{:S(2)}, u32[]{:S(2)}) async-start(bf16[8,72,640]{2,1,0:T(8,128)(2,1)} %get-tuple-element.82), calls=%async_computation.2 | async-start | bytes 1474560 | tf_op jit(solution)/shard_map/all_to_all | solution.py:27
  58.8 10.3 %all-to-all-done.2.refs_1_ = bf16[8,72,640]{2,1,0:T(8,128)(2,1)} async-done(((bf16[8,72,640]{2,1,0:T(8,128)(2,1)}), bf16[8,72,640]{2,1,0:T(8,128)(2,1)}, u32[]{:S(2)}, u32[]{:S(2)}) %all-to-all-start.2) | async-done | bytes 737312 | tf_op jit(solution)/shard_map/all_to_all | solution.py:27
  69.2 7.8 %attend_forward.1 = (bf16[8,72,128]{2,1,0:T(8,128)(2,1)}, f32[8,72,128]{2,1,0:T(8,128)}, f32[8,1,128]{2,1,0:T(1,128)}) custom-call(s32[4]{0:T(128)} %pad_add_fusion.refs_0_, bf16[8,72,640]{2,1,0:T(8,128)(2,1)} %all-to-all-done.2.refs_1_), custom_call_target="tpu_custom_call" | custom-call | flops 1000000000 | bytes 4000000 | tf_op jit(solution)/shard_map/attend_forward/pallas_call | solution.py:214
  77.0 3.4 %all-to-all-start.3 = ((bf16[8,72,128]{2,1,0:T(8,128)(2,1)}), bf16[8,72,128]{2,1,0:T(8,128)(2,1)S(1)}, u32[]{:S(2)}, u32[]{:S(2)}) async-start(bf16[8,72,128]{2,1,0:T(8,128)(2,1)} %get-tuple-element.83), calls=%async_computation.3 | async-start | bytes 294912 | tf_op jit(solution)/shard_map/all_to_all | solution.py:27
  82.5 3.5 %all-to-all-done.3.refs_1_ = bf16[8,72,128]{2,1,0:T(8,128)(2,1)S(1)} async-done(((bf16[8,72,128]{2,1,0:T(8,128)(2,1)}), bf16[8,72,128]{2,1,0:T(8,128)(2,1)S(1)}, u32[]{:S(2)}, u32[]{:S(2)}) %all-to-all-start.3) | async-done | bytes 147488 | tf_op jit(solution)/shard_map/all_to_all | solution.py:27
  89.7 4.9 %all-to-all-start.4 = ((bf16[4,64,1152]{2,1,0:T(8,128)(2,1)}), bf16[4,64,1152]{2,1,0:T(8,128)(2,1)}, u32[]{:S(2)}, u32[]{:S(2)}) async-start(bf16[4,64,1152]{2,1,0:T(8,128)(2,1)} %bitcast.45), calls=%async_computation.4 | async-start | bytes 1179648 | tf_op jit(solution)/shard_map/all_to_all | solution.py:27
  97.3 14.8 %collective-permute-done.10.refs_6_.refs_3_ = bf16[288,1152]{1,0:T(8,128)(2,1)} collective-permute-done((bf16[288,1152]{1,0:T(8,128)(2,1)}, bf16[288,1152]{1,0:T(8,128)(2,1)}, u32[]{:S(2)}, u32[]{:S(2)}) %collective-permute-start.10) | collective-permute-done | bytes 663584 | tf_op jit(solution)/shard_map/ppermute | solution.py:23
  115.0 4.9 %all-to-all-start.5 = ((bf16[4,64,1152]{2,1,0:T(8,128)(2,1)}), bf16[4,64,1152]{2,1,0:T(8,128)(2,1)S(1)}, u32[]{:S(2)}, u32[]{:S(2)}) async-start(bf16[4,64,1152]{2,1,0:T(8,128)(2,1)} %get-tuple-element.88), calls=%async_computation.5 | async-start | bytes 1179648 | tf_op jit(solution)/shard_map/all_to_all | solution.py:27
  122.8 13.5 %collective-permute-done.11.refs_0_ = bf16[288,1152]{1,0:T(8,128)(2,1)S(1)} collective-permute-done((bf16[288,1152]{1,0:T(8,128)(2,1)}, bf16[288,1152]{1,0:T(8,128)(2,1)S(1)}, u32[]{:S(2)}, u32[]{:S(2)}) %collective-permute-start.11) | collective-permute-done | bytes 663584 | tf_op jit(solution)/shard_map/ppermute | solution.py:23
  139.8 10.7 %mlp.1 = (bf16[256,1152]{1,0:T(8,128)(2,1)}, bf16[256,1152]{1,0:T(8,128)(2,1)}, bf16[256,1152]{1,0:T(8,128)(2,1)}, f32[1,1152]{1,0:T(1,128)}, bf16[256,1152]{1,0...) custom-call(s32[7]{0:T(128)} %concatenate.24.refs_0_, ...), custom_call_target="tpu_custom_call" | custom-call | flops 1 | bytes 1 | tf_op jit(solution)/shard_map/mlp/pallas_call | solution.py:366
  150.5 5.0 %all-to-all-start.6 = ((bf16[4,64,1152]{2,1,0:T(8,128)(2,1)}), bf16[4,64,1152]{2,1,0:T(8,128)(2,1)}, u32[]{:S(2)}, u32[]{:S(2)}) async-start(bf16[4,64,1152]{2,1,0:T(8,128)(2,1)} %bitcast.44), calls=%async_computation.6 | async-start | bytes 1179648 | tf_op jit(solution)/shard_map/all_to_all | solution.py:27
  158.7 5.8 %late_weights.1 = (bf16[288,1152]{1,0:T(8,128)(2,1)}, bf16[288,1152]{1,0:T(8,128)(2,1)}, bf16[288,1152]{1,0:T(8,128)(2,1)}, bf16[288,1152]{1,0:T(8,128)(2,1)}) custom-call(s32[7]{0:T(128)} %concatenate.24.refs_0_, bf16[256,1152]{1,0:T(8,128)(2,1)} %bitcast.40, bf16[256,1152]{1,0:T(8,128)(2,1)} %get-tuple-element.89.refs_10_.refs_2_, ...), custom_call_target="tpu_custom_call" | custom-call | flops 1 | bytes 1 | tf_op jit(solution)/shard_map/late_weights/pallas_call | solution.py:366
  164.5 7.5 %all-to-all-done.6.refs_1_ = bf16[4,64,1152]{2,1,0:T(8,128)(2,1)} async-done(((bf16[4,64,1152]{2,1,0:T(8,128)(2,1)}), bf16[4,64,1152]{2,1,0:T(8,128)(2,1)}, u32[]{:S(2)}, u32[]{:S(2)}) %all-to-all-start.6) | async-done | bytes 589856 | tf_op jit(solution)/shard_map/all_to_all | solution.py:27
  175.0 4.2 %all-to-all-start.7 = ((bf16[4,64,1152]{2,1,0:T(8,128)(2,1)}), bf16[4,64,1152]{2,1,0:T(8,128)(2,1)}, u32[]{:S(2)}, u32[]{:S(2)}) async-start(bf16[4,64,1152]{2,1,0:T(8,128)(2,1)} %get-tuple-element.102), calls=%async_computation.7 | async-start | bytes 1179648 | tf_op jit(solution)/shard_map/all_to_all | solution.py:27
  181.4 14.2 %collective-permute-done.18.refs_3_ = bf16[288,1152]{1,0:T(8,128)(2,1)} collective-permute-done((bf16[288,1152]{1,0:T(8,128)(2,1)}, bf16[288,1152]{1,0:T(8,128)(2,1)}, u32[]{:S(2)}, u32[]{:S(2)}) %collective-permute-start.18) | collective-permute-done | bytes 663584 | tf_op jit(solution)/shard_map/ppermute | solution.py:23
  198.9 9.7 %all_to_all.70.refs_2_.refs_1_ = bf16[8,72,128]{2,1,0:T(8,128)(2,1)} all-to-all(bf16[8,72,128]{2,1,0:T(8,128)(2,1)} %get-tuple-element.103.refs_1_), channel_id=1, replica_groups=mesh['dp'=8,'tensor'=4] {'dp'}, dimensions={0} | all-to-all | bytes 294912 | tf_op jit(solution)/shard_map/all_to_all | solution.py:27
  209.2 3.4 %collective-permute-start.22 = (bf16[64,1152]{1,0:T(8,128)(2,1)}, bf16[64,1152]{1,0:T(8,128)(2,1)S(1)}, u32[]{:S(2)}, u32[]{:S(2)}) collective-permute-start(bf16[64,1152]{1,0:T(8,128)(2,1)} %gate.23), channel_id=1, source_target_pairs={{0,3},{1,2},{2,1},{3,0},{4,7},{5,6},{6,5},{7,4},{8,11},{9,10},{10,... | collective-permute-start | bytes 442376 | tf_op jit(solution)/shard_map/ppermute | solution.py:23
  213.5 9.4 %attend_backward.1.refs_0_ = bf16[8,72,640]{2,1,0:T(8,128)(2,1)} custom-call(s32[4]{0:T(128)} %pad_add_fusion.refs_0_, bf16[8,72,640]{2,1,0:T(8,128)(2,1)} %all-to-all-done.2.refs_1_, bf16[8,72,128]{2,1,0:T(8,128)(2,1)} %all_to_all.70.refs_2_.refs_1_, f32[8,72,128]{2,1,0:T(8,128)} %get-tuple-element.107.refs_3_, f32[8,1,128]{2,1,0:T(1,128)} %get-tuple-element.108.refs_4_), custom_call_target="tpu_custom_call" | custom-call | flops 3000000000 | bytes 4000000 | tf_op jit(solution)/shard_map/attend_backward/pallas_call | solution.py:238
  226.3 4.3 %all-to-all-start.9 = ((bf16[8,72,640]{2,1,0:T(8,128)(2,1)}), bf16[8,72,640]{2,1,0:T(8,128)(2,1)}, u32[]{:S(2)}, u32[]{:S(2)}) async-start(bf16[8,72,640]{2,1,0:T(8,128)(2,1)} %gate.25), calls=%async_computation.9 | async-start | bytes 1474560 | tf_op jit(solution)/shard_map/all_to_all | solution.py:27
  242.7 5.1 %unspread.1 = (bf16[256,1152]{1,0:T(8,128)(2,1)}, bf16[256,576]{1,0:T(8,128)(2,1)}, bf16[256,576]{1,0:T(8,128)(2,1)}, bf16[256,576]{1,0:T(8,128)(2,1)}, f32[2,576]{1,0:T(2,128)}) custom-call(s32[7]{0:T(128)} %concatenate.24.refs_0_, bf16[8,72,640]{2,1,0:T(8,128)(2,1)} %all-to-all-done.9.refs_1_, bf16[1152,576]{1,0:T(8,128)(2,1)} %get-tuple-element.109.refs_2_, ...), custom_call_target="tpu_custom_call" | custom-call | flops 20000000000 | bytes 1 | tf_op jit(solution)/shard_map/unspread/pallas_call | solution.py:366
  250.0 5.1 %all-to-all-start.10 = ((bf16[4,64,1152]{2,1,0:T(8,128)(2,1)}), bf16[4,64,1152]{2,1,0:T(8,128)(2,1)}, u32[]{:S(2)}, u32[]{:S(2)}) async-start(bf16[4,64,1152]{2,1,0:T(8,128)(2,1)} %bitcast.43), calls=%async_computation.10 | async-start | bytes 1179648 | tf_op jit(solution)/shard_map/all_to_all | solution.py:27
  256.3 4.9 %early_weights.1 = (bf16[288,576]{1,0:T(8,128)(2,1)}, bf16[288,576]{1,0:T(8,128)(2,1)}, bf16[288,576]{1,0:T(8,128)(2,1)}, bf16[288,576]{1,0:T(8,128)(2,1)}) custom-call(s32[7]{0:T(128)} %concatenate.24.refs_0_, bf16[256,1152]{1,0:T(8,128)(2,1)} %get-tuple-element.118.refs_1_, bf16[256,1152]{1,0:T(8,128)(2,1)} %bitcast.12.refs_1_.refs_2_, ...), custom_call_target="tpu_custom_call" | custom-call | flops 1 | bytes 1 | tf_op jit(solution)/shard_map/early_weights/pallas_call | solution.py:366
  265.5 7.1 %collective-permute-done.31.refs_11_ = bf16[288,576]{1,0:T(8,128)(2,1)} collective-permute-done((bf16[288,576]{1,0:T(8,128)(2,1)}, bf16[288,576]{1,0:T(8,128)(2,1)}, u32[]{:S(2)}, u32[]{:S(2)}) %collective-permute-start.31) | collective-permute-done | bytes 331808 | tf_op jit(solution)/shard_map/ppermute | solution.py:23
  277.2 5.1 %all-to-all-start.11 = ((f32[4,18,288]{2,1,0:T(8,128)}), f32[4,18,288]{2,1,0:T(8,128)S(1)}, u32[]{:S(2)}, u32[]{:S(2)}) async-start(f32[4,18,288]{2,1,0:T(8,128)} %get-tuple-element.126.refs_1_), calls=%async_computation.11 | async-start | bytes 294912 | tf_op jit(solution)/shard_map/all_to_all | solution.py:27
  289.5 3.7 %all-to-all-start.12 = ((f32[8,32,288]{2,1,0:T(8,128)}), f32[8,32,288]{2,1,0:T(8,128)S(1)}, u32[]{:S(2)}, u32[]{:S(2)}) async-start(f32[8,32,288]{2,1,0:T(8,128)} %gate.27.refs_1_), calls=%async_computation.12 | async-start | bytes 786432 | tf_op jit(solution)/shard_map/all_to_all | solution.py:27
  306.4 3.2 all-to-all-start.13
  (243 shorter events, 114.4 us)
Async XLA Ops:
  17.0 18.9 %collective-permute-start.3 = (bf16[288,576]{1,0:T(8,128)(2,1)}, bf16[288,576]{1,0:T(8,128)(2,1)S(1)}, u32[]{:S(2)}, u32[]{:S(2)}) collective-permute-start(bf16[288,576]{1,0:T(8,128)(2,1)} %pad_maximum_fusion.2.refs_1_.refs_0_), channel_id=1, source_target_pairs={{0,16},{4,20},{8,24},{12,28},{16,0},{20,4},{24,8},{28,12},{1,17},{... | collective-permute-start | bytes 995336 | tf_op jit(solution)/shard_map/ppermute | solution.py:23
  18.6 17.5 %collective-permute-start.4 = (bf16[288,576]{1,0:T(8,128)(2,1)}, bf16[288,576]{1,0:T(8,128)(2,1)S(1)}, u32[]{:S(2)}, u32[]{:S(2)}) collective-permute-start(bf16[288,576]{1,0:T(8,128)(2,1)} %pad_maximum_fusion.2.refs_1_.refs_0_), channel_id=1, source_target_pairs={{0,24},{4,28},{8,16},{12,20},{16,8},{20,12},{24,0},{28,4},{1,25},{... | collective-permute-start | bytes 995336 | tf_op jit(solution)/shard_map/ppermute | solution.py:23
  23.3 21.8 %all-to-all-start.1 = ((f32[8,4,18,288]{3,1,2,0:T(4,128)}), f32[8,4,18,288]{3,1,2,0:T(4,128)S(1)}, u32[]{:S(2)}, u32[]{:S(2)}) async-start(f32[8,4,18,288]{3,1,2,0:T(4,128)} %broadcast_in_dim.17), calls=%async_computation.1 | async-start | bytes 1769472 | tf_op jit(solution)/shard_map/all_to_all | solution.py:27
  52.7 16.4 %all-to-all-start.2 = ((bf16[8,72,640]{2,1,0:T(8,128)(2,1)}), bf16[8,72,640]{2,1,0:T(8,128)(2,1)}, u32[]{:S(2)}, u32[]{:S(2)}) async-start(bf16[8,72,640]{2,1,0:T(8,128)(2,1)} %get-tuple-element.82), calls=%async_computation.2 | async-start | bytes 1474560 | tf_op jit(solution)/shard_map/all_to_all | solution.py:27
  57.9 22.5 %collective-permute-start = (bf16[144,1152]{1,0:T(8,128)(2,1)}, bf16[144,1152]{1,0:T(8,128)(2,1)}, u32[]{:S(2)}, u32[]{:S(2)}) collective-permute-start(bf16[144,1152]{1,0:T(8,128)(2,1)} %bitcast_select_fusion), channel_id=1, source_target_pairs={{0,4},{4,0},{8,12},{12,8},{16,20},{20,16},{24,28},{28,24},{1,5},{5... | collective-permute-start | bytes 995336 | tf_op jit(solution)/shard_map/ppermute | solution.py:23
  89.7 22.6 %all-to-all-start.4 = ((bf16[4,64,1152]{2,1,0:T(8,128)(2,1)}), bf16[4,64,1152]{2,1,0:T(8,128)(2,1)}, u32[]{:S(2)}, u32[]{:S(2)}) async-start(bf16[4,64,1152]{2,1,0:T(8,128)(2,1)} %bitcast.45), calls=%async_computation.4 | async-start | bytes 1179648 | tf_op jit(solution)/shard_map/all_to_all | solution.py:27
  95.6 16.5 %collective-permute-start.10 = (bf16[288,1152]{1,0:T(8,128)(2,1)}, bf16[288,1152]{1,0:T(8,128)(2,1)}, u32[]{:S(2)}, u32[]{:S(2)}) collective-permute-start(bf16[288,1152]{1,0:T(8,128)(2,1)} %gate.18.refs_1_), channel_id=1, source_target_pairs={{0,16},{4,20},{8,24},{12,28},{16,0},{20,4},{24,8},{28,12},{1,17},{... | collective-permute-start | bytes 1990664 | tf_op jit(solution)/shard_map/ppermute | solution.py:23
  96.1 16.2 %collective-permute-start.9 = (bf16[288,1152]{1,0:T(8,128)(2,1)}, bf16[288,1152]{1,0:T(8,128)(2,1)}, u32[]{:S(2)}, u32[]{:S(2)}) collective-permute-start(bf16[288,1152]{1,0:T(8,128)(2,1)} %gate.18.refs_1_), channel_id=1, source_target_pairs={{0,8},{4,12},{8,0},{12,4},{16,24},{20,28},{24,16},{28,20},{1,9},{5... | collective-permute-start | bytes 1990664 | tf_op jit(solution)/shard_map/ppermute | solution.py:23
  115.0 21.3 %all-to-all-start.5 = ((bf16[4,64,1152]{2,1,0:T(8,128)(2,1)}), bf16[4,64,1152]{2,1,0:T(8,128)(2,1)S(1)}, u32[]{:S(2)}, u32[]{:S(2)}) async-start(bf16[4,64,1152]{2,1,0:T(8,128)(2,1)} %get-tuple-element.88), calls=%async_computation.5 | async-start | bytes 1179648 | tf_op jit(solution)/shard_map/all_to_all | solution.py:27
  120.7 15.5 %collective-permute-start.11 = (bf16[288,1152]{1,0:T(8,128)(2,1)}, bf16[288,1152]{1,0:T(8,128)(2,1)S(1)}, u32[]{:S(2)}, u32[]{:S(2)}) collective-permute-start(bf16[288,1152]{1,0:T(8,128)(2,1)} %gate.19), channel_id=1, source_target_pairs={{0,24},{4,28},{8,16},{12,20},{16,8},{20,12},{24,0},{28,4},{1,25},{... | collective-permute-start | bytes 1990664 | tf_op jit(solution)/shard_map/ppermute | solution.py:23
  122.3 15.6 %collective-permute-start.12 = (bf16[288,1152]{1,0:T(8,128)(2,1)S(1)}, bf16[288,1152]{1,0:T(8,128)(2,1)S(1)}, u32[]{:S(2)}, u32[]{:S(2)}) collective-permute-start(bf16[288,1152]{1,0:T(8,128)(2,1)S(1)} %copy-done.1), channel_id=1, source_target_pairs={{0,4},{4,0},{8,12},{12,8},{16,20},{20,16},{24,28},{28,24},{1,5},{5... | collective-permute-start | bytes 1990664 | tf_op jit(solution)/shard_map/ppermute | solution.py:23
  122.3 16.5 %collective-permute-start.13 = (bf16[288,1152]{1,0:T(8,128)(2,1)}, bf16[288,1152]{1,0:T(8,128)(2,1)S(1)}, u32[]{:S(2)}, u32[]{:S(2)}) collective-permute-start(bf16[288,1152]{1,0:T(8,128)(2,1)} %collective-permute-done.9.refs_5_.refs_2_), channel_id=1, source_target_pairs={{0,4},{4,0},{8,12},{12,8},{16,20},{20,16},{24,28},{28,24},{1,5},{5... | collective-permute-start | bytes 1990664 | tf_op jit(solution)/shard_map/ppermute | solution.py:23
  122.8 16.8 %collective-permute-start.14 = (bf16[288,1152]{1,0:T(8,128)(2,1)}, bf16[288,1152]{1,0:T(8,128)(2,1)}, u32[]{:S(2)}, u32[]{:S(2)}) collective-permute-start(bf16[288,1152]{1,0:T(8,128)(2,1)} %collective-permute-done.10.refs_6_.refs_3_), channel_id=1, source_target_pairs={{0,4},{4,0},{8,12},{12,8},{16,20},{20,16},{24,28},{28,24},{1,5},{5... | collective-permute-start | bytes 1990664 | tf_op jit(solution)/shard_map/ppermute | solution.py:23
  150.5 21.6 %all-to-all-start.6 = ((bf16[4,64,1152]{2,1,0:T(8,128)(2,1)}), bf16[4,64,1152]{2,1,0:T(8,128)(2,1)}, u32[]{:S(2)}, u32[]{:S(2)}) async-start(bf16[4,64,1152]{2,1,0:T(8,128)(2,1)} %bitcast.44), calls=%async_computation.6 | async-start | bytes 1179648 | tf_op jit(solution)/shard_map/all_to_all | solution.py:27
  175.0 21.0 %all-to-all-start.7 = ((bf16[4,64,1152]{2,1,0:T(8,128)(2,1)}), bf16[4,64,1152]{2,1,0:T(8,128)(2,1)}, u32[]{:S(2)}, u32[]{:S(2)}) async-start(bf16[4,64,1152]{2,1,0:T(8,128)(2,1)} %get-tuple-element.102), calls=%async_computation.7 | async-start | bytes 1179648 | tf_op jit(solution)/shard_map/all_to_all | solution.py:27
  179.2 16.4 %collective-permute-start.18 = (bf16[288,1152]{1,0:T(8,128)(2,1)}, bf16[288,1152]{1,0:T(8,128)(2,1)}, u32[]{:S(2)}, u32[]{:S(2)}) collective-permute-start(bf16[288,1152]{1,0:T(8,128)(2,1)} %get-tuple-element.99.refs_7_), channel_id=1, source_target_pairs={{0,8},{4,12},{8,0},{12,4},{16,24},{20,28},{24,16},{28,20},{1,9},{5... | collective-permute-start | bytes 1990664 | tf_op jit(solution)/shard_map/ppermute | solution.py:23
  180.0 16.1 %collective-permute-start.19 = (bf16[288,1152]{1,0:T(8,128)(2,1)}, bf16[288,1152]{1,0:T(8,128)(2,1)}, u32[]{:S(2)}, u32[]{:S(2)}) collective-permute-start(bf16[288,1152]{1,0:T(8,128)(2,1)} %get-tuple-element.100.refs_8_), channel_id=1, source_target_pairs={{0,16},{4,20},{8,24},{12,28},{16,0},{20,4},{24,8},{28,12},{1,17},{... | collective-permute-start | bytes 1990664 | tf_op jit(solution)/shard_map/ppermute | solution.py:23
  208.6 17.7 %collective-permute-start.26 = (bf16[288,1152]{1,0:T(8,128)(2,1)}, bf16[288,1152]{1,0:T(8,128)(2,1)}, u32[]{:S(2)}, u32[]{:S(2)}) collective-permute-start(bf16[288,1152]{1,0:T(8,128)(2,1)} %gate.24), channel_id=1, source_target_pairs={{0,24},{4,28},{8,16},{12,20},{16,8},{20,12},{24,0},{28,4},{1,25},{... | collective-permute-start | bytes 1990664 | tf_op jit(solution)/shard_map/ppermute | solution.py:23
  209.2 13.8 %collective-permute-start.22 = (bf16[64,1152]{1,0:T(8,128)(2,1)}, bf16[64,1152]{1,0:T(8,128)(2,1)S(1)}, u32[]{:S(2)}, u32[]{:S(2)}) collective-permute-start(bf16[64,1152]{1,0:T(8,128)(2,1)} %gate.23), channel_id=1, source_target_pairs={{0,3},{1,2},{2,1},{3,0},{4,7},{5,6},{6,5},{7,4},{8,11},{9,10},{10,... | collective-permute-start | bytes 442376 | tf_op jit(solution)/shard_map/ppermute | solution.py:23
  212.6 12.6 %collective-permute-start.21 = (bf16[64,1152]{1,0:T(8,128)(2,1)}, bf16[64,1152]{1,0:T(8,128)(2,1)}, u32[]{:S(2)}, u32[]{:S(2)}) collective-permute-start(bf16[64,1152]{1,0:T(8,128)(2,1)} %gate.22), channel_id=1, source_target_pairs={{0,2},{1,3},{2,0},{3,1},{4,6},{5,7},{6,4},{7,5},{8,10},{9,11},{10,... | collective-permute-start | bytes 442376 | tf_op jit(solution)/shard_map/ppermute | solution.py:23
  212.6 12.6 %collective-permute-start.20 = (bf16[64,1152]{1,0:T(8,128)(2,1)}, bf16[64,1152]{1,0:T(8,128)(2,1)}, u32[]{:S(2)}, u32[]{:S(2)}) collective-permute-start(bf16[64,1152]{1,0:T(8,128)(2,1)} %gate.21), channel_id=1, source_target_pairs={{0,1},{1,0},{2,3},{3,2},{4,5},{5,4},{6,7},{7,6},{8,9},{9,8},{10,11... | collective-permute-start | bytes 442376 | tf_op jit(solution)/shard_map/ppermute | solution.py:23
  226.3 16.4 %all-to-all-start.9 = ((bf16[8,72,640]{2,1,0:T(8,128)(2,1)}), bf16[8,72,640]{2,1,0:T(8,128)(2,1)}, u32[]{:S(2)}, u32[]{:S(2)}) async-start(bf16[8,72,640]{2,1,0:T(8,128)(2,1)} %gate.25), calls=%async_computation.9 | async-start | bytes 1474560 | tf_op jit(solution)/shard_map/all_to_all | solution.py:27
  231.2 25.1 %collective-permute-start.27 = (bf16[256,1152]{1,0:T(8,128)(2,1)}, bf16[256,1152]{1,0:T(8,128)(2,1)}, u32[]{:S(2)}, u32[]{:S(2)}) collective-permute-start(bf16[256,1152]{1,0:T(8,128)(2,1)} %get-tuple-element.118.refs_1_), channel_id=1, source_target_pairs={{0,4},{4,0},{8,12},{12,8},{16,20},{20,16},{24,28},{28,24},{1,5},{5... | collective-permute-start | bytes 1769480 | tf_op jit(solution)/shard_map/ppermute | solution.py:23
  231.6 24.7 %collective-permute-start.30 = (bf16[256,576]{1,0:T(8,128)(2,1)}, bf16[256,576]{1,0:T(8,128)(2,1)}, u32[]{:S(2)}, u32[]{:S(2)}) collective-permute-start(bf16[256,576]{1,0:T(8,128)(2,1)} %get-tuple-element.121.refs_5_), channel_id=1, source_target_pairs={{0,4},{4,0},{8,12},{12,8},{16,20},{20,16},{24,28},{28,24},{1,5},{5... | collective-permute-start | bytes 884744 | tf_op jit(solution)/shard_map/ppermute | solution.py:23
  234.1 13.7 %collective-permute-start.23 = (bf16[64,1152]{1,0:T(8,128)(2,1)}, bf16[64,1152]{1,0:T(8,128)(2,1)S(1)}, u32[]{:S(2)}, u32[]{:S(2)}) collective-permute-start(bf16[64,1152]{1,0:T(8,128)(2,1)} %get-tuple-element.106.refs_1_), channel_id=1, source_target_pairs={{0,1},{1,0},{2,3},{3,2},{4,5},{5,4},{6,7},{7,6},{8,9},{9,8},{10,11... | collective-permute-start | bytes 442376 | tf_op jit(solution)/shard_map/ppermute | solution.py:23
  235.7 14.3 %collective-permute-start.24 = (bf16[64,1152]{1,0:T(8,128)(2,1)}, bf16[64,1152]{1,0:T(8,128)(2,1)}, u32[]{:S(2)}, u32[]{:S(2)}) collective-permute-start(bf16[64,1152]{1,0:T(8,128)(2,1)} %get-tuple-element.106.refs_1_), channel_id=1, source_target_pairs={{0,2},{1,3},{2,0},{3,1},{4,6},{5,7},{6,4},{7,5},{8,10},{9,11},{10,... | collective-permute-start | bytes 442376 | tf_op jit(solution)/shard_map/ppermute | solution.py:23
  250.0 24.4 %all-to-all-start.10 = ((bf16[4,64,1152]{2,1,0:T(8,128)(2,1)}), bf16[4,64,1152]{2,1,0:T(8,128)(2,1)}, u32[]{:S(2)}, u32[]{:S(2)}) async-start(bf16[4,64,1152]{2,1,0:T(8,128)(2,1)} %bitcast.43), calls=%async_computation.10 | async-start | bytes 1179648 | tf_op jit(solution)/shard_map/all_to_all | solution.py:27
  256.1 27.7 %collective-permute-start.38 = (f32[144,1152]{1,0:T(8,128)}, f32[144,1152]{1,0:T(8,128)}, u32[]{:S(2)}, u32[]{:S(2)}) collective-permute-start(f32[144,1152]{1,0:T(8,128)} %slice_select_fusion), channel_id=1, source_target_pairs={{0,4},{4,0},{8,12},{12,8},{16,20},{20,16},{24,28},{28,24},{1,5},{5... | collective-permute-start | bytes 1990664 | tf_op jit(solution)/shard_map/ppermute | solution.py:23
  282.3 15.4 %collective-permute-start.36 = (bf16[288,576]{1,0:T(8,128)(2,1)}, bf16[288,576]{1,0:T(8,128)(2,1)S(1)}, u32[]{:S(2)}, u32[]{:S(2)}) collective-permute-start(bf16[288,576]{1,0:T(8,128)(2,1)} %gate.29), channel_id=1, source_target_pairs={{0,24},{4,28},{8,16},{12,20},{16,8},{20,12},{24,0},{28,4},{1,25},{... | collective-permute-start | bytes 995336 | tf_op jit(solution)/shard_map/ppermute | solution.py:23
  293.2 18.4 %collective-permute-start.33 = (bf16[64,1152]{1,0:T(8,128)(2,1)}, bf16[64,1152]{1,0:T(8,128)(2,1)S(1)}, u32[]{:S(2)}, u32[]{:S(2)}) collective-permute-start(bf16[64,1152]{1,0:T(8,128)(2,1)} %gate.28.refs_0_), channel_id=1, source_target_pairs={{0,1},{1,0},{2,3},{3,2},{4,5},{5,4},{6,7},{7,6},{8,9},{9,8},{10,11... | collective-permute-start | bytes 442376 | tf_op jit(solution)/shard_map/ppermute | solution.py:23
  294.2 17.3 %collective-permute-start.34 = (bf16[64,1152]{1,0:T(8,128)(2,1)}, bf16[64,1152]{1,0:T(8,128)(2,1)}, u32[]{:S(2)}, u32[]{:S(2)}) collective-permute-start(bf16[64,1152]{1,0:T(8,128)(2,1)} %gate.28.refs_0_), channel_id=1, source_target_pairs={{0,2},{1,3},{2,0},{3,1},{4,6},{5,7},{6,4},{7,5},{8,10},{9,11},{10,... | collective-permute-start | bytes 442376 | tf_op jit(solution)/shard_map/ppermute | solution.py:23
  295.6 16.0 %collective-permute-start.35 = (bf16[64,1152]{1,0:T(8,128)(2,1)}, bf16[64,1152]{1,0:T(8,128)(2,1)}, u32[]{:S(2)}, u32[]{:S(2)}) collective-permute-start(bf16[64,1152]{1,0:T(8,128)(2,1)} %gate.28.refs_0_), channel_id=1, source_target_pairs={{0,3},{1,2},{2,1},{3,0},{4,7},{5,6},{6,5},{7,4},{8,11},{9,10},{10,... | collective-permute-start | bytes 442376 | tf_op jit(solution)/shard_map/ppermute | solution.py:23
  (58 other events, 332.7 us)

commit v12 on v11

--- a/solution.py
+++ b/solution.py
@@ -248,7 +248,7 @@
             pltpu.VMEM((blocks // 2, DH, STEP), F32),
         ],
         compiler_params=pltpu.CompilerParams(vmem_limit_bytes=VMEM_BYTES),
-        cost_estimate=pl.CostEstimate(flops=3 * 10**9, bytes_accessed=4 * 10**6, transcendentals=10**6),
+        cost_estimate=pl.CostEstimate(flops=1, bytes_accessed=1, transcendentals=0),
         name="attend_backward",
     )(meta, packed, grad, exact, log_total)
 
@@ -264,8 +264,8 @@
         return exchange(out, "dp")
 
     def backward(self, grad, due, beside):
+        beside = swap(gate(beside, grad), "dp", lax.axis_size("dp") - 2)
         grad = exchange(grad, "dp")
-        beside = swap(gate(beside, grad), "dp", lax.axis_size("dp") - 2)
         out = attend_backward(self.meta, self.packed, grad, self.exact, self.log_total)
         return exchange(gate(out, beside, *due), "dp"), beside
 
@@ -809,16 +809,13 @@
     mod_part = mod_part.reshape(latents * 6, features)
     bias_ada = jnp.tile(b_ada.astype(F32), (latents, 1))
     few_chips = n_dp // 2 == 4
-    if few_chips:
-        mod_part = gate(mod_part + jnp.where(my_dp == 0, bias_ada, 0.0), early_rows)
-        mod_wide = gather(mod_part, "tensor", n_tensor)
-        mod_parts = gather(mod_wide, "dp", n_dp).reshape((-1,) + mod_part.shape)
-    else:
-        mod_wide = jnp.sum(gather(mod_part, "dp", n_dp), axis=0) + bias_ada
-        mod_parts = gather(mod_wide, "tensor", n_tensor)
+    mod_sent = gate(jnp.broadcast_to(mod_part[None], (n_dp,) + mod_part.shape))
+    early_rows = gate(early_rows, mod_sent)
+    mod_mine = jnp.sum(exchange(mod_sent, "dp"), axis=0) + bias_ada
+    mod_parts = gather(mod_mine, "tensor", n_tensor)
     early_parts = chip_parts(early_rows) if few_chips else [gather_chips(early_rows)]
 
-    early_parts = list(gate_all(early_parts, mod_wide))
+    early_parts = list(gate_all(early_parts, mod_parts))
     early_parts += [swap(part, "dp", 1) for part in early_parts]
     count = len(early_parts) // 2
     meta = jnp.stack([core, my_dp * rows, my_tensor, my_dp // 2]).astype(jnp.int32)

time: 326 us -> 325 us (level)
  blocking collectives: 9.69 us -> 22.5 us
  Pallas kernels: 72.3 us -> 67.7 us
  starting transfers between devices: 88.4 us -> 84.2 us
    all_to_all x1 -> x2, blocking collectives: 9.69 us -> 22.5 us  [exchange(): return lax.all_to_all(blocks, axis, 0, 0, tiled=True)]
    ppermute x39, waiting for transfers between devices: 69.4 us -> 58.5 us  [swap(): return lax.ppermute(block, axis, route)]
    all_to_all x13 -> x12, waiting for transfers between devices: 34.7 us -> 42.7 us  [exchange(): return lax.all_to_all(blocks, axis, 0, 0, tiled=True)]
    all_to_all x13 -> x12, starting transfers between devices: 58 us -> 51.6 us  [exchange(): return lax.all_to_all(blocks, axis, 0, 0, tiled=True)]
  transfers between devices with their start and end apart: 52 -> 51, of which waited for: 24 -> 21; matrix products, arithmetic and copies ran while one was open for 11% -> 10% of each run, Pallas kernels for 13% -> 12%
where the time goes in v12:
time: 325 us; the launch traced here: 324 us
  waiting for transfers between devices  101 us (31%)
  starting transfers between devices  84.2 us (26%)
  Pallas kernels  67.7 us (21%)
  other arithmetic  24 us (7%)
  local copies, waits for them, and re-layouts  22.7 us (7%)
  blocking collectives  22.5 us (7%)
    ppermute x39, waiting for transfers between devices, swap(): return lax.ppermute(block, axis, route)  58.5 us
    pallas_call x13, Pallas kernels, call(): pl.pallas_call(kernel, out_shape=tuple((jax.ShapeDtypeStruct(shape, kind)...  54.6 us
    all_to_all x12, starting transfers between devices, exchange(): return lax.all_to_all(blocks, axis, 0, 0, tiled=True)  51.6 us
    all_to_all x12, waiting for transfers between devices, exchange(): return lax.all_to_all(blocks, axis, 0, 0, tiled=True)  42.7 us
    ppermute x39, starting transfers between devices, swap(): return lax.ppermute(block, axis, route)  32.6 us
    all_to_all x2, blocking collectives, exchange(): return lax.all_to_all(blocks, axis, 0, 0, tiled=True)  22.5 us
    unnamed x82, local copies, waits for them, and re-layouts  10.8 us
    pallas_call x1, Pallas kernels, attend_backward(): pl.pallas_call(lambda *refs: backward_kernel(meta.shape[0] - 1, *refs), o...  7.18 us
  transfers between devices with their start and end apart: 51, of which 21 were waited for; matrix products, arithmetic and copies ran while one was open for 10% of the time, Pallas kernels for 12%

profile of v12, /device:TPU:0, one launch (start us, length us, event | category | flops | bytes accessed | tf_op | source)
XLA Modules:
  0.0 323.7 jit_solution(8463629199817072789)
XLA Ops:
  12.3 4.2 %all-to-all-start = ((f32[8,18,288]{2,1,0:T(8,128)}), f32[8,18,288]{2,1,0:T(8,128)S(1)}, u32[]{:S(2)}, u32[]{:S(2)}) async-start(f32[8,18,288]{2,1,0:T(8,128)} %gate.17.refs_1_), calls=%async_computation | async-start | bytes 589824 | tf_op jit(solution)/shard_map/all_to_all | solution.py:27
  16.6 16.2 %all-to-all-done = f32[8,18,288]{2,1,0:T(8,128)S(1)} async-done(((f32[8,18,288]{2,1,0:T(8,128)}), f32[8,18,288]{2,1,0:T(8,128)S(1)}, u32[]{:S(2)}, u32[]{:S(2)}) %all-to-all-start) | async-done | bytes 165920 | tf_op jit(solution)/shard_map/all_to_all | solution.py:27
  32.8 11.4 %all_to_all.70.refs_4_.refs_11_ = f32[4,18,288]{2,1,0:T(8,128)} all-to-all(f32[4,18,288]{2,1,0:T(8,128)S(1)} %broadcast_in_dim.15), channel_id=1, replica_groups=mesh['dp'=8,'tensor'=4] {'tensor'}, dimensions={0} | all-to-all | bytes 165888 | tf_op jit(solution)/shard_map/all_to_all | solution.py:27
  49.5 6.1 %project.1 = (bf16[256,1152]{1,0:T(8,128)(2,1)}, bf16[256,1152]{1,0:T(8,128)(2,1)}, bf16[8,72,640]{2,1,0:T(8,128)(2,1)}, bf16[1152,576]{1,0:T(8,128)(2,1)}, bf16...) custom-call(s32[7]{0:T(128)} %concatenate.24.refs_0_, bf16[288,576]{1,0:T(8,128)(2,1)} %get-tuple-element.78.refs_1_, ...), custom_call_target="tpu_custom_call" | custom-call | flops 1 | bytes 1 | tf_op jit(solution)/shard_map/project/pallas_call | solution.py:366
  55.6 4.4 %all-to-all-start.2 = ((bf16[8,72,640]{2,1,0:T(8,128)(2,1)}), bf16[8,72,640]{2,1,0:T(8,128)(2,1)}, u32[]{:S(2)}, u32[]{:S(2)}) async-start(bf16[8,72,640]{2,1,0:T(8,128)(2,1)} %get-tuple-element.82), calls=%async_computation.2 | async-start | bytes 1474560 | tf_op jit(solution)/shard_map/all_to_all | solution.py:27
  61.7 10.3 %all-to-all-done.2.refs_1_ = bf16[8,72,640]{2,1,0:T(8,128)(2,1)} async-done(((bf16[8,72,640]{2,1,0:T(8,128)(2,1)}), bf16[8,72,640]{2,1,0:T(8,128)(2,1)}, u32[]{:S(2)}, u32[]{:S(2)}) %all-to-all-start.2) | async-done | bytes 737312 | tf_op jit(solution)/shard_map/all_to_all | solution.py:27
  72.1 6.0 %attend_forward.1 = (bf16[8,72,128]{2,1,0:T(8,128)(2,1)}, f32[8,72,128]{2,1,0:T(8,128)}, f32[8,1,128]{2,1,0:T(1,128)}) custom-call(s32[4]{0:T(128)} %pad_add_fusion.refs_0_, bf16[8,72,640]{2,1,0:T(8,128)(2,1)} %all-to-all-done.2.refs_1_), custom_call_target="tpu_custom_call" | custom-call | flops 1000000000 | bytes 4000000 | tf_op jit(solution)/shard_map/attend_forward/pallas_call | solution.py:214
  78.0 3.4 %all-to-all-start.3 = ((bf16[8,72,128]{2,1,0:T(8,128)(2,1)}), bf16[8,72,128]{2,1,0:T(8,128)(2,1)S(1)}, u32[]{:S(2)}, u32[]{:S(2)}) async-start(bf16[8,72,128]{2,1,0:T(8,128)(2,1)} %get-tuple-element.83), calls=%async_computation.3 | async-start | bytes 294912 | tf_op jit(solution)/shard_map/all_to_all | solution.py:27
  83.5 3.5 %all-to-all-done.3.refs_1_ = bf16[8,72,128]{2,1,0:T(8,128)(2,1)S(1)} async-done(((bf16[8,72,128]{2,1,0:T(8,128)(2,1)}), bf16[8,72,128]{2,1,0:T(8,128)(2,1)S(1)}, u32[]{:S(2)}, u32[]{:S(2)}) %all-to-all-start.3) | async-done | bytes 147488 | tf_op jit(solution)/shard_map/all_to_all | solution.py:27
  87.7 3.0 attend_out.1
  90.7 4.3 %all-to-all-start.4 = ((bf16[4,64,1152]{2,1,0:T(8,128)(2,1)}), bf16[4,64,1152]{2,1,0:T(8,128)(2,1)}, u32[]{:S(2)}, u32[]{:S(2)}) async-start(bf16[4,64,1152]{2,1,0:T(8,128)(2,1)} %bitcast.43), calls=%async_computation.4 | async-start | bytes 1179648 | tf_op jit(solution)/shard_map/all_to_all | solution.py:27
  97.7 15.1 %collective-permute-done.10.refs_6_.refs_3_ = bf16[288,1152]{1,0:T(8,128)(2,1)} collective-permute-done((bf16[288,1152]{1,0:T(8,128)(2,1)}, bf16[288,1152]{1,0:T(8,128)(2,1)}, u32[]{:S(2)}, u32[]{:S(2)}) %collective-permute-start.10) | collective-permute-done | bytes 663584 | tf_op jit(solution)/shard_map/ppermute | solution.py:23
  115.6 4.9 %all-to-all-start.5 = ((bf16[4,64,1152]{2,1,0:T(8,128)(2,1)}), bf16[4,64,1152]{2,1,0:T(8,128)(2,1)S(1)}, u32[]{:S(2)}, u32[]{:S(2)}) async-start(bf16[4,64,1152]{2,1,0:T(8,128)(2,1)} %get-tuple-element.88), calls=%async_computation.5 | async-start | bytes 1179648 | tf_op jit(solution)/shard_map/all_to_all | solution.py:27
  123.4 13.8 %collective-permute-done.11.refs_0_ = bf16[288,1152]{1,0:T(8,128)(2,1)S(1)} collective-permute-done((bf16[288,1152]{1,0:T(8,128)(2,1)}, bf16[288,1152]{1,0:T(8,128)(2,1)S(1)}, u32[]{:S(2)}, u32[]{:S(2)}) %collective-permute-start.11) | collective-permute-done | bytes 663584 | tf_op jit(solution)/shard_map/ppermute | solution.py:23
  140.7 10.7 %mlp.1 = (bf16[256,1152]{1,0:T(8,128)(2,1)}, bf16[256,1152]{1,0:T(8,128)(2,1)}, bf16[256,1152]{1,0:T(8,128)(2,1)}, f32[1,1152]{1,0:T(1,128)}, bf16[256,1152]{1,0...) custom-call(s32[7]{0:T(128)} %concatenate.24.refs_0_, ...), custom_call_target="tpu_custom_call" | custom-call | flops 1 | bytes 1 | tf_op jit(solution)/shard_map/mlp/pallas_call | solution.py:366
  151.4 4.8 %all-to-all-start.6 = ((bf16[4,64,1152]{2,1,0:T(8,128)(2,1)}), bf16[4,64,1152]{2,1,0:T(8,128)(2,1)}, u32[]{:S(2)}, u32[]{:S(2)}) async-start(bf16[4,64,1152]{2,1,0:T(8,128)(2,1)} %bitcast.42), calls=%async_computation.6 | async-start | bytes 1179648 | tf_op jit(solution)/shard_map/all_to_all | solution.py:27
  159.4 5.8 %late_weights.1 = (bf16[288,1152]{1,0:T(8,128)(2,1)}, bf16[288,1152]{1,0:T(8,128)(2,1)}, bf16[288,1152]{1,0:T(8,128)(2,1)}, bf16[288,1152]{1,0:T(8,128)(2,1)}) custom-call(s32[7]{0:T(128)} %concatenate.24.refs_0_, bf16[256,1152]{1,0:T(8,128)(2,1)} %bitcast.39, bf16[256,1152]{1,0:T(8,128)(2,1)} %get-tuple-element.89.refs_10_.refs_2_, ...), custom_call_target="tpu_custom_call" | custom-call | flops 1 | bytes 1 | tf_op jit(solution)/shard_map/late_weights/pallas_call | solution.py:366
  165.2 7.5 %all-to-all-done.6.refs_1_ = bf16[4,64,1152]{2,1,0:T(8,128)(2,1)} async-done(((bf16[4,64,1152]{2,1,0:T(8,128)(2,1)}), bf16[4,64,1152]{2,1,0:T(8,128)(2,1)}, u32[]{:S(2)}, u32[]{:S(2)}) %all-to-all-start.6) | async-done | bytes 589856 | tf_op jit(solution)/shard_map/all_to_all | solution.py:27
  175.7 4.2 %all-to-all-start.7 = ((bf16[4,64,1152]{2,1,0:T(8,128)(2,1)}), bf16[4,64,1152]{2,1,0:T(8,128)(2,1)}, u32[]{:S(2)}, u32[]{:S(2)}) async-start(bf16[4,64,1152]{2,1,0:T(8,128)(2,1)} %get-tuple-element.102), calls=%async_computation.7 | async-start | bytes 1179648 | tf_op jit(solution)/shard_map/all_to_all | solution.py:27
  182.1 14.2 %collective-permute-done.18.refs_3_ = bf16[288,1152]{1,0:T(8,128)(2,1)} collective-permute-done((bf16[288,1152]{1,0:T(8,128)(2,1)}, bf16[288,1152]{1,0:T(8,128)(2,1)}, u32[]{:S(2)}, u32[]{:S(2)}) %collective-permute-start.18) | collective-permute-done | bytes 663584 | tf_op jit(solution)/shard_map/ppermute | solution.py:23
  201.8 3.4 %collective-permute-start.22 = (bf16[64,1152]{1,0:T(8,128)(2,1)}, bf16[64,1152]{1,0:T(8,128)(2,1)S(1)}, u32[]{:S(2)}, u32[]{:S(2)}) collective-permute-start(bf16[64,1152]{1,0:T(8,128)(2,1)} %gate.25), channel_id=1, source_target_pairs={{0,3},{1,2},{2,1},{3,0},{4,7},{5,6},{6,5},{7,4},{8,11},{9,10},{10,... | collective-permute-start | bytes 442376 | tf_op jit(solution)/shard_map/ppermute | solution.py:23
  206.2 11.0 %all_to_all.71.refs_2_ = bf16[8,72,128]{2,1,0:T(8,128)(2,1)} all-to-all(bf16[8,72,128]{2,1,0:T(8,128)(2,1)S(1)} %copy-done.7), channel_id=1, replica_groups=mesh['dp'=8,'tensor'=4] {'dp'}, dimensions={0} | all-to-all | bytes 294912 | tf_op jit(solution)/shard_map/all_to_all | solution.py:27
  217.2 7.2 %attend_backward.1.refs_0_ = bf16[8,72,640]{2,1,0:T(8,128)(2,1)} custom-call(s32[4]{0:T(128)} %pad_add_fusion.refs_0_, bf16[8,72,640]{2,1,0:T(8,128)(2,1)} %all-to-all-done.2.refs_1_, bf16[8,72,128]{2,1,0:T(8,128)(2,1)} %all_to_all.71.refs_2_, f32[8,72,128]{2,1,0:T(8,128)} %get-tuple-element.107.refs_3_, f32[8,1,128]{2,1,0:T(1,128)} %get-tuple-element.108.refs_4_), custom_call_target="tpu_custom_call" | custom-call | flops 1 | bytes 1 | tf_op jit(solution)/shard_map/attend_backward/pallas_call | solution.py:238
  225.1 4.3 %all-to-all-start.9 = ((bf16[8,72,640]{2,1,0:T(8,128)(2,1)}), bf16[8,72,640]{2,1,0:T(8,128)(2,1)}, u32[]{:S(2)}, u32[]{:S(2)}) async-start(bf16[8,72,640]{2,1,0:T(8,128)(2,1)} %gate.27), calls=%async_computation.9 | async-start | bytes 1474560 | tf_op jit(solution)/shard_map/all_to_all | solution.py:27
  237.2 3.1 convert_add_fusion
  241.5 5.1 %unspread.1 = (bf16[256,1152]{1,0:T(8,128)(2,1)}, bf16[256,576]{1,0:T(8,128)(2,1)}, bf16[256,576]{1,0:T(8,128)(2,1)}, bf16[256,576]{1,0:T(8,128)(2,1)}, f32[2,576]{1,0:T(2,128)}) custom-call(s32[7]{0:T(128)} %concatenate.24.refs_0_, bf16[8,72,640]{2,1,0:T(8,128)(2,1)} %all-to-all-done.9.refs_1_, bf16[1152,576]{1,0:T(8,128)(2,1)} %get-tuple-element.109.refs_2_, ...), custom_call_target="tpu_custom_call" | custom-call | flops 20000000000 | bytes 1 | tf_op jit(solution)/shard_map/unspread/pallas_call | solution.py:366
  248.5 5.1 %all-to-all-start.10 = ((bf16[4,64,1152]{2,1,0:T(8,128)(2,1)}), bf16[4,64,1152]{2,1,0:T(8,128)(2,1)}, u32[]{:S(2)}, u32[]{:S(2)}) async-start(bf16[4,64,1152]{2,1,0:T(8,128)(2,1)} %bitcast.41), calls=%async_computation.10 | async-start | bytes 1179648 | tf_op jit(solution)/shard_map/all_to_all | solution.py:27
  254.8 4.9 %early_weights.1 = (bf16[288,576]{1,0:T(8,128)(2,1)}, bf16[288,576]{1,0:T(8,128)(2,1)}, bf16[288,576]{1,0:T(8,128)(2,1)}, bf16[288,576]{1,0:T(8,128)(2,1)}) custom-call(s32[7]{0:T(128)} %concatenate.24.refs_0_, bf16[256,1152]{1,0:T(8,128)(2,1)} %get-tuple-element.118.refs_1_, bf16[256,1152]{1,0:T(8,128)(2,1)} %bitcast.11.refs_1_.refs_2_, ...), custom_call_target="tpu_custom_call" | custom-call | flops 1 | bytes 1 | tf_op jit(solution)/shard_map/early_weights/pallas_call | solution.py:366
  263.9 7.1 %collective-permute-done.31.refs_11_ = bf16[288,576]{1,0:T(8,128)(2,1)} collective-permute-done((bf16[288,576]{1,0:T(8,128)(2,1)}, bf16[288,576]{1,0:T(8,128)(2,1)}, u32[]{:S(2)}, u32[]{:S(2)}) %collective-permute-start.31) | collective-permute-done | bytes 331808 | tf_op jit(solution)/shard_map/ppermute | solution.py:23
  275.7 5.1 %all-to-all-start.11 = ((f32[4,18,288]{2,1,0:T(8,128)}), f32[4,18,288]{2,1,0:T(8,128)S(1)}, u32[]{:S(2)}, u32[]{:S(2)}) async-start(f32[4,18,288]{2,1,0:T(8,128)} %get-tuple-element.126.refs_1_), calls=%async_computation.11 | async-start | bytes 294912 | tf_op jit(solution)/shard_map/all_to_all | solution.py:27
  288.0 3.7 %all-to-all-start.12 = ((f32[8,32,288]{2,1,0:T(8,128)}), f32[8,32,288]{2,1,0:T(8,128)S(1)}, u32[]{:S(2)}, u32[]{:S(2)}) async-start(f32[8,32,288]{2,1,0:T(8,128)} %gate.29.refs_1_), calls=%async_computation.12 | async-start | bytes 786432 | tf_op jit(solution)/shard_map/all_to_all | solution.py:27
  304.9 3.2 %all-to-all-start.13 = ((f32[32,1,432]{2,1,0:T(1,128)}), f32[32,1,432]{2,1,0:T(1,128)}, u32[]{:S(2)}, u32[]{:S(2)}) async-start(f32[32,1,432]{2,1,0:T(1,128)} %reshape.118), calls=%async_computation.13 | async-start | bytes 131072 | tf_op jit(solution)/shard_map/all_to_all | solution.py:27
  (241 shorter events, 105.6 us)
Async XLA Ops:
  8.3 36.0 %collective-permute-start.2 = (bf16[288,576]{1,0:T(8,128)(2,1)}, bf16[288,576]{1,0:T(8,128)(2,1)S(1)}, u32[]{:S(2)}, u32[]{:S(2)}) collective-permute-start(bf16[288,576]{1,0:T(8,128)(2,1)} %gate.18.refs_0_), channel_id=1, source_target_pairs={{0,8},{4,12},{8,0},{12,4},{16,24},{20,28},{24,16},{28,20},{1,9},{5... | collective-permute-start | bytes 995336 | tf_op jit(solution)/shard_map/ppermute | solution.py:23
  10.8 33.5 %collective-permute-start.3 = (bf16[288,576]{1,0:T(8,128)(2,1)}, bf16[288,576]{1,0:T(8,128)(2,1)S(1)}, u32[]{:S(2)}, u32[]{:S(2)}) collective-permute-start(bf16[288,576]{1,0:T(8,128)(2,1)} %gate.18.refs_0_), channel_id=1, source_target_pairs={{0,16},{4,20},{8,24},{12,28},{16,0},{20,4},{24,8},{28,12},{1,17},{... | collective-permute-start | bytes 995336 | tf_op jit(solution)/shard_map/ppermute | solution.py:23
  12.3 32.0 %collective-permute-start.4 = (bf16[288,576]{1,0:T(8,128)(2,1)}, bf16[288,576]{1,0:T(8,128)(2,1)S(1)}, u32[]{:S(2)}, u32[]{:S(2)}) collective-permute-start(bf16[288,576]{1,0:T(8,128)(2,1)} %gate.18.refs_0_), channel_id=1, source_target_pairs={{0,24},{4,28},{8,16},{12,20},{16,8},{20,12},{24,0},{28,4},{1,25},{... | collective-permute-start | bytes 995336 | tf_op jit(solution)/shard_map/ppermute | solution.py:23
  12.3 20.4 %all-to-all-start = ((f32[8,18,288]{2,1,0:T(8,128)}), f32[8,18,288]{2,1,0:T(8,128)S(1)}, u32[]{:S(2)}, u32[]{:S(2)}) async-start(f32[8,18,288]{2,1,0:T(8,128)} %gate.17.refs_1_), calls=%async_computation | async-start | bytes 589824 | tf_op jit(solution)/shard_map/all_to_all | solution.py:27
  55.6 16.4 %all-to-all-start.2 = ((bf16[8,72,640]{2,1,0:T(8,128)(2,1)}), bf16[8,72,640]{2,1,0:T(8,128)(2,1)}, u32[]{:S(2)}, u32[]{:S(2)}) async-start(bf16[8,72,640]{2,1,0:T(8,128)(2,1)} %get-tuple-element.82), calls=%async_computation.2 | async-start | bytes 1474560 | tf_op jit(solution)/shard_map/all_to_all | solution.py:27
  60.8 20.6 %collective-permute-start = (bf16[144,1152]{1,0:T(8,128)(2,1)}, bf16[144,1152]{1,0:T(8,128)(2,1)}, u32[]{:S(2)}, u32[]{:S(2)}) collective-permute-start(bf16[144,1152]{1,0:T(8,128)(2,1)} %bitcast_select_fusion), channel_id=1, source_target_pairs={{0,4},{4,0},{8,12},{12,8},{16,20},{20,16},{24,28},{28,24},{1,5},{5... | collective-permute-start | bytes 995336 | tf_op jit(solution)/shard_map/ppermute | solution.py:23
  90.7 22.2 %all-to-all-start.4 = ((bf16[4,64,1152]{2,1,0:T(8,128)(2,1)}), bf16[4,64,1152]{2,1,0:T(8,128)(2,1)}, u32[]{:S(2)}, u32[]{:S(2)}) async-start(bf16[4,64,1152]{2,1,0:T(8,128)(2,1)} %bitcast.43), calls=%async_computation.4 | async-start | bytes 1179648 | tf_op jit(solution)/shard_map/all_to_all | solution.py:27
  96.0 16.8 %collective-permute-start.10 = (bf16[288,1152]{1,0:T(8,128)(2,1)}, bf16[288,1152]{1,0:T(8,128)(2,1)}, u32[]{:S(2)}, u32[]{:S(2)}) collective-permute-start(bf16[288,1152]{1,0:T(8,128)(2,1)} %gate.20.refs_1_), channel_id=1, source_target_pairs={{0,16},{4,20},{8,24},{12,28},{16,0},{20,4},{24,8},{28,12},{1,17},{... | collective-permute-start | bytes 1990664 | tf_op jit(solution)/shard_map/ppermute | solution.py:23
  96.5 16.5 %collective-permute-start.9 = (bf16[288,1152]{1,0:T(8,128)(2,1)}, bf16[288,1152]{1,0:T(8,128)(2,1)}, u32[]{:S(2)}, u32[]{:S(2)}) collective-permute-start(bf16[288,1152]{1,0:T(8,128)(2,1)} %gate.20.refs_1_), channel_id=1, source_target_pairs={{0,8},{4,12},{8,0},{12,4},{16,24},{20,28},{24,16},{28,20},{1,9},{5... | collective-permute-start | bytes 1990664 | tf_op jit(solution)/shard_map/ppermute | solution.py:23
  115.6 21.6 %all-to-all-start.5 = ((bf16[4,64,1152]{2,1,0:T(8,128)(2,1)}), bf16[4,64,1152]{2,1,0:T(8,128)(2,1)S(1)}, u32[]{:S(2)}, u32[]{:S(2)}) async-start(bf16[4,64,1152]{2,1,0:T(8,128)(2,1)} %get-tuple-element.88), calls=%async_computation.5 | async-start | bytes 1179648 | tf_op jit(solution)/shard_map/all_to_all | solution.py:27
  121.3 15.8 %collective-permute-start.11 = (bf16[288,1152]{1,0:T(8,128)(2,1)}, bf16[288,1152]{1,0:T(8,128)(2,1)S(1)}, u32[]{:S(2)}, u32[]{:S(2)}) collective-permute-start(bf16[288,1152]{1,0:T(8,128)(2,1)} %gate.21), channel_id=1, source_target_pairs={{0,24},{4,28},{8,16},{12,20},{16,8},{20,12},{24,0},{28,4},{1,25},{... | collective-permute-start | bytes 1990664 | tf_op jit(solution)/shard_map/ppermute | solution.py:23
  122.9 15.9 %collective-permute-start.12 = (bf16[288,1152]{1,0:T(8,128)(2,1)S(1)}, bf16[288,1152]{1,0:T(8,128)(2,1)S(1)}, u32[]{:S(2)}, u32[]{:S(2)}) collective-permute-start(bf16[288,1152]{1,0:T(8,128)(2,1)S(1)} %copy-done.1), channel_id=1, source_target_pairs={{0,4},{4,0},{8,12},{12,8},{16,20},{20,16},{24,28},{28,24},{1,5},{5... | collective-permute-start | bytes 1990664 | tf_op jit(solution)/shard_map/ppermute | solution.py:23
  122.9 16.8 %collective-permute-start.13 = (bf16[288,1152]{1,0:T(8,128)(2,1)}, bf16[288,1152]{1,0:T(8,128)(2,1)S(1)}, u32[]{:S(2)}, u32[]{:S(2)}) collective-permute-start(bf16[288,1152]{1,0:T(8,128)(2,1)} %collective-permute-done.9.refs_5_.refs_2_), channel_id=1, source_target_pairs={{0,4},{4,0},{8,12},{12,8},{16,20},{20,16},{24,28},{28,24},{1,5},{5... | collective-permute-start | bytes 1990664 | tf_op jit(solution)/shard_map/ppermute | solution.py:23
  123.4 17.1 %collective-permute-start.14 = (bf16[288,1152]{1,0:T(8,128)(2,1)}, bf16[288,1152]{1,0:T(8,128)(2,1)}, u32[]{:S(2)}, u32[]{:S(2)}) collective-permute-start(bf16[288,1152]{1,0:T(8,128)(2,1)} %collective-permute-done.10.refs_6_.refs_3_), channel_id=1, source_target_pairs={{0,4},{4,0},{8,12},{12,8},{16,20},{20,16},{24,28},{28,24},{1,5},{5... | collective-permute-start | bytes 1990664 | tf_op jit(solution)/shard_map/ppermute | solution.py:23
  151.4 21.3 %all-to-all-start.6 = ((bf16[4,64,1152]{2,1,0:T(8,128)(2,1)}), bf16[4,64,1152]{2,1,0:T(8,128)(2,1)}, u32[]{:S(2)}, u32[]{:S(2)}) async-start(bf16[4,64,1152]{2,1,0:T(8,128)(2,1)} %bitcast.42), calls=%async_computation.6 | async-start | bytes 1179648 | tf_op jit(solution)/shard_map/all_to_all | solution.py:27
  175.7 21.0 %all-to-all-start.7 = ((bf16[4,64,1152]{2,1,0:T(8,128)(2,1)}), bf16[4,64,1152]{2,1,0:T(8,128)(2,1)}, u32[]{:S(2)}, u32[]{:S(2)}) async-start(bf16[4,64,1152]{2,1,0:T(8,128)(2,1)} %get-tuple-element.102), calls=%async_computation.7 | async-start | bytes 1179648 | tf_op jit(solution)/shard_map/all_to_all | solution.py:27
  179.9 16.4 %collective-permute-start.18 = (bf16[288,1152]{1,0:T(8,128)(2,1)}, bf16[288,1152]{1,0:T(8,128)(2,1)}, u32[]{:S(2)}, u32[]{:S(2)}) collective-permute-start(bf16[288,1152]{1,0:T(8,128)(2,1)} %get-tuple-element.99.refs_7_), channel_id=1, source_target_pairs={{0,8},{4,12},{8,0},{12,4},{16,24},{20,28},{24,16},{28,20},{1,9},{5... | collective-permute-start | bytes 1990664 | tf_op jit(solution)/shard_map/ppermute | solution.py:23
  180.7 16.1 %collective-permute-start.19 = (bf16[288,1152]{1,0:T(8,128)(2,1)}, bf16[288,1152]{1,0:T(8,128)(2,1)}, u32[]{:S(2)}, u32[]{:S(2)}) collective-permute-start(bf16[288,1152]{1,0:T(8,128)(2,1)} %get-tuple-element.100.refs_8_), channel_id=1, source_target_pairs={{0,16},{4,20},{8,24},{12,28},{16,0},{20,4},{24,8},{28,12},{1,17},{... | collective-permute-start | bytes 1990664 | tf_op jit(solution)/shard_map/ppermute | solution.py:23
  199.6 24.8 %collective-permute-start.26 = (bf16[288,1152]{1,0:T(8,128)(2,1)}, bf16[288,1152]{1,0:T(8,128)(2,1)}, u32[]{:S(2)}, u32[]{:S(2)}) collective-permute-start(bf16[288,1152]{1,0:T(8,128)(2,1)} %gate.26), channel_id=1, source_target_pairs={{0,24},{4,28},{8,16},{12,20},{16,8},{20,12},{24,0},{28,4},{1,25},{... | collective-permute-start | bytes 1990664 | tf_op jit(solution)/shard_map/ppermute | solution.py:23
  201.8 22.6 %collective-permute-start.22 = (bf16[64,1152]{1,0:T(8,128)(2,1)}, bf16[64,1152]{1,0:T(8,128)(2,1)S(1)}, u32[]{:S(2)}, u32[]{:S(2)}) collective-permute-start(bf16[64,1152]{1,0:T(8,128)(2,1)} %gate.25), channel_id=1, source_target_pairs={{0,3},{1,2},{2,1},{3,0},{4,7},{5,6},{6,5},{7,4},{8,11},{9,10},{10,... | collective-permute-start | bytes 442376 | tf_op jit(solution)/shard_map/ppermute | solution.py:23
  205.2 19.2 %collective-permute-start.21 = (bf16[64,1152]{1,0:T(8,128)(2,1)}, bf16[64,1152]{1,0:T(8,128)(2,1)}, u32[]{:S(2)}, u32[]{:S(2)}) collective-permute-start(bf16[64,1152]{1,0:T(8,128)(2,1)} %gate.24), channel_id=1, source_target_pairs={{0,2},{1,3},{2,0},{3,1},{4,6},{5,7},{6,4},{7,5},{8,10},{9,11},{10,... | collective-permute-start | bytes 442376 | tf_op jit(solution)/shard_map/ppermute | solution.py:23
  205.2 19.2 %collective-permute-start.20 = (bf16[64,1152]{1,0:T(8,128)(2,1)}, bf16[64,1152]{1,0:T(8,128)(2,1)}, u32[]{:S(2)}, u32[]{:S(2)}) collective-permute-start(bf16[64,1152]{1,0:T(8,128)(2,1)} %gate.23), channel_id=1, source_target_pairs={{0,1},{1,0},{2,3},{3,2},{4,5},{5,4},{6,7},{7,6},{8,9},{9,8},{10,11... | collective-permute-start | bytes 442376 | tf_op jit(solution)/shard_map/ppermute | solution.py:23
  225.1 16.4 %all-to-all-start.9 = ((bf16[8,72,640]{2,1,0:T(8,128)(2,1)}), bf16[8,72,640]{2,1,0:T(8,128)(2,1)}, u32[]{:S(2)}, u32[]{:S(2)}) async-start(bf16[8,72,640]{2,1,0:T(8,128)(2,1)} %gate.27), calls=%async_computation.9 | async-start | bytes 1474560 | tf_op jit(solution)/shard_map/all_to_all | solution.py:27
  230.0 24.8 %collective-permute-start.27 = (bf16[256,1152]{1,0:T(8,128)(2,1)}, bf16[256,1152]{1,0:T(8,128)(2,1)}, u32[]{:S(2)}, u32[]{:S(2)}) collective-permute-start(bf16[256,1152]{1,0:T(8,128)(2,1)} %get-tuple-element.118.refs_1_), channel_id=1, source_target_pairs={{0,4},{4,0},{8,12},{12,8},{16,20},{20,16},{24,28},{28,24},{1,5},{5... | collective-permute-start | bytes 1769480 | tf_op jit(solution)/shard_map/ppermute | solution.py:23
  230.4 24.4 %collective-permute-start.30 = (bf16[256,576]{1,0:T(8,128)(2,1)}, bf16[256,576]{1,0:T(8,128)(2,1)}, u32[]{:S(2)}, u32[]{:S(2)}) collective-permute-start(bf16[256,576]{1,0:T(8,128)(2,1)} %get-tuple-element.121.refs_5_), channel_id=1, source_target_pairs={{0,4},{4,0},{8,12},{12,8},{16,20},{20,16},{24,28},{28,24},{1,5},{5... | collective-permute-start | bytes 884744 | tf_op jit(solution)/shard_map/ppermute | solution.py:23
  234.2 14.3 %collective-permute-start.24 = (bf16[64,1152]{1,0:T(8,128)(2,1)}, bf16[64,1152]{1,0:T(8,128)(2,1)}, u32[]{:S(2)}, u32[]{:S(2)}) collective-permute-start(bf16[64,1152]{1,0:T(8,128)(2,1)} %get-tuple-element.106.refs_1_), channel_id=1, source_target_pairs={{0,2},{1,3},{2,0},{3,1},{4,6},{5,7},{6,4},{7,5},{8,10},{9,11},{10,... | collective-permute-start | bytes 442376 | tf_op jit(solution)/shard_map/ppermute | solution.py:23
  248.5 24.4 %all-to-all-start.10 = ((bf16[4,64,1152]{2,1,0:T(8,128)(2,1)}), bf16[4,64,1152]{2,1,0:T(8,128)(2,1)}, u32[]{:S(2)}, u32[]{:S(2)}) async-start(bf16[4,64,1152]{2,1,0:T(8,128)(2,1)} %bitcast.41), calls=%async_computation.10 | async-start | bytes 1179648 | tf_op jit(solution)/shard_map/all_to_all | solution.py:27
  254.6 27.7 %collective-permute-start.38 = (f32[144,1152]{1,0:T(8,128)}, f32[144,1152]{1,0:T(8,128)}, u32[]{:S(2)}, u32[]{:S(2)}) collective-permute-start(f32[144,1152]{1,0:T(8,128)} %slice_select_fusion), channel_id=1, source_target_pairs={{0,4},{4,0},{8,12},{12,8},{16,20},{20,16},{24,28},{28,24},{1,5},{5... | collective-permute-start | bytes 1990664 | tf_op jit(solution)/shard_map/ppermute | solution.py:23
  280.8 15.4 %collective-permute-start.36 = (bf16[288,576]{1,0:T(8,128)(2,1)}, bf16[288,576]{1,0:T(8,128)(2,1)S(1)}, u32[]{:S(2)}, u32[]{:S(2)}) collective-permute-start(bf16[288,576]{1,0:T(8,128)(2,1)} %gate.31), channel_id=1, source_target_pairs={{0,24},{4,28},{8,16},{12,20},{16,8},{20,12},{24,0},{28,4},{1,25},{... | collective-permute-start | bytes 995336 | tf_op jit(solution)/shard_map/ppermute | solution.py:23
  291.7 18.4 %collective-permute-start.33 = (bf16[64,1152]{1,0:T(8,128)(2,1)}, bf16[64,1152]{1,0:T(8,128)(2,1)S(1)}, u32[]{:S(2)}, u32[]{:S(2)}) collective-permute-start(bf16[64,1152]{1,0:T(8,128)(2,1)} %gate.30.refs_0_), channel_id=1, source_target_pairs={{0,1},{1,0},{2,3},{3,2},{4,5},{5,4},{6,7},{7,6},{8,9},{9,8},{10,11... | collective-permute-start | bytes 442376 | tf_op jit(solution)/shard_map/ppermute | solution.py:23
  292.7 17.3 %collective-permute-start.34 = (bf16[64,1152]{1,0:T(8,128)(2,1)}, bf16[64,1152]{1,0:T(8,128)(2,1)}, u32[]{:S(2)}, u32[]{:S(2)}) collective-permute-start(bf16[64,1152]{1,0:T(8,128)(2,1)} %gate.30.refs_0_), channel_id=1, source_target_pairs={{0,2},{1,3},{2,0},{3,1},{4,6},{5,7},{6,4},{7,5},{8,10},{9,11},{10,... | collective-permute-start | bytes 442376 | tf_op jit(solution)/shard_map/ppermute | solution.py:23
  294.1 16.0 %collective-permute-start.35 = (bf16[64,1152]{1,0:T(8,128)(2,1)}, bf16[64,1152]{1,0:T(8,128)(2,1)}, u32[]{:S(2)}, u32[]{:S(2)}) collective-permute-start(bf16[64,1152]{1,0:T(8,128)(2,1)} %gate.30.refs_0_), channel_id=1, source_target_pairs={{0,3},{1,2},{2,1},{3,0},{4,7},{5,6},{6,5},{7,4},{8,11},{9,10},{10,... | collective-permute-start | bytes 442376 | tf_op jit(solution)/shard_map/ppermute | solution.py:23
  (57 other events, 330.5 us)

commit v13 on v12

--- a/solution.py
+++ b/solution.py
@@ -809,9 +809,8 @@
     mod_part = mod_part.reshape(latents * 6, features)
     bias_ada = jnp.tile(b_ada.astype(F32), (latents, 1))
     few_chips = n_dp // 2 == 4
-    mod_sent = gate(jnp.broadcast_to(mod_part[None], (n_dp,) + mod_part.shape))
-    early_rows = gate(early_rows, mod_sent)
-    mod_mine = jnp.sum(exchange(mod_sent, "dp"), axis=0) + bias_ada
+    mod_mine = jnp.sum(gather(mod_part, "dp", n_dp), axis=0) + bias_ada
+    early_rows = gate(early_rows, mod_mine)
     mod_parts = gather(mod_mine, "tensor", n_tensor)
     early_parts = chip_parts(early_rows) if few_chips else [gather_chips(early_rows)]
 

time: 325 us -> 321 us (0.988)
  waiting for transfers between devices: 101 us -> 95.6 us
    all_to_all x12, waiting for transfers between devices: 42.7 us -> 33.7 us  [exchange(): return lax.all_to_all(blocks, axis, 0, 0, tiled=True)]
    ppermute x39, waiting for transfers between devices: 58.5 us -> 61.9 us  [swap(): return lax.ppermute(block, axis, route)]
    unnamed x82 -> x84, local copies, waits for them, and re-layouts: 10.8 us -> 10.7 us
  transfers between devices with their start and end apart: 51 -> 51, of which waited for: 21 -> 23; matrix products, arithmetic and copies ran while one was open for 10% -> 11% of each run, Pallas kernels for 12% -> 12%
where the time goes in v13:
time: 321 us; the launch traced here: 320 us
  waiting for transfers between devices  95.6 us (30%)
  starting transfers between devices  85.1 us (27%)
  Pallas kernels  67.8 us (21%)
  other arithmetic  24.6 us (8%)
  local copies, waits for them, and re-layouts  22.6 us (7%)
  blocking collectives  22.5 us (7%)
    ppermute x39, waiting for transfers between devices, swap(): return lax.ppermute(block, axis, route)  61.9 us
    pallas_call x13, Pallas kernels, call(): pl.pallas_call(kernel, out_shape=tuple((jax.ShapeDtypeStruct(shape, kind)...  54.6 us
    all_to_all x12, starting transfers between devices, exchange(): return lax.all_to_all(blocks, axis, 0, 0, tiled=True)  53 us
    all_to_all x12, waiting for transfers between devices, exchange(): return lax.all_to_all(blocks, axis, 0, 0, tiled=True)  33.7 us
    ppermute x39, starting transfers between devices, swap(): return lax.ppermute(block, axis, route)  32.1 us
    all_to_all x2, blocking collectives, exchange(): return lax.all_to_all(blocks, axis, 0, 0, tiled=True)  22.5 us
    unnamed x84, local copies, waits for them, and re-layouts  10.7 us
    pallas_call x1, Pallas kernels, attend_backward(): pl.pallas_call(lambda *refs: backward_kernel(meta.shape[0] - 1, *refs), o...  7.18 us
  transfers between devices with their start and end apart: 51, of which 23 were waited for; matrix products, arithmetic and copies ran while one was open for 11% of the time, Pallas kernels for 12%

profile of v13, /device:TPU:0, one launch (start us, length us, event | category | flops | bytes accessed | tf_op | source)
XLA Modules:
  0.0 319.5 jit_solution(641368621807076920)
XLA Ops:
  7.3 4.8 %all-to-all-start = ((f32[8,18,288]{2,1,0:T(8,128)}), f32[8,18,288]{2,1,0:T(8,128)S(1)}, u32[]{:S(2)}, u32[]{:S(2)}) async-start(f32[8,18,288]{2,1,0:T(8,128)} %broadcast_in_dim.14), calls=%async_computation | async-start | bytes 589824 | tf_op jit(solution)/shard_map/all_to_all | solution.py:27
  12.2 7.3 %all-to-all-done = f32[8,18,288]{2,1,0:T(8,128)S(1)} async-done(((f32[8,18,288]{2,1,0:T(8,128)}), f32[8,18,288]{2,1,0:T(8,128)S(1)}, u32[]{:S(2)}, u32[]{:S(2)}) %all-to-all-start) | async-done | bytes 165920 | tf_op jit(solution)/shard_map/all_to_all | solution.py:27
  24.6 11.4 %all_to_all.70.refs_4_.refs_11_ = f32[4,18,288]{2,1,0:T(8,128)} all-to-all(f32[4,18,288]{2,1,0:T(8,128)S(1)} %broadcast_in_dim.15), channel_id=1, replica_groups=mesh['dp'=8,'tensor'=4] {'tensor'}, dimensions={0} | all-to-all | bytes 165888 | tf_op jit(solution)/shard_map/all_to_all | solution.py:27
  36.0 3.9 %collective-permute-done.3.refs_2_ = bf16[288,576]{1,0:T(8,128)(2,1)S(1)} collective-permute-done((bf16[288,576]{1,0:T(8,128)(2,1)}, bf16[288,576]{1,0:T(8,128)(2,1)S(1)}, u32[]{:S(2)}, u32[]{:S(2)}) %collective-permute-start.3) | collective-permute-done | bytes 331808 | tf_op jit(solution)/shard_map/ppermute | solution.py:23
  45.0 6.1 %project.1 = (bf16[256,1152]{1,0:T(8,128)(2,1)}, bf16[256,1152]{1,0:T(8,128)(2,1)}, bf16[8,72,640]{2,1,0:T(8,128)(2,1)}, bf16[1152,576]{1,0:T(8,128)(2,1)}, bf16...) custom-call(s32[7]{0:T(128)} %concatenate.24.refs_0_, bf16[288,576]{1,0:T(8,128)(2,1)} %get-tuple-element.78.refs_1_, ...), custom_call_target="tpu_custom_call" | custom-call | flops 1 | bytes 1 | tf_op jit(solution)/shard_map/project/pallas_call | solution.py:366
  51.2 4.4 %all-to-all-start.2 = ((bf16[8,72,640]{2,1,0:T(8,128)(2,1)}), bf16[8,72,640]{2,1,0:T(8,128)(2,1)}, u32[]{:S(2)}, u32[]{:S(2)}) async-start(bf16[8,72,640]{2,1,0:T(8,128)(2,1)} %get-tuple-element.82), calls=%async_computation.2 | async-start | bytes 1474560 | tf_op jit(solution)/shard_map/all_to_all | solution.py:27
  57.3 10.3 %all-to-all-done.2.refs_1_ = bf16[8,72,640]{2,1,0:T(8,128)(2,1)} async-done(((bf16[8,72,640]{2,1,0:T(8,128)(2,1)}), bf16[8,72,640]{2,1,0:T(8,128)(2,1)}, u32[]{:S(2)}, u32[]{:S(2)}) %all-to-all-start.2) | async-done | bytes 737312 | tf_op jit(solution)/shard_map/all_to_all | solution.py:27
  67.6 6.0 %attend_forward.1 = (bf16[8,72,128]{2,1,0:T(8,128)(2,1)}, f32[8,72,128]{2,1,0:T(8,128)}, f32[8,1,128]{2,1,0:T(1,128)}) custom-call(s32[4]{0:T(128)} %pad_add_fusion.refs_0_, bf16[8,72,640]{2,1,0:T(8,128)(2,1)} %all-to-all-done.2.refs_1_), custom_call_target="tpu_custom_call" | custom-call | flops 1000000000 | bytes 4000000 | tf_op jit(solution)/shard_map/attend_forward/pallas_call | solution.py:214
  73.6 3.4 %all-to-all-start.3 = ((bf16[8,72,128]{2,1,0:T(8,128)(2,1)}), bf16[8,72,128]{2,1,0:T(8,128)(2,1)S(1)}, u32[]{:S(2)}, u32[]{:S(2)}) async-start(bf16[8,72,128]{2,1,0:T(8,128)(2,1)} %get-tuple-element.83), calls=%async_computation.3 | async-start | bytes 294912 | tf_op jit(solution)/shard_map/all_to_all | solution.py:27
  79.1 3.5 %all-to-all-done.3.refs_1_ = bf16[8,72,128]{2,1,0:T(8,128)(2,1)S(1)} async-done(((bf16[8,72,128]{2,1,0:T(8,128)(2,1)}), bf16[8,72,128]{2,1,0:T(8,128)(2,1)S(1)}, u32[]{:S(2)}, u32[]{:S(2)}) %all-to-all-start.3) | async-done | bytes 147488 | tf_op jit(solution)/shard_map/all_to_all | solution.py:27
  86.3 5.0 %all-to-all-start.4 = ((bf16[4,64,1152]{2,1,0:T(8,128)(2,1)}), bf16[4,64,1152]{2,1,0:T(8,128)(2,1)}, u32[]{:S(2)}, u32[]{:S(2)}) async-start(bf16[4,64,1152]{2,1,0:T(8,128)(2,1)} %bitcast.43), calls=%async_computation.4 | async-start | bytes 1179648 | tf_op jit(solution)/shard_map/all_to_all | solution.py:27
  93.9 14.8 %collective-permute-done.10.refs_6_.refs_3_ = bf16[288,1152]{1,0:T(8,128)(2,1)} collective-permute-done((bf16[288,1152]{1,0:T(8,128)(2,1)}, bf16[288,1152]{1,0:T(8,128)(2,1)}, u32[]{:S(2)}, u32[]{:S(2)}) %collective-permute-start.10) | collective-permute-done | bytes 663584 | tf_op jit(solution)/shard_map/ppermute | solution.py:23
  111.6 4.9 %all-to-all-start.5 = ((bf16[4,64,1152]{2,1,0:T(8,128)(2,1)}), bf16[4,64,1152]{2,1,0:T(8,128)(2,1)S(1)}, u32[]{:S(2)}, u32[]{:S(2)}) async-start(bf16[4,64,1152]{2,1,0:T(8,128)(2,1)} %get-tuple-element.88), calls=%async_computation.5 | async-start | bytes 1179648 | tf_op jit(solution)/shard_map/all_to_all | solution.py:27
  119.4 13.5 %collective-permute-done.11.refs_0_ = bf16[288,1152]{1,0:T(8,128)(2,1)S(1)} collective-permute-done((bf16[288,1152]{1,0:T(8,128)(2,1)}, bf16[288,1152]{1,0:T(8,128)(2,1)S(1)}, u32[]{:S(2)}, u32[]{:S(2)}) %collective-permute-start.11) | collective-permute-done | bytes 663584 | tf_op jit(solution)/shard_map/ppermute | solution.py:23
  136.4 10.7 %mlp.1 = (bf16[256,1152]{1,0:T(8,128)(2,1)}, bf16[256,1152]{1,0:T(8,128)(2,1)}, bf16[256,1152]{1,0:T(8,128)(2,1)}, f32[1,1152]{1,0:T(1,128)}, bf16[256,1152]{1,0...) custom-call(s32[7]{0:T(128)} %concatenate.24.refs_0_, ...), custom_call_target="tpu_custom_call" | custom-call | flops 1 | bytes 1 | tf_op jit(solution)/shard_map/mlp/pallas_call | solution.py:366
  147.1 4.8 %all-to-all-start.6 = ((bf16[4,64,1152]{2,1,0:T(8,128)(2,1)}), bf16[4,64,1152]{2,1,0:T(8,128)(2,1)}, u32[]{:S(2)}, u32[]{:S(2)}) async-start(bf16[4,64,1152]{2,1,0:T(8,128)(2,1)} %bitcast.42), calls=%async_computation.6 | async-start | bytes 1179648 | tf_op jit(solution)/shard_map/all_to_all | solution.py:27
  155.1 5.8 %late_weights.1 = (bf16[288,1152]{1,0:T(8,128)(2,1)}, bf16[288,1152]{1,0:T(8,128)(2,1)}, bf16[288,1152]{1,0:T(8,128)(2,1)}, bf16[288,1152]{1,0:T(8,128)(2,1)}) custom-call(s32[7]{0:T(128)} %concatenate.24.refs_0_, bf16[256,1152]{1,0:T(8,128)(2,1)} %bitcast.39, bf16[256,1152]{1,0:T(8,128)(2,1)} %get-tuple-element.89.refs_10_.refs_2_, ...), custom_call_target="tpu_custom_call" | custom-call | flops 1 | bytes 1 | tf_op jit(solution)/shard_map/late_weights/pallas_call | solution.py:366
  160.9 7.5 %all-to-all-done.6.refs_1_ = bf16[4,64,1152]{2,1,0:T(8,128)(2,1)} async-done(((bf16[4,64,1152]{2,1,0:T(8,128)(2,1)}), bf16[4,64,1152]{2,1,0:T(8,128)(2,1)}, u32[]{:S(2)}, u32[]{:S(2)}) %all-to-all-start.6) | async-done | bytes 589856 | tf_op jit(solution)/shard_map/all_to_all | solution.py:27
  171.5 4.2 %all-to-all-start.7 = ((bf16[4,64,1152]{2,1,0:T(8,128)(2,1)}), bf16[4,64,1152]{2,1,0:T(8,128)(2,1)}, u32[]{:S(2)}, u32[]{:S(2)}) async-start(bf16[4,64,1152]{2,1,0:T(8,128)(2,1)} %get-tuple-element.102), calls=%async_computation.7 | async-start | bytes 1179648 | tf_op jit(solution)/shard_map/all_to_all | solution.py:27
  177.9 14.2 %collective-permute-done.18.refs_3_ = bf16[288,1152]{1,0:T(8,128)(2,1)} collective-permute-done((bf16[288,1152]{1,0:T(8,128)(2,1)}, bf16[288,1152]{1,0:T(8,128)(2,1)}, u32[]{:S(2)}, u32[]{:S(2)}) %collective-permute-start.18) | collective-permute-done | bytes 663584 | tf_op jit(solution)/shard_map/ppermute | solution.py:23
  197.5 3.4 %collective-permute-start.22 = (bf16[64,1152]{1,0:T(8,128)(2,1)}, bf16[64,1152]{1,0:T(8,128)(2,1)S(1)}, u32[]{:S(2)}, u32[]{:S(2)}) collective-permute-start(bf16[64,1152]{1,0:T(8,128)(2,1)} %gate.23), channel_id=1, source_target_pairs={{0,3},{1,2},{2,1},{3,0},{4,7},{5,6},{6,5},{7,4},{8,11},{9,10},{10,... | collective-permute-start | bytes 442376 | tf_op jit(solution)/shard_map/ppermute | solution.py:23
  201.9 11.0 %all_to_all.71.refs_2_ = bf16[8,72,128]{2,1,0:T(8,128)(2,1)} all-to-all(bf16[8,72,128]{2,1,0:T(8,128)(2,1)S(1)} %copy-done.7), channel_id=1, replica_groups=mesh['dp'=8,'tensor'=4] {'dp'}, dimensions={0} | all-to-all | bytes 294912 | tf_op jit(solution)/shard_map/all_to_all | solution.py:27
  213.0 7.2 %attend_backward.1.refs_0_ = bf16[8,72,640]{2,1,0:T(8,128)(2,1)} custom-call(s32[4]{0:T(128)} %pad_add_fusion.refs_0_, bf16[8,72,640]{2,1,0:T(8,128)(2,1)} %all-to-all-done.2.refs_1_, bf16[8,72,128]{2,1,0:T(8,128)(2,1)} %all_to_all.71.refs_2_, f32[8,72,128]{2,1,0:T(8,128)} %get-tuple-element.107.refs_3_, f32[8,1,128]{2,1,0:T(1,128)} %get-tuple-element.108.refs_4_), custom_call_target="tpu_custom_call" | custom-call | flops 1 | bytes 1 | tf_op jit(solution)/shard_map/attend_backward/pallas_call | solution.py:238
  220.8 4.3 %all-to-all-start.9 = ((bf16[8,72,640]{2,1,0:T(8,128)(2,1)}), bf16[8,72,640]{2,1,0:T(8,128)(2,1)}, u32[]{:S(2)}, u32[]{:S(2)}) async-start(bf16[8,72,640]{2,1,0:T(8,128)(2,1)} %gate.25), calls=%async_computation.9 | async-start | bytes 1474560 | tf_op jit(solution)/shard_map/all_to_all | solution.py:27
  233.0 3.1 convert_add_fusion
  237.2 5.1 %unspread.1 = (bf16[256,1152]{1,0:T(8,128)(2,1)}, bf16[256,576]{1,0:T(8,128)(2,1)}, bf16[256,576]{1,0:T(8,128)(2,1)}, bf16[256,576]{1,0:T(8,128)(2,1)}, f32[2,576]{1,0:T(2,128)}) custom-call(s32[7]{0:T(128)} %concatenate.24.refs_0_, bf16[8,72,640]{2,1,0:T(8,128)(2,1)} %all-to-all-done.9.refs_1_, bf16[1152,576]{1,0:T(8,128)(2,1)} %get-tuple-element.109.refs_2_, ...), custom_call_target="tpu_custom_call" | custom-call | flops 20000000000 | bytes 1 | tf_op jit(solution)/shard_map/unspread/pallas_call | solution.py:366
  244.3 5.1 %all-to-all-start.10 = ((bf16[4,64,1152]{2,1,0:T(8,128)(2,1)}), bf16[4,64,1152]{2,1,0:T(8,128)(2,1)}, u32[]{:S(2)}, u32[]{:S(2)}) async-start(bf16[4,64,1152]{2,1,0:T(8,128)(2,1)} %bitcast.41), calls=%async_computation.10 | async-start | bytes 1179648 | tf_op jit(solution)/shard_map/all_to_all | solution.py:27
  250.6 4.9 %early_weights.1 = (bf16[288,576]{1,0:T(8,128)(2,1)}, bf16[288,576]{1,0:T(8,128)(2,1)}, bf16[288,576]{1,0:T(8,128)(2,1)}, bf16[288,576]{1,0:T(8,128)(2,1)}) custom-call(s32[7]{0:T(128)} %concatenate.24.refs_0_, bf16[256,1152]{1,0:T(8,128)(2,1)} %get-tuple-element.118.refs_1_, bf16[256,1152]{1,0:T(8,128)(2,1)} %bitcast.11.refs_1_.refs_2_, ...), custom_call_target="tpu_custom_call" | custom-call | flops 1 | bytes 1 | tf_op jit(solution)/shard_map/early_weights/pallas_call | solution.py:366
  259.7 7.1 %collective-permute-done.31.refs_11_ = bf16[288,576]{1,0:T(8,128)(2,1)} collective-permute-done((bf16[288,576]{1,0:T(8,128)(2,1)}, bf16[288,576]{1,0:T(8,128)(2,1)}, u32[]{:S(2)}, u32[]{:S(2)}) %collective-permute-start.31) | collective-permute-done | bytes 331808 | tf_op jit(solution)/shard_map/ppermute | solution.py:23
  271.4 5.1 %all-to-all-start.11 = ((f32[4,18,288]{2,1,0:T(8,128)}), f32[4,18,288]{2,1,0:T(8,128)S(1)}, u32[]{:S(2)}, u32[]{:S(2)}) async-start(f32[4,18,288]{2,1,0:T(8,128)} %get-tuple-element.126.refs_1_), calls=%async_computation.11 | async-start | bytes 294912 | tf_op jit(solution)/shard_map/all_to_all | solution.py:27
  283.8 3.7 %all-to-all-start.12 = ((f32[8,32,288]{2,1,0:T(8,128)}), f32[8,32,288]{2,1,0:T(8,128)S(1)}, u32[]{:S(2)}, u32[]{:S(2)}) async-start(f32[8,32,288]{2,1,0:T(8,128)} %gate.27.refs_1_), calls=%async_computation.12 | async-start | bytes 786432 | tf_op jit(solution)/shard_map/all_to_all | solution.py:27
  300.7 3.3 %all-to-all-start.13 = ((f32[32,1,432]{2,1,0:T(1,128)}), f32[32,1,432]{2,1,0:T(1,128)}, u32[]{:S(2)}, u32[]{:S(2)}) async-start(f32[32,1,432]{2,1,0:T(1,128)} %reshape.119), calls=%async_computation.13 | async-start | bytes 131072 | tf_op jit(solution)/shard_map/all_to_all | solution.py:27
  (242 shorter events, 108.5 us)
Async XLA Ops:
  3.1 17.0 %collective-permute-start.1 = (bf16[144,576]{1,0:T(8,128)(2,1)S(1)}, bf16[144,576]{1,0:T(8,128)(2,1)S(1)}, u32[]{:S(2)}, u32[]{:S(2)}) collective-permute-start(bf16[144,576]{1,0:T(8,128)(2,1)S(1)} %broadcast_select_fusion.7), channel_id=1, source_target_pairs={{0,4},{4,0},{8,12},{12,8},{16,20},{20,16},{24,28},{28,24},{1,5},{5... | collective-permute-start | bytes 497672 | tf_op jit(solution)/shard_map/ppermute | solution.py:23
  21.1 15.0 %collective-permute-start.2 = (bf16[288,576]{1,0:T(8,128)(2,1)}, bf16[288,576]{1,0:T(8,128)(2,1)S(1)}, u32[]{:S(2)}, u32[]{:S(2)}) collective-permute-start(bf16[288,576]{1,0:T(8,128)(2,1)} %gate.16.refs_0_), channel_id=1, source_target_pairs={{0,8},{4,12},{8,0},{12,4},{16,24},{20,28},{24,16},{28,20},{1,9},{5... | collective-permute-start | bytes 995336 | tf_op jit(solution)/shard_map/ppermute | solution.py:23
  21.6 18.3 %collective-permute-start.3 = (bf16[288,576]{1,0:T(8,128)(2,1)}, bf16[288,576]{1,0:T(8,128)(2,1)S(1)}, u32[]{:S(2)}, u32[]{:S(2)}) collective-permute-start(bf16[288,576]{1,0:T(8,128)(2,1)} %gate.16.refs_0_), channel_id=1, source_target_pairs={{0,16},{4,20},{8,24},{12,28},{16,0},{20,4},{24,8},{28,12},{1,17},{... | collective-permute-start | bytes 995336 | tf_op jit(solution)/shard_map/ppermute | solution.py:23
  22.2 17.7 %collective-permute-start.4 = (bf16[288,576]{1,0:T(8,128)(2,1)}, bf16[288,576]{1,0:T(8,128)(2,1)S(1)}, u32[]{:S(2)}, u32[]{:S(2)}) collective-permute-start(bf16[288,576]{1,0:T(8,128)(2,1)} %gate.16.refs_0_), channel_id=1, source_target_pairs={{0,24},{4,28},{8,16},{12,20},{16,8},{20,12},{24,0},{28,4},{1,25},{... | collective-permute-start | bytes 995336 | tf_op jit(solution)/shard_map/ppermute | solution.py:23
  51.2 16.4 %all-to-all-start.2 = ((bf16[8,72,640]{2,1,0:T(8,128)(2,1)}), bf16[8,72,640]{2,1,0:T(8,128)(2,1)}, u32[]{:S(2)}, u32[]{:S(2)}) async-start(bf16[8,72,640]{2,1,0:T(8,128)(2,1)} %get-tuple-element.82), calls=%async_computation.2 | async-start | bytes 1474560 | tf_op jit(solution)/shard_map/all_to_all | solution.py:27
  56.3 20.6 %collective-permute-start = (bf16[144,1152]{1,0:T(8,128)(2,1)}, bf16[144,1152]{1,0:T(8,128)(2,1)}, u32[]{:S(2)}, u32[]{:S(2)}) collective-permute-start(bf16[144,1152]{1,0:T(8,128)(2,1)} %bitcast_select_fusion), channel_id=1, source_target_pairs={{0,4},{4,0},{8,12},{12,8},{16,20},{20,16},{24,28},{28,24},{1,5},{5... | collective-permute-start | bytes 995336 | tf_op jit(solution)/shard_map/ppermute | solution.py:23
  86.3 22.7 %all-to-all-start.4 = ((bf16[4,64,1152]{2,1,0:T(8,128)(2,1)}), bf16[4,64,1152]{2,1,0:T(8,128)(2,1)}, u32[]{:S(2)}, u32[]{:S(2)}) async-start(bf16[4,64,1152]{2,1,0:T(8,128)(2,1)} %bitcast.43), calls=%async_computation.4 | async-start | bytes 1179648 | tf_op jit(solution)/shard_map/all_to_all | solution.py:27
  92.2 16.5 %collective-permute-start.10 = (bf16[288,1152]{1,0:T(8,128)(2,1)}, bf16[288,1152]{1,0:T(8,128)(2,1)}, u32[]{:S(2)}, u32[]{:S(2)}) collective-permute-start(bf16[288,1152]{1,0:T(8,128)(2,1)} %gate.18.refs_1_), channel_id=1, source_target_pairs={{0,16},{4,20},{8,24},{12,28},{16,0},{20,4},{24,8},{28,12},{1,17},{... | collective-permute-start | bytes 1990664 | tf_op jit(solution)/shard_map/ppermute | solution.py:23
  92.7 16.2 %collective-permute-start.9 = (bf16[288,1152]{1,0:T(8,128)(2,1)}, bf16[288,1152]{1,0:T(8,128)(2,1)}, u32[]{:S(2)}, u32[]{:S(2)}) collective-permute-start(bf16[288,1152]{1,0:T(8,128)(2,1)} %gate.18.refs_1_), channel_id=1, source_target_pairs={{0,8},{4,12},{8,0},{12,4},{16,24},{20,28},{24,16},{28,20},{1,9},{5... | collective-permute-start | bytes 1990664 | tf_op jit(solution)/shard_map/ppermute | solution.py:23
  111.6 21.3 %all-to-all-start.5 = ((bf16[4,64,1152]{2,1,0:T(8,128)(2,1)}), bf16[4,64,1152]{2,1,0:T(8,128)(2,1)S(1)}, u32[]{:S(2)}, u32[]{:S(2)}) async-start(bf16[4,64,1152]{2,1,0:T(8,128)(2,1)} %get-tuple-element.88), calls=%async_computation.5 | async-start | bytes 1179648 | tf_op jit(solution)/shard_map/all_to_all | solution.py:27
  117.3 15.5 %collective-permute-start.11 = (bf16[288,1152]{1,0:T(8,128)(2,1)}, bf16[288,1152]{1,0:T(8,128)(2,1)S(1)}, u32[]{:S(2)}, u32[]{:S(2)}) collective-permute-start(bf16[288,1152]{1,0:T(8,128)(2,1)} %gate.19), channel_id=1, source_target_pairs={{0,24},{4,28},{8,16},{12,20},{16,8},{20,12},{24,0},{28,4},{1,25},{... | collective-permute-start | bytes 1990664 | tf_op jit(solution)/shard_map/ppermute | solution.py:23
  118.9 15.6 %collective-permute-start.12 = (bf16[288,1152]{1,0:T(8,128)(2,1)S(1)}, bf16[288,1152]{1,0:T(8,128)(2,1)S(1)}, u32[]{:S(2)}, u32[]{:S(2)}) collective-permute-start(bf16[288,1152]{1,0:T(8,128)(2,1)S(1)} %copy-done.1), channel_id=1, source_target_pairs={{0,4},{4,0},{8,12},{12,8},{16,20},{20,16},{24,28},{28,24},{1,5},{5... | collective-permute-start | bytes 1990664 | tf_op jit(solution)/shard_map/ppermute | solution.py:23
  118.9 16.5 %collective-permute-start.13 = (bf16[288,1152]{1,0:T(8,128)(2,1)}, bf16[288,1152]{1,0:T(8,128)(2,1)S(1)}, u32[]{:S(2)}, u32[]{:S(2)}) collective-permute-start(bf16[288,1152]{1,0:T(8,128)(2,1)} %collective-permute-done.9.refs_5_.refs_2_), channel_id=1, source_target_pairs={{0,4},{4,0},{8,12},{12,8},{16,20},{20,16},{24,28},{28,24},{1,5},{5... | collective-permute-start | bytes 1990664 | tf_op jit(solution)/shard_map/ppermute | solution.py:23
  119.4 16.8 %collective-permute-start.14 = (bf16[288,1152]{1,0:T(8,128)(2,1)}, bf16[288,1152]{1,0:T(8,128)(2,1)}, u32[]{:S(2)}, u32[]{:S(2)}) collective-permute-start(bf16[288,1152]{1,0:T(8,128)(2,1)} %collective-permute-done.10.refs_6_.refs_3_), channel_id=1, source_target_pairs={{0,4},{4,0},{8,12},{12,8},{16,20},{20,16},{24,28},{28,24},{1,5},{5... | collective-permute-start | bytes 1990664 | tf_op jit(solution)/shard_map/ppermute | solution.py:23
  147.1 21.4 %all-to-all-start.6 = ((bf16[4,64,1152]{2,1,0:T(8,128)(2,1)}), bf16[4,64,1152]{2,1,0:T(8,128)(2,1)}, u32[]{:S(2)}, u32[]{:S(2)}) async-start(bf16[4,64,1152]{2,1,0:T(8,128)(2,1)} %bitcast.42), calls=%async_computation.6 | async-start | bytes 1179648 | tf_op jit(solution)/shard_map/all_to_all | solution.py:27
  171.5 21.0 %all-to-all-start.7 = ((bf16[4,64,1152]{2,1,0:T(8,128)(2,1)}), bf16[4,64,1152]{2,1,0:T(8,128)(2,1)}, u32[]{:S(2)}, u32[]{:S(2)}) async-start(bf16[4,64,1152]{2,1,0:T(8,128)(2,1)} %get-tuple-element.102), calls=%async_computation.7 | async-start | bytes 1179648 | tf_op jit(solution)/shard_map/all_to_all | solution.py:27
  175.6 16.4 %collective-permute-start.18 = (bf16[288,1152]{1,0:T(8,128)(2,1)}, bf16[288,1152]{1,0:T(8,128)(2,1)}, u32[]{:S(2)}, u32[]{:S(2)}) collective-permute-start(bf16[288,1152]{1,0:T(8,128)(2,1)} %get-tuple-element.99.refs_7_), channel_id=1, source_target_pairs={{0,8},{4,12},{8,0},{12,4},{16,24},{20,28},{24,16},{28,20},{1,9},{5... | collective-permute-start | bytes 1990664 | tf_op jit(solution)/shard_map/ppermute | solution.py:23
  176.4 16.1 %collective-permute-start.19 = (bf16[288,1152]{1,0:T(8,128)(2,1)}, bf16[288,1152]{1,0:T(8,128)(2,1)}, u32[]{:S(2)}, u32[]{:S(2)}) collective-permute-start(bf16[288,1152]{1,0:T(8,128)(2,1)} %get-tuple-element.100.refs_8_), channel_id=1, source_target_pairs={{0,16},{4,20},{8,24},{12,28},{16,0},{20,4},{24,8},{28,12},{1,17},{... | collective-permute-start | bytes 1990664 | tf_op jit(solution)/shard_map/ppermute | solution.py:23
  195.3 24.8 %collective-permute-start.26 = (bf16[288,1152]{1,0:T(8,128)(2,1)}, bf16[288,1152]{1,0:T(8,128)(2,1)}, u32[]{:S(2)}, u32[]{:S(2)}) collective-permute-start(bf16[288,1152]{1,0:T(8,128)(2,1)} %gate.24), channel_id=1, source_target_pairs={{0,24},{4,28},{8,16},{12,20},{16,8},{20,12},{24,0},{28,4},{1,25},{... | collective-permute-start | bytes 1990664 | tf_op jit(solution)/shard_map/ppermute | solution.py:23
  197.5 22.6 %collective-permute-start.22 = (bf16[64,1152]{1,0:T(8,128)(2,1)}, bf16[64,1152]{1,0:T(8,128)(2,1)S(1)}, u32[]{:S(2)}, u32[]{:S(2)}) collective-permute-start(bf16[64,1152]{1,0:T(8,128)(2,1)} %gate.23), channel_id=1, source_target_pairs={{0,3},{1,2},{2,1},{3,0},{4,7},{5,6},{6,5},{7,4},{8,11},{9,10},{10,... | collective-permute-start | bytes 442376 | tf_op jit(solution)/shard_map/ppermute | solution.py:23
  201.0 19.2 %collective-permute-start.21 = (bf16[64,1152]{1,0:T(8,128)(2,1)}, bf16[64,1152]{1,0:T(8,128)(2,1)}, u32[]{:S(2)}, u32[]{:S(2)}) collective-permute-start(bf16[64,1152]{1,0:T(8,128)(2,1)} %gate.22), channel_id=1, source_target_pairs={{0,2},{1,3},{2,0},{3,1},{4,6},{5,7},{6,4},{7,5},{8,10},{9,11},{10,... | collective-permute-start | bytes 442376 | tf_op jit(solution)/shard_map/ppermute | solution.py:23
  201.0 19.2 %collective-permute-start.20 = (bf16[64,1152]{1,0:T(8,128)(2,1)}, bf16[64,1152]{1,0:T(8,128)(2,1)}, u32[]{:S(2)}, u32[]{:S(2)}) collective-permute-start(bf16[64,1152]{1,0:T(8,128)(2,1)} %gate.21), channel_id=1, source_target_pairs={{0,1},{1,0},{2,3},{3,2},{4,5},{5,4},{6,7},{7,6},{8,9},{9,8},{10,11... | collective-permute-start | bytes 442376 | tf_op jit(solution)/shard_map/ppermute | solution.py:23
  220.8 16.4 %all-to-all-start.9 = ((bf16[8,72,640]{2,1,0:T(8,128)(2,1)}), bf16[8,72,640]{2,1,0:T(8,128)(2,1)}, u32[]{:S(2)}, u32[]{:S(2)}) async-start(bf16[8,72,640]{2,1,0:T(8,128)(2,1)} %gate.25), calls=%async_computation.9 | async-start | bytes 1474560 | tf_op jit(solution)/shard_map/all_to_all | solution.py:27
  225.8 24.8 %collective-permute-start.27 = (bf16[256,1152]{1,0:T(8,128)(2,1)}, bf16[256,1152]{1,0:T(8,128)(2,1)}, u32[]{:S(2)}, u32[]{:S(2)}) collective-permute-start(bf16[256,1152]{1,0:T(8,128)(2,1)} %get-tuple-element.118.refs_1_), channel_id=1, source_target_pairs={{0,4},{4,0},{8,12},{12,8},{16,20},{20,16},{24,28},{28,24},{1,5},{5... | collective-permute-start | bytes 1769480 | tf_op jit(solution)/shard_map/ppermute | solution.py:23
  226.1 24.4 %collective-permute-start.30 = (bf16[256,576]{1,0:T(8,128)(2,1)}, bf16[256,576]{1,0:T(8,128)(2,1)}, u32[]{:S(2)}, u32[]{:S(2)}) collective-permute-start(bf16[256,576]{1,0:T(8,128)(2,1)} %get-tuple-element.121.refs_5_), channel_id=1, source_target_pairs={{0,4},{4,0},{8,12},{12,8},{16,20},{20,16},{24,28},{28,24},{1,5},{5... | collective-permute-start | bytes 884744 | tf_op jit(solution)/shard_map/ppermute | solution.py:23
  230.0 14.3 %collective-permute-start.24 = (bf16[64,1152]{1,0:T(8,128)(2,1)}, bf16[64,1152]{1,0:T(8,128)(2,1)}, u32[]{:S(2)}, u32[]{:S(2)}) collective-permute-start(bf16[64,1152]{1,0:T(8,128)(2,1)} %get-tuple-element.106.refs_1_), channel_id=1, source_target_pairs={{0,2},{1,3},{2,0},{3,1},{4,6},{5,7},{6,4},{7,5},{8,10},{9,11},{10,... | collective-permute-start | bytes 442376 | tf_op jit(solution)/shard_map/ppermute | solution.py:23
  244.3 24.4 %all-to-all-start.10 = ((bf16[4,64,1152]{2,1,0:T(8,128)(2,1)}), bf16[4,64,1152]{2,1,0:T(8,128)(2,1)}, u32[]{:S(2)}, u32[]{:S(2)}) async-start(bf16[4,64,1152]{2,1,0:T(8,128)(2,1)} %bitcast.41), calls=%async_computation.10 | async-start | bytes 1179648 | tf_op jit(solution)/shard_map/all_to_all | solution.py:27
  250.3 27.7 %collective-permute-start.38 = (f32[144,1152]{1,0:T(8,128)}, f32[144,1152]{1,0:T(8,128)}, u32[]{:S(2)}, u32[]{:S(2)}) collective-permute-start(f32[144,1152]{1,0:T(8,128)} %slice_select_fusion), channel_id=1, source_target_pairs={{0,4},{4,0},{8,12},{12,8},{16,20},{20,16},{24,28},{28,24},{1,5},{5... | collective-permute-start | bytes 1990664 | tf_op jit(solution)/shard_map/ppermute | solution.py:23
  276.5 15.4 %collective-permute-start.36 = (bf16[288,576]{1,0:T(8,128)(2,1)}, bf16[288,576]{1,0:T(8,128)(2,1)S(1)}, u32[]{:S(2)}, u32[]{:S(2)}) collective-permute-start(bf16[288,576]{1,0:T(8,128)(2,1)} %gate.29), channel_id=1, source_target_pairs={{0,24},{4,28},{8,16},{12,20},{16,8},{20,12},{24,0},{28,4},{1,25},{... | collective-permute-start | bytes 995336 | tf_op jit(solution)/shard_map/ppermute | solution.py:23
  287.5 18.4 %collective-permute-start.33 = (bf16[64,1152]{1,0:T(8,128)(2,1)}, bf16[64,1152]{1,0:T(8,128)(2,1)S(1)}, u32[]{:S(2)}, u32[]{:S(2)}) collective-permute-start(bf16[64,1152]{1,0:T(8,128)(2,1)} %gate.28.refs_0_), channel_id=1, source_target_pairs={{0,1},{1,0},{2,3},{3,2},{4,5},{5,4},{6,7},{7,6},{8,9},{9,8},{10,11... | collective-permute-start | bytes 442376 | tf_op jit(solution)/shard_map/ppermute | solution.py:23
  288.5 17.4 %collective-permute-start.34 = (bf16[64,1152]{1,0:T(8,128)(2,1)}, bf16[64,1152]{1,0:T(8,128)(2,1)}, u32[]{:S(2)}, u32[]{:S(2)}) collective-permute-start(bf16[64,1152]{1,0:T(8,128)(2,1)} %gate.28.refs_0_), channel_id=1, source_target_pairs={{0,2},{1,3},{2,0},{3,1},{4,6},{5,7},{6,4},{7,5},{8,10},{9,11},{10,... | collective-permute-start | bytes 442376 | tf_op jit(solution)/shard_map/ppermute | solution.py:23
  289.8 16.0 %collective-permute-start.35 = (bf16[64,1152]{1,0:T(8,128)(2,1)}, bf16[64,1152]{1,0:T(8,128)(2,1)}, u32[]{:S(2)}, u32[]{:S(2)}) collective-permute-start(bf16[64,1152]{1,0:T(8,128)(2,1)} %gate.28.refs_0_), channel_id=1, source_target_pairs={{0,3},{1,2},{2,1},{3,0},{4,7},{5,6},{6,5},{7,4},{8,11},{9,10},{10,... | collective-permute-start | bytes 442376 | tf_op jit(solution)/shard_map/ppermute | solution.py:23
  (58 other events, 327.2 us)
